TPU v7x, 32 devices: a whole 2x2x4 slice. The times are simulated.
32 devices in a mesh: section: 2 (over x), dp: 16 (over z, y, core).
Axes of the slice: x: 2, y: 2, z: 4, core: 2. Of those that a mesh axis runs over, the one named last changes fastest.
Arguments:
- chars: bfloat16 [2, 16, 64, 16, 256], P(None, 'dp'), may hold values from -6 to 6
- counts: int32 [2, 16, 64], P(None, 'dp'), may hold values from 1 to 16
- languages: int32 [2, 16], P(None, 'dp'), may hold values from 0 to 7
- language_table: bfloat16 [8, 256], replicated, may hold values from -6 to 6
- char_gain_attn: float32 [256], replicated, may hold values from 0.5 to 1.5
- char_project: bfloat16 [256, 768], replicated, may hold values from -0.375 to 0.375
- char_output: bfloat16 [256, 256], replicated, may hold values from -0.75 to 0.75
- char_gain_mlp: float32 [256], replicated, may hold values from 0.5 to 1.5
- char_expand: bfloat16 [256, 1024], replicated, may hold values from -0.375 to 0.375
- char_shrink: bfloat16 [1024, 256], replicated, may hold values from -0.1875 to 0.1875
- word_input: bfloat16 [256, 512], replicated, may hold values from -0.375 to 0.375
- word_gain_attn: float32 [512], replicated, may hold values from 0.5 to 1.5
- word_project: bfloat16 [512, 1536], replicated, may hold values from -0.25 to 0.25
- word_output: bfloat16 [512, 512], replicated, may hold values from -1 to 1
- word_gain_mlp: float32 [512], replicated, may hold values from 0.5 to 1.5
- word_expand: bfloat16 [512, 2048], replicated, may hold values from -0.25 to 0.25
- word_shrink: bfloat16 [2048, 512], replicated, may hold values from -0.125 to 0.125
- cotangent: bfloat16 [2, 16, 64, 512], P(None, 'dp'), may hold values from -6 to 6
Outputs:
- output: float32 [2, 16, 64, 512], P('section', 'dp')
- chars_grad: float32 [2, 16, 64, 16, 256], P('section', 'dp')
- language_table_grad: float32 [8, 256], P(None, 'dp')
- char_gain_attn_grad: float32 [256], P('dp')
- char_project_grad: float32 [256, 768], P('dp')
- char_output_grad: float32 [256, 256], P('dp')
- char_gain_mlp_grad: float32 [256], P('dp')
- char_expand_grad: float32 [256, 1024], P('dp')
- char_shrink_grad: float32 [1024, 256], P('dp')
- word_input_grad: float32 [256, 512], P('dp')
- word_gain_attn_grad: float32 [512], P('dp')
- word_project_grad: float32 [512, 1536], P('dp')
- word_output_grad: float32 [512, 512], P('dp')
- word_gain_mlp_grad: float32 [512], P('dp')
- word_expand_grad: float32 [512, 2048], P('dp')
- word_shrink_grad: float32 [2048, 512], P('dp')
Inputs may be any that keep to these rules, and one draw needn't show every extreme that they name: `counts`: characters of each word; slots from the count on are padding.
All inputs are finite; a program needn't handle non-finite values.
Results may differ from a plain program's by a relative error of at most 0.015.
Values may be sent and summed in bfloat16 or wider, within the bound.
No kernel may reach another device: no remote copies, remote signals or barrier semaphores. Data moves between devices by JAX's collectives and lax.ppermute only.
A program may use at most 192 MiB of HBM per device.

v0:
```python
import jax
import jax.numpy as jnp
from jax import lax
from jax.sharding import PartitionSpec as P

CH = 4
H = 8


eps = 1e-05


def passed_along(value, axis, steps):
    count = lax.axis_size(axis)
    initial, last = (max(0, -steps), min(count, count - steps))
    return lax.ppermute(value, axis, [(source, source + steps) for source in range(initial, last)])


def for_sending(array):
    return jax.tree.map(lambda a: a.astype(jnp.bfloat16) if a.dtype == jnp.float32 else a, array)


def norm_forward(inputs, gain):
    return inputs * lax.rsqrt(jnp.mean(inputs * inputs, axis=-1, keepdims=True) + eps) * gain


def attend_forward(normed, project, head_count, key_mask):
    row_count, length, channels = normed.shape
    head_size = channels // head_count
    qkv = jnp.einsum("blc,cf->blf", normed, project, preferred_element_type=jnp.float32).astype(
        jnp.bfloat16
    )
    pieces = qkv.reshape(row_count, length, 3, head_count, head_size)
    scores = jnp.einsum(
        "bqhd,bkhd->bhqk", pieces[:, :, 0], pieces[:, :, 1], preferred_element_type=jnp.float32
    ) * head_size ** (-0.5)
    scores = jnp.where(key_mask, scores, -1e30)
    row_max = jnp.max(scores, axis=-1, keepdims=True)
    weights_exp = jnp.exp(scores - row_max)
    row_total = jnp.sum(weights_exp, axis=-1, keepdims=True)
    attn_probs = (weights_exp / row_total).astype(jnp.bfloat16)
    mixed_heads = jnp.einsum(
        "bhqk,bkhd->bqhd", attn_probs, pieces[:, :, 2], preferred_element_type=jnp.float32
    )
    mixed_heads = mixed_heads.reshape(row_count, length, channels).astype(jnp.bfloat16)
    return (qkv, row_max + jnp.log(row_total), mixed_heads)


def attend_backward(
    normed, project, output, qkv, logsum, mixed_heads, dmiddle_low, head_count, key_mask
):
    row_count, length, channels = normed.shape
    head_size = channels // head_count
    scaling = head_size ** (-0.5)
    output_grad = jnp.einsum(
        "blc,bld->cd", mixed_heads, dmiddle_low, preferred_element_type=jnp.float32
    )
    dmixed = jnp.einsum(
        "bld,cd->blc", dmiddle_low, output, preferred_element_type=jnp.float32
    ).astype(jnp.bfloat16)
    dmixed = dmixed.reshape(row_count, length, head_count, head_size)
    pieces = qkv.reshape(row_count, length, 3, head_count, head_size)
    scores = (
        jnp.einsum(
            "bqhd,bkhd->bhqk", pieces[:, :, 0], pieces[:, :, 1], preferred_element_type=jnp.float32
        )
        * scaling
    )
    scores = jnp.where(key_mask, scores, -1e30)
    attn_probs = jnp.exp(scores - logsum)
    dprobs = jnp.einsum(
        "bqhd,bkhd->bhqk", dmixed, pieces[:, :, 2], preferred_element_type=jnp.float32
    )
    row_delta = jnp.sum(attn_probs * dprobs, axis=-1, keepdims=True)
    dscores = (attn_probs * (dprobs - row_delta)).astype(jnp.bfloat16)
    dquery = (
        jnp.einsum("bhqk,bkhd->bqhd", dscores, pieces[:, :, 1], preferred_element_type=jnp.float32)
        * scaling
    )
    dkeys = (
        jnp.einsum("bhqk,bqhd->bkhd", dscores, pieces[:, :, 0], preferred_element_type=jnp.float32)
        * scaling
    )
    dvalues = jnp.einsum(
        "bhqk,bqhd->bkhd",
        attn_probs.astype(jnp.bfloat16),
        dmixed,
        preferred_element_type=jnp.float32,
    )
    dqkv = (
        jnp.stack([dquery, dkeys, dvalues], axis=2)
        .reshape(row_count, length, 3 * channels)
        .astype(jnp.bfloat16)
    )
    project_grad = jnp.einsum("blc,blf->cf", normed, dqkv, preferred_element_type=jnp.float32)
    dnormed = jnp.einsum("blf,cf->blc", dqkv, project, preferred_element_type=jnp.float32)
    return (dnormed, project_grad, output_grad)


def block_forward(inputs, weights, head_count, key_mask):
    gain_attn, project, output, gain_mlp, expand, shrink = weights
    normed = norm_forward(inputs, gain_attn).astype(jnp.bfloat16)
    qkv, logsum, mixed_heads = attend_forward(normed, project, head_count, key_mask)
    middle = inputs + jnp.einsum(
        "blc,cd->bld", mixed_heads, output, preferred_element_type=jnp.float32
    )
    normed_mlp = norm_forward(middle, gain_mlp).astype(jnp.bfloat16)
    before = jnp.einsum("blc,cf->blf", normed_mlp, expand, preferred_element_type=jnp.float32)
    hidden = jax.nn.gelu(before).astype(jnp.bfloat16)
    result = middle + jnp.einsum("blf,fc->blc", hidden, shrink, preferred_element_type=jnp.float32)
    return (result, (inputs, normed, qkv, logsum, mixed_heads, middle, normed_mlp, before, hidden))


def block_backward(dresult, stored, weights, head_count, key_mask):
    gain_attn, project, output, gain_mlp, expand, shrink = weights
    inputs, normed, qkv, logsum, mixed_heads, middle, normed_mlp, before, hidden = stored
    grad_low = dresult.astype(jnp.bfloat16)
    shrink_grad = jnp.einsum("blf,blc->fc", hidden, grad_low, preferred_element_type=jnp.float32)
    dhidden = jnp.einsum(
        "blc,fc->blf", grad_low, shrink, preferred_element_type=jnp.float32
    ).astype(jnp.bfloat16)
    gelu_pull = jax.vjp(jax.nn.gelu, before)[1]
    dbefore = gelu_pull(dhidden.astype(jnp.float32))[0].astype(jnp.bfloat16)
    expand_grad = jnp.einsum("blc,blf->cf", normed_mlp, dbefore, preferred_element_type=jnp.float32)
    dnormed_mlp = jnp.einsum("blf,cf->blc", dbefore, expand, preferred_element_type=jnp.float32)
    norm_pull = jax.vjp(norm_forward, middle, gain_mlp)[1]
    dmiddle_norm, gain_mlp_grad = norm_pull(dnormed_mlp)
    dmiddle = dresult + dmiddle_norm
    dnormed, project_grad, output_grad = attend_backward(
        normed,
        project,
        output,
        qkv,
        logsum,
        mixed_heads,
        dmiddle.astype(jnp.bfloat16),
        head_count,
        key_mask,
    )
    first_pull = jax.vjp(norm_forward, inputs, gain_attn)[1]
    dinputs_norm, gain_attn_grad = first_pull(dnormed)
    return (
        dmiddle + dinputs_norm,
        (gain_attn_grad, project_grad, output_grad, gain_mlp_grad, expand_grad, shrink_grad),
    )


def char_front(char_text, char_count, language, lang_table, weights):
    present = lax.broadcasted_iota(jnp.int32, char_text.shape[:2], 1) < char_count[:, None]
    onehot = (lax.broadcasted_iota(jnp.int32, (lang_table.shape[0],), 0) == language).astype(
        jnp.bfloat16
    )
    lang_row = jnp.dot(onehot, lang_table, preferred_element_type=jnp.float32)
    inputs = char_text.astype(jnp.float32) + lang_row
    result, stored = block_forward(inputs, weights, CH, present[:, None, None, :])
    summed = jnp.sum(jnp.where(present[:, :, None], result, 0.0), axis=1)
    pooled = (summed / char_count[:, None].astype(jnp.float32)).astype(jnp.bfloat16)
    return (pooled, stored, present, onehot)


def char_back(stored, present, onehot, char_count, dpooled, weights):
    spread = dpooled.astype(jnp.float32) / char_count[:, None].astype(jnp.float32)
    dresult = jnp.where(present[:, :, None], spread[:, None, :], 0.0)
    dinputs, gradients = block_backward(dresult, stored, weights, CH, present[:, None, None, :])
    table_grad = onehot.astype(jnp.float32)[:, None] * jnp.sum(dinputs, axis=(0, 1))[None, :]
    return (dinputs, (table_grad,) + gradients)


def word_full(pooled, cot_rows, word_input, weights):
    length = pooled.shape[0]
    word_start = jnp.dot(pooled, word_input, preferred_element_type=jnp.float32)[None]
    causal = (
        lax.broadcasted_iota(jnp.int32, (length, length), 0)
        >= lax.broadcasted_iota(jnp.int32, (length, length), 1)
    )[None, None]
    result, stored = block_forward(word_start, weights, H, causal)
    dstart, gradients = block_backward(
        cot_rows.astype(jnp.float32)[None], stored, weights, H, causal
    )
    grad_low = dstart[0].astype(jnp.bfloat16)
    input_grad = jnp.einsum("wc,wd->cd", pooled, grad_low, preferred_element_type=jnp.float32)
    dpooled = jnp.einsum(
        "wd,cd->wc", grad_low, word_input, preferred_element_type=jnp.float32
    ).astype(jnp.bfloat16)
    return (result[0], dpooled, (input_grad,) + gradients)


def local(
    chars,
    counts,
    languages,
    language_table,
    char_gain_attn,
    char_project,
    char_output,
    char_gain_mlp,
    char_expand,
    char_shrink,
    word_input,
    word_gain_attn,
    word_project,
    word_output,
    word_gain_mlp,
    word_expand,
    word_shrink,
    cotangent,
):
    char_weights = (
        char_gain_attn,
        char_project,
        char_output,
        char_gain_mlp,
        char_expand,
        char_shrink,
    )
    word_weights = (
        word_gain_attn,
        word_project,
        word_output,
        word_gain_mlp,
        word_expand,
        word_shrink,
    )
    section_index = lax.axis_index("section")
    on_first = section_index == 0
    micro_count = chars.shape[0]
    per_section = micro_count // lax.axis_size("section")
    word_count = chars.shape[2]
    char_zeros = tuple(
        (jnp.zeros(entry.shape, jnp.float32) for entry in (language_table,) + char_weights)
    )
    word_zeros = tuple(
        (jnp.zeros(entry.shape, jnp.float32) for entry in (word_input,) + word_weights)
    )
    char_totals = char_zeros
    word_totals = word_zeros
    results = []
    text_grads = []
    for micro_step in range(micro_count):
        char_text = chars[micro_step, 0]
        char_count = counts[micro_step, 0]
        language = languages[micro_step, 0]
        cot_rows = cotangent[micro_step, 0]

        def make_pooled():
            return char_front(char_text, char_count, language, language_table, char_weights)[0]

        def no_pooled():
            return jnp.zeros((word_count, char_text.shape[-1]), jnp.bfloat16)

        pooled = lax.cond(on_first, make_pooled, no_pooled)
        arrived = passed_along(pooled, "section", 1)

        def run_word():
            return word_full(arrived, cot_rows, word_input, word_weights)

        def skip_word():
            return (
                jnp.zeros((word_count, cot_rows.shape[-1]), jnp.float32),
                jnp.zeros(arrived.shape, jnp.bfloat16),
                word_zeros,
            )

        result, dpooled, word_grads = lax.cond(on_first, skip_word, run_word)
        returned = passed_along(dpooled, "section", -1)

        def run_char():
            pooled_again, stored, present, onehot = char_front(
                char_text, char_count, language, language_table, char_weights
            )
            return char_back(stored, present, onehot, char_count, returned, char_weights)

        def skip_char():
            return (jnp.zeros(char_text.shape, jnp.float32), char_zeros)

        text_grad, char_grads = lax.cond(on_first, run_char, skip_char)
        char_totals = tuple((first + second for first, second in zip(char_totals, char_grads)))
        word_totals = tuple((first + second for first, second in zip(word_totals, word_grads)))
        results.append(result)
        text_grads.append(text_grad)
    lower_results = jnp.stack(results[:per_section])[:, None]
    arrived_results = passed_along(lower_results.astype(jnp.bfloat16), "section", -1).astype(
        lower_results.dtype
    )
    output = jnp.where(on_first, arrived_results, jnp.stack(results[per_section:])[:, None])
    upper_grads = jnp.stack(text_grads[per_section:])[:, None]
    arrived_grads = passed_along(upper_grads.astype(jnp.bfloat16), "section", 1).astype(
        upper_grads.dtype
    )
    chars_grad = jnp.where(on_first, jnp.stack(text_grads[:per_section])[:, None], arrived_grads)
    gradients = char_totals + word_totals
    shares = (
        lax.psum_scatter(gradients[0], "dp", scatter_dimension=1, tiled=True),
        lax.psum_scatter(gradients[1], "dp", scatter_dimension=0, tiled=True),
        lax.psum_scatter(gradients[2], "dp", scatter_dimension=0, tiled=True),
        lax.psum_scatter(gradients[3], "dp", scatter_dimension=0, tiled=True),
        lax.psum_scatter(gradients[4], "dp", scatter_dimension=0, tiled=True),
        lax.psum_scatter(gradients[5], "dp", scatter_dimension=0, tiled=True),
        lax.psum_scatter(gradients[6], "dp", scatter_dimension=0, tiled=True),
        lax.psum_scatter(gradients[7], "dp", scatter_dimension=0, tiled=True),
        lax.psum_scatter(gradients[8], "dp", scatter_dimension=0, tiled=True),
        lax.psum_scatter(gradients[9], "dp", scatter_dimension=0, tiled=True),
        lax.psum_scatter(gradients[10], "dp", scatter_dimension=0, tiled=True),
        lax.psum_scatter(gradients[11], "dp", scatter_dimension=0, tiled=True),
        lax.psum_scatter(gradients[12], "dp", scatter_dimension=0, tiled=True),
        lax.psum_scatter(gradients[13], "dp", scatter_dimension=0, tiled=True),
    )
    totals = jax.tree.map(
        lambda part: part.astype(jnp.float32), lax.psum(for_sending(shares), "section")
    )
    return (output, chars_grad) + tuple(totals)


def solution(mesh):
    placed = (
        P(None, "dp", None, None, None),
        P(None, "dp", None),
        P(None, "dp"),
        P(),
        P(),
        P(),
        P(),
        P(),
        P(),
        P(),
        P(),
        P(),
        P(),
        P(),
        P(),
        P(),
        P(),
        P(None, "dp", None, None),
    )
    return jax.shard_map(
        local,
        mesh=mesh,
        in_specs=placed,
        out_specs=(
            P("section", "dp", None, None),
            P("section", "dp", None, None, None),
            P(None, "dp"),
            P("dp"),
            P("dp", None),
            P("dp", None),
            P("dp"),
            P("dp", None),
            P("dp", None),
            P("dp", None),
            P("dp"),
            P("dp", None),
            P("dp", None),
            P("dp"),
            P("dp", None),
            P("dp", None),
        ),
        check_vma=False,
    )
```

profile of v0, /device:TPU:0, one launch (start us, length us, event | category | flops | bytes accessed | tf_op | source)
XLA Modules:
  0.0 942.0 jit_solution(3465480263461199463)
XLA Ops:
  11.2 26.1 %conditional.6 = (bf16[64,256]{1,0:T(8,128)(2,1)S(1)}) conditional(s32[]{:T(128)} %convert_element_type.528, () %tuple.56, (s32[1,1,64]{2,1,0:T(1,128)}, bf16[64,16,256]{2,1,0:T(8,128)(2,1)S(1)}, s32[]{:T(128)}, bf16[8,256]{1,0:T(8,128)(2,1)S(1)}, f32[256]{0:T(256)S(1)}, /*index=5*/bf16[256,768]{1,0:T(8,128)(2,1)S(1)}, ...), branch_computations={%region_0.0_spmd, %region_1.7_spmd} | conditional | flops 1643535360 | bytes 18593804 | solution.py:251
  15.4 5.7 reshape.1002
  21.1 5.3 fusion.285
  26.4 4.2 fusion.286
  30.7 2.1 fusion.12
  34.4 2.9 fusion.14
  38.7 33.1 %conditional.8 = (bf16[64,256]{1,0:T(8,128)(2,1)}) conditional(s32[]{:T(128)} %convert_element_type.528, () %tuple.60, (s32[1,1,64]{2,1,0:T(1,128)S(1)}, bf16[64,16,256]{2,1,0:T(8,128)(2,1)S(1)}, s32[]{:T(128)}, bf16[8,256]{1,0:T(8,128)(2,1)S(1)}, f32[256]{0:T(256)S(1)}, /*index=5*/bf16[256,768]{1,0:T(8,128)(2,1)}, ...), branch_computations={%region_18.19_spmd, %region_19.25_spmd} | conditional | flops 1643535360 | bytes 18593804 | solution.py:251
  40.3 2.8 convolution_convert_fusion.8
  43.1 5.7 reshape.1008
  48.8 4.7 fusion.289
  53.5 4.9 fusion.290
  58.4 2.4 fusion.94
  62.3 2.7 convert_element_type.424
  65.1 2.3 multiply_reduce_fusion.9
  67.4 3.7 fusion.96
  73.7 7.4 conditional.7
  78.5 2.5 broadcast_in_dim.236
  84.3 4.2 conditional.9
  93.3 75.0 %conditional.10 = (f32[8,256]{1,0:T(8,128)S(1)}, f32[256]{0:T(256)}, f32[256,768]{1,0:T(8,128)}, f32[256,256]{1,0:T(8,128)}, f32[256]{0:T(256)}, /*index=5*/f32[...) conditional(s32[]{:T(128)} %convert_element_type.528, () %tuple.64, (s32[]{:T(128)}, ...), branch_computations={%region_36.37_spmd, %region_37.48_spmd} | conditional | flops 4398622720 | bytes 118564744 | solution.py:276
  97.9 2.8 convolution_convert_fusion.16
  100.7 5.9 reshape.1014
  106.6 4.2 fusion.293
  115.2 2.7 convert_element_type.462
  118.0 2.3 multiply_reduce_fusion.23
  121.8 2.1 fusion.193
  123.9 2.6 fusion.180
  126.5 3.5 fusion.167
  131.9 2.4 multiply_reduce_fusion.19
  138.5 2.3 select_add_fusion
  143.1 2.7 reshape.1015
  152.7 3.3 copy.370
  156.0 4.8 convert_element_type.469
  163.6 2.2 multiply_reduce_fusion.21
  168.9 68.4 %conditional.11 = (bf16[64,16,256]{2,1,0:T(8,128)(2,1)}, f32[8,256]{1,0:T(8,128)S(1)}, f32[256]{0:T(256)}, f32[256,768]{1,0:T(8,128)}, f32[256,256]{1,0:T(8,128)...) conditional(s32[]{:T(128)} %convert_element_type.528, () %tuple.66, (s32[1,1,64]{2,1,0:T(1,128)}, ...), branch_computations={%region_48.49_spmd, %region_49.60_spmd} | conditional | flops 4398884864 | bytes 111753064 | solution.py:276
  175.7 3.1 reshape.1016
  178.8 4.2 fusion.295
  187.4 2.8 convert_element_type.482
  190.2 2.3 multiply_reduce_fusion.30
  196.0 2.6 fusion.240
  198.6 3.5 fusion.227
  204.0 2.4 multiply_reduce_fusion.26
  222.4 3.3 copy.387
  225.7 4.8 convert_element_type.489
  232.2 2.2 multiply_reduce_fusion.27
  234.6 2.4 fusion.283
  243.5 2.5 add.402
  247.3 2.7 add.405
  250.1 2.7 add.406
  252.8 5.1 add.409
  258.0 6.6 add.412
  264.7 6.5 add.413
  276.1 35.4 %all-reduce.4 = (bf16[256]{0:T(256)(128)(2,1)S(1)}, bf16[256]{0:T(256)(128)(2,1)S(1)}, bf16[512]{0:T(512)(128)(2,1)S(1)}, bf16[512]{0:T(512)(128)(2,1)S(1)}) all-reduce(f32[256]{0:T(256)S(1)} %add.401, f32[256]{0:T(256)S(1)} %add.404, f32[512]{0:T(512)S(1)} %add.408, f32[512]{0:T(512)S(1)} %add.411), channel_id=3, replica_groups=mesh['section'=2,'dp'=16] {'dp'}, use_global_device_ids=true, to_apply=%region_62.63.clone | all-reduce | flops 1536 | bytes 9216
  315.2 39.7 %reduce-scatter.15.cloned.1.call-done = f32[16,256]{1,0:T(8,128)} async-done(((f32[256,256]{1,0:T(8,128)}), f32[16,256]{1,0:T(8,128)}) %reduce-scatter.15.cloned.1.call-update) | async-done | bytes 16400 | tf_op jit(solution)/shard_map/reduce_scatter | solution.py:296
  356.2 57.1 %reduce-scatter.21.cloned.1.call-done = f32[16,512]{1,0:T(8,128)} async-done(((f32[256,512]{1,0:T(8,128)}), f32[16,512]{1,0:T(8,128)}) %reduce-scatter.21.cloned.1.call-update) | async-done | bytes 32784 | tf_op jit(solution)/shard_map/reduce_scatter | solution.py:300
  414.6 58.0 %reduce-scatter.13.cloned.1.call-done = f32[16,768]{1,0:T(8,128)} async-done(((f32[256,768]{1,0:T(8,128)}), f32[16,768]{1,0:T(8,128)}) %reduce-scatter.13.cloned.1.call-update) | async-done | bytes 49168 | tf_op jit(solution)/shard_map/reduce_scatter | solution.py:295
  474.1 58.5 %reduce-scatter.25.cloned.1.call-done = f32[32,512]{1,0:T(8,128)} async-done(((f32[512,512]{1,0:T(8,128)}), f32[32,512]{1,0:T(8,128)}) %reduce-scatter.25.cloned.1.call-update) | async-done | bytes 65552 | tf_op jit(solution)/shard_map/reduce_scatter | solution.py:303
  534.0 59.5 %reduce-scatter.17.cloned.1.call-done = f32[16,1024]{1,0:T(8,128)} async-done(((f32[256,1024]{1,0:T(8,128)}), f32[16,1024]{1,0:T(8,128)}) %reduce-scatter.17.cloned.1.call-update) | async-done | bytes 65552 | tf_op jit(solution)/shard_map/reduce_scatter | solution.py:298
  595.0 58.6 %reduce-scatter.19.cloned.1.call-done = f32[64,256]{1,0:T(8,128)} async-done(((f32[1024,256]{1,0:T(8,128)}), f32[64,256]{1,0:T(8,128)}) %reduce-scatter.19.cloned.1.call-update) | async-done | bytes 65552 | tf_op jit(solution)/shard_map/reduce_scatter | solution.py:299
  656.5 66.7 %reduce-scatter.23.cloned.1.call-done = f32[32,1536]{1,0:T(8,128)} async-done(((f32[512,1536]{1,0:T(8,128)}), f32[32,1536]{1,0:T(8,128)}) %reduce-scatter.23.cloned.1.call-update) | async-done | bytes 196624 | tf_op jit(solution)/shard_map/reduce_scatter | solution.py:302
  724.7 74.3 %reduce-scatter.27.cloned.1.call-done = f32[32,2048]{1,0:T(8,128)} async-done(((f32[512,2048]{1,0:T(8,128)}), f32[32,2048]{1,0:T(8,128)}) %reduce-scatter.27.cloned.1.call-update) | async-done | bytes 262160 | tf_op jit(solution)/shard_map/reduce_scatter | solution.py:305
  800.7 73.5 %reduce-scatter.29.cloned.1.call-done = f32[128,512]{1,0:T(8,128)} async-done(((f32[2048,512]{1,0:T(8,128)}), f32[128,512]{1,0:T(8,128)}) %reduce-scatter.29.cloned.1.call-update) | async-done | bytes 262160 | tf_op jit(solution)/shard_map/reduce_scatter | solution.py:306
  876.5 2.4 convert_select_fusion
  878.9 22.7 %all-reduce.10.cloned.1.call-done = (bf16[8,16]{1,0:T(8,128)(2,1)}, bf16[16]{0:T(256)(128)(2,1)}, bf16[16,768]{1,0:T(8,128)(2,1)}, bf16[16,256]{1,0:T(8,128)(2,1...) async-done(((bf16[8,16]{1,0:T(8,128)(2,1)}, ...) | async-done | bytes 147920 | tf_op jit(solution)/shard_map/psum | solution.py:309
  915.6 14.3 %all-reduce.12.cloned.1.call-done = (bf16[32,1536]{1,0:T(8,128)(2,1)}, bf16[32,2048]{1,0:T(8,128)(2,1)}, bf16[128,512]{1,0:T(8,128)(2,1)}) async-done(((bf16[32,1536]{1,0:T(8,128)(2,1)}, bf16[32,2048]{1,0:T(8,128)(2,1)}, bf16[128,512]{1,0:T(8,128)(2,1)}), (bf16[32,1536]{1,0:T(8,128)(2,1)}, bf16[32,2048]{1,0:T(8,128)(2,1)}, bf16[128,512]{1,0:T(8,128)(2,1)})) %all-reduce.12.cloned.1.call-update) | async-done | bytes 360464 | tf_op jit(solution)/shard_map/psum | solution.py:309
  (332 shorter events, 147.0 us)
Async XLA Ops:
  7.2 4.0 copy-start.46
  7.2 4.0 copy-start.73
  7.2 4.0 copy-start.24
  7.2 4.0 copy-start.111
  7.2 4.0 copy-start.80
  7.2 4.0 copy-start.77
  7.2 306.6 %reduce-scatter.31.cloned.1.call-start = ((), (), s32[]{:S(2)}) async-start(), calls=%async_computation.19 | async-start | bytes 139264
  8.6 30.1 %copy-start.103 = (s32[1,1,64]{2,1,0:T(1,128)}, s32[1,1,64]{2,1,0:T(1,128)S(1)}, u32[]{:S(2)}) copy-start(s32[1,1,64]{2,1,0:T(1,128)S(1)} %get-tuple-element.381) | copy-start | bytes 772
  37.4 36.3 %collective-permute-start = (bf16[64,256]{1,0:T(8,128)(2,1)S(1)}, bf16[64,256]{1,0:T(8,128)(2,1)S(1)}, u32[]{:S(2)}, u32[]{:S(2)}) collective-permute-start(bf16[64,256]{1,0:T(8,128)(2,1)S(1)} %get-tuple-element.468), channel_id=1, source_target_pairs={{0,16},{1,17},{2,18},{3,19},{4,20},{5,21},{6,22},{7,23},{8,24},{9,... | collective-permute-start | bytes 98312 | tf_op jit(solution)/shard_map/ppermute | solution.py:16
  38.7 35.0 %copy-start = (bf16[512,2048]{1,0:T(8,128)(2,1)S(1)}, bf16[512,2048]{1,0:T(8,128)(2,1)}, u32[]{:S(2)}) copy-start(bf16[512,2048]{1,0:T(8,128)(2,1)} %param.45) | copy-start | bytes 6291460
  38.7 35.0 %copy-start.69 = (f32[512]{0:T(512)S(1)}, f32[512]{0:T(512)}, u32[]{:S(2)}) copy-start(f32[512]{0:T(512)} %param.41) | copy-start | bytes 6148
  38.7 35.0 %copy-start.72 = (f32[512]{0:T(512)S(1)}, f32[512]{0:T(512)}, u32[]{:S(2)}) copy-start(f32[512]{0:T(512)} %param.44) | copy-start | bytes 6148
  71.8 10.6 %collective-permute-start.2 = (bf16[64,256]{1,0:T(8,128)(2,1)}, bf16[64,256]{1,0:T(8,128)(2,1)}, u32[]{:S(2)}, u32[]{:S(2)}) collective-permute-start(bf16[64,256]{1,0:T(8,128)(2,1)} %get-tuple-element.469), channel_id=1, source_target_pairs={{0,16},{1,17},{2,18},{3,19},{4,20},{5,21},{6,22},{7,23},{8,24},{9,... | collective-permute-start | bytes 98312 | tf_op jit(solution)/shard_map/ppermute | solution.py:16
  81.1 3.0 copy-start.7
  81.1 3.3 copy-start.25
  81.1 8.8 collective-permute-start.3
  88.6 3.2 copy-start.4
  88.6 4.2 copy-start.8
  88.6 4.5 copy-start.27
  88.6 4.7 copy-start.49
  88.6 79.7 %collective-permute-start.4 = (bf16[64,256]{1,0:T(8,128)(2,1)}, bf16[64,256]{1,0:T(8,128)(2,1)}, u32[]{:S(2)}, u32[]{:S(2)}) collective-permute-start(bf16[64,256]{1,0:T(8,128)(2,1)} %get-tuple-element.246), channel_id=1, source_target_pairs={{16,0},{17,1},{18,2},{19,3},{20,4},{21,5},{22,6},{23,7},{24,8},{25... | collective-permute-start | bytes 98312 | tf_op jit(solution)/shard_map/ppermute | solution.py:16
  95.9 22.1 %copy-start.83 = (f32[1,256]{1,0:T(1,128)}, f32[1,256]{1,0:T(1,128)S(1)}, u32[]{:S(2)}) copy-start(f32[1,256]{1,0:T(1,128)S(1)} %fusion.211) | copy-start | bytes 3076 | tf_op jit(solution)/shard_map/cond
  96.6 14.2 %copy-start.85 = (pred[64,16]{1,0:T(8,128)(4,1)}, pred[64,16]{1,0:T(8,128)(4,1)S(1)}, u32[]{:S(2)}) copy-start(pred[64,16]{1,0:T(8,128)(4,1)S(1)} %iota_compare_fusion.4) | copy-start | bytes 3076 | tf_op jit(solution)/shard_map/cond
  121.8 2.1 copy-start.86
  123.9 2.6 copy-start.109
  126.5 3.5 copy-start.5
  126.5 3.5 copy-start.74
  138.5 2.3 copy-start.53
  156.0 5.9 copy-start.81
  156.0 5.9 copy-start.84
  163.6 2.4 copy-start.10
  165.8 2.2 copy-start.107
  172.1 18.1 %copy-start.78 = (f32[1,256]{1,0:T(1,128)}, f32[1,256]{1,0:T(1,128)S(1)}, u32[]{:S(2)}) copy-start(f32[1,256]{1,0:T(1,128)S(1)} %fusion.271) | copy-start | bytes 3076 | tf_op jit(solution)/shard_map/cond
  172.8 10.3 %copy-start.87 = (pred[64,16]{1,0:T(8,128)(4,1)}, pred[64,16]{1,0:T(8,128)(4,1)S(1)}, u32[]{:S(2)}) copy-start(pred[64,16]{1,0:T(8,128)(4,1)S(1)} %iota_compare_fusion.5) | copy-start | bytes 3076 | tf_op jit(solution)/shard_map/cond
  187.4 6.6 copy-start.48
  196.0 2.6 copy-start.110
  198.6 3.5 copy-start.6
  198.6 3.5 copy-start.75
  206.4 6.3 copy-start.54
  225.7 4.8 copy-start.79
  225.7 4.8 copy-start.82
  232.2 2.4 copy-start.12
  234.4 2.6 copy-start.108
  239.4 115.5 %reduce-scatter.15.cloned.1.call-start = ((), (), s32[]{:S(2)}) async-start(), calls=%async_computation.11 | async-start | bytes 278528 | tf_op jit(solution)/shard_map/reduce_scatter | solution.py:296
  241.2 172.0 %reduce-scatter.21.cloned.1.call-start = ((), (), s32[]{:S(2)}) async-start(), calls=%async_computation.14 | async-start | bytes 557056 | tf_op jit(solution)/shard_map/reduce_scatter | solution.py:300
  243.4 2.6 copy-start.26
  243.4 2.6 copy-start.28
  243.4 229.3 %reduce-scatter.13.cloned.1.call-start = ((), (), s32[]{:S(2)}) async-start(), calls=%async_computation.10 | async-start | bytes 835584 | tf_op jit(solution)/shard_map/reduce_scatter | solution.py:295
  246.0 286.6 %reduce-scatter.25.cloned.1.call-start = ((), (), s32[]{:S(2)}) async-start(), calls=%async_computation.16 | async-start | bytes 1114112 | tf_op jit(solution)/shard_map/reduce_scatter | solution.py:303
  247.2 346.3 %reduce-scatter.17.cloned.1.call-start = ((), (), s32[]{:S(2)}) async-start(), calls=%async_computation.12 | async-start | bytes 1114112 | tf_op jit(solution)/shard_map/reduce_scatter | solution.py:298
  250.0 403.6 %reduce-scatter.19.cloned.1.call-start = ((), (), s32[]{:S(2)}) async-start(), calls=%async_computation.13 | async-start | bytes 1114112 | tf_op jit(solution)/shard_map/reduce_scatter | solution.py:299
  252.8 470.4 %reduce-scatter.23.cloned.1.call-start = ((), (), s32[]{:S(2)}) async-start(), calls=%async_computation.15 | async-start | bytes 3342336 | tf_op jit(solution)/shard_map/reduce_scatter | solution.py:302
  258.0 541.1 %reduce-scatter.27.cloned.1.call-start = ((), (), s32[]{:S(2)}) async-start(), calls=%async_computation.17 | async-start | bytes 4456448 | tf_op jit(solution)/shard_map/reduce_scatter | solution.py:305
  264.6 609.5 %reduce-scatter.29.cloned.1.call-start = ((), (), s32[]{:S(2)}) async-start(), calls=%async_computation.18 | async-start | bytes 4456448 | tf_op jit(solution)/shard_map/reduce_scatter | solution.py:306
  271.2 3.5 copy-start.95
  271.2 3.5 copy-start.96
  271.2 3.5 copy-start.97
  271.2 3.5 copy-start.98
  271.2 383.9 %copy-start.76 = (bf16[64,512]{1,0:T(8,128)(2,1)S(1)}, bf16[64,512]{1,0:T(8,128)(2,1)}, u32[]{:S(2)}) copy-start(bf16[64,512]{1,0:T(8,128)(2,1)} %get-tuple-element.242) | copy-start | bytes 196612
  271.2 604.6 %copy-start.63 = (f32[1,1,64,512]{3,2,1,0:T(8,128)S(1)}, f32[1,1,64,512]{3,2,1,0:T(8,128)}, u32[]{:S(2)}) copy-start(f32[1,1,64,512]{3,2,1,0:T(8,128)} %get-tuple-element.243) | copy-start | bytes 393220
  271.3 630.3 %all-reduce.10.cloned.1.call-start = ((), (), s32[]{:S(2)}) async-start(), calls=%async_computation.20 | async-start | bytes 303104 | tf_op jit(solution)/shard_map/psum | solution.py:309
  271.3 605.2 %collective-permute-start.5 = (bf16[1,1,64,16,256]{4,3,2,1,0:T(8,128)(2,1)}, bf16[1,1,64,16,256]{4,3,2,1,0:T(8,128)(2,1)S(1)}, u32[]{:S(2)}, u32[]{:S(2)}) collective-permute-start(bf16[1,1,64,16,256]{4,3,2,1,0:T(8,128)(2,1)} %bitcast.344), channel_id=1, source_target_pairs={{0,16},{1,17},{2,18},{3,19},{4,20},{5,21},{6,22},{7,23},{8,24},{9,... | collective-permute-start | bytes 1572872 | tf_op jit(solution)/shard_map/ppermute | solution.py:16
  655.1 274.8 %all-reduce.12.cloned.1.call-start = ((), (), s32[]{:S(2)}) async-start(), calls=%async_computation.21 | async-start | bytes 720896 | tf_op jit(solution)/shard_map/psum | solution.py:309
  655.2 220.7 %collective-permute-start.1 = (bf16[1,1,64,512]{3,2,1,0:T(8,128)(2,1)S(1)}, bf16[1,1,64,512]{3,2,1,0:T(8,128)(2,1)S(1)}, u32[]{:S(2)}, u32[]{:S(2)}) collective-permute-start(bf16[1,1,64,512]{3,2,1,0:T(8,128)(2,1)S(1)} %bitcast.440), channel_id=1, source_target_pairs={{16,0},{17,1},{18,2},{19,3},{20,4},{21,5},{22,6},{23,7},{24,8},{25... | collective-permute-start | bytes 196616 | tf_op jit(solution)/shard_map/ppermute | solution.py:16
  (26 other events, 39.2 us)
Sparse Core Ops, SparseCore 0:
  239.5 56.8 reduce-scatter.30
  300.5 54.3 reduce-scatter.14
  358.4 54.8 reduce-scatter.20
  417.1 55.5 reduce-scatter.12
  476.1 56.3 reduce-scatter.24
  537.1 56.4 reduce-scatter.16
  597.1 56.4 reduce-scatter.18
  657.9 65.1 reduce-scatter.22
  727.5 71.5 reduce-scatter.26
  802.7 71.3 reduce-scatter.28
  878.6 22.9 all-reduce.9
  904.6 25.3 all-reduce.11
where the time goes:
time: 952 us; the launch traced here: 942 us
  waiting for transfers between devices  583 us (61%)
  local copies, waits for them, and re-layouts  112 us (12%)
  other arithmetic  95.5 us (10%)
  matrix products  88.6 us (9%)
  blocking collectives  35.4 us (4%)
  between operations  16.4 us (2%)
    reduce_scatter x1, waiting for transfers between devices, local(): lax.psum_scatter(gradients[12], 'dp', scatter_dimension=0, tiled=True)  74.3 us
    reduce_scatter x1, waiting for transfers between devices, local(): lax.psum_scatter(gradients[13], 'dp', scatter_dimension=0, tiled=True)  73.5 us
    reduce_scatter x1, waiting for transfers between devices, local(): lax.psum_scatter(gradients[9], 'dp', scatter_dimension=0, tiled=True)  66.7 us
    reduce_scatter x1, waiting for transfers between devices, local(): lax.psum_scatter(gradients[5], 'dp', scatter_dimension=0, tiled=True)  59.5 us
    reduce_scatter x1, waiting for transfers between devices, local(): lax.psum_scatter(gradients[6], 'dp', scatter_dimension=0, tiled=True)  58.6 us
    reduce_scatter x1, waiting for transfers between devices, local(): lax.psum_scatter(gradients[10], 'dp', scatter_dimension=0, tiled=True)  58.5 us
    reduce_scatter x1, waiting for transfers between devices, local(): lax.psum_scatter(gradients[2], 'dp', scatter_dimension=0, tiled=True)  58 us
    reduce_scatter x1, waiting for transfers between devices, local(): lax.psum_scatter(gradients[7], 'dp', scatter_dimension=0, tiled=True)  57.1 us
  transfers between devices with their start and end apart: 18, of which 11 were waited for; matrix products, arithmetic and copies ran while one was open for 19% of the time, Pallas kernels for 0%

commit v1 on v0

--- a/solution.py
+++ b/solution.py
@@ -8,16 +8,6 @@
 
 
 eps = 1e-05
-
-
-def passed_along(value, axis, steps):
-    count = lax.axis_size(axis)
-    initial, last = (max(0, -steps), min(count, count - steps))
-    return lax.ppermute(value, axis, [(source, source + steps) for source in range(initial, last)])
-
-
-def for_sending(array):
-    return jax.tree.map(lambda a: a.astype(jnp.bfloat16) if a.dtype == jnp.float32 else a, array)
 
 
 def norm_forward(inputs, gain):
@@ -183,6 +173,39 @@
         "wd,cd->wc", grad_low, word_input, preferred_element_type=jnp.float32
     ).astype(jnp.bfloat16)
     return (result[0], dpooled, (input_grad,) + gradients)
+
+
+def reduce_rows(gradients):
+    shards = lax.axis_size("dp")
+    flat = []
+    for place, gradient in enumerate(gradients):
+        if place == 0:
+            gradient = gradient.T
+        flat.append(gradient.astype(jnp.bfloat16).reshape(shards, -1))
+    packed = jnp.concatenate(flat, axis=1)
+    me = lax.axis_index("dp")
+    packed = jnp.take(packed, jnp.arange(shards) ^ me, axis=0)
+    bit = 1
+    while packed.shape[0] > 1:
+        pairs = packed.reshape(packed.shape[0] // 2, 2, packed.shape[1])
+        arrived = lax.ppermute(pairs[:, 1], "dp", [(i, i ^ bit) for i in range(shards)])
+        packed = (pairs[:, 0].astype(jnp.float32) + arrived.astype(jnp.float32)).astype(
+            jnp.bfloat16
+        )
+        bit *= 2
+    arrived = lax.ppermute(packed, "section", [(0, 1), (1, 0)])
+    total = (packed.astype(jnp.float32) + arrived.astype(jnp.float32))[0]
+    outs = []
+    at = 0
+    for place, gradient in enumerate(gradients):
+        size = gradient.size // shards
+        piece = total[at : at + size]
+        at += size
+        if place == 0:
+            outs.append(piece.reshape(-1, gradient.shape[0]).T)
+        else:
+            outs.append(piece.reshape((gradient.shape[0] // shards,) + gradient.shape[1:]))
+    return tuple(outs)
 
 
 def local(
@@ -222,93 +245,17 @@
         word_shrink,
     )
     section_index = lax.axis_index("section")
-    on_first = section_index == 0
-    micro_count = chars.shape[0]
-    per_section = micro_count // lax.axis_size("section")
-    word_count = chars.shape[2]
-    char_zeros = tuple(
-        (jnp.zeros(entry.shape, jnp.float32) for entry in (language_table,) + char_weights)
-    )
-    word_zeros = tuple(
-        (jnp.zeros(entry.shape, jnp.float32) for entry in (word_input,) + word_weights)
-    )
-    char_totals = char_zeros
-    word_totals = word_zeros
-    results = []
-    text_grads = []
-    for micro_step in range(micro_count):
-        char_text = chars[micro_step, 0]
-        char_count = counts[micro_step, 0]
-        language = languages[micro_step, 0]
-        cot_rows = cotangent[micro_step, 0]
-
-        def make_pooled():
-            return char_front(char_text, char_count, language, language_table, char_weights)[0]
-
-        def no_pooled():
-            return jnp.zeros((word_count, char_text.shape[-1]), jnp.bfloat16)
-
-        pooled = lax.cond(on_first, make_pooled, no_pooled)
-        arrived = passed_along(pooled, "section", 1)
-
-        def run_word():
-            return word_full(arrived, cot_rows, word_input, word_weights)
-
-        def skip_word():
-            return (
-                jnp.zeros((word_count, cot_rows.shape[-1]), jnp.float32),
-                jnp.zeros(arrived.shape, jnp.bfloat16),
-                word_zeros,
-            )
-
-        result, dpooled, word_grads = lax.cond(on_first, skip_word, run_word)
-        returned = passed_along(dpooled, "section", -1)
-
-        def run_char():
-            pooled_again, stored, present, onehot = char_front(
-                char_text, char_count, language, language_table, char_weights
-            )
-            return char_back(stored, present, onehot, char_count, returned, char_weights)
-
-        def skip_char():
-            return (jnp.zeros(char_text.shape, jnp.float32), char_zeros)
-
-        text_grad, char_grads = lax.cond(on_first, run_char, skip_char)
-        char_totals = tuple((first + second for first, second in zip(char_totals, char_grads)))
-        word_totals = tuple((first + second for first, second in zip(word_totals, word_grads)))
-        results.append(result)
-        text_grads.append(text_grad)
-    lower_results = jnp.stack(results[:per_section])[:, None]
-    arrived_results = passed_along(lower_results.astype(jnp.bfloat16), "section", -1).astype(
-        lower_results.dtype
-    )
-    output = jnp.where(on_first, arrived_results, jnp.stack(results[per_section:])[:, None])
-    upper_grads = jnp.stack(text_grads[per_section:])[:, None]
-    arrived_grads = passed_along(upper_grads.astype(jnp.bfloat16), "section", 1).astype(
-        upper_grads.dtype
-    )
-    chars_grad = jnp.where(on_first, jnp.stack(text_grads[:per_section])[:, None], arrived_grads)
-    gradients = char_totals + word_totals
-    shares = (
-        lax.psum_scatter(gradients[0], "dp", scatter_dimension=1, tiled=True),
-        lax.psum_scatter(gradients[1], "dp", scatter_dimension=0, tiled=True),
-        lax.psum_scatter(gradients[2], "dp", scatter_dimension=0, tiled=True),
-        lax.psum_scatter(gradients[3], "dp", scatter_dimension=0, tiled=True),
-        lax.psum_scatter(gradients[4], "dp", scatter_dimension=0, tiled=True),
-        lax.psum_scatter(gradients[5], "dp", scatter_dimension=0, tiled=True),
-        lax.psum_scatter(gradients[6], "dp", scatter_dimension=0, tiled=True),
-        lax.psum_scatter(gradients[7], "dp", scatter_dimension=0, tiled=True),
-        lax.psum_scatter(gradients[8], "dp", scatter_dimension=0, tiled=True),
-        lax.psum_scatter(gradients[9], "dp", scatter_dimension=0, tiled=True),
-        lax.psum_scatter(gradients[10], "dp", scatter_dimension=0, tiled=True),
-        lax.psum_scatter(gradients[11], "dp", scatter_dimension=0, tiled=True),
-        lax.psum_scatter(gradients[12], "dp", scatter_dimension=0, tiled=True),
-        lax.psum_scatter(gradients[13], "dp", scatter_dimension=0, tiled=True),
-    )
-    totals = jax.tree.map(
-        lambda part: part.astype(jnp.float32), lax.psum(for_sending(shares), "section")
-    )
-    return (output, chars_grad) + tuple(totals)
+    char_text = chars[section_index, 0]
+    char_count = counts[section_index, 0]
+    language = languages[section_index, 0]
+    cot_rows = cotangent[section_index, 0]
+    pooled, stored, present, onehot = char_front(
+        char_text, char_count, language, language_table, char_weights
+    )
+    result, dpooled, word_grads = word_full(pooled, cot_rows, word_input, word_weights)
+    text_grad, char_grads = char_back(stored, present, onehot, char_count, dpooled, char_weights)
+    totals = reduce_rows(char_grads + word_grads)
+    return (result[None, None], text_grad[None, None]) + totals
 
 
 def solution(mesh):

time: 952 us -> 427 us (0.45)
  waiting for transfers between devices: 583 us -> 138 us
  local copies, waits for them, and re-layouts: 112 us -> 168 us
  other arithmetic: 95.5 us -> 46.2 us
  blocking collectives: 35.4 us -> 0 us
  matrix products: 88.6 us -> 55.7 us
  between operations: 16.4 us -> 2.34 us
    reduce_scatter x9 -> x0, waiting for transfers between devices: 546 us -> none  [the longest x1 74.3 us: local(): lax.psum_scatter(gradients[12], 'dp', scatter_dimension=0, tiled=True)]
    ppermute x6 -> x5, waiting for transfers between devices: 0.02 us -> 138 us  [the longest x4 117 us: reduce_rows(): lax.ppermute(pairs[:, 1], 'dp', [(i, i ^ bit) for i in range(shards)])]
    psum x2 -> x0, waiting for transfers between devices: 37 us -> none  [local(): lax.psum(for_sending(shares), 'section')]
    unnamed x1 -> x0, blocking collectives: 35.4 us -> none
    reshape x0 -> x21, local copies, waits for them, and re-layouts: none -> 32.1 us  [the longest x9 17.3 us: reduce_rows(): flat.append(gradient.astype(jnp.bfloat16).reshape(shards, -1))]
    add x14 -> x1, other arithmetic: 33.2 us -> 1.89 us  [reduce_rows(): total = (packed.astype(jnp.float32) + arrived.astype(jnp.float32))[0]]
    unnamed x65 -> x183, local copies, waits for them, and re-layouts: 11.7 us -> 40.2 us
    gather x0 -> x6, local copies, waits for them, and re-layouts: none -> 28.4 us  [reduce_rows(): packed = jnp.take(packed, jnp.arange(shards) ^ me, axis=0)]
  transfers between devices with their start and end apart: 18 -> 5, of which waited for: 11 -> 5; matrix products, arithmetic and copies ran while one was open for 19% -> 0% of each run, Pallas kernels for 0% -> 0%
where the time goes in v1:
time: 427 us; the launch traced here: 419 us
  local copies, waits for them, and re-layouts  168 us (39%)
  waiting for transfers between devices  138 us (32%)
  matrix products  55.7 us (13%)
  other arithmetic  46.2 us (11%)
  starting transfers between devices  8.99 us (2%)
    ppermute x4, waiting for transfers between devices, reduce_rows(): lax.ppermute(pairs[:, 1], 'dp', [(i, i ^ bit) for i in range(shards)])  117 us
    unnamed x183, local copies, waits for them, and re-layouts  40.2 us
    gather x6, local copies, waits for them, and re-layouts, reduce_rows(): packed = jnp.take(packed, jnp.arange(shards) ^ me, axis=0)  28.4 us
    concatenate x2, local copies, waits for them, and re-layouts, reduce_rows(): packed = jnp.concatenate(flat, axis=1)  22.4 us
    ppermute x1, waiting for transfers between devices, reduce_rows(): arrived = lax.ppermute(packed, 'section', [(0, 1), (1, 0)])  21.6 us
    reshape x9, local copies, waits for them, and re-layouts, reduce_rows(): flat.append(gradient.astype(jnp.bfloat16).reshape(shards, -1))  17.3 us
    unnamed x2, other arithmetic  12.4 us
    slice x2, local copies, waits for them, and re-layouts, reduce_rows(): pairs[:, 0].astype(jnp.float32) + arrived.astype(jnp.float32)  11.6 us
  transfers between devices with their start and end apart: 5, of which 5 were waited for; matrix products, arithmetic and copies ran while one was open for 0% of the time, Pallas kernels for 0%

profile of v1, /device:TPU:0, one launch (start us, length us, event | category | flops | bytes accessed | tf_op | source)
XLA Modules:
  0.0 419.1 jit_solution(5798016133466205497)
XLA Ops:
  4.8 1.5 fusion.114
  9.5 3.0 convolution_convert_fusion.5
  12.4 5.7 %reshape.619 = bf16[64,16,3,4,64]{4,3,2,1,0:T(4,128)(2,1)} reshape(bf16[64,16,768]{2,1,0:T(8,128)(2,1)} %convolution_convert_fusion.5) | data formatting | bytes 3145728 | tf_op jit(solution)/shard_map/reshape | solution.py:23
  18.1 4.2 %fusion.137 = (bf16[64,16,1,4,64]{4,3,2,1,0:T(4,128)(2,1)S(1)}, bf16[64,16,1,4,64]{4,3,2,1,0:T(4,128)(2,1)S(1)}, bf16[64,16,1,4,64]{4,3,2,1,0:T(4,128)(2,1)S(1)}) fusion(bf16[64,16,3,4,64]{4,3,2,1,0:T(4,128)(2,1)} %reshape.619), kind=kLoop, calls=%fused_computation.263 | loop fusion | bytes 3145728 | tf_op jit(solution)/shard_map/slice | solution.py:33
  25.6 1.5 convert_element_type.330
  27.0 1.6 multiply_reduce_fusion.3
  28.7 4.3 %multiply_convert_fusion = (bf16[64,16,1024]{2,1,0:T(8,128)(2,1)S(1)}, f32[64,16,1024]{2,1,0:T(8,128)}) fusion(bf16[256,1024]{1,0:T(8,128)(2,1)} %param.26, f32[64,16,256]{2,1,0:T(8,128)S(1)} %get-tuple-element.97, f32[256]{0:T(256)S(1)} %copy-done.60, f32[64,16]{1,0:T(8,128)S(1)} %fusion.113), kind=kOutput, calls=%fused_computation.22 | convolution fusion | flops 547094528 | bytes 7869440 | tf_op jit(solution)/shard_map/blc,cf->blf/dot_general | solution.py:98
  36.7 1.8 fusion.139
  41.4 1.5 multiply_reduce_fusion.9
  53.6 2.0 multiply_reduce_fusion.6
  57.6 1.7 convolution_convert_fusion.9
  59.2 2.0 convolution_convert_fusion.8
  61.3 1.7 fusion.19
  63.8 3.5 fusion.3
  67.3 1.6 fusion.18
  73.5 2.4 reshape.625
  82.6 1.6 copy.132
  84.2 2.9 convert_element_type.365
  87.2 3.2 fusion.20
  90.4 2.2 fusion.42
  93.4 2.1 convolution_convert_fusion
  95.5 2.1 convolution_convert_fusion.1
  99.0 2.1 reshape.629
  101.1 1.8 reshape.630
  102.9 2.1 reshape.632
  107.8 2.0 reshape.626
  109.7 2.8 fusion.40
  114.2 3.2 reshape.634
  117.4 3.3 reshape.633
  124.0 3.7 dynamic-update-slice.6
  127.7 2.0 dynamic-update-slice.7
  129.7 1.5 dynamic-update-slice.8
  131.2 4.9 %dynamic-update-slice.9 = bf16[16,106688]{1,0:T(8,128)(2,1)} dynamic-update-slice(bf16[16,106688]{1,0:T(8,128)(2,1)} %dynamic-update-slice.8, bf16[16,16384]{1,0:T(8,128)(2,1)S(1)} %copy-done.29, s32[]{} %constant.102, s32[]{} %constant.110) | dynamic-update-slice | bytes 1048580
  136.0 4.9 %dynamic-update-slice.10 = bf16[16,106688]{1,0:T(8,128)(2,1)} dynamic-update-slice(bf16[16,106688]{1,0:T(8,128)(2,1)} %dynamic-update-slice.9, bf16[16,16384]{1,0:T(8,128)(2,1)S(1)} %copy-done.28, s32[]{} %constant.102, s32[]{} %constant.111) | dynamic-update-slice | bytes 1048580
  140.9 3.7 dynamic-update-slice.11
  146.1 9.5 %dynamic-update-slice.13 = bf16[16,106688]{1,0:T(8,128)(2,1)} dynamic-update-slice(bf16[16,106688]{1,0:T(8,128)(2,1)} %dynamic-update-slice.12, bf16[16,49152]{1,0:T(8,128)(2,1)S(1)} %reshape.631, s32[]{} %constant.102, s32[]{} %constant.114) | dynamic-update-slice | bytes 3145732 | tf_op jit(solution)/shard_map/concatenate | solution.py:185
  155.6 2.1 mini-gather-slice.3
  158.6 2.3 pad_maximum_fusion.1
  160.9 8.4 %gather_fusion.2 = bf16[16,84704]{1,0:T(8,128)(2,1)} fusion(bf16[16,84704]{1,0:T(8,128)(2,1)} %pad_maximum_fusion.1, s32[1024]{0:T(1024)} %pad_clamp_fusion), kind=kCustom, calls=%fused_computation.2 | custom fusion | bytes 5421120 | tf_op jit(solution)/shard_map/jit(_take)/gather | solution.py:187
  169.3 4.3 %gather_fusion = bf16[16,84736]{1,0:T(8,128)(2,1)} fusion(bf16[16,84736]{1,0:T(8,128)(2,1)S(1)} %mini-gather-slice.3, s32[1024]{0:T(1024)} %pad_clamp_fusion), kind=kCustom, calls=%fused_computation | custom fusion | bytes 5423168 | tf_op jit(solution)/shard_map/jit(_take)/gather | solution.py:187
  175.7 12.9 %dynamic-update-slice.3 = bf16[16,131104]{1,0:T(8,128)(2,1)} dynamic-update-slice(bf16[16,131104]{1,0:T(8,128)(2,1)} %dynamic-update-slice.2, bf16[16,65536]{1,0:T(8,128)(2,1)} %reshape.633, s32[]{} %constant.102, s32[]{} %constant.105) | dynamic-update-slice | bytes 4194308 | tf_op jit(solution)/shard_map/concatenate | solution.py:185
  188.6 2.5 mini-gather-slice.4
  191.1 4.0 gather_fusion.1
  195.1 11.8 %pad_maximum_fusion = bf16[16,254176]{1,0:T(8,128)(2,1)} fusion(bf16[16,84704]{1,0:T(8,128)(2,1)} %gather_fusion.2, bf16[16,84736]{1,0:T(8,128)(2,1)} %gather_fusion.1, bf16[16,84736]{1,0:T(8,128)(2,1)} %gather_fusion), kind=kLoop, calls=%fused_computation.3 | loop fusion | flops 24400896 | bytes 16267264
  206.9 7.1 %gather.7 = bf16[8,2,254176]{2,1,0:T(2,128)(2,1)} reshape(bf16[16,254176]{1,0:T(8,128)(2,1)} %pad_maximum_fusion) | data formatting | bytes 16267264 | tf_op jit(solution)/shard_map/jit(_take)/gather | solution.py:187
  214.0 6.0 %copy_select_fusion = bf16[8,2,254176]{2,0,1:T(8,128)(2,1)S(1)} fusion(bf16[8,2,254176]{2,1,0:T(2,128)(2,1)} %gather.7, pred[8,2]{0,1:T(4,128)(4,1)S(1)} %copy-done.72), kind=kLoop, calls=%fused_computation.6 | loop fusion | flops 4066816 | bytes 16267280 | tf_op jit(solution)/shard_map/jit(_take)/select_n | solution.py:187
  220.9 6.6 %collective-permute-done = bf16[8,254176]{1,0:T(8,128)(2,1)S(1)} collective-permute-done((bf16[8,254176]{1,0:T(8,128)(2,1)S(1)}, bf16[8,254176]{1,0:T(8,128)(2,1)S(1)}, u32[]{:S(2)}, u32[]{:S(2)}) %collective-permute-start) | collective-permute-done | bytes 4066848 | tf_op jit(solution)/shard_map/ppermute | solution.py:191
  227.5 2.4 fusion
  229.9 5.6 %reshape.635 = bf16[4,2,254176]{2,1,0:T(2,128)(2,1)} reshape(bf16[8,254176]{1,0:T(8,128)(2,1)} %fusion) | data formatting | bytes 8133632 | tf_op jit(solution)/shard_map/reshape | solution.py:190
  235.5 8.7 %fusion.136 = (bf16[4,1,254176]{2,1,0:T(2,128)(2,1)S(1)}, bf16[4,1,254176]{2,1,0:T(2,128)(2,1)S(1)}) fusion(bf16[4,2,254176]{2,1,0:T(2,128)(2,1)} %reshape.635), kind=kLoop, calls=%fused_computation.262 | loop fusion | bytes 8133632 | tf_op jit(solution)/shard_map/slice | solution.py:192
  244.2 2.7 copy.204
  246.9 3.0 collective-permute-start.1
  249.8 44.6 %collective-permute-done.1 = bf16[4,254176]{1,0:T(4,128)(2,1)S(1)} collective-permute-done((bf16[4,254176]{1,0:T(4,128)(2,1)S(1)}, bf16[4,254176]{1,0:T(4,128)(2,1)S(1)}, u32[]{:S(2)}, u32[]{:S(2)}) %collective-permute-start.1) | collective-permute-done | bytes 2033440 | tf_op jit(solution)/shard_map/ppermute | solution.py:191
  294.4 4.0 fusion.11
  298.4 3.1 reshape.636
  301.5 2.9 fusion.138
  304.4 2.7 copy.205
  307.1 1.9 collective-permute-start.2
  309.0 22.2 %collective-permute-done.2 = bf16[2,254176]{1,0:T(2,128)(2,1)S(1)} collective-permute-done((bf16[2,254176]{1,0:T(2,128)(2,1)S(1)}, bf16[2,254176]{1,0:T(2,128)(2,1)S(1)}, u32[]{:S(2)}, u32[]{:S(2)}) %collective-permute-start.2) | collective-permute-done | bytes 1016736 | tf_op jit(solution)/shard_map/ppermute | solution.py:191
  331.2 2.6 fusion.50
  335.0 2.5 collective-permute-start.3
  337.5 43.3 %collective-permute-done.3 = bf16[1,254176]{1,0:T(2,128)(2,1)S(1)} collective-permute-done((bf16[1,254176]{1,0:T(2,128)(2,1)S(1)}, bf16[1,254176]{1,0:T(2,128)(2,1)S(1)}, u32[]{:S(2)}, u32[]{:S(2)}) %collective-permute-start.3) | collective-permute-done | bytes 508384 | tf_op jit(solution)/shard_map/ppermute | solution.py:191
  384.4 21.6 %collective-permute-done.4 = bf16[1,254176]{1,0:T(2,128)(2,1)S(1)} collective-permute-done((bf16[1,254176]{1,0:T(2,128)(2,1)S(1)}, bf16[1,254176]{1,0:T(2,128)(2,1)S(1)}, u32[]{:S(2)}, u32[]{:S(2)}) %collective-permute-start.4) | collective-permute-done | bytes 508384 | tf_op jit(solution)/shard_map/ppermute | solution.py:196
  406.0 1.9 convert_add_fusion.4
  (271 shorter events, 71.7 us)
Async XLA Ops:
  0.6 42.3 %copy-start = (bf16[512,2048]{1,0:T(8,128)(2,1)S(1)}, bf16[512,2048]{1,0:T(8,128)(2,1)}, u32[]{:S(2)}) copy-start(bf16[512,2048]{1,0:T(8,128)(2,1)} %param.33) | copy-start | bytes 6291460
  6.2 20.8 %copy-start.58 = (f32[1,256]{1,0:T(1,128)}, f32[1,256]{1,0:T(1,128)S(1)}, u32[]{:S(2)}) copy-start(f32[1,256]{1,0:T(1,128)S(1)} %fusion.114) | copy-start | bytes 3076
  6.9 26.9 %copy-start.67 = (f32[64]{0:T(128)}, f32[64]{0:T(128)S(1)}, u32[]{:S(2)}) copy-start(f32[64]{0:T(128)S(1)} %get-tuple-element.77) | copy-start | bytes 772
  25.0 2.0 copy-start.42
  25.0 3.6 copy-start.60
  28.7 4.3 %copy-start.77 = (bf16[1024,256]{1,0:T(8,128)(2,1)S(1)}, bf16[1024,256]{1,0:T(8,128)(2,1)}, u32[]{:S(2)}) copy-start(bf16[1024,256]{1,0:T(8,128)(2,1)} %param.27) | copy-start | bytes 1572868
  33.0 2.3 copy-start.8
  33.0 2.2 copy-start.55
  34.9 5.9 %copy-start.62 = (f32[64]{0:T(128)}, f32[64]{0:T(128)S(1)}, u32[]{:S(2)}) copy-start(f32[64]{0:T(128)S(1)} %fusion.126) | copy-start | bytes 772
  36.7 6.3 %copy-start.56 = (f32[512]{0:T(512)S(1)}, f32[512]{0:T(512)}, u32[]{:S(2)}) copy-start(f32[512]{0:T(512)} %param.32) | copy-start | bytes 6148
  40.7 2.8 copy-start.24
  40.8 2.8 copy-start.52
  43.0 2.8 copy-start.65
  43.5 2.2 copy-start.10
  43.6 2.3 copy-start.26
  45.8 3.1 copy-start.20
  46.2 7.4 %copy-start.9 = (bf16[512,1536]{1,0:T(8,128)(2,1)S(1)}, bf16[512,1536]{1,0:T(8,128)(2,1)}, u32[]{:S(2)}) copy-start(bf16[512,1536]{1,0:T(8,128)(2,1)} %param.30) | copy-start | bytes 4718596
  48.9 7.3 %copy-start.63 = (f32[64]{0:T(128)S(1)}, f32[64]{0:T(128)}, u32[]{:S(2)}) copy-start(f32[64]{0:T(128)} %copy-done.62) | copy-start | bytes 772
  50.0 7.5 %copy-start.48 = (f32[64,256]{1,0:T(8,128)S(1)}, f32[64,256]{1,0:T(8,128)}, u32[]{:S(2)}) copy-start(f32[64,256]{1,0:T(8,128)} %copy-done.47) | copy-start | bytes 196612
  53.6 9.4 %copy-start.30 = (bf16[64,1536]{1,0:T(8,128)(2,1)}, bf16[64,1536]{1,0:T(8,128)(2,1)S(1)}, u32[]{:S(2)}) copy-start(bf16[64,1536]{1,0:T(8,128)(2,1)S(1)} %convert_element_type.352) | copy-start | bytes 589828
  53.6 7.6 %copy-start.82 = (bf16[64,16,1024]{2,1,0:T(8,128)(2,1)S(1)}, bf16[64,16,1024]{2,1,0:T(8,128)(2,1)}, u32[]{:S(2)}) copy-start(bf16[64,16,1024]{2,1,0:T(8,128)(2,1)} %copy-done.81) | copy-start | bytes 6291460
  61.3 2.5 copy-start.83
  63.8 3.5 copy-start.61
  72.4 3.6 copy-start.38
  72.4 4.6 %copy-start.3 = (f32[64,4,16,16]{2,3,1,0:T(8,128)S(1)}, f32[64,4,16,16]{2,3,1,0:T(8,128)}, u32[]{:S(2)}) copy-start(f32[64,4,16,16]{2,3,1,0:T(8,128)} %copy-done.2) | copy-start | bytes 786436
  84.2 2.9 copy-start.50
  84.2 2.9 copy-start.59
  84.2 2.9 copy-start.71
  87.1 3.2 copy-start.21
  87.1 3.2 copy-start.33
  87.2 3.2 copy-start.80
  90.4 2.3 copy-start.31
  90.4 2.2 copy-start.64
  90.4 2.9 copy-start.11
  90.4 2.9 copy-start.53
  92.6 2.8 copy-start.35
  92.6 2.8 copy-start.57
  92.6 2.8 copy-start.66
  93.3 4.3 %copy-start.74 = (s32[16]{0:T(128)S(1)}, s32[16]{0:T(128)}, u32[]{:S(2)}) copy-start(s32[16]{0:T(128)} %fusion.124) | copy-start | bytes 196
  93.3 4.9 %copy-start.75 = (f32[8]{0:T(128)S(1)}, f32[8]{0:T(128)}, u32[]{:S(2)}) copy-start(f32[8]{0:T(128)} %fusion.123) | copy-start | bytes 100
  93.4 5.5 %copy-start.68 = (bf16[512]{0:T(512)(128)(2,1)S(1)}, bf16[512]{0:T(512)(128)(2,1)}, u32[]{:S(2)}) copy-start(bf16[512]{0:T(512)(128)(2,1)} %get-tuple-element.75) | copy-start | bytes 3076
  93.4 5.6 %copy-start.69 = (bf16[512]{0:T(512)(128)(2,1)S(1)}, bf16[512]{0:T(512)(128)(2,1)}, u32[]{:S(2)}) copy-start(bf16[512]{0:T(512)(128)(2,1)} %get-tuple-element.73) | copy-start | bytes 3076
  95.5 10.5 %copy-start.23 = (bf16[256,1024]{1,0:T(8,128)(2,1)S(1)}, bf16[256,1024]{1,0:T(8,128)(2,1)}, u32[]{:S(2)}) copy-start(bf16[256,1024]{1,0:T(8,128)(2,1)} %fusion.18) | copy-start | bytes 1572868
  95.5 11.6 %copy-start.76 = (bf16[256]{0:T(256)(128)(2,1)S(1)}, bf16[256]{0:T(256)(128)(2,1)}, u32[]{:S(2)}) copy-start(bf16[256]{0:T(256)(128)(2,1)} %get-tuple-element.66) | copy-start | bytes 1540
  95.5 12.2 %copy-start.45 = (f32[64,16]{1,0:T(8,128)S(1)}, f32[64,16]{1,0:T(8,128)}, u32[]{:S(2)}) copy-start(f32[64,16]{1,0:T(8,128)} %copy-done.44) | copy-start | bytes 12292
  95.5 12.2 %copy-start.54 = (f32[64,16]{1,0:T(8,128)S(1)}, f32[64,16]{1,0:T(8,128)}, u32[]{:S(2)}) copy-start(f32[64,16]{1,0:T(8,128)} %get-tuple-element.113) | copy-start | bytes 12292
  97.6 12.1 %copy-start.6 = (f32[64,16,256]{2,1,0:T(8,128)S(1)}, f32[64,16,256]{2,1,0:T(8,128)}, u32[]{:S(2)}) copy-start(f32[64,16,256]{2,1,0:T(8,128)} %copy-done.5) | copy-start | bytes 3145732
  97.6 12.1 %copy-start.51 = (f32[64,16]{1,0:T(8,128)S(1)}, f32[64,16]{1,0:T(8,128)}, u32[]{:S(2)}) copy-start(f32[64,16]{1,0:T(8,128)} %copy-done.49) | copy-start | bytes 12292
  117.4 6.6 %copy-start.32 = (bf16[16,12288]{1,0:T(8,128)(2,1)S(1)}, bf16[16,12288]{1,0:T(8,128)(2,1)}, u32[]{:S(2)}) copy-start(bf16[16,12288]{1,0:T(8,128)(2,1)} %reshape.626) | copy-start | bytes 1179652
  120.8 10.4 %copy-start.29 = (bf16[16,16384]{1,0:T(8,128)(2,1)S(1)}, bf16[16,16384]{1,0:T(8,128)(2,1)}, u32[]{:S(2)}) copy-start(bf16[16,16384]{1,0:T(8,128)(2,1)} %reshape.628) | copy-start | bytes 1572868
  120.8 15.3 %copy-start.28 = (bf16[16,16384]{1,0:T(8,128)(2,1)S(1)}, bf16[16,16384]{1,0:T(8,128)(2,1)}, u32[]{:S(2)}) copy-start(bf16[16,16384]{1,0:T(8,128)(2,1)} %reshape.629) | copy-start | bytes 1572868
  120.8 20.2 %copy-start.36 = (bf16[16,8192]{1,0:T(8,128)(2,1)S(1)}, bf16[16,8192]{1,0:T(8,128)(2,1)}, u32[]{:S(2)}) copy-start(bf16[16,8192]{1,0:T(8,128)(2,1)} %reshape.630) | copy-start | bytes 786436
  155.6 2.4 copy-start.4
  155.6 3.0 copy-start.7
  169.3 4.3 %copy-start.27 = (bf16[16,16384]{1,0:T(8,128)(2,1)S(1)}, bf16[16,16384]{1,0:T(8,128)(2,1)}, u32[]{:S(2)}) copy-start(bf16[16,16384]{1,0:T(8,128)(2,1)} %reshape.632) | copy-start | bytes 1572868
  206.9 7.1 %copy-start.72 = (pred[8,2]{0,1:T(4,128)(4,1)S(1)}, pred[8,2]{0,1:T(4,128)(4,1)}, u32[]{:S(2)}) copy-start(pred[8,2]{0,1:T(4,128)(4,1)} %compare_and_fusion) | copy-start | bytes 52
  220.4 7.1 %collective-permute-start = (bf16[8,254176]{1,0:T(8,128)(2,1)S(1)}, bf16[8,254176]{1,0:T(8,128)(2,1)S(1)}, u32[]{:S(2)}, u32[]{:S(2)}) collective-permute-start(bf16[8,254176]{1,0:T(8,128)(2,1)S(1)} %slice_bitcast_fusion), channel_id=1, source_target_pairs={{0,1},{1,0},{2,3},{3,2},{4,5},{5,4},{6,7},{7,6},{8,9},{9,8},{10,11... | collective-permute-start | bytes 12200456 | tf_op jit(solution)/shard_map/ppermute | solution.py:191
  246.9 47.5 %collective-permute-start.1 = (bf16[4,254176]{1,0:T(4,128)(2,1)S(1)}, bf16[4,254176]{1,0:T(4,128)(2,1)S(1)}, u32[]{:S(2)}, u32[]{:S(2)}) collective-permute-start(bf16[4,254176]{1,0:T(4,128)(2,1)S(1)} %bitcast.265), channel_id=1, source_target_pairs={{0,2},{1,3},{2,0},{3,1},{4,6},{5,7},{6,4},{7,5},{8,10},{9,11},{10,... | collective-permute-start | bytes 6100232 | tf_op jit(solution)/shard_map/ppermute | solution.py:191
  307.1 24.1 %collective-permute-start.2 = (bf16[2,254176]{1,0:T(2,128)(2,1)S(1)}, bf16[2,254176]{1,0:T(2,128)(2,1)S(1)}, u32[]{:S(2)}, u32[]{:S(2)}) collective-permute-start(bf16[2,254176]{1,0:T(2,128)(2,1)S(1)} %bitcast.268), channel_id=1, source_target_pairs={{0,4},{1,5},{2,6},{3,7},{4,0},{5,1},{6,2},{7,3},{8,12},{9,13},{10,... | collective-permute-start | bytes 3050120 | tf_op jit(solution)/shard_map/ppermute | solution.py:191
  333.8 49.5 %copy-start.12 = (f32[64,2048]{1,0:T(8,128)S(1)}, f32[64,2048]{1,0:T(8,128)}, u32[]{:S(2)}) copy-start(f32[64,2048]{1,0:T(8,128)} %copy-done.10) | copy-start | bytes 1572868
  333.8 49.5 %copy-start.25 = (bf16[2048,512]{1,0:T(8,128)(2,1)S(1)}, bf16[2048,512]{1,0:T(8,128)(2,1)}, u32[]{:S(2)}) copy-start(bf16[2048,512]{1,0:T(8,128)(2,1)} %param.34) | copy-start | bytes 6291460
  335.0 45.9 %collective-permute-start.3 = (bf16[1,254176]{1,0:T(2,128)(2,1)S(1)}, bf16[1,254176]{1,0:T(2,128)(2,1)S(1)}, u32[]{:S(2)}, u32[]{:S(2)}) collective-permute-start(bf16[1,254176]{1,0:T(2,128)(2,1)S(1)} %slice_bitcast_fusion.2), channel_id=1, source_target_pairs={{0,8},{1,9},{2,10},{3,11},{4,12},{5,13},{6,14},{7,15},{8,0},{9,1},... | collective-permute-start | bytes 1525064 | tf_op jit(solution)/shard_map/ppermute | solution.py:191
  382.2 23.8 %collective-permute-start.4 = (bf16[1,254176]{1,0:T(2,128)(2,1)S(1)}, bf16[1,254176]{1,0:T(2,128)(2,1)S(1)}, u32[]{:S(2)}, u32[]{:S(2)}) collective-permute-start(bf16[1,254176]{1,0:T(2,128)(2,1)S(1)} %fusion.53), channel_id=1, source_target_pairs={{0,16},{16,0},{1,17},{17,1},{2,18},{18,2},{3,19},{19,3},{4,20},{20... | collective-permute-start | bytes 1525064 | tf_op jit(solution)/shard_map/ppermute | solution.py:196
  406.0 12.6 %copy-start.1 = (bf16[512,2048]{1,0:T(8,128)(2,1)S(1)}, bf16[512,2048]{1,0:T(8,128)(2,1)}, u32[]{:S(2)}) copy-start(bf16[512,2048]{1,0:T(8,128)(2,1)} %param.33) | copy-start | bytes 6291460
  (25 other events, 32.1 us)

commit v2 on v1

--- a/solution.py
+++ b/solution.py
@@ -1,13 +1,927 @@
+import functools
+
 import jax
 import jax.numpy as jnp
 from jax import lax
+from jax.experimental import pallas as pl
+from jax.experimental.pallas import tpu as pltpu
 from jax.sharding import PartitionSpec as P
 
 CH = 4
 H = 8
-
+HEAD = 64
+SLAB = 256
+BLOCK = 128
+STEP = 256
+VMEM_LIMIT = 60 * 1024 * 1024
 
 eps = 1e-05
+
+f32 = jnp.float32
+bf16 = jnp.bfloat16
+
+
+def dot(a, b):
+    return jnp.dot(a, b, preferred_element_type=f32)
+
+
+def dot_nt(a, b):
+    return lax.dot_general(a, b, (((1,), (1,)), ((), ())), preferred_element_type=f32)
+
+
+def lanes(shape):
+    return lax.broadcasted_iota(jnp.int32, shape, 1)
+
+
+def rows_of(shape):
+    return lax.broadcasted_iota(jnp.int32, shape, 0)
+
+
+def flip(a):
+    size = a.shape[1]
+    width = min(size, 256)
+    eye = jnp.where(rows_of((width, width)) == lanes((width, width)), 1.0, 0.0).astype(bf16)
+    return jnp.concatenate(
+        [dot_nt(eye, a[:, at : at + width]).astype(bf16) for at in range(0, size, width)], axis=0
+    )
+
+
+def head_mask(head):
+    return jnp.where(lanes((1, SLAB)) // HEAD == head, 1.0, 0.0).astype(bf16)
+
+
+def stack_heads(a):
+    return jnp.concatenate([a * head_mask(head) for head in range(SLAB // HEAD)], axis=0)
+
+
+def merge_heads(a):
+    rows = a.shape[0] // (SLAB // HEAD)
+    head = lanes((rows, SLAB)) // HEAD
+    total = a[:rows]
+    for place in range(1, SLAB // HEAD):
+        total = jnp.where(head == place, a[place * rows : (place + 1) * rows], total)
+    return total
+
+
+def compact(scores, length):
+    group = lanes((length, BLOCK)) // length
+    total = scores[:length]
+    for place in range(1, BLOCK // length):
+        total = jnp.where(group == place, scores[place * length : (place + 1) * length], total)
+    return total
+
+
+def expand(values, length):
+    group = lanes((length, BLOCK)) // length
+    return jnp.concatenate(
+        [jnp.where(group == place, values, 0.0) for place in range(BLOCK // length)], axis=0
+    ).astype(bf16)
+
+
+def attend(q, k, v, key_mask, length):
+    heads = SLAB // HEAD
+    scores = dot_nt(stack_heads(k), q)
+    v_flipped = flip(v)
+    kept = []
+    mixed = []
+    for head in range(heads):
+        piece = compact(scores[head * BLOCK : (head + 1) * BLOCK], length) * HEAD**-0.5
+        piece = jnp.where(key_mask, piece, -1e30)
+        weights = jnp.exp(piece - jnp.max(piece, axis=0, keepdims=True))
+        probs = weights / jnp.sum(weights, axis=0, keepdims=True)
+        kept.append(probs)
+        mixed.append(dot(v_flipped[head * HEAD : (head + 1) * HEAD], expand(probs, length)))
+    return (kept, jnp.concatenate(mixed, axis=0).astype(bf16))
+
+
+def attend_back(q, k, v, probs, dmixed, length):
+    heads = SLAB // HEAD
+    dprobs = dot_nt(stack_heads(v), dmixed)
+    k_flipped = flip(k)
+    dq = []
+    dk = []
+    dv = []
+    for head in range(heads):
+        own = probs[head]
+        piece = compact(dprobs[head * BLOCK : (head + 1) * BLOCK], length)
+        delta = jnp.sum(own * piece, axis=0, keepdims=True)
+        dscores = expand(own * (piece - delta), length)
+        dq.append(dot(k_flipped[head * HEAD : (head + 1) * HEAD], dscores))
+        dk.append(dot(dscores, q))
+        dv.append(dot(expand(own, length), dmixed))
+    scaling = HEAD**-0.5
+    dq = flip((jnp.concatenate(dq, axis=0) * scaling).astype(bf16))
+    dk = (merge_heads(jnp.concatenate(dk, axis=0)) * scaling).astype(bf16)
+    dv = merge_heads(jnp.concatenate(dv, axis=0)).astype(bf16)
+    return (dq, dk, dv)
+
+
+def unit(x):
+    scale = lax.rsqrt(jnp.mean(x * x, axis=-1, keepdims=True) + eps)
+    return (x * scale, scale)
+
+
+def unit_back(dnormed, gain, normal, scale):
+    weighted = dnormed * gain
+    return scale * (weighted - normal * jnp.mean(normal * weighted, axis=-1, keepdims=True))
+
+
+def gelu_parts(before):
+    c = 0.7978845608028654
+    square = before * before
+    half = 0.5 * jnp.tanh(before * (c + (c * 0.044715) * square)) + 0.5
+    value = before * half
+    slope = half + value * (1.0 - half) * (2.0 * c + (6.0 * c * 0.044715) * square)
+    return (value, slope)
+
+
+def char_rows(chars_ref, table_ref, language):
+    table = table_ref[...].astype(f32)
+    row = jnp.sum(jnp.where(rows_of(table.shape) == language, table, 0.0), axis=0, keepdims=True)
+    return chars_ref[0].astype(f32) + row
+
+
+def counts_by_row(counts_ref, step, slots):
+    words = counts_ref.shape[-1]
+    counts = jnp.broadcast_to(counts_ref[0].astype(f32), (8, words)).astype(bf16)
+    shape = (words, STEP)
+    member = (lanes(shape) + step * STEP) // slots == rows_of(shape)
+    return dot(counts, jnp.where(member, 1.0, 0.0).astype(bf16))[:1]
+
+
+def char_forward_kernel(
+    slots,
+    where_ref,
+    chars_ref,
+    counts_ref,
+    table_ref,
+    gain_attn_ref,
+    project_ref,
+    output_ref,
+    gain_mlp_ref,
+    expand_ref,
+    shrink_ref,
+    pooled_ref,
+    hidden_sum_ref,
+    qkv_ref,
+    probs_ref,
+    mixed_ref,
+    middle_ref,
+    slope_ref,
+    sums,
+):
+    step = pl.program_id(0)
+    x = char_rows(chars_ref, table_ref, where_ref[1])
+    normal, _ = unit(x)
+    normed = (normal * gain_attn_ref[...]).astype(bf16)
+    qkv = dot(normed, project_ref[...]).astype(bf16)
+    qkv_ref[...] = qkv
+    row_counts = counts_by_row(counts_ref, step, slots)
+    mixed = []
+    for block in range(STEP // BLOCK):
+        part = slice(block * BLOCK, (block + 1) * BLOCK)
+        key_mask = rows_of((slots, BLOCK)).astype(f32) < row_counts[:, part]
+        probs, piece = attend(
+            qkv[part, :SLAB], qkv[part, SLAB : 2 * SLAB], qkv[part, 2 * SLAB :], key_mask, slots
+        )
+        for head in range(CH):
+            probs_ref[head * slots : (head + 1) * slots, part] = probs[head]
+        mixed_ref[:, part] = piece
+        mixed.append(flip(piece))
+    mixed = jnp.concatenate(mixed, axis=0)
+    middle = x + dot(mixed, output_ref[...])
+    middle_ref[...] = middle
+    normal, _ = unit(middle)
+    normed = (normal * gain_mlp_ref[...]).astype(bf16)
+    word_shape = (STEP // slots, STEP)
+    lane = lanes(word_shape)
+    member = (lane // slots == rows_of(word_shape)) & ((lane % slots).astype(f32) < row_counts)
+    member = jnp.where(member, 1.0, 0.0).astype(bf16)
+    words = pl.ds(pl.multiple_of(step * (STEP // slots), STEP // slots), STEP // slots)
+    for at in range(0, expand_ref.shape[1], 256):
+        part = slice(at, at + 256)
+        value, slope = gelu_parts(dot(normed, expand_ref[:, part]))
+        slope_ref[:, part] = slope.astype(bf16)
+        hidden_sum_ref[words, part] = dot(member, value.astype(bf16)).astype(bf16)
+    high = middle.astype(bf16)
+    low = (middle - high.astype(f32)).astype(bf16)
+    sums[words, :] = dot(member, high) + dot(member, low)
+
+    @pl.when(step == pl.num_programs(0) - 1)
+    def _():
+        words = counts_ref.shape[-1]
+        shape = (words, words)
+        column = jnp.sum(
+            jnp.where(
+                rows_of(shape) == lanes(shape),
+                jnp.broadcast_to(counts_ref[0].astype(f32), shape),
+                0.0,
+            ),
+            axis=1,
+            keepdims=True,
+        )
+        total = sums[...] + dot(hidden_sum_ref[...], shrink_ref[...])
+        pooled_ref[...] = (total / column).astype(bf16)
+
+
+def char_forward(where, chars, counts, table, weights, slots):
+    gain_attn, project, output, gain_mlp, expand_w, shrink = weights
+    rows, width = chars.shape[1:]
+    words = rows // slots
+    hidden = expand_w.shape[1]
+
+    def whole(array):
+        return pl.BlockSpec(array.shape, lambda i, w: (0,) * array.ndim)
+
+    return pl.pallas_call(
+        functools.partial(char_forward_kernel, slots),
+        grid_spec=pltpu.PrefetchScalarGridSpec(
+            num_scalar_prefetch=1,
+            grid=(rows // STEP,),
+            in_specs=[
+                pl.BlockSpec((1, STEP, width), lambda i, w: (w[0], i, 0)),
+                pl.BlockSpec((1, 1, words), lambda i, w: (w[0], 0, 0)),
+                whole(table),
+                whole(gain_attn),
+                whole(project),
+                whole(output),
+                whole(gain_mlp),
+                whole(expand_w),
+                whole(shrink),
+            ],
+            out_specs=[
+                pl.BlockSpec((words, width), lambda i, w: (0, 0)),
+                pl.BlockSpec((words, hidden), lambda i, w: (0, 0)),
+                pl.BlockSpec((STEP, 3 * width), lambda i, w: (i, 0)),
+                pl.BlockSpec((CH * slots, STEP), lambda i, w: (0, i)),
+                pl.BlockSpec((width, STEP), lambda i, w: (0, i)),
+                pl.BlockSpec((STEP, width), lambda i, w: (i, 0)),
+                pl.BlockSpec((STEP, hidden), lambda i, w: (i, 0)),
+            ],
+            scratch_shapes=[pltpu.VMEM((words, width), f32)],
+        ),
+        out_shape=[
+            jax.ShapeDtypeStruct((words, width), bf16),
+            jax.ShapeDtypeStruct((words, hidden), bf16),
+            jax.ShapeDtypeStruct((rows, 3 * width), bf16),
+            jax.ShapeDtypeStruct((CH * slots, rows), f32),
+            jax.ShapeDtypeStruct((width, rows), bf16),
+            jax.ShapeDtypeStruct((rows, width), f32),
+            jax.ShapeDtypeStruct((rows, hidden), bf16),
+        ],
+        compiler_params=pltpu.CompilerParams(vmem_limit_bytes=VMEM_LIMIT),
+        name="char_forward",
+    )(where, chars, counts, table, gain_attn, project, output, gain_mlp, expand_w, shrink)
+
+
+CHAR_SLOT = 208
+
+
+def char_backward_kernel(
+    slots,
+    shards,
+    where_ref,
+    chars_ref,
+    counts_ref,
+    table_ref,
+    gain_attn_ref,
+    project_ref,
+    output_ref,
+    gain_mlp_ref,
+    expand_ref,
+    shrink_ref,
+    dpooled_ref,
+    hidden_sum_ref,
+    qkv_ref,
+    probs_ref,
+    mixed_ref,
+    middle_ref,
+    slope_ref,
+    grad_ref,
+    keep_ref,
+    send_ref,
+    spread_high,
+    spread_low,
+    dhidden_words,
+    dbefore,
+    dqkv,
+    dy,
+    normed_t,
+    normed_mlp_t,
+    gains,
+    packed,
+    sems,
+):
+    step = pl.program_id(0)
+    words = counts_ref.shape[-1]
+
+    @pl.when(step == 0)
+    def _():
+        shape = (words, words)
+        column = jnp.sum(
+            jnp.where(
+                rows_of(shape) == lanes(shape),
+                jnp.broadcast_to(counts_ref[0].astype(f32), shape),
+                0.0,
+            ),
+            axis=1,
+            keepdims=True,
+        )
+        spread = dpooled_ref[...].astype(f32) / column
+        high = spread.astype(bf16)
+        spread_high[...] = high
+        spread_low[...] = (spread - high.astype(f32)).astype(bf16)
+        dhidden_words[...] = dot_nt(high, shrink_ref[...]).astype(bf16)
+        gains[...] = jnp.zeros_like(gains)
+
+    at_step = pl.ds(pl.multiple_of(step * STEP, STEP), STEP)
+    shape = (STEP, words)
+    row = rows_of(shape) + step * STEP
+    member = (row // slots == lanes(shape)) & (row % slots < counts_ref[0])
+    member = jnp.where(member, 1.0, 0.0).astype(bf16)
+    dnormed = jnp.zeros((STEP, gain_mlp_ref.shape[1]), f32)
+    for at in range(0, expand_ref.shape[1], 256):
+        part = slice(at, at + 256)
+        piece = dot(member, dhidden_words[:, part]).astype(bf16) * slope_ref[:, part]
+        dbefore[at_step, part] = piece
+    dnormed = dot_nt(dbefore[at_step, :], expand_ref[...])
+    normal, scale = unit(middle_ref[...])
+    normed_mlp_t[:, at_step] = flip((normal * gain_mlp_ref[...]).astype(bf16))
+    gains[1:2] += jnp.sum(dnormed * normal, axis=0, keepdims=True)
+    dmiddle = (
+        dot(member, spread_high[...])
+        + dot(member, spread_low[...])
+        + unit_back(dnormed, gain_mlp_ref[...], normal, scale)
+    )
+    dy_low = dmiddle.astype(bf16)
+    dy[at_step, :] = dy_low
+    dmixed = dot_nt(dy_low, output_ref[...]).astype(bf16)
+    for block in range(STEP // BLOCK):
+        part = slice(block * BLOCK, (block + 1) * BLOCK)
+        probs = [probs_ref[head * slots : (head + 1) * slots, part] for head in range(CH)]
+        pieces = attend_back(
+            qkv_ref[part, :SLAB],
+            qkv_ref[part, SLAB : 2 * SLAB],
+            qkv_ref[part, 2 * SLAB :],
+            probs,
+            dmixed[part],
+            slots,
+        )
+        at_block = pl.ds(pl.multiple_of(step * STEP + block * BLOCK, BLOCK), BLOCK)
+        for place in range(3):
+            dqkv[at_block, place * SLAB : (place + 1) * SLAB] = pieces[place]
+    dnormed = dot_nt(dqkv[at_step, :], project_ref[...])
+    normal, scale = unit(char_rows(chars_ref, table_ref, where_ref[1]))
+    normed_t[:, at_step] = flip((normal * gain_attn_ref[...]).astype(bf16))
+    gains[0:1] += jnp.sum(dnormed * normal, axis=0, keepdims=True)
+    dx = dmiddle + unit_back(dnormed, gain_attn_ref[...], normal, scale)
+    grad_ref[...] = dx
+    row_sum = jnp.sum(dx, axis=0, keepdims=True)
+    gains[8:16] += jnp.where(rows_of((8, 1)) == where_ref[1], row_sum, 0.0)
+
+    @pl.when(step == pl.num_programs(0) - 1)
+    def _():
+        me = where_ref[2]
+        width = gains.shape[1]
+
+        def place(shard):
+            other = shard ^ me
+            return (other & 1) * 8 + ((other >> 1) & 3) * 2 + (other >> 3)
+
+        def put(gradient, at):
+            size = gradient.shape[0] // shards
+            for shard in range(shards):
+                piece = gradient[shard * size : (shard + 1) * size].astype(bf16)
+                for column in range(gradient.shape[1] // width):
+                    start = at + column * size
+                    packed[place(shard), start : start + size] = piece[
+                        :, column * width : (column + 1) * width
+                    ]
+            return at + size * (gradient.shape[1] // width)
+
+        at = put(dot(normed_t[...], dqkv[...]), 0)
+        at = put(dot(mixed_ref[...], dy[...]), at)
+        at = put(dot(normed_mlp_t[...], dbefore[...]), at)
+        at = put(dot(flip(hidden_sum_ref[...]), spread_high[...]), at)
+        extra = gains[...].astype(bf16)
+        for shard in range(shards):
+            packed[shard, at : at + 16] = extra
+        half = shards // 2
+        copies = [
+            pltpu.make_async_copy(packed.at[pl.ds(half, half)], send_ref, sems.at[0]),
+            pltpu.make_async_copy(packed.at[pl.ds(0, half)], keep_ref, sems.at[1]),
+        ]
+        for copy in copies:
+            copy.start()
+        for copy in copies:
+            copy.wait()
+
+
+def char_backward(where, chars, counts, table, weights, dpooled, stored, slots, shards):
+    gain_attn, project, output, gain_mlp, expand_w, shrink = weights
+    hidden_sum, qkv, probs, mixed, middle, slope = stored
+    rows, width = chars.shape[1:]
+    words = rows // slots
+    hidden = expand_w.shape[1]
+
+    def whole(array):
+        return pl.BlockSpec(array.shape, lambda i, w: (0,) * array.ndim)
+
+    half = (shards // 2, CHAR_SLOT, width)
+    return pl.pallas_call(
+        functools.partial(char_backward_kernel, slots, shards),
+        grid_spec=pltpu.PrefetchScalarGridSpec(
+            num_scalar_prefetch=1,
+            grid=(rows // STEP,),
+            in_specs=[
+                pl.BlockSpec((1, STEP, width), lambda i, w: (w[0], i, 0)),
+                pl.BlockSpec((1, 1, words), lambda i, w: (w[0], 0, 0)),
+                whole(table),
+                whole(gain_attn),
+                whole(project),
+                whole(output),
+                whole(gain_mlp),
+                whole(expand_w),
+                whole(shrink),
+                whole(dpooled),
+                whole(hidden_sum),
+                pl.BlockSpec((STEP, 3 * width), lambda i, w: (i, 0)),
+                pl.BlockSpec((CH * slots, STEP), lambda i, w: (0, i)),
+                whole(mixed),
+                pl.BlockSpec((STEP, width), lambda i, w: (i, 0)),
+                pl.BlockSpec((STEP, hidden), lambda i, w: (i, 0)),
+            ],
+            out_specs=[
+                pl.BlockSpec((STEP, width), lambda i, w: (i, 0)),
+                pl.BlockSpec(memory_space=pl.ANY),
+                pl.BlockSpec(memory_space=pl.ANY),
+            ],
+            scratch_shapes=[
+                pltpu.VMEM((words, width), bf16),
+                pltpu.VMEM((words, width), bf16),
+                pltpu.VMEM((words, hidden), bf16),
+                pltpu.VMEM((rows, hidden), bf16),
+                pltpu.VMEM((rows, 3 * width), bf16),
+                pltpu.VMEM((rows, width), bf16),
+                pltpu.VMEM((width, rows), bf16),
+                pltpu.VMEM((width, rows), bf16),
+                pltpu.VMEM((16, width), f32),
+                pltpu.VMEM((shards, CHAR_SLOT, width), bf16),
+                pltpu.SemaphoreType.DMA((2,)),
+            ],
+        ),
+        out_shape=[
+            jax.ShapeDtypeStruct((rows, width), f32),
+            jax.ShapeDtypeStruct(half, bf16),
+            jax.ShapeDtypeStruct(half, bf16),
+        ],
+        compiler_params=pltpu.CompilerParams(vmem_limit_bytes=VMEM_LIMIT),
+        name="char_backward",
+    )(
+        where,
+        chars,
+        counts,
+        table,
+        gain_attn,
+        project,
+        output,
+        gain_mlp,
+        expand_w,
+        shrink,
+        dpooled,
+        hidden_sum,
+        qkv,
+        probs,
+        mixed,
+        middle,
+        slope,
+    )
+
+
+WORD_SLOT = 416
+
+
+def word_kernel(
+    length,
+    shards,
+    where_ref,
+    own_ref,
+    core_ref,
+    high_ref,
+    section_ref,
+    both_ref,
+    cot_ref,
+    cot_core_ref,
+    cot_high_ref,
+    input_ref,
+    gain_attn_ref,
+    project_ref,
+    output_ref,
+    gain_mlp_ref,
+    expand_ref,
+    shrink_ref,
+    result_ref,
+    dpooled_ref,
+    keep_ref,
+    send0_ref,
+    send1_ref,
+    send2_ref,
+    pooled,
+    dz,
+    start,
+    normed,
+    normed_t,
+    qkv,
+    kept,
+    mixed_t,
+    middle,
+    normed_mlp_t,
+    hidden,
+    slope,
+    dbefore,
+    dmixed,
+    dqkv,
+    dy,
+    packed,
+    sems,
+):
+    total = pooled.shape[0]
+    width = output_ref.shape[0]
+    section = where_ref[0]
+    me = where_ref[2]
+    slabs = width // SLAB
+    pooled[0:length] = own_ref[...]
+    pooled[length : 2 * length] = core_ref[...]
+    for place, ref in enumerate((high_ref, section_ref, both_ref)):
+        pooled[(2 + 2 * place) * length : (4 + 2 * place) * length] = ref[...]
+    at = 0
+    for other in (section, 1 - section):
+        dz[at : at + length] = cot_ref[other]
+        dz[at + length : at + 2 * length] = cot_core_ref[other]
+        dz[at + 2 * length : at + 3 * length] = cot_high_ref[0, other]
+        dz[at + 3 * length : at + 4 * length] = cot_high_ref[1, other]
+        at += 4 * length
+
+    x = dot(pooled[...], input_ref[...])
+    start[...] = x
+    normal, _ = unit(x)
+    low = (normal * gain_attn_ref[...]).astype(bf16)
+    normed[...] = low
+    normed_t[...] = flip(low)
+    qkv[...] = dot(low, project_ref[...]).astype(bf16)
+    causal = rows_of((length, BLOCK)) <= lanes((length, BLOCK)) % length
+    for block in range(total // BLOCK):
+        part = slice(block * BLOCK, (block + 1) * BLOCK)
+        for slab in range(slabs):
+            at = slab * SLAB
+            probs, piece = attend(
+                qkv[part, at : at + SLAB],
+                qkv[part, width + at : width + at + SLAB],
+                qkv[part, 2 * width + at : 2 * width + at + SLAB],
+                causal,
+                length,
+            )
+            for head in range(SLAB // HEAD):
+                kept[block * slabs + slab, head] = probs[head]
+            mixed_t[at : at + SLAB, part] = piece
+            dmixed[part, at : at + SLAB] = flip(piece)
+    x = x + dot(dmixed[...], output_ref[...])
+    middle[...] = x
+    normal, _ = unit(x)
+    low = (normal * gain_mlp_ref[...]).astype(bf16)
+    normed_mlp_t[...] = flip(low)
+    dz_all = dz[...]
+    for at in range(0, expand_ref.shape[1], 256):
+        part = slice(at, at + 256)
+        value, bend = gelu_parts(dot(low, expand_ref[:, part]))
+        hidden[:, part] = value.astype(bf16)
+        dhidden = dot_nt(dz_all, shrink_ref[part, :]).astype(bf16)
+        dbefore[:, part] = dhidden * bend.astype(bf16)
+    result_ref[...] = middle[:length] + dot(hidden[:length], shrink_ref[...])
+
+    dnormed = dot_nt(dbefore[...], expand_ref[...])
+    normal, scale = unit(middle[...])
+    gain_mlp_grad = jnp.sum(dnormed * normal, axis=0, keepdims=True)
+    dmiddle = dz_all.astype(f32) + unit_back(dnormed, gain_mlp_ref[...], normal, scale)
+    dy_low = dmiddle.astype(bf16)
+    dy[...] = dy_low
+    dmixed[...] = dot_nt(dy_low, output_ref[...]).astype(bf16)
+    for block in range(total // BLOCK):
+        part = slice(block * BLOCK, (block + 1) * BLOCK)
+        for slab in range(slabs):
+            at = slab * SLAB
+            pieces = attend_back(
+                qkv[part, at : at + SLAB],
+                qkv[part, width + at : width + at + SLAB],
+                qkv[part, 2 * width + at : 2 * width + at + SLAB],
+                [kept[block * slabs + slab, head] for head in range(SLAB // HEAD)],
+                dmixed[part, at : at + SLAB],
+                length,
+            )
+            for place in range(3):
+                dqkv[part, place * width + at : place * width + at + SLAB] = pieces[place]
+    dnormed = dot_nt(dqkv[...], project_ref[...])
+    normal, scale = unit(start[...])
+    gain_attn_grad = jnp.sum(dnormed * normal, axis=0, keepdims=True)
+    dword = (dmiddle + unit_back(dnormed, gain_attn_ref[...], normal, scale)).astype(bf16)
+    dpooled_ref[...] = dot_nt(dword[:length], input_ref[...]).astype(bf16)
+    normed[...] = dword
+
+    low_shards = [0, 1, 2, 3]
+
+    def shard_of(place):
+        return (me & 9) | (place << 1)
+
+    def slot_of(place):
+        return place ^ ((me >> 1) & 3)
+
+    def own_rows(flipped, size):
+        return jnp.concatenate(
+            [
+                flipped[pl.ds(pl.multiple_of(shard_of(place) * size, size), size), :]
+                for place in low_shards
+            ],
+            axis=0,
+        )
+
+    def own_columns(ref, size):
+        return ref[:, pl.ds(pl.multiple_of(section * size, size), size)]
+
+    def put(gradient, at):
+        size = gradient.shape[0] // len(low_shards)
+        for place in low_shards:
+            piece = gradient[place * size : (place + 1) * size].astype(bf16)
+            for column in range(gradient.shape[1] // SLAB):
+                first = at + column * size
+                packed[slot_of(place), first : first + size] = piece[
+                    :, column * SLAB : (column + 1) * SLAB
+                ]
+        return at + size * (gradient.shape[1] // SLAB)
+
+    dmixed[:, :SLAB] = pooled[...]
+    pooled_t = flip(dmixed[:, :SLAB])
+    mixed_holder = normed_t
+    size = normed_t.shape[0] // shards
+    lhs = own_rows(normed_t, size)
+    mixed_holder[0 : pooled_t.shape[0]] = pooled_t
+    at = put(
+        dot(
+            own_rows(mixed_holder, pooled_t.shape[0] // shards),
+            own_columns(normed, width // 2),
+        ),
+        0,
+    )
+    at = put(dot(lhs, own_columns(dqkv, 3 * width // 2)), at)
+    at = put(dot(own_rows(mixed_t, size), own_columns(dy, width // 2)), at)
+    at = put(dot(own_rows(normed_mlp_t, size), own_columns(dbefore, expand_ref.shape[1] // 2)), at)
+    size = hidden.shape[1] // shards
+    lhs = jnp.concatenate(
+        [
+            flip(hidden[:, pl.ds(pl.multiple_of(shard_of(place) * size, size), size)])
+            for place in low_shards
+        ],
+        axis=0,
+    )
+    at = put(dot(lhs, own_columns(dz, width // 2)), at)
+    extra = jnp.concatenate(
+        [gain_attn_grad[:, :SLAB], gain_attn_grad[:, SLAB:]]
+        + [gain_mlp_grad[:, :SLAB], gain_mlp_grad[:, SLAB:]]
+        + [jnp.zeros((12, SLAB), f32)],
+        axis=0,
+    ).astype(bf16)
+    for place in low_shards:
+        packed[place, at : at + 16] = extra
+    copies = [
+        pltpu.make_async_copy(packed.at[place], ref, sems.at[place])
+        for place, ref in enumerate((keep_ref, send0_ref, send1_ref, send2_ref))
+    ]
+    for copy in copies:
+        copy.start()
+    for copy in copies:
+        copy.wait()
+
+
+def word_group(where, pooled, cotangents, word_input, weights, shards):
+    gain_attn, project, output, gain_mlp, expand_w, shrink = weights
+    length, channels = pooled[0].shape
+    width = output.shape[0]
+    hidden = expand_w.shape[1]
+    total = 8 * length
+    slot = (WORD_SLOT, SLAB)
+    vmem = pl.BlockSpec(memory_space=pltpu.VMEM)
+    hbm = pl.BlockSpec(memory_space=pl.ANY)
+    return pl.pallas_call(
+        functools.partial(word_kernel, length, shards),
+        in_specs=[pl.BlockSpec(memory_space=pltpu.SMEM)] + [vmem] * 15,
+        out_specs=[vmem, vmem, hbm, hbm, hbm, hbm],
+        out_shape=[
+            jax.ShapeDtypeStruct((length, width), f32),
+            jax.ShapeDtypeStruct((length, channels), bf16),
+        ]
+        + [jax.ShapeDtypeStruct(slot, bf16)] * 4,
+        scratch_shapes=[
+            pltpu.VMEM((total, channels), bf16),
+            pltpu.VMEM((total, width), bf16),
+            pltpu.VMEM((total, width), f32),
+            pltpu.VMEM((total, width), bf16),
+            pltpu.VMEM((width, total), bf16),
+            pltpu.VMEM((total, 3 * width), bf16),
+            pltpu.VMEM((total // BLOCK * (width // SLAB), SLAB // HEAD, length, BLOCK), f32),
+            pltpu.VMEM((width, total), bf16),
+            pltpu.VMEM((total, width), f32),
+            pltpu.VMEM((width, total), bf16),
+            pltpu.VMEM((total, hidden), bf16),
+            pltpu.VMEM((8, 128), bf16),
+            pltpu.VMEM((total, hidden), bf16),
+            pltpu.VMEM((total, width), bf16),
+            pltpu.VMEM((total, 3 * width), bf16),
+            pltpu.VMEM((total, width), bf16),
+            pltpu.VMEM((4,) + slot, bf16),
+            pltpu.SemaphoreType.DMA((4,)),
+        ],
+        compiler_params=pltpu.CompilerParams(vmem_limit_bytes=VMEM_LIMIT),
+        name="word_group",
+    )(where, *pooled, *cotangents, word_input, gain_attn, project, output, gain_mlp, expand_w, shrink)
+
+
+def core_sum_kernel(keep_ref, arrived_ref, *out_refs):
+    for place, ref in enumerate(out_refs):
+        part = slice(2 * place, 2 * place + 2)
+        ref[...] = (keep_ref[part].astype(f32) + arrived_ref[part].astype(f32)).astype(bf16)
+
+
+def core_sum(keep, arrived):
+    piece = jax.ShapeDtypeStruct((2,) + keep.shape[1:], bf16)
+    return pl.pallas_call(
+        core_sum_kernel,
+        out_shape=[piece] * (keep.shape[0] // 2),
+        compiler_params=pltpu.CompilerParams(vmem_limit_bytes=VMEM_LIMIT),
+        name="core_sum",
+    )(keep, arrived)
+
+
+def plane_sum_kernel(*refs):
+    word, char, near_ref, far_ref = (refs[:4], refs[4:8], refs[8], refs[9])
+    rows = word[0].shape[0]
+
+    def total(parts, pick):
+        return functools.reduce(lambda a, b: a + b, [pick(part).astype(f32) for part in parts])
+
+    near_ref[:rows] = total(word, lambda r: r[...]).astype(bf16)
+    near_ref[rows:] = total(char, lambda r: r[0]).astype(bf16)
+    far_ref[...] = total(char, lambda r: r[1]).astype(bf16)
+
+
+def plane_sum(word, char):
+    rows = word[0].shape[0] + char[0].shape[1]
+    return pl.pallas_call(
+        plane_sum_kernel,
+        out_shape=[
+            jax.ShapeDtypeStruct((rows, SLAB), bf16),
+            jax.ShapeDtypeStruct(char[0].shape[1:], bf16),
+        ],
+        compiler_params=pltpu.CompilerParams(vmem_limit_bytes=VMEM_LIMIT),
+        name="plane_sum",
+    )(*word, *char)
+
+
+def last_sum_kernel(shapes, where_ref, near_ref, section_ref, high_ref, both_ref, *outs):
+    word_rows = WORD_SLOT
+    section = where_ref[0]
+    me = where_ref[2]
+    own = near_ref[:word_rows].astype(f32)
+    other = section_ref[:word_rows].astype(f32)
+    halves = (jnp.where(section == 0, own, other), jnp.where(section == 0, other, own))
+    char = (
+        near_ref[word_rows:].astype(f32)
+        + section_ref[word_rows:].astype(f32)
+        + high_ref[...].astype(f32)
+        + both_ref[...].astype(f32)
+    )
+
+    def mine(vector, size):
+        turned = pltpu.roll(vector, lax.rem(SLAB - lax.rem(me * size, SLAB), SLAB), 1)
+        return turned[:, :size]
+
+    (
+        table_ref,
+        gain_attn_ref,
+        project_ref,
+        output_ref,
+        gain_mlp_ref,
+        expand_ref,
+        shrink_ref,
+        w_input_ref,
+        w_gain_attn_ref,
+        w_project_ref,
+        w_output_ref,
+        w_gain_mlp_ref,
+        w_expand_ref,
+        w_shrink_ref,
+    ) = outs
+    at = 0
+    for ref in (project_ref, output_ref, expand_ref, shrink_ref):
+        size = ref.shape[0]
+        for column in range(ref.shape[1] // SLAB):
+            ref[:, column * SLAB : (column + 1) * SLAB] = char[at : at + size]
+            at += size
+    size = gain_attn_ref.shape[1]
+    extra = char[at : at + 16]
+    turned = mine(extra, size)
+    gain_attn_ref[...] = turned[0:1]
+    gain_mlp_ref[...] = turned[1:2]
+    table_ref[...] = turned[8:16]
+    at = 0
+    for ref in (w_input_ref, w_project_ref, w_output_ref, w_expand_ref, w_shrink_ref):
+        size = ref.shape[0]
+        columns = ref.shape[1] // (2 * SLAB)
+        for column in range(columns):
+            for half in range(2):
+                first = (half * columns + column) * SLAB
+                ref[:, first : first + SLAB] = halves[half][at : at + size]
+            at += size
+    size = w_gain_attn_ref.shape[1]
+    extra = own[at : at + 8]
+    turned = mine(extra, size)
+    upper = me * size >= SLAB
+    w_gain_attn_ref[...] = jnp.where(upper, turned[1:2], turned[0:1])
+    w_gain_mlp_ref[...] = jnp.where(upper, turned[3:4], turned[2:3])
+
+
+def last_sum(where, near, arrived, shapes):
+    vmem = pl.BlockSpec(memory_space=pltpu.VMEM)
+    return pl.pallas_call(
+        functools.partial(last_sum_kernel, shapes),
+        in_specs=[pl.BlockSpec(memory_space=pltpu.SMEM)] + [vmem] * 4,
+        out_specs=[vmem] * len(shapes),
+        out_shape=[jax.ShapeDtypeStruct(shape, f32) for shape in shapes],
+        compiler_params=pltpu.CompilerParams(vmem_limit_bytes=VMEM_LIMIT),
+        name="last_sum",
+    )(where, near, *arrived)
+
+
+def exchange(value, section_bit, dp_bits):
+    shards = lax.axis_size("dp")
+    pairs = [
+        (s * shards + d, (s ^ section_bit) * shards + (d ^ dp_bits))
+        for s in range(lax.axis_size("section"))
+        for d in range(shards)
+    ]
+    return lax.ppermute(value, ("section", "dp"), pairs)
+
+
+CORE, SIDE, NEAR, FAR = (1, 2, 4, 8)
+
+
+def local_grouped(
+    chars, counts, languages, language_table, char_weights, word_input, word_weights, cotangent
+):
+    section = lax.axis_index("section")
+    me = lax.axis_index("dp")
+    shards = lax.axis_size("dp")
+    micros, _, words, slots, width = chars.shape
+    rows = words * slots
+    where = jnp.stack([section, languages[section, 0], me]).astype(jnp.int32)
+    cot = cotangent[:, 0]
+    cot_core = exchange(cot, 0, CORE)
+    cot_high = exchange(jnp.stack([cot, cot_core]), 0, FAR)
+    char_weights = tuple(w[None] if w.ndim == 1 else w for w in char_weights)
+    word_weights = tuple(w[None] if w.ndim == 1 else w for w in word_weights)
+    chars = chars.reshape(micros, rows, width)
+    counts = counts.reshape(micros, 1, words)
+    pooled, *stored = char_forward(where, chars, counts, language_table, char_weights, slots)
+    pooled_core = exchange(pooled, 0, CORE)
+    pair = jnp.concatenate([pooled, pooled_core])
+    others = (exchange(pair, 0, FAR), exchange(pair, 1, 0), exchange(pair, 1, FAR))
+    result, dpooled, *pieces = word_group(
+        where,
+        (pooled, pooled_core) + others,
+        (cot, cot_core, cot_high),
+        word_input,
+        word_weights,
+        shards,
+    )
+    word = (pieces[0],) + tuple(
+        exchange(piece, 0, bits) for piece, bits in zip(pieces[1:], (SIDE, NEAR, SIDE | NEAR))
+    )
+    chars_grad, keep, send = char_backward(
+        where, chars, counts, language_table, char_weights, dpooled, stored, slots, shards
+    )
+    pieces = core_sum(keep, exchange(send, 0, CORE))
+    char = (pieces[0],) + tuple(
+        exchange(piece, 0, bits) for piece, bits in zip(pieces[1:], (SIDE, NEAR, SIDE | NEAR))
+    )
+    near, far = plane_sum(word, char)
+    arrived = (exchange(near, 1, 0), exchange(far, 0, FAR), exchange(far, 1, FAR))
+    shapes = [(language_table.shape[0], language_table.shape[1] // shards)]
+    for weight in char_weights + (word_input,) + word_weights:
+        if weight.shape[0] == 1:
+            shapes.append((1, weight.shape[1] // shards))
+        else:
+            shapes.append((weight.shape[0] // shards, weight.shape[1]))
+    totals = last_sum(where, near, arrived, shapes)
+    totals = [total[0] if total.shape[0] == 1 else total for total in totals]
+    return (result[None, None], chars_grad.reshape((1, 1, words, slots, width))) + tuple(totals)
 
 
 def norm_forward(inputs, gain):
@@ -244,6 +1158,17 @@
         word_expand,
         word_shrink,
     )
+    if lax.axis_size("dp") == 16:
+        return local_grouped(
+            chars,
+            counts,
+            languages,
+            language_table,
+            char_weights,
+            word_input,
+            word_weights,
+            cotangent,
+        )
     section_index = lax.axis_index("section")
     char_text = chars[section_index, 0]
     char_count = counts[section_index, 0]

time: 427 us -> 120 us (0.28); the launches traced: 419 us -> 120 us
  local copies, waits for them, and re-layouts: 168 us -> 5.17 us
  waiting for transfers between devices: 138 us -> 34.2 us
  Pallas kernels: 0 us -> 57.7 us
  matrix products: 55.7 us -> 0 us
  other arithmetic: 46.2 us -> 1.29 us
  starting transfers between devices: 8.99 us -> 20.6 us
    ppermute x5 -> x16, waiting for transfers between devices: 138 us -> 34.2 us  [exchange(): return lax.ppermute(value, ('section', 'dp'), pairs)]
    pallas_call x0 -> x6, Pallas kernels: none -> 57.7 us  [the longest x1 20.9 us: word_group(): pl.pallas_call(functools.partial(word_kernel, length, shards), in_specs=[...]
    dot_general x40 -> x0, matrix products: 55.7 us -> none  [the longest x2 4.78 us: block_forward(): jnp.einsum('blc,cf->blf', normed_mlp, expand, preferred_element_type=jnp....]
    reshape x24 -> x0, local copies, waits for them, and re-layouts: 41.2 us -> none  [the longest x9 17.3 us: reduce_rows(): flat.append(gradient.astype(jnp.bfloat16).reshape(shards, -1))]
    unnamed x183 -> x43, local copies, waits for them, and re-layouts: 40.2 us -> 4.58 us
    gather x6 -> x0, local copies, waits for them, and re-layouts: 28.4 us -> none  [reduce_rows(): packed = jnp.take(packed, jnp.arange(shards) ^ me, axis=0)]
    concatenate x2 -> x1, local copies, waits for them, and re-layouts: 22.4 us -> 0.01 us  [local_grouped(): pair = jnp.concatenate([pooled, pooled_core])]
    slice x13 -> x0, local copies, waits for them, and re-layouts: 21.6 us -> none  [the longest x2 11.6 us: reduce_rows(): pairs[:, 0].astype(jnp.float32) + arrived.astype(jnp.float32)]
  transfers between devices with their start and end apart: 5 -> 16, of which waited for: 5 -> 7; matrix products, arithmetic and copies ran while one was open for 0% -> 2% of each run, Pallas kernels for 0% -> 13%
where the time goes in v2:
time: 120 us
  Pallas kernels  57.7 us (48%)
  waiting for transfers between devices  34.2 us (29%)
  starting transfers between devices  20.6 us (17%)
  local copies, waits for them, and re-layouts  5.17 us (4%)
  other arithmetic  1.29 us (1%)
    ppermute x16, waiting for transfers between devices, exchange(): return lax.ppermute(value, ('section', 'dp'), pairs)  34.2 us
    pallas_call x1, Pallas kernels, word_group(): pl.pallas_call(functools.partial(word_kernel, length, shards), in_specs=[...  20.9 us
    ppermute x16, starting transfers between devices, exchange(): return lax.ppermute(value, ('section', 'dp'), pairs)  20.6 us
    pallas_call x1, Pallas kernels, char_backward(): pl.pallas_call(functools.partial(char_backward_kernel, slots, shards), gr...  16.3 us
    pallas_call x1, Pallas kernels, char_forward(): pl.pallas_call(functools.partial(char_forward_kernel, slots), grid_spec=p...  13.5 us
    unnamed x43, local copies, waits for them, and re-layouts  4.58 us
    pallas_call x1, Pallas kernels, plane_sum(): pl.pallas_call(plane_sum_kernel, out_shape=[jax.ShapeDtypeStruct((rows, S...  2.41 us
    pallas_call x1, Pallas kernels, core_sum(): pl.pallas_call(core_sum_kernel, out_shape=[piece] * (keep.shape[0] // 2),...  2.4 us
  transfers between devices with their start and end apart: 16, of which 7 were waited for; matrix products, arithmetic and copies ran while one was open for 2% of the time, Pallas kernels for 13%

profile of v2, /device:TPU:0, one launch (start us, length us, event | category | flops | bytes accessed | tf_op | source)
XLA Modules:
  0.0 119.8 jit_solution(17469453359430475109)
XLA Ops:
  0.6 0.0 copy-start
  0.7 0.0 copy-start.2
  0.7 0.5 collective-permute-start.4
  1.2 0.1 copy-done
  1.3 0.6 constant_dynamic-slice_fusion
  1.9 1.3 %pad_add_fusion.where_ref = s32[3]{0:T(128)} fusion(s32[1]{0:T(128)} %bitcast.2, s32[1]{0:T(128)} %bitcast.1, s32[1]{0:T(128)} %bitcast), kind=kLoop, calls=%fused_computation.3 | loop fusion | flops 6 | bytes 24 | tf_op jit(solution)/shard_map/stack | solution.py:884
  3.2 13.5 %char_forward.1 = (bf16[64,256]{1,0:T(8,128)(2,1)}, bf16[64,1024]{1,0:T(8,128)(2,1)}, bf16[1024,768]{1,0:T(8,128)(2,1)}, f32[64,1024]{1,0:T(8,128)}, bf16[256,10...) custom-call(s32[3]{0:T(128)} %pad_add_fusion.where_ref, bf16[2,1024,256]{2,1,0:T(8,128)(2,1)} %bitcast.17, ...), custom_call_target="tpu_custom_call" | custom-call | tf_op jit(solution)/shard_map/char_forward/pallas_call | solution.py:236
  16.7 0.5 collective-permute-start
  17.1 0.0 collective-permute-done.4.cot_core_ref
  17.2 0.0 copy-done.2
  17.2 3.7 %collective-permute-start.5 = (bf16[2,2,64,512]{3,2,1,0:T(8,128)(2,1)S(1)}, bf16[2,2,64,512]{3,2,1,0:T(8,128)(2,1)S(1)}, u32[]{:S(2)}, u32[]{:S(2)}) collective-permute-start(bf16[2,2,64,512]{3,2,1,0:T(8,128)(2,1)S(1)} %pad_maximum_fusion), channel_id=1, source_target_pairs={{0,8},{1,9},{2,10},{3,11},{4,12},{5,13},{6,14},{7,15},{8,0},{9,1},... | collective-permute-start | bytes 786440 | tf_op jit(solution)/shard_map/ppermute | solution.py:870
  20.9 0.8 constant_dynamic-update-slice_fusion.1
  21.6 0.0 collective-permute-done.core_ref
  21.7 1.4 %collective-permute-start.3 = (bf16[128,256]{1,0:T(8,128)(2,1)S(1)}, bf16[128,256]{1,0:T(8,128)(2,1)S(1)}, u32[]{:S(2)}, u32[]{:S(2)}) collective-permute-start(bf16[128,256]{1,0:T(8,128)(2,1)S(1)} %constant_dynamic-update-slice_fusion), channel_id=1, source_target_pairs={{0,24},{1,25},{2,26},{3,27},{4,28},{5,29},{6,30},{7,31},{8,16},{9,... | collective-permute-start | bytes 196616 | tf_op jit(solution)/shard_map/ppermute | solution.py:870
  23.1 0.5 collective-permute-start.2
  23.6 2.5 %collective-permute-start.1 = (bf16[128,256]{1,0:T(8,128)(2,1)S(1)}, bf16[128,256]{1,0:T(8,128)(2,1)S(1)}, u32[]{:S(2)}, u32[]{:S(2)}) collective-permute-start(bf16[128,256]{1,0:T(8,128)(2,1)S(1)} %constant_dynamic-update-slice_fusion), channel_id=1, source_target_pairs={{0,8},{1,9},{2,10},{3,11},{4,12},{5,13},{6,14},{7,15},{8,0},{9,1},... | collective-permute-start | bytes 196616 | tf_op jit(solution)/shard_map/ppermute | solution.py:870
  26.1 12.9 %collective-permute-done.3.both_ref = bf16[128,256]{1,0:T(8,128)(2,1)S(1)} collective-permute-done((bf16[128,256]{1,0:T(8,128)(2,1)S(1)}, bf16[128,256]{1,0:T(8,128)(2,1)S(1)}, u32[]{:S(2)}, u32[]{:S(2)}) %collective-permute-start.3) | collective-permute-done | bytes 65568 | tf_op jit(solution)/shard_map/ppermute | solution.py:870
  39.1 0.0 collective-permute-done.2.section_ref
  39.1 0.0 collective-permute-done.1.high_ref
  39.1 0.0 copy-start.17
  39.1 0.0 collective-permute-done.5.cot_high_ref
  39.1 0.0 copy-start.5
  39.1 0.0 copy-done.3
  39.1 0.0 copy-done.12
  39.1 0.6 copy-done.15
  39.7 0.0 copy-done.16
  39.7 0.0 copy-done.17
  39.7 0.1 copy-done.5
  39.8 20.9 %word_group.1 = (f32[64,512]{1,0:T(8,128)}, bf16[64,256]{1,0:T(8,128)(2,1)}, bf16[416,256]{1,0:T(8,128)(2,1)}, bf16[416,256]{1,0:T(8,128)(2,1)}, bf16[416,256]{1,0:T(8,128)(2,1)}, /*index=5*/bf16[416,256]{1,0:T(8,128)(2,1)}) custom-call(s32[3]{0:T(128)} %pad_add_fusion.where_ref, bf16[64,256]{1,0:T(8,128)(2,1)} %get-tuple-element.52.own_ref, ...), custom_call_target="tpu_custom_call" | custom-call | tf_op jit(solution)/shard_map/word_group/pallas_call | solution.py:713
  60.7 0.0 copy-start.20
  60.7 0.0 copy-start.19
  60.7 0.0 copy-start.18
  60.7 16.3 %char_backward.1 = (f32[1024,256]{1,0:T(8,128)}, bf16[8,208,256]{2,1,0:T(8,128)(2,1)}, bf16[8,208,256]{2,1,0:T(8,128)(2,1)}) custom-call(s32[3]{0:T(128)} %pad_add_fusion.where_ref, bf16[2,1024,256]{2,1,0:T(8,128)(2,1)} %bitcast.18, s32[2,1,64]{2,1,0:T(1,128)} %counts_ref.3, bf16[8,256]{1,0:T(8,128)(2,1)} %table_ref.3, f32[1,256]{1,0:T(1,128)} %bitcast.24, ...), custom_call_target="tpu_custom_call" | custom-call | tf_op jit(solution)/shard_map/char_backward/pallas_call | solution.py:431
  77.1 0.1 collective-permute-start.9
  77.2 0.0 copy-done.20
  77.2 1.6 %collective-permute-start.6 = (bf16[416,256]{1,0:T(8,128)(2,1)S(1)}, bf16[416,256]{1,0:T(8,128)(2,1)S(1)}, u32[]{:S(2)}, u32[]{:S(2)}) collective-permute-start(bf16[416,256]{1,0:T(8,128)(2,1)S(1)} %copy-done.20), channel_id=1, source_target_pairs={{0,2},{1,3},{2,0},{3,1},{4,6},{5,7},{6,4},{7,5},{8,10},{9,11},{10,... | collective-permute-start | bytes 638984 | tf_op jit(solution)/shard_map/ppermute | solution.py:870
  78.8 0.0 copy-done.19
  78.8 0.7 collective-permute-start.7
  79.5 1.3 %collective-permute-start.8 = (bf16[416,256]{1,0:T(8,128)(2,1)S(1)}, bf16[416,256]{1,0:T(8,128)(2,1)S(1)}, u32[]{:S(2)}, u32[]{:S(2)}) collective-permute-start(bf16[416,256]{1,0:T(8,128)(2,1)S(1)} %copy-done.18), channel_id=1, source_target_pairs={{0,6},{1,7},{2,4},{3,5},{4,2},{5,3},{6,0},{7,1},{8,14},{9,15},{10,... | collective-permute-start | bytes 638984 | tf_op jit(solution)/shard_map/ppermute | solution.py:870
  80.7 0.0 collective-permute-done.9.arrived_ref
  80.7 0.9 copy-done.1
  81.6 2.4 %core_sum.1 = (bf16[2,208,256]{2,1,0:T(8,128)(2,1)}, bf16[2,208,256]{2,1,0:T(8,128)(2,1)}, bf16[2,208,256]{2,1,0:T(8,128)(2,1)}, bf16[2,208,256]{2,1,0:T(8,128)(2,1)}) custom-call(bf16[8,208,256]{2,1,0:T(8,128)(2,1)} %get-tuple-element.66.keep_ref, bf16[8,208,256]{2,1,0:T(8,128)(2,1)} %copy-done.1), custom_call_target="tpu_custom_call" | custom-call | tf_op jit(solution)/shard_map/core_sum/pallas_call | solution.py:755
  84.0 1.5 %collective-permute-start.10 = (bf16[2,208,256]{2,1,0:T(8,128)(2,1)}, bf16[2,208,256]{2,1,0:T(8,128)(2,1)S(1)}, u32[]{:S(2)}, u32[]{:S(2)}) collective-permute-start(bf16[2,208,256]{2,1,0:T(8,128)(2,1)} %get-tuple-element.69), channel_id=1, source_target_pairs={{0,2},{1,3},{2,0},{3,1},{4,6},{5,7},{6,4},{7,5},{8,10},{9,11},{10,... | collective-permute-start | bytes 638984 | tf_op jit(solution)/shard_map/ppermute | solution.py:870
  85.6 0.7 collective-permute-start.11
  86.3 0.0 collective-permute-done.6.refs_1_
  86.3 1.3 %collective-permute-start.12 = (bf16[2,208,256]{2,1,0:T(8,128)(2,1)}, bf16[2,208,256]{2,1,0:T(8,128)(2,1)S(1)}, u32[]{:S(2)}, u32[]{:S(2)}) collective-permute-start(bf16[2,208,256]{2,1,0:T(8,128)(2,1)} %get-tuple-element.71), channel_id=1, source_target_pairs={{0,6},{1,7},{2,4},{3,5},{4,2},{5,3},{6,0},{7,1},{8,14},{9,15},{10,... | collective-permute-start | bytes 638984 | tf_op jit(solution)/shard_map/ppermute | solution.py:870
  87.5 0.0 collective-permute-done.7.refs_2_
  87.5 3.9 %collective-permute-done.8.refs_3_ = bf16[416,256]{1,0:T(8,128)(2,1)S(1)} collective-permute-done((bf16[416,256]{1,0:T(8,128)(2,1)S(1)}, bf16[416,256]{1,0:T(8,128)(2,1)S(1)}, u32[]{:S(2)}, u32[]{:S(2)}) %collective-permute-start.8) | collective-permute-done | bytes 213024 | tf_op jit(solution)/shard_map/ppermute | solution.py:870
  91.4 4.1 %collective-permute-done.10.refs_5_ = bf16[2,208,256]{2,1,0:T(8,128)(2,1)S(1)} collective-permute-done((bf16[2,208,256]{2,1,0:T(8,128)(2,1)}, bf16[2,208,256]{2,1,0:T(8,128)(2,1)S(1)}, u32[]{:S(2)}, u32[]{:S(2)}) %collective-permute-start.10) | collective-permute-done | bytes 213024 | tf_op jit(solution)/shard_map/ppermute | solution.py:870
  95.5 0.5 collective-permute-done.11.refs_6_
  96.0 3.7 %collective-permute-done.12.refs_7_ = bf16[2,208,256]{2,1,0:T(8,128)(2,1)S(1)} collective-permute-done((bf16[2,208,256]{2,1,0:T(8,128)(2,1)}, bf16[2,208,256]{2,1,0:T(8,128)(2,1)S(1)}, u32[]{:S(2)}, u32[]{:S(2)}) %collective-permute-start.12) | collective-permute-done | bytes 213024 | tf_op jit(solution)/shard_map/ppermute | solution.py:870
  99.8 0.0 copy-done.7
  99.8 0.7 copy-done.11
  100.4 2.4 %plane_sum.1 = (bf16[624,256]{1,0:T(8,128)(2,1)}, bf16[208,256]{1,0:T(8,128)(2,1)}) custom-call(bf16[416,256]{1,0:T(8,128)(2,1)} %get-tuple-element.62.refs_0_, bf16[416,256]{1,0:T(8,128)(2,1)} %copy-done.6, bf16[416,256]{1,0:T(8,128)(2,1)} %copy-done.7, bf16[416,256]{1,0:T(8,128)(2,1)} %copy-done.8, bf16[2,208,256]{2,1,0:T(8,128)(2,1)} %get-tuple-element.68.refs_4_, ...), custom_call_target="tpu_custom_call" | custom-call | tf_op jit(solution)/shard_map/plane_sum/pallas_call | solution.py:777
  102.8 1.6 %collective-permute-start.13 = (bf16[624,256]{1,0:T(8,128)(2,1)}, bf16[624,256]{1,0:T(8,128)(2,1)S(1)}, u32[]{:S(2)}, u32[]{:S(2)}) collective-permute-start(bf16[624,256]{1,0:T(8,128)(2,1)} %get-tuple-element.72.near_ref), channel_id=1, source_target_pairs={{0,16},{1,17},{2,18},{3,19},{4,20},{5,21},{6,22},{7,23},{8,24},{9,... | collective-permute-start | bytes 958472 | tf_op jit(solution)/shard_map/ppermute | solution.py:870
  104.4 2.2 %collective-permute-start.15 = (bf16[208,256]{1,0:T(8,128)(2,1)}, bf16[208,256]{1,0:T(8,128)(2,1)S(1)}, u32[]{:S(2)}, u32[]{:S(2)}) collective-permute-start(bf16[208,256]{1,0:T(8,128)(2,1)} %get-tuple-element.73), channel_id=1, source_target_pairs={{0,24},{1,25},{2,26},{3,27},{4,28},{5,29},{6,30},{7,31},{8,16},{9,... | collective-permute-start | bytes 319496 | tf_op jit(solution)/shard_map/ppermute | solution.py:870
  106.6 0.6 collective-permute-start.14
  107.2 8.5 %collective-permute-done.15.both_ref = bf16[208,256]{1,0:T(8,128)(2,1)S(1)} collective-permute-done((bf16[208,256]{1,0:T(8,128)(2,1)}, bf16[208,256]{1,0:T(8,128)(2,1)S(1)}, u32[]{:S(2)}, u32[]{:S(2)}) %collective-permute-start.15) | collective-permute-done | bytes 106528 | tf_op jit(solution)/shard_map/ppermute | solution.py:870
  115.8 0.5 collective-permute-done.14.high_ref
  116.3 0.0 collective-permute-done.13.section_ref
  116.3 0.1 copy-done.13
  116.4 0.5 copy-done.14
  116.9 0.7 copy-done.4
  117.7 2.1 %last_sum.1 = (f32[8,16]{1,0:T(8,128)}, f32[1,16]{1,0:T(1,128)}, f32[16,768]{1,0:T(8,128)}, f32[16,256]{1,0:T(8,128)}, f32[1,16]{1,0:T(1,128)}, /*index=5*/f32[1...) custom-call(s32[3]{0:T(128)} %pad_add_fusion.where_ref, ...), custom_call_target="tpu_custom_call" | custom-call | tf_op jit(solution)/shard_map/last_sum/pallas_call | solution.py:853
  (21 shorter events, 0.1 us)
Async XLA Ops:
  0.6 0.7 copy-start
  0.7 16.5 %copy-start.2 = (bf16[2,1,64,512]{3,2,1,0:T(8,128)(2,1)S(1)}, bf16[2,1,64,512]{3,2,1,0:T(8,128)(2,1)}, u32[]{:S(2)}) copy-start(bf16[2,1,64,512]{3,2,1,0:T(8,128)(2,1)} %param.35) | copy-start | bytes 393220
  0.7 16.5 %collective-permute-start.4 = (bf16[2,64,512]{2,1,0:T(8,128)(2,1)}, bf16[2,64,512]{2,1,0:T(8,128)(2,1)S(1)}, u32[]{:S(2)}, u32[]{:S(2)}) collective-permute-start(bf16[2,64,512]{2,1,0:T(8,128)(2,1)} %bitcast.19), channel_id=1, source_target_pairs={{0,1},{1,0},{2,3},{3,2},{4,5},{5,4},{6,7},{7,6},{8,9},{9,8},{10,11... | collective-permute-start | bytes 393224 | tf_op jit(solution)/shard_map/ppermute | solution.py:870
  16.7 5.0 %collective-permute-start = (bf16[64,256]{1,0:T(8,128)(2,1)}, bf16[64,256]{1,0:T(8,128)(2,1)S(1)}, u32[]{:S(2)}, u32[]{:S(2)}) collective-permute-start(bf16[64,256]{1,0:T(8,128)(2,1)} %get-tuple-element.52.own_ref), channel_id=1, source_target_pairs={{0,1},{1,0},{2,3},{3,2},{4,5},{5,4},{6,7},{7,6},{8,9},{9,8},{10,11... | collective-permute-start | bytes 98312 | tf_op jit(solution)/shard_map/ppermute | solution.py:870
  17.1 22.0 %copy-start.3 = (bf16[2,64,512]{2,1,0:T(8,128)(2,1)}, bf16[2,64,512]{2,1,0:T(8,128)(2,1)S(1)}, u32[]{:S(2)}) copy-start(bf16[2,64,512]{2,1,0:T(8,128)(2,1)S(1)} %collective-permute-done.4.cot_core_ref) | copy-start | bytes 393220
  17.2 21.9 %collective-permute-start.5 = (bf16[2,2,64,512]{3,2,1,0:T(8,128)(2,1)S(1)}, bf16[2,2,64,512]{3,2,1,0:T(8,128)(2,1)S(1)}, u32[]{:S(2)}, u32[]{:S(2)}) collective-permute-start(bf16[2,2,64,512]{3,2,1,0:T(8,128)(2,1)S(1)} %pad_maximum_fusion), channel_id=1, source_target_pairs={{0,8},{1,9},{2,10},{3,11},{4,12},{5,13},{6,14},{7,15},{8,0},{9,1},... | collective-permute-start | bytes 786440 | tf_op jit(solution)/shard_map/ppermute | solution.py:870
  21.6 17.5 %copy-start.12 = (bf16[64,256]{1,0:T(8,128)(2,1)}, bf16[64,256]{1,0:T(8,128)(2,1)S(1)}, u32[]{:S(2)}) copy-start(bf16[64,256]{1,0:T(8,128)(2,1)S(1)} %collective-permute-done.core_ref) | copy-start | bytes 98308
  21.7 17.4 %collective-permute-start.3 = (bf16[128,256]{1,0:T(8,128)(2,1)S(1)}, bf16[128,256]{1,0:T(8,128)(2,1)S(1)}, u32[]{:S(2)}, u32[]{:S(2)}) collective-permute-start(bf16[128,256]{1,0:T(8,128)(2,1)S(1)} %constant_dynamic-update-slice_fusion), channel_id=1, source_target_pairs={{0,24},{1,25},{2,26},{3,27},{4,28},{5,29},{6,30},{7,31},{8,16},{9,... | collective-permute-start | bytes 196616 | tf_op jit(solution)/shard_map/ppermute | solution.py:870
  23.1 16.0 %collective-permute-start.2 = (bf16[128,256]{1,0:T(8,128)(2,1)S(1)}, bf16[128,256]{1,0:T(8,128)(2,1)S(1)}, u32[]{:S(2)}, u32[]{:S(2)}) collective-permute-start(bf16[128,256]{1,0:T(8,128)(2,1)S(1)} %constant_dynamic-update-slice_fusion), channel_id=1, source_target_pairs={{0,16},{1,17},{2,18},{3,19},{4,20},{5,21},{6,22},{7,23},{8,24},{9,... | collective-permute-start | bytes 196616 | tf_op jit(solution)/shard_map/ppermute | solution.py:870
  23.6 15.4 %collective-permute-start.1 = (bf16[128,256]{1,0:T(8,128)(2,1)S(1)}, bf16[128,256]{1,0:T(8,128)(2,1)S(1)}, u32[]{:S(2)}, u32[]{:S(2)}) collective-permute-start(bf16[128,256]{1,0:T(8,128)(2,1)S(1)} %constant_dynamic-update-slice_fusion), channel_id=1, source_target_pairs={{0,8},{1,9},{2,10},{3,11},{4,12},{5,13},{6,14},{7,15},{8,0},{9,1},... | collective-permute-start | bytes 196616 | tf_op jit(solution)/shard_map/ppermute | solution.py:870
  39.1 0.6 copy-start.15
  39.1 0.6 copy-start.16
  39.1 0.7 copy-start.17
  39.1 0.7 copy-start.5
  60.7 16.4 %copy-start.20 = (bf16[416,256]{1,0:T(8,128)(2,1)S(1)}, bf16[416,256]{1,0:T(8,128)(2,1)}, u32[]{:S(2)}) copy-start(bf16[416,256]{1,0:T(8,128)(2,1)} %get-tuple-element.63) | copy-start | bytes 638980
  60.7 18.0 %copy-start.19 = (bf16[416,256]{1,0:T(8,128)(2,1)S(1)}, bf16[416,256]{1,0:T(8,128)(2,1)}, u32[]{:S(2)}) copy-start(bf16[416,256]{1,0:T(8,128)(2,1)} %get-tuple-element.64) | copy-start | bytes 638980
  60.7 18.7 %copy-start.18 = (bf16[416,256]{1,0:T(8,128)(2,1)S(1)}, bf16[416,256]{1,0:T(8,128)(2,1)}, u32[]{:S(2)}) copy-start(bf16[416,256]{1,0:T(8,128)(2,1)} %get-tuple-element.65) | copy-start | bytes 638980
  77.1 3.7 %collective-permute-start.9 = (bf16[8,208,256]{2,1,0:T(8,128)(2,1)}, bf16[8,208,256]{2,1,0:T(8,128)(2,1)S(1)}, u32[]{:S(2)}, u32[]{:S(2)}) collective-permute-start(bf16[8,208,256]{2,1,0:T(8,128)(2,1)} %get-tuple-element.67), channel_id=1, source_target_pairs={{0,1},{1,0},{2,3},{3,2},{4,5},{5,4},{6,7},{7,6},{8,9},{9,8},{10,11... | collective-permute-start | bytes 2555912 | tf_op jit(solution)/shard_map/ppermute | solution.py:870
  77.2 9.1 %collective-permute-start.6 = (bf16[416,256]{1,0:T(8,128)(2,1)S(1)}, bf16[416,256]{1,0:T(8,128)(2,1)S(1)}, u32[]{:S(2)}, u32[]{:S(2)}) collective-permute-start(bf16[416,256]{1,0:T(8,128)(2,1)S(1)} %copy-done.20), channel_id=1, source_target_pairs={{0,2},{1,3},{2,0},{3,1},{4,6},{5,7},{6,4},{7,5},{8,10},{9,11},{10,... | collective-permute-start | bytes 638984 | tf_op jit(solution)/shard_map/ppermute | solution.py:870
  78.8 8.8 %collective-permute-start.7 = (bf16[416,256]{1,0:T(8,128)(2,1)S(1)}, bf16[416,256]{1,0:T(8,128)(2,1)S(1)}, u32[]{:S(2)}, u32[]{:S(2)}) collective-permute-start(bf16[416,256]{1,0:T(8,128)(2,1)S(1)} %copy-done.19), channel_id=1, source_target_pairs={{0,4},{1,5},{2,6},{3,7},{4,0},{5,1},{6,2},{7,3},{8,12},{9,13},{10,... | collective-permute-start | bytes 638984 | tf_op jit(solution)/shard_map/ppermute | solution.py:870
  79.5 11.9 %collective-permute-start.8 = (bf16[416,256]{1,0:T(8,128)(2,1)S(1)}, bf16[416,256]{1,0:T(8,128)(2,1)S(1)}, u32[]{:S(2)}, u32[]{:S(2)}) collective-permute-start(bf16[416,256]{1,0:T(8,128)(2,1)S(1)} %copy-done.18), channel_id=1, source_target_pairs={{0,6},{1,7},{2,4},{3,5},{4,2},{5,3},{6,0},{7,1},{8,14},{9,15},{10,... | collective-permute-start | bytes 638984 | tf_op jit(solution)/shard_map/ppermute | solution.py:870
  80.7 0.9 copy-start.1
  84.0 11.5 %collective-permute-start.10 = (bf16[2,208,256]{2,1,0:T(8,128)(2,1)}, bf16[2,208,256]{2,1,0:T(8,128)(2,1)S(1)}, u32[]{:S(2)}, u32[]{:S(2)}) collective-permute-start(bf16[2,208,256]{2,1,0:T(8,128)(2,1)} %get-tuple-element.69), channel_id=1, source_target_pairs={{0,2},{1,3},{2,0},{3,1},{4,6},{5,7},{6,4},{7,5},{8,10},{9,11},{10,... | collective-permute-start | bytes 638984 | tf_op jit(solution)/shard_map/ppermute | solution.py:870
  85.6 10.5 %collective-permute-start.11 = (bf16[2,208,256]{2,1,0:T(8,128)(2,1)}, bf16[2,208,256]{2,1,0:T(8,128)(2,1)S(1)}, u32[]{:S(2)}, u32[]{:S(2)}) collective-permute-start(bf16[2,208,256]{2,1,0:T(8,128)(2,1)} %get-tuple-element.70), channel_id=1, source_target_pairs={{0,4},{1,5},{2,6},{3,7},{4,0},{5,1},{6,2},{7,3},{8,12},{9,13},{10,... | collective-permute-start | bytes 638984 | tf_op jit(solution)/shard_map/ppermute | solution.py:870
  86.3 13.5 %copy-start.6 = (bf16[416,256]{1,0:T(8,128)(2,1)}, bf16[416,256]{1,0:T(8,128)(2,1)S(1)}, u32[]{:S(2)}) copy-start(bf16[416,256]{1,0:T(8,128)(2,1)S(1)} %collective-permute-done.6.refs_1_) | copy-start | bytes 638980
  86.3 13.5 %collective-permute-start.12 = (bf16[2,208,256]{2,1,0:T(8,128)(2,1)}, bf16[2,208,256]{2,1,0:T(8,128)(2,1)S(1)}, u32[]{:S(2)}, u32[]{:S(2)}) collective-permute-start(bf16[2,208,256]{2,1,0:T(8,128)(2,1)} %get-tuple-element.71), channel_id=1, source_target_pairs={{0,6},{1,7},{2,4},{3,5},{4,2},{5,3},{6,0},{7,1},{8,14},{9,15},{10,... | collective-permute-start | bytes 638984 | tf_op jit(solution)/shard_map/ppermute | solution.py:870
  87.5 12.2 %copy-start.7 = (bf16[416,256]{1,0:T(8,128)(2,1)}, bf16[416,256]{1,0:T(8,128)(2,1)S(1)}, u32[]{:S(2)}) copy-start(bf16[416,256]{1,0:T(8,128)(2,1)S(1)} %collective-permute-done.7.refs_2_) | copy-start | bytes 638980
  91.4 8.4 %copy-start.8 = (bf16[416,256]{1,0:T(8,128)(2,1)}, bf16[416,256]{1,0:T(8,128)(2,1)S(1)}, u32[]{:S(2)}) copy-start(bf16[416,256]{1,0:T(8,128)(2,1)S(1)} %collective-permute-done.8.refs_3_) | copy-start | bytes 638980
  95.5 4.2 %copy-start.9 = (bf16[2,208,256]{2,1,0:T(8,128)(2,1)}, bf16[2,208,256]{2,1,0:T(8,128)(2,1)S(1)}, u32[]{:S(2)}) copy-start(bf16[2,208,256]{2,1,0:T(8,128)(2,1)S(1)} %collective-permute-done.10.refs_5_) | copy-start | bytes 638980
  96.0 3.7 %copy-start.10 = (bf16[2,208,256]{2,1,0:T(8,128)(2,1)}, bf16[2,208,256]{2,1,0:T(8,128)(2,1)S(1)}, u32[]{:S(2)}) copy-start(bf16[2,208,256]{2,1,0:T(8,128)(2,1)S(1)} %collective-permute-done.11.refs_6_) | copy-start | bytes 638980
  99.7 0.7 copy-start.11
  102.8 13.5 %collective-permute-start.13 = (bf16[624,256]{1,0:T(8,128)(2,1)}, bf16[624,256]{1,0:T(8,128)(2,1)S(1)}, u32[]{:S(2)}, u32[]{:S(2)}) collective-permute-start(bf16[624,256]{1,0:T(8,128)(2,1)} %get-tuple-element.72.near_ref), channel_id=1, source_target_pairs={{0,16},{1,17},{2,18},{3,19},{4,20},{5,21},{6,22},{7,23},{8,24},{9,... | collective-permute-start | bytes 958472 | tf_op jit(solution)/shard_map/ppermute | solution.py:870
  104.4 11.3 %collective-permute-start.15 = (bf16[208,256]{1,0:T(8,128)(2,1)}, bf16[208,256]{1,0:T(8,128)(2,1)S(1)}, u32[]{:S(2)}, u32[]{:S(2)}) collective-permute-start(bf16[208,256]{1,0:T(8,128)(2,1)} %get-tuple-element.73), channel_id=1, source_target_pairs={{0,24},{1,25},{2,26},{3,27},{4,28},{5,29},{6,30},{7,31},{8,16},{9,... | collective-permute-start | bytes 319496 | tf_op jit(solution)/shard_map/ppermute | solution.py:870
  106.6 9.7 %collective-permute-start.14 = (bf16[208,256]{1,0:T(8,128)(2,1)}, bf16[208,256]{1,0:T(8,128)(2,1)S(1)}, u32[]{:S(2)}, u32[]{:S(2)}) collective-permute-start(bf16[208,256]{1,0:T(8,128)(2,1)} %get-tuple-element.73), channel_id=1, source_target_pairs={{0,8},{1,9},{2,10},{3,11},{4,12},{5,13},{6,14},{7,15},{8,0},{9,1},... | collective-permute-start | bytes 319496 | tf_op jit(solution)/shard_map/ppermute | solution.py:870
  115.8 0.6 copy-start.13
  116.3 0.6 copy-start.14
  116.9 0.7 copy-start.4

commit v3 on v2

--- a/solution.py
+++ b/solution.py
@@ -12,8 +12,7 @@
 HEAD = 64
 SLAB = 256
 BLOCK = 128
-STEP = 256
-VMEM_LIMIT = 60 * 1024 * 1024
+MIB = 1024 * 1024
 
 eps = 1e-05
 
@@ -27,6 +26,10 @@
 
 def dot_nt(a, b):
     return lax.dot_general(a, b, (((1,), (1,)), ((), ())), preferred_element_type=f32)
+
+
+def position():
+    return (lax.axis_index("section"), lax.axis_index("dp"))
 
 
 def lanes(shape):
@@ -135,23 +138,62 @@
     return (value, slope)
 
 
-def char_rows(chars_ref, table_ref, language):
+def char_rows(chars, table_ref, language):
     table = table_ref[...].astype(f32)
     row = jnp.sum(jnp.where(rows_of(table.shape) == language, table, 0.0), axis=0, keepdims=True)
-    return chars_ref[0].astype(f32) + row
-
-
-def counts_by_row(counts_ref, step, slots):
-    words = counts_ref.shape[-1]
-    counts = jnp.broadcast_to(counts_ref[0].astype(f32), (8, words)).astype(bf16)
-    shape = (words, STEP)
-    member = (lanes(shape) + step * STEP) // slots == rows_of(shape)
+    return chars.astype(f32) + row
+
+
+def counts_by_row(counts, rows, slots):
+    words = counts.shape[-1]
+    counts = jnp.broadcast_to(counts.astype(f32), (8, words)).astype(bf16)
+    shape = (words, rows)
+    member = lanes(shape) // slots == rows_of(shape)
     return dot(counts, jnp.where(member, 1.0, 0.0).astype(bf16))[:1]
+
+
+def counts_column(counts):
+    words = counts.shape[-1]
+    shape = (words, words)
+    spread = jnp.broadcast_to(counts.astype(f32), shape)
+    return jnp.sum(
+        jnp.where(rows_of(shape) == lanes(shape), spread, 0.0), axis=1, keepdims=True
+    )
+
+
+def fetch_all(sources, targets, sems):
+    fetches = [
+        pltpu.make_async_copy(source, target, sems.at[place])
+        for place, (source, target) in enumerate(zip(sources, targets))
+    ]
+    for fetch in fetches:
+        fetch.start()
+    return fetches
+
+
+def in_hbm(array):
+    return pltpu.with_memory_space_constraint(array, pltpu.HBM)
 
 
 def char_forward_kernel(
     slots,
-    where_ref,
+    languages_ref,
+    chars_hbm,
+    counts_hbm,
+    table_hbm,
+    gain_attn_hbm,
+    project_hbm,
+    output_hbm,
+    gain_mlp_hbm,
+    expand_hbm,
+    shrink_hbm,
+    pooled_ref,
+    hidden_sum_ref,
+    qkv_ref,
+    probs_ref,
+    mixed_ref,
+    middle_ref,
+    slope_ref,
     chars_ref,
     counts_ref,
     table_ref,
@@ -161,105 +203,96 @@
     gain_mlp_ref,
     expand_ref,
     shrink_ref,
-    pooled_ref,
-    hidden_sum_ref,
-    qkv_ref,
-    probs_ref,
-    mixed_ref,
-    middle_ref,
-    slope_ref,
-    sums,
+    sems,
 ):
-    step = pl.program_id(0)
-    x = char_rows(chars_ref, table_ref, where_ref[1])
+    section, _ = position()
+    fetches = fetch_all(
+        (
+            counts_hbm,
+            table_hbm,
+            gain_attn_hbm,
+            chars_hbm.at[section],
+            project_hbm,
+            output_hbm,
+            gain_mlp_hbm,
+            expand_hbm,
+            shrink_hbm,
+        ),
+        (
+            counts_ref,
+            table_ref,
+            gain_attn_ref,
+            chars_ref,
+            project_ref,
+            output_ref,
+            gain_mlp_ref,
+            expand_ref,
+            shrink_ref,
+        ),
+        sems,
+    )
+    fetches[0].wait()
+    counts = counts_ref[section]
+    rows = chars_ref.shape[0]
+    words = counts.shape[-1]
+    row_counts = counts_by_row(counts, rows, slots)
+    for fetch in fetches[1:4]:
+        fetch.wait()
+    x = char_rows(chars_ref[...], table_ref, languages_ref[section, 0])
     normal, _ = unit(x)
     normed = (normal * gain_attn_ref[...]).astype(bf16)
-    qkv = dot(normed, project_ref[...]).astype(bf16)
-    qkv_ref[...] = qkv
-    row_counts = counts_by_row(counts_ref, step, slots)
+    fetches[4].wait()
+    qkv_ref[...] = dot(normed, project_ref[...]).astype(bf16)
     mixed = []
-    for block in range(STEP // BLOCK):
+    for block in range(rows // BLOCK):
         part = slice(block * BLOCK, (block + 1) * BLOCK)
         key_mask = rows_of((slots, BLOCK)).astype(f32) < row_counts[:, part]
         probs, piece = attend(
-            qkv[part, :SLAB], qkv[part, SLAB : 2 * SLAB], qkv[part, 2 * SLAB :], key_mask, slots
+            qkv_ref[part, :SLAB],
+            qkv_ref[part, SLAB : 2 * SLAB],
+            qkv_ref[part, 2 * SLAB :],
+            key_mask,
+            slots,
         )
         for head in range(CH):
             probs_ref[head * slots : (head + 1) * slots, part] = probs[head]
         mixed_ref[:, part] = piece
         mixed.append(flip(piece))
     mixed = jnp.concatenate(mixed, axis=0)
+    fetches[5].wait()
     middle = x + dot(mixed, output_ref[...])
     middle_ref[...] = middle
     normal, _ = unit(middle)
+    fetches[6].wait()
     normed = (normal * gain_mlp_ref[...]).astype(bf16)
-    word_shape = (STEP // slots, STEP)
+    word_shape = (words, rows)
     lane = lanes(word_shape)
     member = (lane // slots == rows_of(word_shape)) & ((lane % slots).astype(f32) < row_counts)
     member = jnp.where(member, 1.0, 0.0).astype(bf16)
-    words = pl.ds(pl.multiple_of(step * (STEP // slots), STEP // slots), STEP // slots)
+    fetches[7].wait()
     for at in range(0, expand_ref.shape[1], 256):
         part = slice(at, at + 256)
         value, slope = gelu_parts(dot(normed, expand_ref[:, part]))
         slope_ref[:, part] = slope.astype(bf16)
-        hidden_sum_ref[words, part] = dot(member, value.astype(bf16)).astype(bf16)
+        hidden_sum_ref[:, part] = dot(member, value.astype(bf16)).astype(bf16)
     high = middle.astype(bf16)
     low = (middle - high.astype(f32)).astype(bf16)
-    sums[words, :] = dot(member, high) + dot(member, low)
-
-    @pl.when(step == pl.num_programs(0) - 1)
-    def _():
-        words = counts_ref.shape[-1]
-        shape = (words, words)
-        column = jnp.sum(
-            jnp.where(
-                rows_of(shape) == lanes(shape),
-                jnp.broadcast_to(counts_ref[0].astype(f32), shape),
-                0.0,
-            ),
-            axis=1,
-            keepdims=True,
-        )
-        total = sums[...] + dot(hidden_sum_ref[...], shrink_ref[...])
-        pooled_ref[...] = (total / column).astype(bf16)
-
-
-def char_forward(where, chars, counts, table, weights, slots):
-    gain_attn, project, output, gain_mlp, expand_w, shrink = weights
+    fetches[8].wait()
+    total = dot(member, high) + dot(member, low) + dot(hidden_sum_ref[...], shrink_ref[...])
+    pooled_ref[...] = (total / counts_column(counts)).astype(bf16)
+
+
+def char_forward(languages, chars, counts, table, weights, slots):
     rows, width = chars.shape[1:]
     words = rows // slots
-    hidden = expand_w.shape[1]
-
-    def whole(array):
-        return pl.BlockSpec(array.shape, lambda i, w: (0,) * array.ndim)
-
+    hidden = weights[4].shape[1]
+    vmem = pl.BlockSpec(memory_space=pltpu.VMEM)
+    hbm = pl.BlockSpec(memory_space=pltpu.HBM)
+    fetched = (counts, table) + tuple(weights)
     return pl.pallas_call(
         functools.partial(char_forward_kernel, slots),
-        grid_spec=pltpu.PrefetchScalarGridSpec(
-            num_scalar_prefetch=1,
-            grid=(rows // STEP,),
-            in_specs=[
-                pl.BlockSpec((1, STEP, width), lambda i, w: (w[0], i, 0)),
-                pl.BlockSpec((1, 1, words), lambda i, w: (w[0], 0, 0)),
-                whole(table),
-                whole(gain_attn),
-                whole(project),
-                whole(output),
-                whole(gain_mlp),
-                whole(expand_w),
-                whole(shrink),
-            ],
-            out_specs=[
-                pl.BlockSpec((words, width), lambda i, w: (0, 0)),
-                pl.BlockSpec((words, hidden), lambda i, w: (0, 0)),
-                pl.BlockSpec((STEP, 3 * width), lambda i, w: (i, 0)),
-                pl.BlockSpec((CH * slots, STEP), lambda i, w: (0, i)),
-                pl.BlockSpec((width, STEP), lambda i, w: (0, i)),
-                pl.BlockSpec((STEP, width), lambda i, w: (i, 0)),
-                pl.BlockSpec((STEP, hidden), lambda i, w: (i, 0)),
-            ],
-            scratch_shapes=[pltpu.VMEM((words, width), f32)],
-        ),
+        in_specs=[pl.BlockSpec(memory_space=pltpu.SMEM)] + [hbm] * 9,
+        out_specs=[vmem] * 7,
         out_shape=[
             jax.ShapeDtypeStruct((words, width), bf16),
             jax.ShapeDtypeStruct((words, hidden), bf16),
@@ -269,94 +302,170 @@
             jax.ShapeDtypeStruct((rows, width), f32),
             jax.ShapeDtypeStruct((rows, hidden), bf16),
         ],
-        compiler_params=pltpu.CompilerParams(vmem_limit_bytes=VMEM_LIMIT),
+        scratch_shapes=[pltpu.VMEM(chars.shape[1:], bf16)]
+        + [pltpu.VMEM(array.shape, array.dtype) for array in fetched]
+        + [pltpu.SemaphoreType.DMA((9,))],
+        compiler_params=pltpu.CompilerParams(vmem_limit_bytes=16 * MIB),
+        cost_estimate=pl.CostEstimate(
+            flops=64 * rows * width * width, bytes_accessed=8 * MIB, transcendentals=0
+        ),
         name="char_forward",
-    )(where, chars, counts, table, gain_attn, project, output, gain_mlp, expand_w, shrink)
-
-
-CHAR_SLOT = 208
-
-
-def char_backward_kernel(
+    )(languages, *[in_hbm(array) for array in (chars,) + fetched])
+
+
+CHAR_MLP_SLOT = 128
+CHAR_ATTN_SLOT = 80
+
+
+def char_slot(shard, me):
+    other = shard ^ me
+    return (other & 1) * 8 + ((other >> 1) & 3) * 2 + (other >> 3)
+
+
+def put_char(packed, me, shards, gradient, at):
+    size = gradient.shape[0] // shards
+    for shard in range(shards):
+        piece = gradient[shard * size : (shard + 1) * size].astype(bf16)
+        for column in range(gradient.shape[1] // SLAB):
+            start = at + column * size
+            packed[char_slot(shard, me), start : start + size] = piece[
+                :, column * SLAB : (column + 1) * SLAB
+            ]
+    return at + size * (gradient.shape[1] // SLAB)
+
+
+def hand_out(packed, keep_ref, send_ref, sems):
+    half = packed.shape[0] // 2
+    copies = [
+        pltpu.make_async_copy(packed.at[pl.ds(half, half)], send_ref, sems.at[0]),
+        pltpu.make_async_copy(packed.at[pl.ds(0, half)], keep_ref, sems.at[1]),
+    ]
+    for copy in copies:
+        copy.start()
+    for copy in copies:
+        copy.wait()
+
+
+def char_mlp_back_kernel(
     slots,
     shards,
-    where_ref,
-    chars_ref,
-    counts_ref,
-    table_ref,
-    gain_attn_ref,
-    project_ref,
-    output_ref,
+    counts_hbm,
     gain_mlp_ref,
     expand_ref,
     shrink_ref,
     dpooled_ref,
     hidden_sum_ref,
+    middle_ref,
+    slope_ref,
+    dmiddle_ref,
+    gain_ref,
+    keep_ref,
+    send_ref,
+    counts_ref,
+    dhidden_words,
+    dbefore,
+    packed,
+    sems,
+):
+    section, me = position()
+    fetch = pltpu.make_async_copy(counts_hbm, counts_ref, sems.at[2])
+    fetch.start()
+    fetch.wait()
+    counts = counts_ref[section]
+    rows, width = middle_ref.shape
+    words = counts.shape[-1]
+    spread = dpooled_ref[...].astype(f32) / counts_column(counts)
+    spread_high = spread.astype(bf16)
+    spread_low = (spread - spread_high.astype(f32)).astype(bf16)
+    dhidden_words[...] = dot_nt(spread_high, shrink_ref[...]).astype(bf16)
+    shape = (rows, words)
+    row = rows_of(shape)
+    member = (row // slots == lanes(shape)) & (row % slots < counts)
+    member = jnp.where(member, 1.0, 0.0).astype(bf16)
+    for at in range(0, expand_ref.shape[1], 256):
+        part = slice(at, at + 256)
+        dbefore[:, part] = dot(member, dhidden_words[:, part]).astype(bf16) * slope_ref[:, part]
+    dnormed = dot_nt(dbefore[...], expand_ref[...])
+    normal, scale = unit(middle_ref[...])
+    normed_mlp_t = flip((normal * gain_mlp_ref[...]).astype(bf16))
+    gain_ref[...] = jnp.broadcast_to(
+        jnp.sum(dnormed * normal, axis=0, keepdims=True), gain_ref.shape
+    )
+    dmiddle_ref[...] = (
+        dot(member, spread_high)
+        + dot(member, spread_low)
+        + unit_back(dnormed, gain_mlp_ref[...], normal, scale)
+    )
+    at = put_char(packed, me, shards, dot(normed_mlp_t, dbefore[...]), 0)
+    put_char(packed, me, shards, dot(flip(hidden_sum_ref[...]), spread_high), at)
+    hand_out(packed, keep_ref, send_ref, sems)
+
+
+def char_mlp_back(counts, weights, dpooled, stored, slots, shards):
+    _, _, _, gain_mlp, expand_w, shrink = weights
+    hidden_sum, _, _, _, middle, slope = stored
+    rows, width = middle.shape
+    words = rows // slots
+    hidden = expand_w.shape[1]
+    half = (shards // 2, CHAR_MLP_SLOT, width)
+    vmem = pl.BlockSpec(memory_space=pltpu.VMEM)
+    hbm = pl.BlockSpec(memory_space=pltpu.HBM)
+    return pl.pallas_call(
+        functools.partial(char_mlp_back_kernel, slots, shards),
+        in_specs=[hbm] + [vmem] * 7,
+        out_specs=[vmem, vmem, hbm, hbm],
+        out_shape=[
+            jax.ShapeDtypeStruct((rows, width), f32),
+            jax.ShapeDtypeStruct((8, width), f32),
+            jax.ShapeDtypeStruct(half, bf16),
+            jax.ShapeDtypeStruct(half, bf16),
+        ],
+        scratch_shapes=[
+            pltpu.VMEM(counts.shape, counts.dtype),
+            pltpu.VMEM((words, hidden), bf16),
+            pltpu.VMEM((rows, hidden), bf16),
+            pltpu.VMEM((shards, CHAR_MLP_SLOT, width), bf16),
+            pltpu.SemaphoreType.DMA((3,)),
+        ],
+        compiler_params=pltpu.CompilerParams(vmem_limit_bytes=16 * MIB),
+        cost_estimate=pl.CostEstimate(
+            flops=64 * rows * width * width, bytes_accessed=8 * MIB, transcendentals=0
+        ),
+        name="char_mlp_back",
+    )(in_hbm(counts), gain_mlp, expand_w, shrink, dpooled, hidden_sum, middle, slope)
+
+
+def char_attn_back_kernel(
+    slots,
+    shards,
+    languages_ref,
+    _,
+    chars_hbm,
+    table_ref,
+    gain_attn_ref,
+    project_ref,
+    output_ref,
+    dmiddle_ref,
+    gain_mlp_grad_ref,
     qkv_ref,
     probs_ref,
     mixed_ref,
-    middle_ref,
-    slope_ref,
     grad_ref,
     keep_ref,
     send_ref,
-    spread_high,
-    spread_low,
-    dhidden_words,
-    dbefore,
+    chars_ref,
     dqkv,
-    dy,
-    normed_t,
-    normed_mlp_t,
-    gains,
     packed,
     sems,
 ):
-    step = pl.program_id(0)
-    words = counts_ref.shape[-1]
-
-    @pl.when(step == 0)
-    def _():
-        shape = (words, words)
-        column = jnp.sum(
-            jnp.where(
-                rows_of(shape) == lanes(shape),
-                jnp.broadcast_to(counts_ref[0].astype(f32), shape),
-                0.0,
-            ),
-            axis=1,
-            keepdims=True,
-        )
-        spread = dpooled_ref[...].astype(f32) / column
-        high = spread.astype(bf16)
-        spread_high[...] = high
-        spread_low[...] = (spread - high.astype(f32)).astype(bf16)
-        dhidden_words[...] = dot_nt(high, shrink_ref[...]).astype(bf16)
-        gains[...] = jnp.zeros_like(gains)
-
-    at_step = pl.ds(pl.multiple_of(step * STEP, STEP), STEP)
-    shape = (STEP, words)
-    row = rows_of(shape) + step * STEP
-    member = (row // slots == lanes(shape)) & (row % slots < counts_ref[0])
-    member = jnp.where(member, 1.0, 0.0).astype(bf16)
-    dnormed = jnp.zeros((STEP, gain_mlp_ref.shape[1]), f32)
-    for at in range(0, expand_ref.shape[1], 256):
-        part = slice(at, at + 256)
-        piece = dot(member, dhidden_words[:, part]).astype(bf16) * slope_ref[:, part]
-        dbefore[at_step, part] = piece
-    dnormed = dot_nt(dbefore[at_step, :], expand_ref[...])
-    normal, scale = unit(middle_ref[...])
-    normed_mlp_t[:, at_step] = flip((normal * gain_mlp_ref[...]).astype(bf16))
-    gains[1:2] += jnp.sum(dnormed * normal, axis=0, keepdims=True)
-    dmiddle = (
-        dot(member, spread_high[...])
-        + dot(member, spread_low[...])
-        + unit_back(dnormed, gain_mlp_ref[...], normal, scale)
-    )
-    dy_low = dmiddle.astype(bf16)
-    dy[at_step, :] = dy_low
-    dmixed = dot_nt(dy_low, output_ref[...]).astype(bf16)
-    for block in range(STEP // BLOCK):
+    section, me = position()
+    fetch = pltpu.make_async_copy(chars_hbm.at[section], chars_ref, sems.at[2])
+    fetch.start()
+    rows, width = dmiddle_ref.shape
+    language = languages_ref[section, 0]
+    dy = dmiddle_ref[...].astype(bf16)
+    dmixed = dot_nt(dy, output_ref[...]).astype(bf16)
+    for block in range(rows // BLOCK):
         part = slice(block * BLOCK, (block + 1) * BLOCK)
         probs = [probs_ref[head * slots : (head + 1) * slots, part] for head in range(CH)]
         pieces = attend_back(
@@ -367,134 +476,74 @@
             dmixed[part],
             slots,
         )
-        at_block = pl.ds(pl.multiple_of(step * STEP + block * BLOCK, BLOCK), BLOCK)
-        for place in range(3):
-            dqkv[at_block, place * SLAB : (place + 1) * SLAB] = pieces[place]
-    dnormed = dot_nt(dqkv[at_step, :], project_ref[...])
-    normal, scale = unit(char_rows(chars_ref, table_ref, where_ref[1]))
-    normed_t[:, at_step] = flip((normal * gain_attn_ref[...]).astype(bf16))
-    gains[0:1] += jnp.sum(dnormed * normal, axis=0, keepdims=True)
-    dx = dmiddle + unit_back(dnormed, gain_attn_ref[...], normal, scale)
+        for number in range(3):
+            dqkv[part, number * SLAB : (number + 1) * SLAB] = pieces[number]
+    dnormed = dot_nt(dqkv[...], project_ref[...])
+    fetch.wait()
+    normal, scale = unit(char_rows(chars_ref[...], table_ref, language))
+    normed_t = flip((normal * gain_attn_ref[...]).astype(bf16))
+    gain_attn_grad = jnp.sum(dnormed * normal, axis=0, keepdims=True)
+    dx = dmiddle_ref[...] + unit_back(dnormed, gain_attn_ref[...], normal, scale)
     grad_ref[...] = dx
     row_sum = jnp.sum(dx, axis=0, keepdims=True)
-    gains[8:16] += jnp.where(rows_of((8, 1)) == where_ref[1], row_sum, 0.0)
-
-    @pl.when(step == pl.num_programs(0) - 1)
-    def _():
-        me = where_ref[2]
-        width = gains.shape[1]
-
-        def place(shard):
-            other = shard ^ me
-            return (other & 1) * 8 + ((other >> 1) & 3) * 2 + (other >> 3)
-
-        def put(gradient, at):
-            size = gradient.shape[0] // shards
-            for shard in range(shards):
-                piece = gradient[shard * size : (shard + 1) * size].astype(bf16)
-                for column in range(gradient.shape[1] // width):
-                    start = at + column * size
-                    packed[place(shard), start : start + size] = piece[
-                        :, column * width : (column + 1) * width
-                    ]
-            return at + size * (gradient.shape[1] // width)
-
-        at = put(dot(normed_t[...], dqkv[...]), 0)
-        at = put(dot(mixed_ref[...], dy[...]), at)
-        at = put(dot(normed_mlp_t[...], dbefore[...]), at)
-        at = put(dot(flip(hidden_sum_ref[...]), spread_high[...]), at)
-        extra = gains[...].astype(bf16)
-        for shard in range(shards):
-            packed[shard, at : at + 16] = extra
-        half = shards // 2
-        copies = [
-            pltpu.make_async_copy(packed.at[pl.ds(half, half)], send_ref, sems.at[0]),
-            pltpu.make_async_copy(packed.at[pl.ds(0, half)], keep_ref, sems.at[1]),
-        ]
-        for copy in copies:
-            copy.start()
-        for copy in copies:
-            copy.wait()
-
-
-def char_backward(where, chars, counts, table, weights, dpooled, stored, slots, shards):
-    gain_attn, project, output, gain_mlp, expand_w, shrink = weights
-    hidden_sum, qkv, probs, mixed, middle, slope = stored
-    rows, width = chars.shape[1:]
-    words = rows // slots
-    hidden = expand_w.shape[1]
-
-    def whole(array):
-        return pl.BlockSpec(array.shape, lambda i, w: (0,) * array.ndim)
-
-    half = (shards // 2, CHAR_SLOT, width)
+    at = put_char(packed, me, shards, dot(normed_t, dqkv[...]), 0)
+    at = put_char(packed, me, shards, dot(mixed_ref[...], dy), at)
+    extra = jnp.concatenate(
+        [
+            gain_attn_grad,
+            gain_mlp_grad_ref[:7],
+            jnp.where(rows_of((8, 1)) == language, row_sum, 0.0),
+        ],
+        axis=0,
+    ).astype(bf16)
+    for shard in range(shards):
+        packed[shard, at : at + 16] = extra
+    hand_out(packed, keep_ref, send_ref, sems)
+
+
+def char_attn_back(
+    languages, chars, table, weights, dmiddle, gain_mlp_grad, stored, slots, shards, after
+):
+    gain_attn, project, output, _, _, _ = weights
+    _, qkv, probs, mixed, _, _ = stored
+    rows, width = dmiddle.shape
+    half = (shards // 2, CHAR_ATTN_SLOT, width)
+    vmem = pl.BlockSpec(memory_space=pltpu.VMEM)
+    hbm = pl.BlockSpec(memory_space=pltpu.HBM)
     return pl.pallas_call(
-        functools.partial(char_backward_kernel, slots, shards),
-        grid_spec=pltpu.PrefetchScalarGridSpec(
-            num_scalar_prefetch=1,
-            grid=(rows // STEP,),
-            in_specs=[
-                pl.BlockSpec((1, STEP, width), lambda i, w: (w[0], i, 0)),
-                pl.BlockSpec((1, 1, words), lambda i, w: (w[0], 0, 0)),
-                whole(table),
-                whole(gain_attn),
-                whole(project),
-                whole(output),
-                whole(gain_mlp),
-                whole(expand_w),
-                whole(shrink),
-                whole(dpooled),
-                whole(hidden_sum),
-                pl.BlockSpec((STEP, 3 * width), lambda i, w: (i, 0)),
-                pl.BlockSpec((CH * slots, STEP), lambda i, w: (0, i)),
-                whole(mixed),
-                pl.BlockSpec((STEP, width), lambda i, w: (i, 0)),
-                pl.BlockSpec((STEP, hidden), lambda i, w: (i, 0)),
-            ],
-            out_specs=[
-                pl.BlockSpec((STEP, width), lambda i, w: (i, 0)),
-                pl.BlockSpec(memory_space=pl.ANY),
-                pl.BlockSpec(memory_space=pl.ANY),
-            ],
-            scratch_shapes=[
-                pltpu.VMEM((words, width), bf16),
-                pltpu.VMEM((words, width), bf16),
-                pltpu.VMEM((words, hidden), bf16),
-                pltpu.VMEM((rows, hidden), bf16),
-                pltpu.VMEM((rows, 3 * width), bf16),
-                pltpu.VMEM((rows, width), bf16),
-                pltpu.VMEM((width, rows), bf16),
-                pltpu.VMEM((width, rows), bf16),
-                pltpu.VMEM((16, width), f32),
-                pltpu.VMEM((shards, CHAR_SLOT, width), bf16),
-                pltpu.SemaphoreType.DMA((2,)),
-            ],
-        ),
+        functools.partial(char_attn_back_kernel, slots, shards),
+        in_specs=[pl.BlockSpec(memory_space=pltpu.SMEM), pl.BlockSpec(memory_space=pl.ANY), hbm]
+        + [vmem] * 9,
+        out_specs=[vmem, hbm, hbm],
         out_shape=[
             jax.ShapeDtypeStruct((rows, width), f32),
             jax.ShapeDtypeStruct(half, bf16),
             jax.ShapeDtypeStruct(half, bf16),
         ],
-        compiler_params=pltpu.CompilerParams(vmem_limit_bytes=VMEM_LIMIT),
-        name="char_backward",
+        scratch_shapes=[
+            pltpu.VMEM((rows, width), bf16),
+            pltpu.VMEM((rows, 3 * width), bf16),
+            pltpu.VMEM((shards, CHAR_ATTN_SLOT, width), bf16),
+            pltpu.SemaphoreType.DMA((3,)),
+        ],
+        compiler_params=pltpu.CompilerParams(vmem_limit_bytes=16 * MIB),
+        cost_estimate=pl.CostEstimate(
+            flops=64 * rows * width * width, bytes_accessed=8 * MIB, transcendentals=0
+        ),
+        name="char_attn_back",
     )(
-        where,
-        chars,
-        counts,
+        languages,
+        after,
+        in_hbm(chars),
         table,
         gain_attn,
         project,
         output,
-        gain_mlp,
-        expand_w,
-        shrink,
-        dpooled,
-        hidden_sum,
+        dmiddle,
+        gain_mlp_grad,
         qkv,
         probs,
         mixed,
-        middle,
-        slope,
     )
 
 
@@ -504,15 +553,12 @@
 def word_kernel(
     length,
     shards,
-    where_ref,
     own_ref,
-    core_ref,
-    high_ref,
+    far_ref,
     section_ref,
     both_ref,
     cot_ref,
-    cot_core_ref,
-    cot_high_ref,
+    cot_far_ref,
     input_ref,
     gain_attn_ref,
     project_ref,
@@ -523,9 +569,7 @@
     result_ref,
     dpooled_ref,
     keep_ref,
-    send0_ref,
-    send1_ref,
-    send2_ref,
+    send_ref,
     pooled,
     dz,
     start,
@@ -537,7 +581,7 @@
     middle,
     normed_mlp_t,
     hidden,
-    slope,
+    pooled_t,
     dbefore,
     dmixed,
     dqkv,
@@ -547,20 +591,14 @@
 ):
     total = pooled.shape[0]
     width = output_ref.shape[0]
-    section = where_ref[0]
-    me = where_ref[2]
+    section, me = position()
     slabs = width // SLAB
-    pooled[0:length] = own_ref[...]
-    pooled[length : 2 * length] = core_ref[...]
-    for place, ref in enumerate((high_ref, section_ref, both_ref)):
-        pooled[(2 + 2 * place) * length : (4 + 2 * place) * length] = ref[...]
-    at = 0
-    for other in (section, 1 - section):
-        dz[at : at + length] = cot_ref[other]
-        dz[at + length : at + 2 * length] = cot_core_ref[other]
-        dz[at + 2 * length : at + 3 * length] = cot_high_ref[0, other]
-        dz[at + 3 * length : at + 4 * length] = cot_high_ref[1, other]
-        at += 4 * length
+    for place, ref in enumerate((own_ref, far_ref, section_ref, both_ref)):
+        pooled[place * length : (place + 1) * length] = ref[...]
+    for place, (ref, other) in enumerate(
+        ((cot_ref, section), (cot_far_ref, section), (cot_ref, 1 - section), (cot_far_ref, 1 - section))
+    ):
+        dz[place * length : (place + 1) * length] = ref[other]
 
     x = dot(pooled[...], input_ref[...])
     start[...] = x
@@ -627,22 +665,18 @@
     dpooled_ref[...] = dot_nt(dword[:length], input_ref[...]).astype(bf16)
     normed[...] = dword
 
-    low_shards = [0, 1, 2, 3]
+    low_shards = range(shards // 2)
 
     def shard_of(place):
-        return (me & 9) | (place << 1)
+        return (me & 8) | place
 
     def slot_of(place):
-        return place ^ ((me >> 1) & 3)
+        other = place ^ (me & 7)
+        return (other & 1) * 4 + (other >> 1)
 
     def own_rows(flipped, size):
-        return jnp.concatenate(
-            [
-                flipped[pl.ds(pl.multiple_of(shard_of(place) * size, size), size), :]
-                for place in low_shards
-            ],
-            axis=0,
-        )
+        first = pl.multiple_of(shard_of(0) * size, 8 * size)
+        return flipped[pl.ds(first, 8 * size), :]
 
     def own_columns(ref, size):
         return ref[:, pl.ds(pl.multiple_of(section * size, size), size)]
@@ -658,15 +692,12 @@
                 ]
         return at + size * (gradient.shape[1] // SLAB)
 
-    dmixed[:, :SLAB] = pooled[...]
-    pooled_t = flip(dmixed[:, :SLAB])
-    mixed_holder = normed_t
     size = normed_t.shape[0] // shards
     lhs = own_rows(normed_t, size)
-    mixed_holder[0 : pooled_t.shape[0]] = pooled_t
+    pooled_t[...] = flip(pooled[...])
     at = put(
         dot(
-            own_rows(mixed_holder, pooled_t.shape[0] // shards),
+            own_rows(pooled_t, pooled_t.shape[0] // shards),
             own_columns(normed, width // 2),
         ),
         0,
@@ -674,14 +705,8 @@
     at = put(dot(lhs, own_columns(dqkv, 3 * width // 2)), at)
     at = put(dot(own_rows(mixed_t, size), own_columns(dy, width // 2)), at)
     at = put(dot(own_rows(normed_mlp_t, size), own_columns(dbefore, expand_ref.shape[1] // 2)), at)
-    size = hidden.shape[1] // shards
-    lhs = jnp.concatenate(
-        [
-            flip(hidden[:, pl.ds(pl.multiple_of(shard_of(place) * size, size), size)])
-            for place in low_shards
-        ],
-        axis=0,
-    )
+    size = hidden.shape[1] // 2
+    lhs = flip(hidden[:, pl.ds(pl.multiple_of((me >> 3) * size, size), size)])
     at = put(dot(lhs, own_columns(dz, width // 2)), at)
     extra = jnp.concatenate(
         [gain_attn_grad[:, :SLAB], gain_attn_grad[:, SLAB:]]
@@ -691,34 +716,28 @@
     ).astype(bf16)
     for place in low_shards:
         packed[place, at : at + 16] = extra
-    copies = [
-        pltpu.make_async_copy(packed.at[place], ref, sems.at[place])
-        for place, ref in enumerate((keep_ref, send0_ref, send1_ref, send2_ref))
-    ]
-    for copy in copies:
-        copy.start()
-    for copy in copies:
-        copy.wait()
-
-
-def word_group(where, pooled, cotangents, word_input, weights, shards):
+    hand_out(packed, keep_ref, send_ref, sems)
+
+
+def word_group(pooled, cotangents, word_input, weights, shards):
     gain_attn, project, output, gain_mlp, expand_w, shrink = weights
     length, channels = pooled[0].shape
     width = output.shape[0]
     hidden = expand_w.shape[1]
-    total = 8 * length
-    slot = (WORD_SLOT, SLAB)
+    total = 4 * length
+    half = (4, WORD_SLOT, SLAB)
     vmem = pl.BlockSpec(memory_space=pltpu.VMEM)
-    hbm = pl.BlockSpec(memory_space=pl.ANY)
+    hbm = pl.BlockSpec(memory_space=pltpu.HBM)
     return pl.pallas_call(
         functools.partial(word_kernel, length, shards),
-        in_specs=[pl.BlockSpec(memory_space=pltpu.SMEM)] + [vmem] * 15,
-        out_specs=[vmem, vmem, hbm, hbm, hbm, hbm],
+        in_specs=[vmem] * 13,
+        out_specs=[vmem, vmem, hbm, hbm],
         out_shape=[
             jax.ShapeDtypeStruct((length, width), f32),
             jax.ShapeDtypeStruct((length, channels), bf16),
-        ]
-        + [jax.ShapeDtypeStruct(slot, bf16)] * 4,
+            jax.ShapeDtypeStruct(half, bf16),
+            jax.ShapeDtypeStruct(half, bf16),
+        ],
         scratch_shapes=[
             pltpu.VMEM((total, channels), bf16),
             pltpu.VMEM((total, width), bf16),
@@ -731,64 +750,82 @@
             pltpu.VMEM((total, width), f32),
             pltpu.VMEM((width, total), bf16),
             pltpu.VMEM((total, hidden), bf16),
-            pltpu.VMEM((8, 128), bf16),
+            pltpu.VMEM((channels, total), bf16),
             pltpu.VMEM((total, hidden), bf16),
             pltpu.VMEM((total, width), bf16),
             pltpu.VMEM((total, 3 * width), bf16),
             pltpu.VMEM((total, width), bf16),
-            pltpu.VMEM((4,) + slot, bf16),
-            pltpu.SemaphoreType.DMA((4,)),
+            pltpu.VMEM((8, WORD_SLOT, SLAB), bf16),
+            pltpu.SemaphoreType.DMA((2,)),
         ],
-        compiler_params=pltpu.CompilerParams(vmem_limit_bytes=VMEM_LIMIT),
+        compiler_params=pltpu.CompilerParams(vmem_limit_bytes=20 * MIB),
+        cost_estimate=pl.CostEstimate(
+            flops=total * width * width * 25 * 4, bytes_accessed=8 * MIB, transcendentals=0
+        ),
         name="word_group",
-    )(where, *pooled, *cotangents, word_input, gain_attn, project, output, gain_mlp, expand_w, shrink)
-
-
-def core_sum_kernel(keep_ref, arrived_ref, *out_refs):
-    for place, ref in enumerate(out_refs):
-        part = slice(2 * place, 2 * place + 2)
-        ref[...] = (keep_ref[part].astype(f32) + arrived_ref[part].astype(f32)).astype(bf16)
-
-
-def core_sum(keep, arrived):
-    piece = jax.ShapeDtypeStruct((2,) + keep.shape[1:], bf16)
+    )(*pooled, *cotangents, word_input, gain_attn, project, output, gain_mlp, expand_w, shrink)
+
+
+def added(*refs):
+    return functools.reduce(lambda a, b: a + b, [ref.astype(f32) for ref in refs]).astype(bf16)
+
+
+def core_sum_kernel(groups, *refs):
+    ins = refs[: 2 * groups]
+    outs = refs[-4:]
+    for place, out in enumerate(outs):
+        at = 0
+        for keep, arrived in zip(ins[0::2], ins[1::2]):
+            many = keep.shape[0] // len(outs)
+            for entry in range(place * many, (place + 1) * many):
+                size = keep.shape[1]
+                out[at : at + size] = added(keep[entry], arrived[entry])
+                at += size
+
+
+def core_sum(*pairs, after=()):
+    rows = sum(keep.shape[0] // 4 * keep.shape[1] for keep, _ in pairs)
     return pl.pallas_call(
-        core_sum_kernel,
-        out_shape=[piece] * (keep.shape[0] // 2),
-        compiler_params=pltpu.CompilerParams(vmem_limit_bytes=VMEM_LIMIT),
+        functools.partial(core_sum_kernel, len(pairs)),
+        in_specs=[pl.BlockSpec(memory_space=pltpu.VMEM)] * (2 * len(pairs))
+        + [pl.BlockSpec(memory_space=pl.ANY)] * len(after),
+        out_shape=[jax.ShapeDtypeStruct((rows, SLAB), bf16)] * 4,
+        compiler_params=pltpu.CompilerParams(vmem_limit_bytes=14 * MIB),
         name="core_sum",
-    )(keep, arrived)
+    )(*[array for pair in pairs for array in pair], *after)
 
 
 def plane_sum_kernel(*refs):
-    word, char, near_ref, far_ref = (refs[:4], refs[4:8], refs[8], refs[9])
-    rows = word[0].shape[0]
-
-    def total(parts, pick):
-        return functools.reduce(lambda a, b: a + b, [pick(part).astype(f32) for part in parts])
-
-    near_ref[:rows] = total(word, lambda r: r[...]).astype(bf16)
-    near_ref[rows:] = total(char, lambda r: r[0]).astype(bf16)
-    far_ref[...] = total(char, lambda r: r[1]).astype(bf16)
-
-
-def plane_sum(word, char):
-    rows = word[0].shape[0] + char[0].shape[1]
+    first, second, near_ref, far_ref = (refs[:4], refs[4:8], refs[8], refs[9])
+    near_ref[:WORD_SLOT] = added(*[ref[:WORD_SLOT] for ref in first])
+    size = CHAR_MLP_SLOT
+    for half, out in ((0, near_ref), (1, far_ref)):
+        start = WORD_SLOT + half * size
+        at = WORD_SLOT if half == 0 else 0
+        out[at : at + size] = added(*[ref[start : start + size] for ref in first])
+        at += size
+        start = half * CHAR_ATTN_SLOT
+        out[at : at + CHAR_ATTN_SLOT] = added(
+            *[ref[start : start + CHAR_ATTN_SLOT] for ref in second]
+        )
+
+
+def plane_sum(first, second):
+    rows = CHAR_MLP_SLOT + CHAR_ATTN_SLOT
     return pl.pallas_call(
         plane_sum_kernel,
         out_shape=[
+            jax.ShapeDtypeStruct((WORD_SLOT + rows, SLAB), bf16),
             jax.ShapeDtypeStruct((rows, SLAB), bf16),
-            jax.ShapeDtypeStruct(char[0].shape[1:], bf16),
         ],
-        compiler_params=pltpu.CompilerParams(vmem_limit_bytes=VMEM_LIMIT),
+        compiler_params=pltpu.CompilerParams(vmem_limit_bytes=12 * MIB),
         name="plane_sum",
-    )(*word, *char)
-
-
-def last_sum_kernel(shapes, where_ref, near_ref, section_ref, high_ref, both_ref, *outs):
+    )(*first, *second)
+
+
+def last_sum_kernel(near_ref, section_ref, high_ref, both_ref, *outs):
     word_rows = WORD_SLOT
-    section = where_ref[0]
-    me = where_ref[2]
+    section, me = position()
     own = near_ref[:word_rows].astype(f32)
     other = section_ref[:word_rows].astype(f32)
     halves = (jnp.where(section == 0, own, other), jnp.where(section == 0, other, own))
@@ -820,7 +857,7 @@
         w_shrink_ref,
     ) = outs
     at = 0
-    for ref in (project_ref, output_ref, expand_ref, shrink_ref):
+    for ref in (expand_ref, shrink_ref, project_ref, output_ref):
         size = ref.shape[0]
         for column in range(ref.shape[1] // SLAB):
             ref[:, column * SLAB : (column + 1) * SLAB] = char[at : at + size]
@@ -848,16 +885,13 @@
     w_gain_mlp_ref[...] = jnp.where(upper, turned[3:4], turned[2:3])
 
 
-def last_sum(where, near, arrived, shapes):
-    vmem = pl.BlockSpec(memory_space=pltpu.VMEM)
+def last_sum(near, arrived, shapes):
     return pl.pallas_call(
-        functools.partial(last_sum_kernel, shapes),
-        in_specs=[pl.BlockSpec(memory_space=pltpu.SMEM)] + [vmem] * 4,
-        out_specs=[vmem] * len(shapes),
+        last_sum_kernel,
         out_shape=[jax.ShapeDtypeStruct(shape, f32) for shape in shapes],
-        compiler_params=pltpu.CompilerParams(vmem_limit_bytes=VMEM_LIMIT),
+        compiler_params=pltpu.CompilerParams(vmem_limit_bytes=12 * MIB),
         name="last_sum",
-    )(where, near, *arrived)
+    )(near, *arrived)
 
 
 def exchange(value, section_bit, dp_bits):
@@ -873,45 +907,48 @@
 CORE, SIDE, NEAR, FAR = (1, 2, 4, 8)
 
 
+def plane_exchange(pieces):
+    return (pieces[0],) + tuple(
+        exchange(piece, 0, bits) for piece, bits in zip(pieces[1:], (SIDE, NEAR, SIDE | NEAR))
+    )
+
+
 def local_grouped(
     chars, counts, languages, language_table, char_weights, word_input, word_weights, cotangent
 ):
-    section = lax.axis_index("section")
-    me = lax.axis_index("dp")
     shards = lax.axis_size("dp")
     micros, _, words, slots, width = chars.shape
     rows = words * slots
-    where = jnp.stack([section, languages[section, 0], me]).astype(jnp.int32)
     cot = cotangent[:, 0]
-    cot_core = exchange(cot, 0, CORE)
-    cot_high = exchange(jnp.stack([cot, cot_core]), 0, FAR)
+    cot_far = exchange(cot, 0, FAR)
     char_weights = tuple(w[None] if w.ndim == 1 else w for w in char_weights)
     word_weights = tuple(w[None] if w.ndim == 1 else w for w in word_weights)
     chars = chars.reshape(micros, rows, width)
     counts = counts.reshape(micros, 1, words)
-    pooled, *stored = char_forward(where, chars, counts, language_table, char_weights, slots)
-    pooled_core = exchange(pooled, 0, CORE)
-    pair = jnp.concatenate([pooled, pooled_core])
-    others = (exchange(pair, 0, FAR), exchange(pair, 1, 0), exchange(pair, 1, FAR))
-    result, dpooled, *pieces = word_group(
-        where,
-        (pooled, pooled_core) + others,
-        (cot, cot_core, cot_high),
-        word_input,
-        word_weights,
+    pooled, *stored = char_forward(languages, chars, counts, language_table, char_weights, slots)
+    others = (exchange(pooled, 0, FAR), exchange(pooled, 1, 0), exchange(pooled, 1, FAR))
+    result, dpooled, keep, send = word_group(
+        (pooled,) + others, (cot, cot_far), word_input, word_weights, shards
+    )
+    word = (keep, exchange(send, 0, CORE))
+    dmiddle, gain_mlp_grad, keep, send = char_mlp_back(
+        counts, char_weights, dpooled, stored, slots, shards
+    )
+    first = plane_exchange(core_sum(word, (keep, exchange(send, 0, CORE))))
+    chars_grad, keep, send = char_attn_back(
+        languages,
+        chars,
+        language_table,
+        char_weights,
+        dmiddle,
+        gain_mlp_grad,
+        stored,
+        slots,
         shards,
-    )
-    word = (pieces[0],) + tuple(
-        exchange(piece, 0, bits) for piece, bits in zip(pieces[1:], (SIDE, NEAR, SIDE | NEAR))
-    )
-    chars_grad, keep, send = char_backward(
-        where, chars, counts, language_table, char_weights, dpooled, stored, slots, shards
-    )
-    pieces = core_sum(keep, exchange(send, 0, CORE))
-    char = (pieces[0],) + tuple(
-        exchange(piece, 0, bits) for piece, bits in zip(pieces[1:], (SIDE, NEAR, SIDE | NEAR))
-    )
-    near, far = plane_sum(word, char)
+        first[0],
+    )
+    second = plane_exchange(core_sum((keep, exchange(send, 0, CORE)), after=first[1:]))
+    near, far = plane_sum(first, second)
     arrived = (exchange(near, 1, 0), exchange(far, 0, FAR), exchange(far, 1, FAR))
     shapes = [(language_table.shape[0], language_table.shape[1] // shards)]
     for weight in char_weights + (word_input,) + word_weights:
@@ -919,7 +956,7 @@
             shapes.append((1, weight.shape[1] // shards))
         else:
             shapes.append((weight.shape[0] // shards, weight.shape[1]))
-    totals = last_sum(where, near, arrived, shapes)
+    totals = last_sum(near, arrived, shapes)
     totals = [total[0] if total.shape[0] == 1 else total for total in totals]
     return (result[None, None], chars_grad.reshape((1, 1, words, slots, width))) + tuple(totals)
 

time: 120 us -> 79.9 us (0.67)
  Pallas kernels: 57.7 us -> 34.2 us
  waiting for transfers between devices: 34.2 us -> 22.9 us
  local copies, waits for them, and re-layouts: 5.17 us -> 0.82 us
  other arithmetic: 1.29 us -> 0 us
    pallas_call x5 -> x7, Pallas kernels: 36.8 us -> 23.9 us  [the longest x1 9.84 us: char_forward(): pl.pallas_call(functools.partial(char_forward_kernel, slots), in_specs=[p...]
    ppermute x16, waiting for transfers between devices: 34.2 us -> 22.9 us  [exchange(): return lax.ppermute(value, ('section', 'dp'), pairs)]
    pallas_call x1, Pallas kernels: 20.9 us -> 10.3 us  [word_group(): pl.pallas_call(functools.partial(word_kernel, length, shards), in_specs=[...]
    unnamed x43 -> x31, local copies, waits for them, and re-layouts: 4.58 us -> 0.82 us
    another operation x2 -> x0, other arithmetic: 1.29 us -> none  [the longest x1 1.26 us: local_grouped(): where = jnp.stack([section, languages[section, 0], me]).astype(jnp.int32)]
  transfers between devices with their start and end apart: 16 -> 16, of which waited for: 7 -> 10; matrix products, arithmetic and copies ran while one was open for 2% -> 1% of each run, Pallas kernels for 13% -> 28%
where the time goes in v3:
time: 79.9 us; the launch traced here: 79.7 us
  Pallas kernels  34.2 us (43%)
  waiting for transfers between devices  22.9 us (29%)
  starting transfers between devices  20.9 us (26%)
  between operations  0.89 us (1%)
  local copies, waits for them, and re-layouts  0.82 us (1%)
    ppermute x16, waiting for transfers between devices, exchange(): return lax.ppermute(value, ('section', 'dp'), pairs)  22.9 us
    ppermute x16, starting transfers between devices, exchange(): return lax.ppermute(value, ('section', 'dp'), pairs)  20.9 us
    pallas_call x1, Pallas kernels, word_group(): pl.pallas_call(functools.partial(word_kernel, length, shards), in_specs=[...  10.3 us
    pallas_call x1, Pallas kernels, char_forward(): pl.pallas_call(functools.partial(char_forward_kernel, slots), in_specs=[p...  9.84 us
    pallas_call x1, Pallas kernels, char_attn_back(): pl.pallas_call(functools.partial(char_attn_back_kernel, slots, shards), i...  8.61 us
    pallas_call x1, Pallas kernels, char_mlp_back(): pl.pallas_call(functools.partial(char_mlp_back_kernel, slots, shards), in...  3.81 us
  transfers between devices with their start and end apart: 16, of which 10 were waited for; matrix products, arithmetic and copies ran while one was open for 1% of the time, Pallas kernels for 28%

profile of v3, /device:TPU:0, one launch (start us, length us, event | category | flops | bytes accessed | tf_op | source)
XLA Modules:
  0.0 79.7 jit_solution(14838036302616487320)
XLA Ops:
  0.6 4.1 %collective-permute-start.3 = (bf16[2,64,512]{2,1,0:T(8,128)(2,1)}, bf16[2,64,512]{2,1,0:T(8,128)(2,1)S(1)}, u32[]{:S(2)}, u32[]{:S(2)}) collective-permute-start(bf16[2,64,512]{2,1,0:T(8,128)(2,1)} %bitcast.12), channel_id=1, source_target_pairs={{0,8},{1,9},{2,10},{3,11},{4,12},{5,13},{6,14},{7,15},{8,0},{9,1},... | collective-permute-start | bytes 393224 | tf_op jit(solution)/shard_map/ppermute | solution.py:904
  4.7 0.7 copy.34.languages_ref
  5.5 0.0 copy-start.7
  5.5 0.0 copy-start.8
  5.5 0.0 copy-start.11
  5.5 0.0 copy-start.12
  5.5 9.8 %char_forward.1 = (bf16[64,256]{1,0:T(8,128)(2,1)S(1)}, bf16[64,1024]{1,0:T(8,128)(2,1)S(1)}, bf16[1024,768]{1,0:T(8,128)(2,1)S(1)}, f32[64,1024]{1,0:T(8,128)S(...) custom-call(s32[2,1]{1,0:T(2,128)S(1)} %copy.34.languages_ref, ...), custom_call_target="tpu_custom_call" | custom-call | flops 4294967296 | bytes 8388608 | tf_op jit(solution)/shard_map/char_forward/pallas_call | solution.py:292
  15.4 1.3 %collective-permute-start.2 = (bf16[64,256]{1,0:T(8,128)(2,1)S(1)}, bf16[64,256]{1,0:T(8,128)(2,1)S(1)}, u32[]{:S(2)}, u32[]{:S(2)}) collective-permute-start(bf16[64,256]{1,0:T(8,128)(2,1)S(1)} %get-tuple-element.58.own_ref), channel_id=1, source_target_pairs={{0,24},{1,25},{2,26},{3,27},{4,28},{5,29},{6,30},{7,31},{8,16},{9,... | collective-permute-start | bytes 98312 | tf_op jit(solution)/shard_map/ppermute | solution.py:904
  16.7 0.3 collective-permute-start.1
  17.0 2.8 %collective-permute-start = (bf16[64,256]{1,0:T(8,128)(2,1)S(1)}, bf16[64,256]{1,0:T(8,128)(2,1)S(1)}, u32[]{:S(2)}, u32[]{:S(2)}) collective-permute-start(bf16[64,256]{1,0:T(8,128)(2,1)S(1)} %get-tuple-element.58.own_ref), channel_id=1, source_target_pairs={{0,8},{1,9},{2,10},{3,11},{4,12},{5,13},{6,14},{7,15},{8,0},{9,1},... | collective-permute-start | bytes 98312 | tf_op jit(solution)/shard_map/ppermute | solution.py:904
  19.9 1.6 %collective-permute-done.2.both_ref = bf16[64,256]{1,0:T(8,128)(2,1)S(1)} collective-permute-done((bf16[64,256]{1,0:T(8,128)(2,1)S(1)}, bf16[64,256]{1,0:T(8,128)(2,1)S(1)}, u32[]{:S(2)}, u32[]{:S(2)}) %collective-permute-start.2) | collective-permute-done | bytes 32800 | tf_op jit(solution)/shard_map/ppermute | solution.py:904
  21.5 0.0 collective-permute-done.1.section_ref
  21.5 0.4 collective-permute-done.far_ref
  21.9 0.0 collective-permute-done.3.cot_far_ref
  21.9 0.0 copy-done
  21.9 0.0 copy-done.1
  21.9 0.0 copy-done.2
  21.9 0.0 copy-done.3
  21.9 0.0 copy-done.7
  21.9 0.0 copy-done.8
  21.9 0.0 copy-done.11
  21.9 0.0 copy-start.4
  22.0 0.0 copy-start.5
  22.0 0.0 copy-start.13
  22.0 10.3 %word_group.1 = (f32[64,512]{1,0:T(8,128)}, bf16[64,256]{1,0:T(8,128)(2,1)S(1)}, bf16[4,416,256]{2,1,0:T(8,128)(2,1)S(1)}, bf16[4,416,256]{2,1,0:T(8,128)(2,1)S(1)}) custom-call(bf16[64,256]{1,0:T(8,128)(2,1)S(1)} %get-tuple-element.58.own_ref, bf16[64,256]{1,0:T(8,128)(2,1)S(1)} %collective-permute-done.far_ref, ...), custom_call_target="tpu_custom_call" | custom-call | flops 6710886400 | bytes 8388608 | tf_op jit(solution)/shard_map/word_group/pallas_call | solution.py:731
  32.3 0.1 collective-permute-start.4
  32.4 0.0 copy-done.4
  32.4 0.0 copy-done.5
  32.4 0.0 copy-done.13
  32.4 3.8 %char_mlp_back.1 = (f32[1024,256]{1,0:T(8,128)S(1)}, f32[8,256]{1,0:T(8,128)S(1)}, bf16[8,128,256]{2,1,0:T(8,128)(2,1)S(1)}, bf16[8,128,256]{2,1,0:T(8,128)(2,1)S(1)}) custom-call(s32[2,1,64]{2,1,0:T(1,128)} %counts_hbm.3, f32[1,256]{1,0:T(1,128)S(1)} %bitcast.17, bf16[256,1024]{1,0:T(8,128)(2,1)S(1)} %copy-done.4, bf16[1024,256]{1,0:T(8,128)(2,1)S(1)} %copy-done.5, ...), custom_call_target="tpu_custom_call" | custom-call | flops 4294967296 | bytes 8388608 | tf_op jit(solution)/shard_map/char_mlp_back/pallas_call | solution.py:413
  36.2 0.0 copy-start.6
  36.3 0.0 copy-start.9
  36.3 0.0 copy-start.10
  36.3 0.0 copy-start.14
  36.3 0.5 collective-permute-start.5
  36.8 1.5 %collective-permute-done.5.refs_3_ = bf16[8,128,256]{2,1,0:T(8,128)(2,1)S(1)} collective-permute-done((bf16[8,128,256]{2,1,0:T(8,128)(2,1)S(1)}, bf16[8,128,256]{2,1,0:T(8,128)(2,1)S(1)}, u32[]{:S(2)}, u32[]{:S(2)}) %collective-permute-start.5) | collective-permute-done | bytes 524320 | tf_op jit(solution)/shard_map/ppermute | solution.py:904
  38.4 0.0 collective-permute-done.4.refs_1_
  38.4 0.3 core_sum.2
  38.7 2.1 %collective-permute-start.6 = (bf16[672,256]{1,0:T(8,128)(2,1)S(1)}, bf16[672,256]{1,0:T(8,128)(2,1)S(1)}, u32[]{:S(2)}, u32[]{:S(2)}) collective-permute-start(bf16[672,256]{1,0:T(8,128)(2,1)S(1)} %get-tuple-element.75), channel_id=1, source_target_pairs={{0,2},{1,3},{2,0},{3,1},{4,6},{5,7},{6,4},{7,5},{8,10},{9,11},{10,... | collective-permute-start | bytes 1032200 | tf_op jit(solution)/shard_map/ppermute | solution.py:904
  40.8 1.2 %collective-permute-start.7 = (bf16[672,256]{1,0:T(8,128)(2,1)S(1)}, bf16[672,256]{1,0:T(8,128)(2,1)S(1)}, u32[]{:S(2)}, u32[]{:S(2)}) collective-permute-start(bf16[672,256]{1,0:T(8,128)(2,1)S(1)} %get-tuple-element.76), channel_id=1, source_target_pairs={{0,4},{1,5},{2,6},{3,7},{4,0},{5,1},{6,2},{7,3},{8,12},{9,13},{10,... | collective-permute-start | bytes 1032200 | tf_op jit(solution)/shard_map/ppermute | solution.py:904
  42.1 0.3 collective-permute-start.8
  42.4 0.0 copy-done.6
  42.4 0.0 copy-done.10
  42.4 8.6 %char_attn_back.1 = (f32[1024,256]{1,0:T(8,128)}, bf16[8,80,256]{2,1,0:T(8,128)(2,1)S(1)}, bf16[8,80,256]{2,1,0:T(8,128)(2,1)S(1)}) custom-call(s32[2,1]{1,0:T(2,128)S(1)} %copy.34.languages_ref, bf16[672,256]{1,0:T(8,128)(2,1)S(1)} %get-tuple-element.68._.refs_0_, bf16[2,1024,256]{2,1,0:T(8,128)(2,1)} %bitcast.21, bf16[8,256]{1,0:T(8,128)(2,1)S(1)} %copy-done.10, ...), custom_call_target="tpu_custom_call" | custom-call | flops 4294967296 | bytes 8388608 | tf_op jit(solution)/shard_map/char_attn_back/pallas_call | solution.py:513
  51.0 0.1 collective-permute-start.9
  51.1 1.6 %collective-permute-done.9.refs_1_ = bf16[8,80,256]{2,1,0:T(8,128)(2,1)S(1)} collective-permute-done((bf16[8,80,256]{2,1,0:T(8,128)(2,1)S(1)}, bf16[8,80,256]{2,1,0:T(8,128)(2,1)S(1)}, u32[]{:S(2)}, u32[]{:S(2)}) %collective-permute-start.9) | collective-permute-done | bytes 327712 | tf_op jit(solution)/shard_map/ppermute | solution.py:904
  52.7 0.0 collective-permute-done.6.refs_2_.refs_1_
  52.7 0.0 collective-permute-done.7.refs_3_.refs_2_
  52.7 5.3 %collective-permute-done.8.refs_4_.refs_3_ = bf16[672,256]{1,0:T(8,128)(2,1)S(1)} collective-permute-done((bf16[672,256]{1,0:T(8,128)(2,1)S(1)}, bf16[672,256]{1,0:T(8,128)(2,1)S(1)}, u32[]{:S(2)}, u32[]{:S(2)}) %collective-permute-start.8) | collective-permute-done | bytes 344096 | tf_op jit(solution)/shard_map/ppermute | solution.py:904
  58.1 0.1 core_sum.3
  58.1 1.7 %collective-permute-start.10 = (bf16[160,256]{1,0:T(8,128)(2,1)S(1)}, bf16[160,256]{1,0:T(8,128)(2,1)S(1)}, u32[]{:S(2)}, u32[]{:S(2)}) collective-permute-start(bf16[160,256]{1,0:T(8,128)(2,1)S(1)} %get-tuple-element.81), channel_id=1, source_target_pairs={{0,2},{1,3},{2,0},{3,1},{4,6},{5,7},{6,4},{7,5},{8,10},{9,11},{10,... | collective-permute-start | bytes 245768 | tf_op jit(solution)/shard_map/ppermute | solution.py:904
  59.9 1.2 %collective-permute-start.11 = (bf16[160,256]{1,0:T(8,128)(2,1)S(1)}, bf16[160,256]{1,0:T(8,128)(2,1)S(1)}, u32[]{:S(2)}, u32[]{:S(2)}) collective-permute-start(bf16[160,256]{1,0:T(8,128)(2,1)S(1)} %get-tuple-element.82), channel_id=1, source_target_pairs={{0,4},{1,5},{2,6},{3,7},{4,0},{5,1},{6,2},{7,3},{8,12},{9,13},{10,... | collective-permute-start | bytes 245768 | tf_op jit(solution)/shard_map/ppermute | solution.py:904
  61.1 0.6 collective-permute-start.12
  61.7 1.0 %collective-permute-done.10.refs_5_ = bf16[160,256]{1,0:T(8,128)(2,1)S(1)} collective-permute-done((bf16[160,256]{1,0:T(8,128)(2,1)S(1)}, bf16[160,256]{1,0:T(8,128)(2,1)S(1)}, u32[]{:S(2)}, u32[]{:S(2)}) %collective-permute-start.10) | collective-permute-done | bytes 81952 | tf_op jit(solution)/shard_map/ppermute | solution.py:904
  62.7 1.6 %collective-permute-done.11.refs_6_ = bf16[160,256]{1,0:T(8,128)(2,1)S(1)} collective-permute-done((bf16[160,256]{1,0:T(8,128)(2,1)S(1)}, bf16[160,256]{1,0:T(8,128)(2,1)S(1)}, u32[]{:S(2)}, u32[]{:S(2)}) %collective-permute-start.11) | collective-permute-done | bytes 81952 | tf_op jit(solution)/shard_map/ppermute | solution.py:904
  64.3 2.1 %collective-permute-done.12.refs_7_ = bf16[160,256]{1,0:T(8,128)(2,1)S(1)} collective-permute-done((bf16[160,256]{1,0:T(8,128)(2,1)S(1)}, bf16[160,256]{1,0:T(8,128)(2,1)S(1)}, u32[]{:S(2)}, u32[]{:S(2)}) %collective-permute-start.12) | collective-permute-done | bytes 81952 | tf_op jit(solution)/shard_map/ppermute | solution.py:904
  66.5 0.2 plane_sum.1
  66.7 1.6 %collective-permute-start.13 = (bf16[624,256]{1,0:T(8,128)(2,1)S(1)}, bf16[624,256]{1,0:T(8,128)(2,1)S(1)}, u32[]{:S(2)}, u32[]{:S(2)}) collective-permute-start(bf16[624,256]{1,0:T(8,128)(2,1)S(1)} %get-tuple-element.84.near_ref), channel_id=1, source_target_pairs={{0,16},{1,17},{2,18},{3,19},{4,20},{5,21},{6,22},{7,23},{8,24},{9,... | collective-permute-start | bytes 958472 | tf_op jit(solution)/shard_map/ppermute | solution.py:904
  68.2 2.8 %collective-permute-start.15 = (bf16[208,256]{1,0:T(8,128)(2,1)S(1)}, bf16[208,256]{1,0:T(8,128)(2,1)S(1)}, u32[]{:S(2)}, u32[]{:S(2)}) collective-permute-start(bf16[208,256]{1,0:T(8,128)(2,1)S(1)} %get-tuple-element.85), channel_id=1, source_target_pairs={{0,24},{1,25},{2,26},{3,27},{4,28},{5,29},{6,30},{7,31},{8,16},{9,... | collective-permute-start | bytes 319496 | tf_op jit(solution)/shard_map/ppermute | solution.py:904
  71.0 0.1 collective-permute-start.14
  71.1 6.9 %collective-permute-done.15.both_ref = bf16[208,256]{1,0:T(8,128)(2,1)S(1)} collective-permute-done((bf16[208,256]{1,0:T(8,128)(2,1)S(1)}, bf16[208,256]{1,0:T(8,128)(2,1)S(1)}, u32[]{:S(2)}, u32[]{:S(2)}) %collective-permute-start.15) | collective-permute-done | bytes 106528 | tf_op jit(solution)/shard_map/ppermute | solution.py:904
  78.0 0.7 collective-permute-done.14.high_ref
  78.7 0.0 collective-permute-done.13.section_ref
  78.7 1.0 %last_sum.1 = (f32[8,16]{1,0:T(8,128)}, f32[1,16]{1,0:T(1,128)}, f32[16,768]{1,0:T(8,128)}, f32[16,256]{1,0:T(8,128)}, f32[1,16]{1,0:T(1,128)}, /*index=5*/f32[1...) custom-call(bf16[624,256]{1,0:T(8,128)(2,1)S(1)} %get-tuple-element., ...), custom_call_target="tpu_custom_call" | custom-call | tf_op jit(solution)/shard_map/last_sum/pallas_call | solution.py:889
  (7 shorter events, 0.0 us)
Async XLA Ops:
  0.6 21.2 %collective-permute-start.3 = (bf16[2,64,512]{2,1,0:T(8,128)(2,1)}, bf16[2,64,512]{2,1,0:T(8,128)(2,1)S(1)}, u32[]{:S(2)}, u32[]{:S(2)}) collective-permute-start(bf16[2,64,512]{2,1,0:T(8,128)(2,1)} %bitcast.12), channel_id=1, source_target_pairs={{0,8},{1,9},{2,10},{3,11},{4,12},{5,13},{6,14},{7,15},{8,0},{9,1},... | collective-permute-start | bytes 393224 | tf_op jit(solution)/shard_map/ppermute | solution.py:904
  5.5 16.4 %copy-start = (bf16[512,2048]{1,0:T(8,128)(2,1)S(1)}, bf16[512,2048]{1,0:T(8,128)(2,1)}, u32[]{:S(2)}) copy-start(bf16[512,2048]{1,0:T(8,128)(2,1)} %expand_ref.2) | copy-start | bytes 6291460
  5.5 16.4 %copy-start.1 = (bf16[2048,512]{1,0:T(8,128)(2,1)S(1)}, bf16[2048,512]{1,0:T(8,128)(2,1)}, u32[]{:S(2)}) copy-start(bf16[2048,512]{1,0:T(8,128)(2,1)} %shrink_ref.2) | copy-start | bytes 6291460
  5.5 16.4 %copy-start.2 = (bf16[512,1536]{1,0:T(8,128)(2,1)S(1)}, bf16[512,1536]{1,0:T(8,128)(2,1)}, u32[]{:S(2)}) copy-start(bf16[512,1536]{1,0:T(8,128)(2,1)} %project_ref.2) | copy-start | bytes 4718596
  5.5 16.4 %copy-start.3 = (bf16[512,512]{1,0:T(8,128)(2,1)S(1)}, bf16[512,512]{1,0:T(8,128)(2,1)}, u32[]{:S(2)}) copy-start(bf16[512,512]{1,0:T(8,128)(2,1)} %output_ref.2) | copy-start | bytes 1572868
  5.5 16.4 %copy-start.7 = (bf16[256,512]{1,0:T(8,128)(2,1)S(1)}, bf16[256,512]{1,0:T(8,128)(2,1)}, u32[]{:S(2)}) copy-start(bf16[256,512]{1,0:T(8,128)(2,1)} %input_ref.1) | copy-start | bytes 786436
  5.5 16.4 %copy-start.8 = (bf16[2,1,64,512]{3,2,1,0:T(8,128)(2,1)S(1)}, bf16[2,1,64,512]{3,2,1,0:T(8,128)(2,1)}, u32[]{:S(2)}) copy-start(bf16[2,1,64,512]{3,2,1,0:T(8,128)(2,1)} %param.35) | copy-start | bytes 393220
  5.5 16.4 %copy-start.11 = (f32[512]{0:T(512)S(1)}, f32[512]{0:T(512)}, u32[]{:S(2)}) copy-start(f32[512]{0:T(512)} %param.29) | copy-start | bytes 6148
  5.5 16.4 %copy-start.12 = (f32[512]{0:T(512)S(1)}, f32[512]{0:T(512)}, u32[]{:S(2)}) copy-start(f32[512]{0:T(512)} %param.32) | copy-start | bytes 6148
  15.4 6.1 %collective-permute-start.2 = (bf16[64,256]{1,0:T(8,128)(2,1)S(1)}, bf16[64,256]{1,0:T(8,128)(2,1)S(1)}, u32[]{:S(2)}, u32[]{:S(2)}) collective-permute-start(bf16[64,256]{1,0:T(8,128)(2,1)S(1)} %get-tuple-element.58.own_ref), channel_id=1, source_target_pairs={{0,24},{1,25},{2,26},{3,27},{4,28},{5,29},{6,30},{7,31},{8,16},{9,... | collective-permute-start | bytes 98312 | tf_op jit(solution)/shard_map/ppermute | solution.py:904
  16.7 4.8 %collective-permute-start.1 = (bf16[64,256]{1,0:T(8,128)(2,1)S(1)}, bf16[64,256]{1,0:T(8,128)(2,1)S(1)}, u32[]{:S(2)}, u32[]{:S(2)}) collective-permute-start(bf16[64,256]{1,0:T(8,128)(2,1)S(1)} %get-tuple-element.58.own_ref), channel_id=1, source_target_pairs={{0,16},{1,17},{2,18},{3,19},{4,20},{5,21},{6,22},{7,23},{8,24},{9,... | collective-permute-start | bytes 98312 | tf_op jit(solution)/shard_map/ppermute | solution.py:904
  17.0 4.8 %collective-permute-start = (bf16[64,256]{1,0:T(8,128)(2,1)S(1)}, bf16[64,256]{1,0:T(8,128)(2,1)S(1)}, u32[]{:S(2)}, u32[]{:S(2)}) collective-permute-start(bf16[64,256]{1,0:T(8,128)(2,1)S(1)} %get-tuple-element.58.own_ref), channel_id=1, source_target_pairs={{0,8},{1,9},{2,10},{3,11},{4,12},{5,13},{6,14},{7,15},{8,0},{9,1},... | collective-permute-start | bytes 98312 | tf_op jit(solution)/shard_map/ppermute | solution.py:904
  21.9 10.5 %copy-start.4 = (bf16[256,1024]{1,0:T(8,128)(2,1)S(1)}, bf16[256,1024]{1,0:T(8,128)(2,1)}, u32[]{:S(2)}) copy-start(bf16[256,1024]{1,0:T(8,128)(2,1)} %expand_ref.3) | copy-start | bytes 1572868
  22.0 10.5 %copy-start.5 = (bf16[1024,256]{1,0:T(8,128)(2,1)S(1)}, bf16[1024,256]{1,0:T(8,128)(2,1)}, u32[]{:S(2)}) copy-start(bf16[1024,256]{1,0:T(8,128)(2,1)} %shrink_ref.3) | copy-start | bytes 1572868
  22.0 10.4 %copy-start.13 = (f32[256]{0:T(256)S(1)}, f32[256]{0:T(256)}, u32[]{:S(2)}) copy-start(f32[256]{0:T(256)} %param.25) | copy-start | bytes 3076
  32.3 6.1 %collective-permute-start.4 = (bf16[4,416,256]{2,1,0:T(8,128)(2,1)S(1)}, bf16[4,416,256]{2,1,0:T(8,128)(2,1)S(1)}, u32[]{:S(2)}, u32[]{:S(2)}) collective-permute-start(bf16[4,416,256]{2,1,0:T(8,128)(2,1)S(1)} %get-tuple-element.61), channel_id=1, source_target_pairs={{0,1},{1,0},{2,3},{3,2},{4,5},{5,4},{6,7},{7,6},{8,9},{9,8},{10,11... | collective-permute-start | bytes 2555912 | tf_op jit(solution)/shard_map/ppermute | solution.py:904
  36.2 6.1 %copy-start.6 = (bf16[256,768]{1,0:T(8,128)(2,1)S(1)}, bf16[256,768]{1,0:T(8,128)(2,1)}, u32[]{:S(2)}) copy-start(bf16[256,768]{1,0:T(8,128)(2,1)} %project_ref.3) | copy-start | bytes 1179652
  36.3 6.1 %copy-start.9 = (bf16[256,256]{1,0:T(8,128)(2,1)S(1)}, bf16[256,256]{1,0:T(8,128)(2,1)}, u32[]{:S(2)}) copy-start(bf16[256,256]{1,0:T(8,128)(2,1)} %output_ref.3) | copy-start | bytes 393220
  36.3 6.1 %copy-start.10 = (bf16[8,256]{1,0:T(8,128)(2,1)S(1)}, bf16[8,256]{1,0:T(8,128)(2,1)}, u32[]{:S(2)}) copy-start(bf16[8,256]{1,0:T(8,128)(2,1)} %table_ref.1) | copy-start | bytes 12292
  36.3 6.1 %copy-start.14 = (f32[256]{0:T(256)S(1)}, f32[256]{0:T(256)}, u32[]{:S(2)}) copy-start(f32[256]{0:T(256)} %param.22) | copy-start | bytes 3076
  36.3 2.1 %collective-permute-start.5 = (bf16[8,128,256]{2,1,0:T(8,128)(2,1)S(1)}, bf16[8,128,256]{2,1,0:T(8,128)(2,1)S(1)}, u32[]{:S(2)}, u32[]{:S(2)}) collective-permute-start(bf16[8,128,256]{2,1,0:T(8,128)(2,1)S(1)} %get-tuple-element.67), channel_id=1, source_target_pairs={{0,1},{1,0},{2,3},{3,2},{4,5},{5,4},{6,7},{7,6},{8,9},{9,8},{10,11... | collective-permute-start | bytes 1572872 | tf_op jit(solution)/shard_map/ppermute | solution.py:904
  38.7 14.0 %collective-permute-start.6 = (bf16[672,256]{1,0:T(8,128)(2,1)S(1)}, bf16[672,256]{1,0:T(8,128)(2,1)S(1)}, u32[]{:S(2)}, u32[]{:S(2)}) collective-permute-start(bf16[672,256]{1,0:T(8,128)(2,1)S(1)} %get-tuple-element.75), channel_id=1, source_target_pairs={{0,2},{1,3},{2,0},{3,1},{4,6},{5,7},{6,4},{7,5},{8,10},{9,11},{10,... | collective-permute-start | bytes 1032200 | tf_op jit(solution)/shard_map/ppermute | solution.py:904
  40.8 11.9 %collective-permute-start.7 = (bf16[672,256]{1,0:T(8,128)(2,1)S(1)}, bf16[672,256]{1,0:T(8,128)(2,1)S(1)}, u32[]{:S(2)}, u32[]{:S(2)}) collective-permute-start(bf16[672,256]{1,0:T(8,128)(2,1)S(1)} %get-tuple-element.76), channel_id=1, source_target_pairs={{0,4},{1,5},{2,6},{3,7},{4,0},{5,1},{6,2},{7,3},{8,12},{9,13},{10,... | collective-permute-start | bytes 1032200 | tf_op jit(solution)/shard_map/ppermute | solution.py:904
  42.1 16.0 %collective-permute-start.8 = (bf16[672,256]{1,0:T(8,128)(2,1)S(1)}, bf16[672,256]{1,0:T(8,128)(2,1)S(1)}, u32[]{:S(2)}, u32[]{:S(2)}) collective-permute-start(bf16[672,256]{1,0:T(8,128)(2,1)S(1)} %get-tuple-element.77), channel_id=1, source_target_pairs={{0,6},{1,7},{2,4},{3,5},{4,2},{5,3},{6,0},{7,1},{8,14},{9,15},{10,... | collective-permute-start | bytes 1032200 | tf_op jit(solution)/shard_map/ppermute | solution.py:904
  51.0 1.7 %collective-permute-start.9 = (bf16[8,80,256]{2,1,0:T(8,128)(2,1)S(1)}, bf16[8,80,256]{2,1,0:T(8,128)(2,1)S(1)}, u32[]{:S(2)}, u32[]{:S(2)}) collective-permute-start(bf16[8,80,256]{2,1,0:T(8,128)(2,1)S(1)} %get-tuple-element.79), channel_id=1, source_target_pairs={{0,1},{1,0},{2,3},{3,2},{4,5},{5,4},{6,7},{7,6},{8,9},{9,8},{10,11... | collective-permute-start | bytes 983048 | tf_op jit(solution)/shard_map/ppermute | solution.py:904
  58.1 4.6 %collective-permute-start.10 = (bf16[160,256]{1,0:T(8,128)(2,1)S(1)}, bf16[160,256]{1,0:T(8,128)(2,1)S(1)}, u32[]{:S(2)}, u32[]{:S(2)}) collective-permute-start(bf16[160,256]{1,0:T(8,128)(2,1)S(1)} %get-tuple-element.81), channel_id=1, source_target_pairs={{0,2},{1,3},{2,0},{3,1},{4,6},{5,7},{6,4},{7,5},{8,10},{9,11},{10,... | collective-permute-start | bytes 245768 | tf_op jit(solution)/shard_map/ppermute | solution.py:904
  59.9 4.4 %collective-permute-start.11 = (bf16[160,256]{1,0:T(8,128)(2,1)S(1)}, bf16[160,256]{1,0:T(8,128)(2,1)S(1)}, u32[]{:S(2)}, u32[]{:S(2)}) collective-permute-start(bf16[160,256]{1,0:T(8,128)(2,1)S(1)} %get-tuple-element.82), channel_id=1, source_target_pairs={{0,4},{1,5},{2,6},{3,7},{4,0},{5,1},{6,2},{7,3},{8,12},{9,13},{10,... | collective-permute-start | bytes 245768 | tf_op jit(solution)/shard_map/ppermute | solution.py:904
  61.1 5.3 %collective-permute-start.12 = (bf16[160,256]{1,0:T(8,128)(2,1)S(1)}, bf16[160,256]{1,0:T(8,128)(2,1)S(1)}, u32[]{:S(2)}, u32[]{:S(2)}) collective-permute-start(bf16[160,256]{1,0:T(8,128)(2,1)S(1)} %get-tuple-element.83), channel_id=1, source_target_pairs={{0,6},{1,7},{2,4},{3,5},{4,2},{5,3},{6,0},{7,1},{8,14},{9,15},{10,... | collective-permute-start | bytes 245768 | tf_op jit(solution)/shard_map/ppermute | solution.py:904
  66.7 12.0 %collective-permute-start.13 = (bf16[624,256]{1,0:T(8,128)(2,1)S(1)}, bf16[624,256]{1,0:T(8,128)(2,1)S(1)}, u32[]{:S(2)}, u32[]{:S(2)}) collective-permute-start(bf16[624,256]{1,0:T(8,128)(2,1)S(1)} %get-tuple-element.84.near_ref), channel_id=1, source_target_pairs={{0,16},{1,17},{2,18},{3,19},{4,20},{5,21},{6,22},{7,23},{8,24},{9,... | collective-permute-start | bytes 958472 | tf_op jit(solution)/shard_map/ppermute | solution.py:904
  68.2 9.8 %collective-permute-start.15 = (bf16[208,256]{1,0:T(8,128)(2,1)S(1)}, bf16[208,256]{1,0:T(8,128)(2,1)S(1)}, u32[]{:S(2)}, u32[]{:S(2)}) collective-permute-start(bf16[208,256]{1,0:T(8,128)(2,1)S(1)} %get-tuple-element.85), channel_id=1, source_target_pairs={{0,24},{1,25},{2,26},{3,27},{4,28},{5,29},{6,30},{7,31},{8,16},{9,... | collective-permute-start | bytes 319496 | tf_op jit(solution)/shard_map/ppermute | solution.py:904
  71.0 7.7 %collective-permute-start.14 = (bf16[208,256]{1,0:T(8,128)(2,1)S(1)}, bf16[208,256]{1,0:T(8,128)(2,1)S(1)}, u32[]{:S(2)}, u32[]{:S(2)}) collective-permute-start(bf16[208,256]{1,0:T(8,128)(2,1)S(1)} %get-tuple-element.85), channel_id=1, source_target_pairs={{0,8},{1,9},{2,10},{3,11},{4,12},{5,13},{6,14},{7,15},{8,0},{9,1},... | collective-permute-start | bytes 319496 | tf_op jit(solution)/shard_map/ppermute | solution.py:904

commit v4 on v3

--- a/solution.py
+++ b/solution.py
@@ -11,6 +11,7 @@
 H = 8
 HEAD = 64
 SLAB = 256
+HEADS = SLAB // HEAD
 BLOCK = 128
 MIB = 1024 * 1024
 
@@ -40,30 +41,10 @@
     return lax.broadcasted_iota(jnp.int32, shape, 0)
 
 
-def flip(a):
-    size = a.shape[1]
-    width = min(size, 256)
-    eye = jnp.where(rows_of((width, width)) == lanes((width, width)), 1.0, 0.0).astype(bf16)
-    return jnp.concatenate(
-        [dot_nt(eye, a[:, at : at + width]).astype(bf16) for at in range(0, size, width)], axis=0
-    )
-
-
-def head_mask(head):
-    return jnp.where(lanes((1, SLAB)) // HEAD == head, 1.0, 0.0).astype(bf16)
-
-
 def stack_heads(a):
-    return jnp.concatenate([a * head_mask(head) for head in range(SLAB // HEAD)], axis=0)
-
-
-def merge_heads(a):
-    rows = a.shape[0] // (SLAB // HEAD)
-    head = lanes((rows, SLAB)) // HEAD
-    total = a[:rows]
-    for place in range(1, SLAB // HEAD):
-        total = jnp.where(head == place, a[place * rows : (place + 1) * rows], total)
-    return total
+    head = lanes((1, SLAB)) // HEAD
+    masks = [jnp.where(head == place, 1.0, 0.0).astype(bf16) for place in range(HEADS)]
+    return jnp.concatenate([a * mask for mask in masks], axis=0)
 
 
 def compact(scores, length):
@@ -74,6 +55,12 @@
     return total
 
 
+def compact_heads(scores, length):
+    return [
+        compact(scores[:, head * BLOCK : (head + 1) * BLOCK], length) for head in range(HEADS)
+    ]
+
+
 def expand(values, length):
     group = lanes((length, BLOCK)) // length
     return jnp.concatenate(
@@ -81,42 +68,57 @@
     ).astype(bf16)
 
 
-def attend(q, k, v, key_mask, length):
-    heads = SLAB // HEAD
-    scores = dot_nt(stack_heads(k), q)
-    v_flipped = flip(v)
-    kept = []
+def expand_heads(values, tile, length):
+    first = tile * HEADS * BLOCK
+    return [
+        expand(values[:, first + head * BLOCK : first + (head + 1) * BLOCK], length)
+        for head in range(HEADS)
+    ]
+
+
+def head_rows(a, head):
+    return a[head * HEAD : (head + 1) * HEAD]
+
+
+def attend(load, tiles, key_mask, length):
+    scores = []
+    for tile in tiles:
+        scores += compact_heads(dot_nt(load(tile, 1), stack_heads(load(tile, 0))), length)
+    scores = jnp.concatenate(scores, axis=1) * HEAD**-0.5
+    scores = jnp.where(key_mask, scores, -1e30)
+    weights = jnp.exp(scores - jnp.max(scores, axis=0, keepdims=True))
+    probs = weights / jnp.sum(weights, axis=0, keepdims=True)
     mixed = []
-    for head in range(heads):
-        piece = compact(scores[head * BLOCK : (head + 1) * BLOCK], length) * HEAD**-0.5
-        piece = jnp.where(key_mask, piece, -1e30)
-        weights = jnp.exp(piece - jnp.max(piece, axis=0, keepdims=True))
-        probs = weights / jnp.sum(weights, axis=0, keepdims=True)
-        kept.append(probs)
-        mixed.append(dot(v_flipped[head * HEAD : (head + 1) * HEAD], expand(probs, length)))
-    return (kept, jnp.concatenate(mixed, axis=0).astype(bf16))
-
-
-def attend_back(q, k, v, probs, dmixed, length):
-    heads = SLAB // HEAD
-    dprobs = dot_nt(stack_heads(v), dmixed)
-    k_flipped = flip(k)
-    dq = []
-    dk = []
-    dv = []
-    for head in range(heads):
-        own = probs[head]
-        piece = compact(dprobs[head * BLOCK : (head + 1) * BLOCK], length)
-        delta = jnp.sum(own * piece, axis=0, keepdims=True)
-        dscores = expand(own * (piece - delta), length)
-        dq.append(dot(k_flipped[head * HEAD : (head + 1) * HEAD], dscores))
-        dk.append(dot(dscores, q))
-        dv.append(dot(expand(own, length), dmixed))
+    for number, tile in enumerate(tiles):
+        values = load(tile, 2).T
+        parts = expand_heads(probs, number, length)
+        mixed.append(
+            jnp.concatenate(
+                [dot(head_rows(values, head), parts[head]) for head in range(HEADS)], axis=0
+            ).astype(bf16)
+        )
+    return (probs, mixed)
+
+
+def attend_back(load, load_dmixed, tiles, probs, store, length):
+    dprobs = []
+    for number, tile in enumerate(tiles):
+        stacked = stack_heads(load_dmixed(tile))
+        dprobs += compact_heads(dot_nt(load(tile, 2), stacked), length)
+        parts = jnp.concatenate(expand_heads(probs, number, length), axis=1)
+        store(tile, 2, dot(parts, stacked).astype(bf16))
+    dprobs = jnp.concatenate(dprobs, axis=1)
+    dscores = probs * (dprobs - jnp.sum(probs * dprobs, axis=0, keepdims=True))
     scaling = HEAD**-0.5
-    dq = flip((jnp.concatenate(dq, axis=0) * scaling).astype(bf16))
-    dk = (merge_heads(jnp.concatenate(dk, axis=0)) * scaling).astype(bf16)
-    dv = merge_heads(jnp.concatenate(dv, axis=0)).astype(bf16)
-    return (dq, dk, dv)
+    for number, tile in enumerate(tiles):
+        parts = expand_heads(dscores, number, length)
+        keys = load(tile, 1).T
+        dq = jnp.concatenate(
+            [dot(head_rows(keys, head), parts[head]) for head in range(HEADS)], axis=0
+        )
+        store(tile, 0, (dq * scaling).astype(bf16).T)
+        dk = dot(jnp.concatenate(parts, axis=1), stack_heads(load(tile, 0)))
+        store(tile, 1, (dk * scaling).astype(bf16))
 
 
 def unit(x):
@@ -136,6 +138,10 @@
     value = before * half
     slope = half + value * (1.0 - half) * (2.0 * c + (6.0 * c * 0.044715) * square)
     return (value, slope)
+
+
+def pick(row, place):
+    return jnp.sum(jnp.where(lanes(row.shape) == place, row, 0), axis=1, keepdims=True)
 
 
 def char_rows(chars, table_ref, language):
@@ -177,8 +183,8 @@
 
 def char_forward_kernel(
     slots,
-    languages_ref,
     chars_hbm,
+    languages_hbm,
     counts_hbm,
     table_hbm,
     gain_attn_hbm,
@@ -195,6 +201,7 @@
     middle_ref,
     slope_ref,
     chars_ref,
+    languages_ref,
     counts_ref,
     table_ref,
     gain_attn_ref,
@@ -208,6 +215,7 @@
     section, _ = position()
     fetches = fetch_all(
         (
+            languages_hbm,
             counts_hbm,
             table_hbm,
             gain_attn_hbm,
@@ -219,6 +227,7 @@
             shrink_hbm,
         ),
         (
+            languages_ref,
             counts_ref,
             table_ref,
             gain_attn_ref,
@@ -231,45 +240,45 @@
         ),
         sems,
     )
-    fetches[0].wait()
+    for fetch in fetches[:2]:
+        fetch.wait()
     counts = counts_ref[section]
     rows = chars_ref.shape[0]
     words = counts.shape[-1]
     row_counts = counts_by_row(counts, rows, slots)
-    for fetch in fetches[1:4]:
+    for fetch in fetches[2:5]:
         fetch.wait()
-    x = char_rows(chars_ref[...], table_ref, languages_ref[section, 0])
+    x = char_rows(chars_ref[...], table_ref, pick(languages_ref[...], section))
     normal, _ = unit(x)
     normed = (normal * gain_attn_ref[...]).astype(bf16)
-    fetches[4].wait()
+    fetches[5].wait()
     qkv_ref[...] = dot(normed, project_ref[...]).astype(bf16)
-    mixed = []
-    for block in range(rows // BLOCK):
-        part = slice(block * BLOCK, (block + 1) * BLOCK)
-        key_mask = rows_of((slots, BLOCK)).astype(f32) < row_counts[:, part]
-        probs, piece = attend(
-            qkv_ref[part, :SLAB],
-            qkv_ref[part, SLAB : 2 * SLAB],
-            qkv_ref[part, 2 * SLAB :],
-            key_mask,
-            slots,
-        )
-        for head in range(CH):
-            probs_ref[head * slots : (head + 1) * slots, part] = probs[head]
-        mixed_ref[:, part] = piece
-        mixed.append(flip(piece))
-    mixed = jnp.concatenate(mixed, axis=0)
-    fetches[5].wait()
+    blocks = range(rows // BLOCK)
+
+    def load(block, which):
+        return qkv_ref[block * BLOCK : (block + 1) * BLOCK, which * SLAB : (which + 1) * SLAB]
+
+    by_head = jnp.concatenate(
+        [row_counts[:, block * BLOCK : (block + 1) * BLOCK] for block in blocks for _ in range(HEADS)],
+        axis=1,
+    )
+    key_mask = rows_of((slots, rows * HEADS)).astype(f32) < by_head
+    probs, mixed = attend(load, blocks, key_mask, slots)
+    probs_ref[...] = probs
+    for block in blocks:
+        mixed_ref[:, block * BLOCK : (block + 1) * BLOCK] = mixed[block]
+    mixed = mixed_ref[...].T
+    fetches[6].wait()
     middle = x + dot(mixed, output_ref[...])
     middle_ref[...] = middle
     normal, _ = unit(middle)
-    fetches[6].wait()
+    fetches[7].wait()
     normed = (normal * gain_mlp_ref[...]).astype(bf16)
     word_shape = (words, rows)
     lane = lanes(word_shape)
     member = (lane // slots == rows_of(word_shape)) & ((lane % slots).astype(f32) < row_counts)
     member = jnp.where(member, 1.0, 0.0).astype(bf16)
-    fetches[7].wait()
+    fetches[8].wait()
     for at in range(0, expand_ref.shape[1], 256):
         part = slice(at, at + 256)
         value, slope = gelu_parts(dot(normed, expand_ref[:, part]))
@@ -277,7 +286,7 @@
         hidden_sum_ref[:, part] = dot(member, value.astype(bf16)).astype(bf16)
     high = middle.astype(bf16)
     low = (middle - high.astype(f32)).astype(bf16)
-    fetches[8].wait()
+    fetches[9].wait()
     total = dot(member, high) + dot(member, low) + dot(hidden_sum_ref[...], shrink_ref[...])
     pooled_ref[...] = (total / counts_column(counts)).astype(bf16)
 
@@ -288,62 +297,55 @@
     hidden = weights[4].shape[1]
     vmem = pl.BlockSpec(memory_space=pltpu.VMEM)
     hbm = pl.BlockSpec(memory_space=pltpu.HBM)
-    fetched = (counts, table) + tuple(weights)
+    fetched = (languages, counts, table) + tuple(weights)
     return pl.pallas_call(
         functools.partial(char_forward_kernel, slots),
-        in_specs=[pl.BlockSpec(memory_space=pltpu.SMEM)] + [hbm] * 9,
+        in_specs=[hbm] * 10,
         out_specs=[vmem] * 7,
         out_shape=[
             jax.ShapeDtypeStruct((words, width), bf16),
             jax.ShapeDtypeStruct((words, hidden), bf16),
             jax.ShapeDtypeStruct((rows, 3 * width), bf16),
-            jax.ShapeDtypeStruct((CH * slots, rows), f32),
+            jax.ShapeDtypeStruct((slots, rows * HEADS), f32),
             jax.ShapeDtypeStruct((width, rows), bf16),
             jax.ShapeDtypeStruct((rows, width), f32),
             jax.ShapeDtypeStruct((rows, hidden), bf16),
         ],
         scratch_shapes=[pltpu.VMEM(chars.shape[1:], bf16)]
         + [pltpu.VMEM(array.shape, array.dtype) for array in fetched]
-        + [pltpu.SemaphoreType.DMA((9,))],
+        + [pltpu.SemaphoreType.DMA((10,))],
         compiler_params=pltpu.CompilerParams(vmem_limit_bytes=16 * MIB),
         cost_estimate=pl.CostEstimate(
             flops=64 * rows * width * width, bytes_accessed=8 * MIB, transcendentals=0
         ),
         name="char_forward",
-    )(languages, *[in_hbm(array) for array in (chars,) + fetched])
-
-
-CHAR_MLP_SLOT = 128
-CHAR_ATTN_SLOT = 80
-
-
-def char_slot(shard, me):
-    other = shard ^ me
-    return (other & 1) * 8 + ((other >> 1) & 3) * 2 + (other >> 3)
-
-
-def put_char(packed, me, shards, gradient, at):
-    size = gradient.shape[0] // shards
-    for shard in range(shards):
-        piece = gradient[shard * size : (shard + 1) * size].astype(bf16)
-        for column in range(gradient.shape[1] // SLAB):
+    )(*[in_hbm(array) for array in (chars,) + fetched])
+
+
+CHAR_FIRST_SLOT = 144
+CHAR_LAST_SLOT = 64
+
+
+def char_shard(slot, me):
+    return me ^ ((slot >> 3) | (((slot >> 1) & 3) << 1) | ((slot & 1) << 3))
+
+
+def put_shards(gradient, slots, shard_of, at):
+    width = SLAB
+    columns = gradient.shape[1] // width
+    size = gradient.shape[0] // len(slots)
+    for number, (ref, place) in enumerate(slots):
+        first = pl.multiple_of(shard_of(number) * size, size)
+        for column in range(columns):
             start = at + column * size
-            packed[char_slot(shard, me), start : start + size] = piece[
-                :, column * SLAB : (column + 1) * SLAB
-            ]
-    return at + size * (gradient.shape[1] // SLAB)
-
-
-def hand_out(packed, keep_ref, send_ref, sems):
-    half = packed.shape[0] // 2
-    copies = [
-        pltpu.make_async_copy(packed.at[pl.ds(half, half)], send_ref, sems.at[0]),
-        pltpu.make_async_copy(packed.at[pl.ds(0, half)], keep_ref, sems.at[1]),
-    ]
-    for copy in copies:
-        copy.start()
-    for copy in copies:
-        copy.wait()
+            ref[place, start : start + size] = gradient[
+                pl.ds(first, size), column * width : (column + 1) * width
+            ].astype(bf16)
+    return at + size * columns
+
+
+def slot_refs(*refs):
+    return [(ref, place) for ref in refs for place in range(ref.shape[0])]
 
 
 def char_mlp_back_kernel(
@@ -355,6 +357,7 @@
     shrink_ref,
     dpooled_ref,
     hidden_sum_ref,
+    mixed_ref,
     middle_ref,
     slope_ref,
     dmiddle_ref,
@@ -364,11 +367,13 @@
     counts_ref,
     dhidden_words,
     dbefore,
-    packed,
-    sems,
+    expand_grad,
+    shrink_grad,
+    output_grad,
+    sem,
 ):
     section, me = position()
-    fetch = pltpu.make_async_copy(counts_hbm, counts_ref, sems.at[2])
+    fetch = pltpu.make_async_copy(counts_hbm, counts_ref, sem)
     fetch.start()
     fetch.wait()
     counts = counts_ref[section]
@@ -387,33 +392,38 @@
         dbefore[:, part] = dot(member, dhidden_words[:, part]).astype(bf16) * slope_ref[:, part]
     dnormed = dot_nt(dbefore[...], expand_ref[...])
     normal, scale = unit(middle_ref[...])
-    normed_mlp_t = flip((normal * gain_mlp_ref[...]).astype(bf16))
+    normed_t = (normal * gain_mlp_ref[...]).astype(bf16).T
     gain_ref[...] = jnp.broadcast_to(
         jnp.sum(dnormed * normal, axis=0, keepdims=True), gain_ref.shape
     )
-    dmiddle_ref[...] = (
+    dmiddle = (
         dot(member, spread_high)
         + dot(member, spread_low)
         + unit_back(dnormed, gain_mlp_ref[...], normal, scale)
     )
-    at = put_char(packed, me, shards, dot(normed_mlp_t, dbefore[...]), 0)
-    put_char(packed, me, shards, dot(flip(hidden_sum_ref[...]), spread_high), at)
-    hand_out(packed, keep_ref, send_ref, sems)
+    dmiddle_ref[...] = dmiddle
+    expand_grad[...] = dot(normed_t, dbefore[...])
+    shrink_grad[...] = dot(hidden_sum_ref[...].T, spread_high)
+    output_grad[...] = dot(mixed_ref[...], dmiddle.astype(bf16))
+    targets = slot_refs(keep_ref, send_ref)
+    at = 0
+    for gradient in (expand_grad, shrink_grad, output_grad):
+        at = put_shards(gradient, targets, lambda slot: char_shard(slot, me), at)
 
 
 def char_mlp_back(counts, weights, dpooled, stored, slots, shards):
-    _, _, _, gain_mlp, expand_w, shrink = weights
-    hidden_sum, _, _, _, middle, slope = stored
+    _, _, output, gain_mlp, expand_w, shrink = weights
+    hidden_sum, _, _, mixed, middle, slope = stored
     rows, width = middle.shape
     words = rows // slots
     hidden = expand_w.shape[1]
-    half = (shards // 2, CHAR_MLP_SLOT, width)
+    half = (shards // 2, CHAR_FIRST_SLOT, width)
     vmem = pl.BlockSpec(memory_space=pltpu.VMEM)
     hbm = pl.BlockSpec(memory_space=pltpu.HBM)
     return pl.pallas_call(
         functools.partial(char_mlp_back_kernel, slots, shards),
-        in_specs=[hbm] + [vmem] * 7,
-        out_specs=[vmem, vmem, hbm, hbm],
+        in_specs=[hbm] + [vmem] * 8,
+        out_specs=[vmem] * 4,
         out_shape=[
             jax.ShapeDtypeStruct((rows, width), f32),
             jax.ShapeDtypeStruct((8, width), f32),
@@ -424,23 +434,25 @@
             pltpu.VMEM(counts.shape, counts.dtype),
             pltpu.VMEM((words, hidden), bf16),
             pltpu.VMEM((rows, hidden), bf16),
-            pltpu.VMEM((shards, CHAR_MLP_SLOT, width), bf16),
-            pltpu.SemaphoreType.DMA((3,)),
+            pltpu.VMEM(expand_w.shape, f32),
+            pltpu.VMEM(shrink.shape, f32),
+            pltpu.VMEM(output.shape, f32),
+            pltpu.SemaphoreType.DMA,
         ],
         compiler_params=pltpu.CompilerParams(vmem_limit_bytes=16 * MIB),
         cost_estimate=pl.CostEstimate(
             flops=64 * rows * width * width, bytes_accessed=8 * MIB, transcendentals=0
         ),
         name="char_mlp_back",
-    )(in_hbm(counts), gain_mlp, expand_w, shrink, dpooled, hidden_sum, middle, slope)
+    )(in_hbm(counts), gain_mlp, expand_w, shrink, dpooled, hidden_sum, mixed, middle, slope)
 
 
 def char_attn_back_kernel(
     slots,
     shards,
-    languages_ref,
     _,
     chars_hbm,
+    languages_hbm,
     table_ref,
     gain_attn_ref,
     project_ref,
@@ -449,45 +461,50 @@
     gain_mlp_grad_ref,
     qkv_ref,
     probs_ref,
-    mixed_ref,
-    grad_ref,
+    grad_hbm,
     keep_ref,
     send_ref,
+    send_more_ref,
     chars_ref,
+    languages_ref,
+    dmixed,
     dqkv,
-    packed,
+    grad,
+    project_grad,
     sems,
 ):
     section, me = position()
-    fetch = pltpu.make_async_copy(chars_hbm.at[section], chars_ref, sems.at[2])
-    fetch.start()
+    fetches = fetch_all(
+        (chars_hbm.at[section], languages_hbm), (chars_ref, languages_ref), sems
+    )
     rows, width = dmiddle_ref.shape
-    language = languages_ref[section, 0]
-    dy = dmiddle_ref[...].astype(bf16)
-    dmixed = dot_nt(dy, output_ref[...]).astype(bf16)
-    for block in range(rows // BLOCK):
-        part = slice(block * BLOCK, (block + 1) * BLOCK)
-        probs = [probs_ref[head * slots : (head + 1) * slots, part] for head in range(CH)]
-        pieces = attend_back(
-            qkv_ref[part, :SLAB],
-            qkv_ref[part, SLAB : 2 * SLAB],
-            qkv_ref[part, 2 * SLAB :],
-            probs,
-            dmixed[part],
-            slots,
-        )
-        for number in range(3):
-            dqkv[part, number * SLAB : (number + 1) * SLAB] = pieces[number]
+    dmixed[...] = dot_nt(dmiddle_ref[...].astype(bf16), output_ref[...]).astype(bf16)
+
+    def load(block, which):
+        return qkv_ref[block * BLOCK : (block + 1) * BLOCK, which * SLAB : (which + 1) * SLAB]
+
+    def load_dmixed(block):
+        return dmixed[block * BLOCK : (block + 1) * BLOCK]
+
+    def store(block, which, value):
+        dqkv[block * BLOCK : (block + 1) * BLOCK, which * SLAB : (which + 1) * SLAB] = value
+
+    attend_back(load, load_dmixed, range(rows // BLOCK), probs_ref[...], store, slots)
     dnormed = dot_nt(dqkv[...], project_ref[...])
-    fetch.wait()
+    for fetch in fetches:
+        fetch.wait()
+    language = pick(languages_ref[...], section)
     normal, scale = unit(char_rows(chars_ref[...], table_ref, language))
-    normed_t = flip((normal * gain_attn_ref[...]).astype(bf16))
     gain_attn_grad = jnp.sum(dnormed * normal, axis=0, keepdims=True)
     dx = dmiddle_ref[...] + unit_back(dnormed, gain_attn_ref[...], normal, scale)
-    grad_ref[...] = dx
+    grad[...] = dx
+    leave = pltpu.make_async_copy(grad, grad_hbm, sems.at[2])
+    leave.start()
     row_sum = jnp.sum(dx, axis=0, keepdims=True)
-    at = put_char(packed, me, shards, dot(normed_t, dqkv[...]), 0)
-    at = put_char(packed, me, shards, dot(mixed_ref[...], dy), at)
+    normed_t = (normal * gain_attn_ref[...]).astype(bf16).T
+    project_grad[...] = dot(normed_t, dqkv[...])
+    targets = slot_refs(keep_ref, send_ref, send_more_ref)
+    at = put_shards(project_grad, targets, lambda slot: char_shard(slot, me), 0)
     extra = jnp.concatenate(
         [
             gain_attn_grad,
@@ -496,34 +513,38 @@
         ],
         axis=0,
     ).astype(bf16)
-    for shard in range(shards):
-        packed[shard, at : at + 16] = extra
-    hand_out(packed, keep_ref, send_ref, sems)
+    for ref, place in targets:
+        ref[place, at : at + 16] = extra
+    leave.wait()
 
 
 def char_attn_back(
     languages, chars, table, weights, dmiddle, gain_mlp_grad, stored, slots, shards, after
 ):
     gain_attn, project, output, _, _, _ = weights
-    _, qkv, probs, mixed, _, _ = stored
+    _, qkv, probs, _, _, _ = stored
     rows, width = dmiddle.shape
-    half = (shards // 2, CHAR_ATTN_SLOT, width)
+    half = (shards // 2, CHAR_LAST_SLOT, width)
+    quarter = (shards // 4, CHAR_LAST_SLOT, width)
     vmem = pl.BlockSpec(memory_space=pltpu.VMEM)
     hbm = pl.BlockSpec(memory_space=pltpu.HBM)
     return pl.pallas_call(
         functools.partial(char_attn_back_kernel, slots, shards),
-        in_specs=[pl.BlockSpec(memory_space=pltpu.SMEM), pl.BlockSpec(memory_space=pl.ANY), hbm]
-        + [vmem] * 9,
-        out_specs=[vmem, hbm, hbm],
+        in_specs=[pl.BlockSpec(memory_space=pl.ANY), hbm, hbm] + [vmem] * 8,
+        out_specs=[hbm, vmem, vmem, vmem],
         out_shape=[
             jax.ShapeDtypeStruct((rows, width), f32),
             jax.ShapeDtypeStruct(half, bf16),
-            jax.ShapeDtypeStruct(half, bf16),
+            jax.ShapeDtypeStruct(quarter, bf16),
+            jax.ShapeDtypeStruct(quarter, bf16),
         ],
         scratch_shapes=[
             pltpu.VMEM((rows, width), bf16),
+            pltpu.VMEM(languages.shape, languages.dtype),
+            pltpu.VMEM((rows, width), bf16),
             pltpu.VMEM((rows, 3 * width), bf16),
-            pltpu.VMEM((shards, CHAR_ATTN_SLOT, width), bf16),
+            pltpu.VMEM((rows, width), f32),
+            pltpu.VMEM(project.shape, f32),
             pltpu.SemaphoreType.DMA((3,)),
         ],
         compiler_params=pltpu.CompilerParams(vmem_limit_bytes=16 * MIB),
@@ -532,9 +553,9 @@
         ),
         name="char_attn_back",
     )(
-        languages,
         after,
         in_hbm(chars),
+        in_hbm(languages),
         table,
         gain_attn,
         project,
@@ -543,7 +564,6 @@
         gain_mlp_grad,
         qkv,
         probs,
-        mixed,
     )
 
 
@@ -566,14 +586,14 @@
     gain_mlp_ref,
     expand_ref,
     shrink_ref,
-    result_ref,
+    result_hbm,
     dpooled_ref,
     keep_ref,
     send_ref,
     pooled,
+    pooled_t,
     dz,
     start,
-    normed,
     normed_t,
     qkv,
     kept,
@@ -581,13 +601,18 @@
     middle,
     normed_mlp_t,
     hidden,
-    pooled_t,
     dbefore,
     dmixed,
     dqkv,
     dy,
-    packed,
-    sems,
+    dstart,
+    result,
+    input_grad,
+    project_grad,
+    output_grad,
+    expand_grad,
+    shrink_grad,
+    sem,
 ):
     total = pooled.shape[0]
     width = output_ref.shape[0]
@@ -604,30 +629,26 @@
     start[...] = x
     normal, _ = unit(x)
     low = (normal * gain_attn_ref[...]).astype(bf16)
-    normed[...] = low
-    normed_t[...] = flip(low)
+    normed_t[...] = low.T
     qkv[...] = dot(low, project_ref[...]).astype(bf16)
-    causal = rows_of((length, BLOCK)) <= lanes((length, BLOCK)) % length
-    for block in range(total // BLOCK):
-        part = slice(block * BLOCK, (block + 1) * BLOCK)
-        for slab in range(slabs):
-            at = slab * SLAB
-            probs, piece = attend(
-                qkv[part, at : at + SLAB],
-                qkv[part, width + at : width + at + SLAB],
-                qkv[part, 2 * width + at : 2 * width + at + SLAB],
-                causal,
-                length,
-            )
-            for head in range(SLAB // HEAD):
-                kept[block * slabs + slab, head] = probs[head]
-            mixed_t[at : at + SLAB, part] = piece
-            dmixed[part, at : at + SLAB] = flip(piece)
-    x = x + dot(dmixed[...], output_ref[...])
+    tiles = [(block, slab) for block in range(total // BLOCK) for slab in range(slabs)]
+
+    def load(tile, which):
+        block, slab = tile
+        at = which * width + slab * SLAB
+        return qkv[block * BLOCK : (block + 1) * BLOCK, at : at + SLAB]
+
+    mask_shape = (length, len(tiles) * HEADS * BLOCK)
+    causal = rows_of(mask_shape) <= lanes(mask_shape) % length
+    probs, mixed = attend(load, tiles, causal, length)
+    kept[...] = probs
+    for (block, slab), piece in zip(tiles, mixed):
+        mixed_t[slab * SLAB : (slab + 1) * SLAB, block * BLOCK : (block + 1) * BLOCK] = piece
+    x = x + dot(mixed_t[...].T, output_ref[...])
     middle[...] = x
     normal, _ = unit(x)
     low = (normal * gain_mlp_ref[...]).astype(bf16)
-    normed_mlp_t[...] = flip(low)
+    normed_mlp_t[...] = low.T
     dz_all = dz[...]
     for at in range(0, expand_ref.shape[1], 256):
         part = slice(at, at + 256)
@@ -635,7 +656,9 @@
         hidden[:, part] = value.astype(bf16)
         dhidden = dot_nt(dz_all, shrink_ref[part, :]).astype(bf16)
         dbefore[:, part] = dhidden * bend.astype(bf16)
-    result_ref[...] = middle[:length] + dot(hidden[:length], shrink_ref[...])
+    result[...] = middle[:length] + dot(hidden[:length], shrink_ref[...])
+    leave = pltpu.make_async_copy(result, result_hbm, sem)
+    leave.start()
 
     dnormed = dot_nt(dbefore[...], expand_ref[...])
     normal, scale = unit(middle[...])
@@ -644,79 +667,60 @@
     dy_low = dmiddle.astype(bf16)
     dy[...] = dy_low
     dmixed[...] = dot_nt(dy_low, output_ref[...]).astype(bf16)
-    for block in range(total // BLOCK):
-        part = slice(block * BLOCK, (block + 1) * BLOCK)
-        for slab in range(slabs):
-            at = slab * SLAB
-            pieces = attend_back(
-                qkv[part, at : at + SLAB],
-                qkv[part, width + at : width + at + SLAB],
-                qkv[part, 2 * width + at : 2 * width + at + SLAB],
-                [kept[block * slabs + slab, head] for head in range(SLAB // HEAD)],
-                dmixed[part, at : at + SLAB],
-                length,
-            )
-            for place in range(3):
-                dqkv[part, place * width + at : place * width + at + SLAB] = pieces[place]
+
+    def load_dmixed(tile):
+        block, slab = tile
+        return dmixed[block * BLOCK : (block + 1) * BLOCK, slab * SLAB : (slab + 1) * SLAB]
+
+    def store(tile, which, value):
+        block, slab = tile
+        at = which * width + slab * SLAB
+        dqkv[block * BLOCK : (block + 1) * BLOCK, at : at + SLAB] = value
+
+    attend_back(load, load_dmixed, tiles, kept[...], store, length)
     dnormed = dot_nt(dqkv[...], project_ref[...])
     normal, scale = unit(start[...])
     gain_attn_grad = jnp.sum(dnormed * normal, axis=0, keepdims=True)
     dword = (dmiddle + unit_back(dnormed, gain_attn_ref[...], normal, scale)).astype(bf16)
     dpooled_ref[...] = dot_nt(dword[:length], input_ref[...]).astype(bf16)
-    normed[...] = dword
-
-    low_shards = range(shards // 2)
-
-    def shard_of(place):
-        return (me & 8) | place
-
-    def slot_of(place):
-        other = place ^ (me & 7)
-        return (other & 1) * 4 + (other >> 1)
-
-    def own_rows(flipped, size):
-        first = pl.multiple_of(shard_of(0) * size, 8 * size)
-        return flipped[pl.ds(first, 8 * size), :]
-
-    def own_columns(ref, size):
-        return ref[:, pl.ds(pl.multiple_of(section * size, size), size)]
-
-    def put(gradient, at):
-        size = gradient.shape[0] // len(low_shards)
-        for place in low_shards:
-            piece = gradient[place * size : (place + 1) * size].astype(bf16)
-            for column in range(gradient.shape[1] // SLAB):
-                first = at + column * size
-                packed[slot_of(place), first : first + size] = piece[
-                    :, column * SLAB : (column + 1) * SLAB
-                ]
-        return at + size * (gradient.shape[1] // SLAB)
-
-    size = normed_t.shape[0] // shards
-    lhs = own_rows(normed_t, size)
-    pooled_t[...] = flip(pooled[...])
-    at = put(
-        dot(
-            own_rows(pooled_t, pooled_t.shape[0] // shards),
-            own_columns(normed, width // 2),
-        ),
-        0,
-    )
-    at = put(dot(lhs, own_columns(dqkv, 3 * width // 2)), at)
-    at = put(dot(own_rows(mixed_t, size), own_columns(dy, width // 2)), at)
-    at = put(dot(own_rows(normed_mlp_t, size), own_columns(dbefore, expand_ref.shape[1] // 2)), at)
-    size = hidden.shape[1] // 2
-    lhs = flip(hidden[:, pl.ds(pl.multiple_of((me >> 3) * size, size), size)])
-    at = put(dot(lhs, own_columns(dz, width // 2)), at)
+    dstart[...] = dword
+
+    def shard_of(slot):
+        return (me & 7) ^ ((slot >> 2) | ((slot & 3) << 1))
+
+    def own_rows(flipped):
+        many = flipped.shape[0] // 2
+        return flipped[pl.ds(pl.multiple_of((me >> 3) * many, many), many), :]
+
+    def half_columns(ref, place):
+        many = ref.shape[1] // 2
+        return ref[:, pl.ds(pl.multiple_of(place * many, many), many)]
+
+    def own_columns(ref):
+        return half_columns(ref, section)
+
+    pooled_t[...] = pooled[...].T
+    hidden_t = half_columns(hidden, me >> 3).T
+    targets = slot_refs(keep_ref, send_ref)
+    at = 0
+    for lhs, rhs, ref in (
+        (own_rows(pooled_t), own_columns(dstart), input_grad),
+        (own_rows(normed_t), own_columns(dqkv), project_grad),
+        (own_rows(mixed_t), own_columns(dy), output_grad),
+        (own_rows(normed_mlp_t), own_columns(dbefore), expand_grad),
+        (hidden_t, own_columns(dz), shrink_grad),
+    ):
+        ref[...] = dot(lhs, rhs)
+        at = put_shards(ref, targets, shard_of, at)
     extra = jnp.concatenate(
         [gain_attn_grad[:, :SLAB], gain_attn_grad[:, SLAB:]]
         + [gain_mlp_grad[:, :SLAB], gain_mlp_grad[:, SLAB:]]
         + [jnp.zeros((12, SLAB), f32)],
         axis=0,
     ).astype(bf16)
-    for place in low_shards:
-        packed[place, at : at + 16] = extra
-    hand_out(packed, keep_ref, send_ref, sems)
+    for ref, place in targets:
+        ref[place, at : at + 16] = extra
+    leave.wait()
 
 
 def word_group(pooled, cotangents, word_input, weights, shards):
@@ -731,7 +735,7 @@
     return pl.pallas_call(
         functools.partial(word_kernel, length, shards),
         in_specs=[vmem] * 13,
-        out_specs=[vmem, vmem, hbm, hbm],
+        out_specs=[hbm, vmem, vmem, vmem],
         out_shape=[
             jax.ShapeDtypeStruct((length, width), f32),
             jax.ShapeDtypeStruct((length, channels), bf16),
@@ -740,23 +744,28 @@
         ],
         scratch_shapes=[
             pltpu.VMEM((total, channels), bf16),
+            pltpu.VMEM((channels, total), bf16),
             pltpu.VMEM((total, width), bf16),
             pltpu.VMEM((total, width), f32),
-            pltpu.VMEM((total, width), bf16),
             pltpu.VMEM((width, total), bf16),
             pltpu.VMEM((total, 3 * width), bf16),
-            pltpu.VMEM((total // BLOCK * (width // SLAB), SLAB // HEAD, length, BLOCK), f32),
+            pltpu.VMEM((length, total * (width // HEAD)), f32),
             pltpu.VMEM((width, total), bf16),
             pltpu.VMEM((total, width), f32),
             pltpu.VMEM((width, total), bf16),
             pltpu.VMEM((total, hidden), bf16),
-            pltpu.VMEM((channels, total), bf16),
             pltpu.VMEM((total, hidden), bf16),
             pltpu.VMEM((total, width), bf16),
             pltpu.VMEM((total, 3 * width), bf16),
             pltpu.VMEM((total, width), bf16),
-            pltpu.VMEM((8, WORD_SLOT, SLAB), bf16),
-            pltpu.SemaphoreType.DMA((2,)),
+            pltpu.VMEM((total, width), bf16),
+            pltpu.VMEM((length, width), f32),
+            pltpu.VMEM((channels // 2, width // 2), f32),
+            pltpu.VMEM((width // 2, 3 * width // 2), f32),
+            pltpu.VMEM((width // 2, width // 2), f32),
+            pltpu.VMEM((width // 2, hidden // 2), f32),
+            pltpu.VMEM((hidden // 2, width // 2), f32),
+            pltpu.SemaphoreType.DMA,
         ],
         compiler_params=pltpu.CompilerParams(vmem_limit_bytes=20 * MIB),
         cost_estimate=pl.CostEstimate(
@@ -766,52 +775,105 @@
     )(*pooled, *cotangents, word_input, gain_attn, project, output, gain_mlp, expand_w, shrink)
 
 
-def added(*refs):
-    return functools.reduce(lambda a, b: a + b, [ref.astype(f32) for ref in refs]).astype(bf16)
-
-
-def core_sum_kernel(groups, *refs):
-    ins = refs[: 2 * groups]
-    outs = refs[-4:]
+def summed(*parts):
+    return functools.reduce(lambda a, b: a + b, [part.astype(f32) for part in parts])
+
+
+def added(*parts):
+    return summed(*parts).astype(bf16)
+
+
+def by_section(section, low, high):
+    return (jnp.where(section == 0, low, high), jnp.where(section == 0, high, low))
+
+
+def first_sum_kernel(word_keep, word_arrived, char_keep, char_arrived, *outs):
+    *word, stay_ref, go_ref = outs
+    section, _ = position()
+    for place, ref in enumerate(word):
+        ref[...] = added(word_keep[place], word_arrived[place])
+    half = SLAB // 2
+    for place in range(char_keep.shape[0]):
+        total = added(char_keep[place], char_arrived[place])
+        stay_ref[place], go_ref[place] = by_section(section, total[:, :half], total[:, half:])
+
+
+def first_sum(word, char):
+    half = jax.ShapeDtypeStruct(char[0].shape[:2] + (SLAB // 2,), bf16)
+    *pieces, stay, go = pl.pallas_call(
+        first_sum_kernel,
+        out_shape=[jax.ShapeDtypeStruct((WORD_SLOT, SLAB), bf16)] * 4 + [half, half],
+        compiler_params=pltpu.CompilerParams(vmem_limit_bytes=12 * MIB),
+        name="first_sum",
+    )(*word, *char)
+    return (pieces, stay, go)
+
+
+def second_sum_kernel(char, last_keep, arrived, arrived_more, *outs):
+    half = SLAB // 2
     for place, out in enumerate(outs):
-        at = 0
-        for keep, arrived in zip(ins[0::2], ins[1::2]):
-            many = keep.shape[0] // len(outs)
-            for entry in range(place * many, (place + 1) * many):
-                size = keep.shape[1]
-                out[at : at + size] = added(keep[entry], arrived[entry])
-                at += size
-
-
-def core_sum(*pairs, after=()):
-    rows = sum(keep.shape[0] // 4 * keep.shape[1] for keep, _ in pairs)
+        at = CHAR_FIRST_SLOT
+        for far in range(2):
+            entry = 2 * place + far
+            out[:CHAR_FIRST_SLOT, far * half : (far + 1) * half] = char[entry]
+            many = arrived.shape[0]
+            other = arrived[entry] if entry < many else arrived_more[entry - many]
+            out[at : at + CHAR_LAST_SLOT] = added(last_keep[entry], other)
+            at += CHAR_LAST_SLOT
+
+
+def middle_sum_kernel(*refs):
+    *pieces, stay, arrived, word_ref, char_ref = refs
+    word_ref[...] = added(*[ref[...] for ref in pieces])
+    char_ref[...] = added(stay[...], arrived[...])
+
+
+def middle_sum(pieces, stay, arrived):
     return pl.pallas_call(
-        functools.partial(core_sum_kernel, len(pairs)),
-        in_specs=[pl.BlockSpec(memory_space=pltpu.VMEM)] * (2 * len(pairs))
-        + [pl.BlockSpec(memory_space=pl.ANY)] * len(after),
+        middle_sum_kernel,
+        out_shape=[
+            jax.ShapeDtypeStruct(pieces[0].shape, bf16),
+            jax.ShapeDtypeStruct(stay.shape, bf16),
+        ],
+        compiler_params=pltpu.CompilerParams(vmem_limit_bytes=12 * MIB),
+        cost_estimate=pl.CostEstimate(
+            flops=20_000_000_000, bytes_accessed=8 * MIB, transcendentals=0
+        ),
+        name="middle_sum",
+    )(*pieces, stay, arrived)
+
+
+def second_sum(first, last):
+    rows = CHAR_FIRST_SLOT + 2 * CHAR_LAST_SLOT
+    return pl.pallas_call(
+        second_sum_kernel,
         out_shape=[jax.ShapeDtypeStruct((rows, SLAB), bf16)] * 4,
-        compiler_params=pltpu.CompilerParams(vmem_limit_bytes=14 * MIB),
-        name="core_sum",
-    )(*[array for pair in pairs for array in pair], *after)
+        compiler_params=pltpu.CompilerParams(vmem_limit_bytes=12 * MIB),
+        name="second_sum",
+    )(first, *last)
+
+
+FOLD = 80
 
 
 def plane_sum_kernel(*refs):
-    first, second, near_ref, far_ref = (refs[:4], refs[4:8], refs[8], refs[9])
-    near_ref[:WORD_SLOT] = added(*[ref[:WORD_SLOT] for ref in first])
-    size = CHAR_MLP_SLOT
-    for half, out in ((0, near_ref), (1, far_ref)):
-        start = WORD_SLOT + half * size
-        at = WORD_SLOT if half == 0 else 0
-        out[at : at + size] = added(*[ref[start : start + size] for ref in first])
-        at += size
-        start = half * CHAR_ATTN_SLOT
-        out[at : at + CHAR_ATTN_SLOT] = added(
-            *[ref[start : start + CHAR_ATTN_SLOT] for ref in second]
+    word, char, near_ref, far_ref = (refs[0], refs[1:5], refs[5], refs[6])
+    near_ref[:WORD_SLOT] = word[...]
+    half = SLAB // 2
+    for far, out, at in ((0, near_ref, WORD_SLOT), (1, far_ref, 0)):
+        columns = slice(far * half, (far + 1) * half)
+        total = added(*[ref[:CHAR_FIRST_SLOT, columns] for ref in char])
+        out[at : at + FOLD, :half] = total[:FOLD]
+        out[at : at + FOLD, half:] = total[CHAR_FIRST_SLOT - FOLD :]
+        first = CHAR_FIRST_SLOT + far * CHAR_LAST_SLOT
+        at += FOLD
+        out[at : at + CHAR_LAST_SLOT] = added(
+            *[ref[first : first + CHAR_LAST_SLOT] for ref in char]
         )
 
 
-def plane_sum(first, second):
-    rows = CHAR_MLP_SLOT + CHAR_ATTN_SLOT
+def plane_sum(word, char):
+    rows = FOLD + CHAR_LAST_SLOT
     return pl.pallas_call(
         plane_sum_kernel,
         out_shape=[
@@ -820,20 +882,30 @@
         ],
         compiler_params=pltpu.CompilerParams(vmem_limit_bytes=12 * MIB),
         name="plane_sum",
-    )(*first, *second)
+    )(word, *char)
 
 
 def last_sum_kernel(near_ref, section_ref, high_ref, both_ref, *outs):
     word_rows = WORD_SLOT
     section, me = position()
     own = near_ref[:word_rows].astype(f32)
-    other = section_ref[:word_rows].astype(f32)
-    halves = (jnp.where(section == 0, own, other), jnp.where(section == 0, other, own))
-    char = (
-        near_ref[word_rows:].astype(f32)
-        + section_ref[word_rows:].astype(f32)
-        + high_ref[...].astype(f32)
-        + both_ref[...].astype(f32)
+    halves = by_section(section, own, section_ref[:word_rows].astype(f32))
+    half = SLAB // 2
+
+    def unfold(near, far):
+        total = summed(near[word_rows : word_rows + FOLD], far[:FOLD])
+        return jnp.concatenate(
+            [total[:, :half], total[2 * FOLD - CHAR_FIRST_SLOT :, half:]], axis=0
+        )
+
+    first = jnp.concatenate(
+        by_section(section, unfold(near_ref, high_ref), unfold(section_ref, both_ref)), axis=1
+    )
+    last = summed(
+        near_ref[word_rows + FOLD :],
+        section_ref[word_rows + FOLD :],
+        high_ref[FOLD:],
+        both_ref[FOLD:],
     )
 
     def mine(vector, size):
@@ -856,14 +928,15 @@
         w_expand_ref,
         w_shrink_ref,
     ) = outs
-    at = 0
-    for ref in (expand_ref, shrink_ref, project_ref, output_ref):
-        size = ref.shape[0]
-        for column in range(ref.shape[1] // SLAB):
-            ref[:, column * SLAB : (column + 1) * SLAB] = char[at : at + size]
-            at += size
+    for char, refs in ((first, (expand_ref, shrink_ref, output_ref)), (last, (project_ref,))):
+        at = 0
+        for ref in refs:
+            size = ref.shape[0]
+            for column in range(ref.shape[1] // SLAB):
+                ref[:, column * SLAB : (column + 1) * SLAB] = char[at : at + size]
+                at += size
     size = gain_attn_ref.shape[1]
-    extra = char[at : at + 16]
+    extra = last[at : at + 16]
     turned = mine(extra, size)
     gain_attn_ref[...] = turned[0:1]
     gain_mlp_ref[...] = turned[1:2]
@@ -925,6 +998,7 @@
     word_weights = tuple(w[None] if w.ndim == 1 else w for w in word_weights)
     chars = chars.reshape(micros, rows, width)
     counts = counts.reshape(micros, 1, words)
+    languages = languages.reshape(1, micros)
     pooled, *stored = char_forward(languages, chars, counts, language_table, char_weights, slots)
     others = (exchange(pooled, 0, FAR), exchange(pooled, 1, 0), exchange(pooled, 1, FAR))
     result, dpooled, keep, send = word_group(
@@ -934,8 +1008,10 @@
     dmiddle, gain_mlp_grad, keep, send = char_mlp_back(
         counts, char_weights, dpooled, stored, slots, shards
     )
-    first = plane_exchange(core_sum(word, (keep, exchange(send, 0, CORE))))
-    chars_grad, keep, send = char_attn_back(
+    pieces, stay, go = first_sum(word, (keep, exchange(send, 0, CORE)))
+    word = plane_exchange(pieces)
+    arrived = exchange(go, 1, 0)
+    chars_grad, keep, *sends = char_attn_back(
         languages,
         chars,
         language_table,
@@ -945,10 +1021,12 @@
         stored,
         slots,
         shards,
-        first[0],
-    )
-    second = plane_exchange(core_sum((keep, exchange(send, 0, CORE)), after=first[1:]))
-    near, far = plane_sum(first, second)
+        stay,
+    )
+    last = (keep,) + tuple(exchange(send, 0, CORE) for send in sends)
+    word, first = middle_sum(word, stay, arrived)
+    char = plane_exchange(second_sum(first, last))
+    near, far = plane_sum(word, char)
     arrived = (exchange(near, 1, 0), exchange(far, 0, FAR), exchange(far, 1, FAR))
     shapes = [(language_table.shape[0], language_table.shape[1] // shards)]
     for weight in char_weights + (word_input,) + word_weights:

time: 79.9 us -> 67.7 us (0.85)
  Pallas kernels: 34.2 us -> 25.5 us
  waiting for transfers between devices: 22.9 us -> 18 us
  starting transfers between devices: 20.9 us -> 23 us
    ppermute x16 -> x18, waiting for transfers between devices: 22.9 us -> 18 us  [exchange(): return lax.ppermute(value, ('section', 'dp'), pairs)]
    pallas_call x1, Pallas kernels: 8.61 us -> 5.22 us  [char_attn_back(): pl.pallas_call(functools.partial(char_attn_back_kernel, slots, shards), i...]
    pallas_call x1, Pallas kernels: 10.3 us -> 7.26 us  [word_group(): pl.pallas_call(functools.partial(word_kernel, length, shards), in_specs=[...]
    pallas_call x3 -> x4, Pallas kernels: 10.3 us -> 8.03 us  [the longest x1 7.36 us: char_forward(): pl.pallas_call(functools.partial(char_forward_kernel, slots), in_specs=[h...]
    ppermute x16 -> x18, starting transfers between devices: 20.9 us -> 23 us  [exchange(): return lax.ppermute(value, ('section', 'dp'), pairs)]
  transfers between devices with their start and end apart: 16 -> 18, of which waited for: 10 -> 9; matrix products, arithmetic and copies ran while one was open for 1% -> 0% of each run, Pallas kernels for 28% -> 25%
where the time goes in v4:
time: 67.7 us; the launch traced here: 67.5 us
  Pallas kernels  25.5 us (38%)
  starting transfers between devices  23 us (34%)
  waiting for transfers between devices  18 us (27%)
  between operations  0.98 us (1%)
    ppermute x18, starting transfers between devices, exchange(): return lax.ppermute(value, ('section', 'dp'), pairs)  23 us
    ppermute x18, waiting for transfers between devices, exchange(): return lax.ppermute(value, ('section', 'dp'), pairs)  18 us
    pallas_call x1, Pallas kernels, char_forward(): pl.pallas_call(functools.partial(char_forward_kernel, slots), in_specs=[h...  7.36 us
    pallas_call x1, Pallas kernels, word_group(): pl.pallas_call(functools.partial(word_kernel, length, shards), in_specs=[...  7.26 us
    pallas_call x1, Pallas kernels, char_attn_back(): pl.pallas_call(functools.partial(char_attn_back_kernel, slots, shards), i...  5.22 us
    pallas_call x1, Pallas kernels, char_mlp_back(): pl.pallas_call(functools.partial(char_mlp_back_kernel, slots, shards), in...  3.9 us
  transfers between devices with their start and end apart: 18, of which 9 were waited for; matrix products, arithmetic and copies ran while one was open for 0% of the time, Pallas kernels for 25%

profile of v4, /device:TPU:0, one launch (start us, length us, event | category | flops | bytes accessed | tf_op | source)
XLA Modules:
  0.0 67.5 jit_solution(15495131354760215099)
XLA Ops:
  0.6 4.1 %collective-permute-start.3 = (bf16[2,64,512]{2,1,0:T(8,128)(2,1)}, bf16[2,64,512]{2,1,0:T(8,128)(2,1)S(1)}, u32[]{:S(2)}, u32[]{:S(2)}) collective-permute-start(bf16[2,64,512]{2,1,0:T(8,128)(2,1)} %bitcast.13), channel_id=1, source_target_pairs={{0,8},{1,9},{2,10},{3,11},{4,12},{5,13},{6,14},{7,15},{8,0},{9,1},... | collective-permute-start | bytes 393224 | tf_op jit(solution)/shard_map/ppermute | solution.py:977
  4.8 0.0 copy-start.7
  4.8 7.4 %char_forward.1 = (bf16[64,256]{1,0:T(8,128)(2,1)S(1)}, bf16[64,1024]{1,0:T(8,128)(2,1)S(1)}, bf16[1024,768]{1,0:T(8,128)(2,1)S(1)}, f32[16,4096]{1,0:T(8,128)S(...) custom-call(bf16[2,1024,256]{2,1,0:T(8,128)(2,1)} %bitcast.21, ...), custom_call_target="tpu_custom_call" | custom-call | flops 4294967296 | bytes 8388608 | tf_op jit(solution)/shard_map/char_forward/pallas_call | solution.py:301
  12.2 1.3 %collective-permute-start.2 = (bf16[64,256]{1,0:T(8,128)(2,1)S(1)}, bf16[64,256]{1,0:T(8,128)(2,1)S(1)}, u32[]{:S(2)}, u32[]{:S(2)}) collective-permute-start(bf16[64,256]{1,0:T(8,128)(2,1)S(1)} %get-tuple-element.63.own_ref), channel_id=1, source_target_pairs={{0,24},{1,25},{2,26},{3,27},{4,28},{5,29},{6,30},{7,31},{8,16},{9,... | collective-permute-start | bytes 98312 | tf_op jit(solution)/shard_map/ppermute | solution.py:977
  13.5 0.3 collective-permute-start.1
  13.8 2.8 %collective-permute-start = (bf16[64,256]{1,0:T(8,128)(2,1)S(1)}, bf16[64,256]{1,0:T(8,128)(2,1)S(1)}, u32[]{:S(2)}, u32[]{:S(2)}) collective-permute-start(bf16[64,256]{1,0:T(8,128)(2,1)S(1)} %get-tuple-element.63.own_ref), channel_id=1, source_target_pairs={{0,8},{1,9},{2,10},{3,11},{4,12},{5,13},{6,14},{7,15},{8,0},{9,1},... | collective-permute-start | bytes 98312 | tf_op jit(solution)/shard_map/ppermute | solution.py:977
  16.6 1.6 %collective-permute-done.2.both_ref = bf16[64,256]{1,0:T(8,128)(2,1)S(1)} collective-permute-done((bf16[64,256]{1,0:T(8,128)(2,1)S(1)}, bf16[64,256]{1,0:T(8,128)(2,1)S(1)}, u32[]{:S(2)}, u32[]{:S(2)}) %collective-permute-start.2) | collective-permute-done | bytes 32800 | tf_op jit(solution)/shard_map/ppermute | solution.py:977
  18.3 0.0 collective-permute-done.1.section_ref
  18.3 0.4 collective-permute-done.far_ref
  18.6 0.0 collective-permute-done.3.cot_far_ref
  18.7 0.0 copy-done.2
  18.7 0.0 copy-done.3
  18.7 0.0 copy-done.7
  18.7 0.0 copy-done.8
  18.7 0.0 copy-done.11
  18.7 0.0 copy-done.12
  18.7 0.0 copy-start.4
  18.7 0.0 copy-start.5
  18.7 0.0 copy-start.13
  18.8 7.3 %word_group.1 = (f32[64,512]{1,0:T(8,128)}, bf16[64,256]{1,0:T(8,128)(2,1)S(1)}, bf16[4,416,256]{2,1,0:T(8,128)(2,1)S(1)}, bf16[4,416,256]{2,1,0:T(8,128)(2,1)S(1)}) custom-call(bf16[64,256]{1,0:T(8,128)(2,1)S(1)} %get-tuple-element.63.own_ref, bf16[64,256]{1,0:T(8,128)(2,1)S(1)} %collective-permute-done.far_ref, ...), custom_call_target="tpu_custom_call" | custom-call | flops 6710886400 | bytes 8388608 | tf_op jit(solution)/shard_map/word_group/pallas_call | solution.py:735
  26.0 0.1 collective-permute-start.4
  26.1 0.0 copy-done.4
  26.1 0.0 copy-done.5
  26.1 0.0 copy-done.13
  26.1 3.9 %char_mlp_back.1 = (f32[1024,256]{1,0:T(8,128)S(1)}, f32[8,256]{1,0:T(8,128)S(1)}, bf16[8,144,256]{2,1,0:T(8,128)(2,1)S(1)}, bf16[8,144,256]{2,1,0:T(8,128)(2,1)S(1)}) custom-call(s32[2,1,64]{2,1,0:T(1,128)} %counts_hbm.3, f32[1,256]{1,0:T(1,128)S(1)} %bitcast.18, bf16[256,1024]{1,0:T(8,128)(2,1)S(1)} %copy-done.4, bf16[1024,256]{1,0:T(8,128)(2,1)S(1)} %copy-done.5, ...), custom_call_target="tpu_custom_call" | custom-call | flops 4294967296 | bytes 8388608 | tf_op jit(solution)/shard_map/char_mlp_back/pallas_call | solution.py:423
  30.0 0.0 copy-start.6
  30.1 0.0 copy-start.9
  30.1 0.0 copy-start.10
  30.1 0.0 copy-start.14
  30.1 0.5 collective-permute-start.5
  30.6 1.6 %collective-permute-done.5.char_arrived = bf16[8,144,256]{2,1,0:T(8,128)(2,1)S(1)} collective-permute-done((bf16[8,144,256]{2,1,0:T(8,128)(2,1)S(1)}, bf16[8,144,256]{2,1,0:T(8,128)(2,1)S(1)}, u32[]{:S(2)}, u32[]{:S(2)}) %collective-permute-start.5) | collective-permute-done | bytes 589856 | tf_op jit(solution)/shard_map/ppermute | solution.py:977
  32.3 0.0 collective-permute-done.4.word_arrived
  32.3 0.4 first_sum.1
  32.7 2.2 %collective-permute-start.6 = (bf16[416,256]{1,0:T(8,128)(2,1)S(1)}, bf16[416,256]{1,0:T(8,128)(2,1)S(1)}, u32[]{:S(2)}, u32[]{:S(2)}) collective-permute-start(bf16[416,256]{1,0:T(8,128)(2,1)S(1)} %get-tuple-element.81), channel_id=1, source_target_pairs={{0,2},{1,3},{2,0},{3,1},{4,6},{5,7},{6,4},{7,5},{8,10},{9,11},{10,... | collective-permute-start | bytes 638984 | tf_op jit(solution)/shard_map/ppermute | solution.py:977
  34.8 1.2 %collective-permute-start.7 = (bf16[416,256]{1,0:T(8,128)(2,1)S(1)}, bf16[416,256]{1,0:T(8,128)(2,1)S(1)}, u32[]{:S(2)}, u32[]{:S(2)}) collective-permute-start(bf16[416,256]{1,0:T(8,128)(2,1)S(1)} %get-tuple-element.82), channel_id=1, source_target_pairs={{0,4},{1,5},{2,6},{3,7},{4,0},{5,1},{6,2},{7,3},{8,12},{9,13},{10,... | collective-permute-start | bytes 638984 | tf_op jit(solution)/shard_map/ppermute | solution.py:977
  36.1 0.3 collective-permute-start.8
  36.4 1.6 %collective-permute-start.9 = (bf16[8,144,128]{2,1,0:T(8,128)(2,1)S(1)}, bf16[8,144,128]{2,1,0:T(8,128)(2,1)S(1)}, u32[]{:S(2)}, u32[]{:S(2)}) collective-permute-start(bf16[8,144,128]{2,1,0:T(8,128)(2,1)S(1)} %get-tuple-element.84), channel_id=1, source_target_pairs={{0,16},{1,17},{2,18},{3,19},{4,20},{5,21},{6,22},{7,23},{8,24},{9,... | collective-permute-start | bytes 884744 | tf_op jit(solution)/shard_map/ppermute | solution.py:977
  38.0 0.0 copy-done.6
  38.0 0.0 copy-done.10
  38.0 5.2 %char_attn_back.1 = (f32[1024,256]{1,0:T(8,128)}, bf16[8,64,256]{2,1,0:T(8,128)(2,1)S(1)}, bf16[4,64,256]{2,1,0:T(8,128)(2,1)S(1)}, bf16[4,64,256]{2,1,0:T(8,128)(2,1)S(1)}) custom-call(bf16[8,144,128]{2,1,0:T(8,128)(2,1)S(1)} %get-tuple-element.74._.refs_4_, bf16[2,1024,256]{2,1,0:T(8,128)(2,1)} %bitcast.22, s32[1,2]{1,0:T(1,128)} %bitcast.24, ...), custom_call_target="tpu_custom_call" | custom-call | flops 4294967296 | bytes 8388608 | tf_op jit(solution)/shard_map/char_attn_back/pallas_call | solution.py:531
  43.2 0.1 collective-permute-start.10
  43.3 0.0 collective-permute-done.6.refs_1_
  43.3 0.5 collective-permute-start.11
  43.8 0.0 collective-permute-done.7.refs_2_
  43.8 2.7 %collective-permute-done.8.refs_3_ = bf16[416,256]{1,0:T(8,128)(2,1)S(1)} collective-permute-done((bf16[416,256]{1,0:T(8,128)(2,1)S(1)}, bf16[416,256]{1,0:T(8,128)(2,1)S(1)}, u32[]{:S(2)}, u32[]{:S(2)}) %collective-permute-start.8) | collective-permute-done | bytes 213024 | tf_op jit(solution)/shard_map/ppermute | solution.py:977
  46.4 0.0 collective-permute-done.9.refs_5_
  46.4 0.2 middle_sum.1
  46.6 0.0 collective-permute-done.10.arrived
  46.6 0.0 collective-permute-done.11.arrived_more
  46.6 0.1 second_sum.1
  46.7 1.7 %collective-permute-start.12 = (bf16[272,256]{1,0:T(8,128)(2,1)S(1)}, bf16[272,256]{1,0:T(8,128)(2,1)S(1)}, u32[]{:S(2)}, u32[]{:S(2)}) collective-permute-start(bf16[272,256]{1,0:T(8,128)(2,1)S(1)} %get-tuple-element.91), channel_id=1, source_target_pairs={{0,2},{1,3},{2,0},{3,1},{4,6},{5,7},{6,4},{7,5},{8,10},{9,11},{10,... | collective-permute-start | bytes 417800 | tf_op jit(solution)/shard_map/ppermute | solution.py:977
  48.5 1.2 %collective-permute-start.13 = (bf16[272,256]{1,0:T(8,128)(2,1)S(1)}, bf16[272,256]{1,0:T(8,128)(2,1)S(1)}, u32[]{:S(2)}, u32[]{:S(2)}) collective-permute-start(bf16[272,256]{1,0:T(8,128)(2,1)S(1)} %get-tuple-element.92), channel_id=1, source_target_pairs={{0,4},{1,5},{2,6},{3,7},{4,0},{5,1},{6,2},{7,3},{8,12},{9,13},{10,... | collective-permute-start | bytes 417800 | tf_op jit(solution)/shard_map/ppermute | solution.py:977
  49.7 0.6 collective-permute-start.14
  50.3 1.7 %collective-permute-done.12.refs_2_ = bf16[272,256]{1,0:T(8,128)(2,1)S(1)} collective-permute-done((bf16[272,256]{1,0:T(8,128)(2,1)S(1)}, bf16[272,256]{1,0:T(8,128)(2,1)S(1)}, u32[]{:S(2)}, u32[]{:S(2)}) %collective-permute-start.12) | collective-permute-done | bytes 139296 | tf_op jit(solution)/shard_map/ppermute | solution.py:977
  52.0 2.5 %collective-permute-done.13.refs_3_ = bf16[272,256]{1,0:T(8,128)(2,1)S(1)} collective-permute-done((bf16[272,256]{1,0:T(8,128)(2,1)S(1)}, bf16[272,256]{1,0:T(8,128)(2,1)S(1)}, u32[]{:S(2)}, u32[]{:S(2)}) %collective-permute-start.13) | collective-permute-done | bytes 139296 | tf_op jit(solution)/shard_map/ppermute | solution.py:977
  54.5 1.8 %collective-permute-done.14.refs_4_ = bf16[272,256]{1,0:T(8,128)(2,1)S(1)} collective-permute-done((bf16[272,256]{1,0:T(8,128)(2,1)S(1)}, bf16[272,256]{1,0:T(8,128)(2,1)S(1)}, u32[]{:S(2)}, u32[]{:S(2)}) %collective-permute-start.14) | collective-permute-done | bytes 139296 | tf_op jit(solution)/shard_map/ppermute | solution.py:977
  56.3 0.1 plane_sum.1
  56.4 1.4 %collective-permute-start.15 = (bf16[560,256]{1,0:T(8,128)(2,1)S(1)}, bf16[560,256]{1,0:T(8,128)(2,1)S(1)}, u32[]{:S(2)}, u32[]{:S(2)}) collective-permute-start(bf16[560,256]{1,0:T(8,128)(2,1)S(1)} %get-tuple-element.94.near_ref), channel_id=1, source_target_pairs={{0,16},{1,17},{2,18},{3,19},{4,20},{5,21},{6,22},{7,23},{8,24},{9,... | collective-permute-start | bytes 860168 | tf_op jit(solution)/shard_map/ppermute | solution.py:977
  57.8 2.6 %collective-permute-start.17 = (bf16[144,256]{1,0:T(8,128)(2,1)S(1)}, bf16[144,256]{1,0:T(8,128)(2,1)S(1)}, u32[]{:S(2)}, u32[]{:S(2)}) collective-permute-start(bf16[144,256]{1,0:T(8,128)(2,1)S(1)} %get-tuple-element.95), channel_id=1, source_target_pairs={{0,24},{1,25},{2,26},{3,27},{4,28},{5,29},{6,30},{7,31},{8,16},{9,... | collective-permute-start | bytes 221192 | tf_op jit(solution)/shard_map/ppermute | solution.py:977
  60.4 0.5 collective-permute-start.16
  60.9 5.0 %collective-permute-done.17.both_ref = bf16[144,256]{1,0:T(8,128)(2,1)S(1)} collective-permute-done((bf16[144,256]{1,0:T(8,128)(2,1)S(1)}, bf16[144,256]{1,0:T(8,128)(2,1)S(1)}, u32[]{:S(2)}, u32[]{:S(2)}) %collective-permute-start.17) | collective-permute-done | bytes 73760 | tf_op jit(solution)/shard_map/ppermute | solution.py:977
  65.8 0.7 collective-permute-done.16.high_ref
  66.5 0.0 collective-permute-done.15.section_ref
  66.5 1.0 %last_sum.1 = (f32[8,16]{1,0:T(8,128)}, f32[1,16]{1,0:T(1,128)}, f32[16,768]{1,0:T(8,128)}, f32[16,256]{1,0:T(8,128)}, f32[1,16]{1,0:T(1,128)}, /*index=5*/f32[1...) custom-call(bf16[560,256]{1,0:T(8,128)(2,1)S(1)} %get-tuple-element., ...), custom_call_target="tpu_custom_call" | custom-call | tf_op jit(solution)/shard_map/last_sum/pallas_call | solution.py:962
  (11 shorter events, 0.0 us)
Async XLA Ops:
  0.6 18.0 %collective-permute-start.3 = (bf16[2,64,512]{2,1,0:T(8,128)(2,1)}, bf16[2,64,512]{2,1,0:T(8,128)(2,1)S(1)}, u32[]{:S(2)}, u32[]{:S(2)}) collective-permute-start(bf16[2,64,512]{2,1,0:T(8,128)(2,1)} %bitcast.13), channel_id=1, source_target_pairs={{0,8},{1,9},{2,10},{3,11},{4,12},{5,13},{6,14},{7,15},{8,0},{9,1},... | collective-permute-start | bytes 393224 | tf_op jit(solution)/shard_map/ppermute | solution.py:977
  4.8 13.9 %copy-start = (bf16[512,2048]{1,0:T(8,128)(2,1)S(1)}, bf16[512,2048]{1,0:T(8,128)(2,1)}, u32[]{:S(2)}) copy-start(bf16[512,2048]{1,0:T(8,128)(2,1)} %expand_ref.2) | copy-start | bytes 6291460
  4.8 13.9 %copy-start.1 = (bf16[2048,512]{1,0:T(8,128)(2,1)S(1)}, bf16[2048,512]{1,0:T(8,128)(2,1)}, u32[]{:S(2)}) copy-start(bf16[2048,512]{1,0:T(8,128)(2,1)} %shrink_ref.2) | copy-start | bytes 6291460
  4.8 13.9 %copy-start.2 = (bf16[512,1536]{1,0:T(8,128)(2,1)S(1)}, bf16[512,1536]{1,0:T(8,128)(2,1)}, u32[]{:S(2)}) copy-start(bf16[512,1536]{1,0:T(8,128)(2,1)} %project_ref.2) | copy-start | bytes 4718596
  4.8 13.9 %copy-start.3 = (bf16[512,512]{1,0:T(8,128)(2,1)S(1)}, bf16[512,512]{1,0:T(8,128)(2,1)}, u32[]{:S(2)}) copy-start(bf16[512,512]{1,0:T(8,128)(2,1)} %output_ref.2) | copy-start | bytes 1572868
  4.8 13.9 %copy-start.7 = (bf16[256,512]{1,0:T(8,128)(2,1)S(1)}, bf16[256,512]{1,0:T(8,128)(2,1)}, u32[]{:S(2)}) copy-start(bf16[256,512]{1,0:T(8,128)(2,1)} %input_ref.1) | copy-start | bytes 786436
  4.8 13.9 %copy-start.8 = (bf16[2,1,64,512]{3,2,1,0:T(8,128)(2,1)S(1)}, bf16[2,1,64,512]{3,2,1,0:T(8,128)(2,1)}, u32[]{:S(2)}) copy-start(bf16[2,1,64,512]{3,2,1,0:T(8,128)(2,1)} %param.35) | copy-start | bytes 393220
  4.8 13.9 %copy-start.11 = (f32[512]{0:T(512)S(1)}, f32[512]{0:T(512)}, u32[]{:S(2)}) copy-start(f32[512]{0:T(512)} %param.29) | copy-start | bytes 6148
  4.8 13.9 %copy-start.12 = (f32[512]{0:T(512)S(1)}, f32[512]{0:T(512)}, u32[]{:S(2)}) copy-start(f32[512]{0:T(512)} %param.32) | copy-start | bytes 6148
  12.2 6.1 %collective-permute-start.2 = (bf16[64,256]{1,0:T(8,128)(2,1)S(1)}, bf16[64,256]{1,0:T(8,128)(2,1)S(1)}, u32[]{:S(2)}, u32[]{:S(2)}) collective-permute-start(bf16[64,256]{1,0:T(8,128)(2,1)S(1)} %get-tuple-element.63.own_ref), channel_id=1, source_target_pairs={{0,24},{1,25},{2,26},{3,27},{4,28},{5,29},{6,30},{7,31},{8,16},{9,... | collective-permute-start | bytes 98312 | tf_op jit(solution)/shard_map/ppermute | solution.py:977
  13.5 4.8 %collective-permute-start.1 = (bf16[64,256]{1,0:T(8,128)(2,1)S(1)}, bf16[64,256]{1,0:T(8,128)(2,1)S(1)}, u32[]{:S(2)}, u32[]{:S(2)}) collective-permute-start(bf16[64,256]{1,0:T(8,128)(2,1)S(1)} %get-tuple-element.63.own_ref), channel_id=1, source_target_pairs={{0,16},{1,17},{2,18},{3,19},{4,20},{5,21},{6,22},{7,23},{8,24},{9,... | collective-permute-start | bytes 98312 | tf_op jit(solution)/shard_map/ppermute | solution.py:977
  13.8 4.8 %collective-permute-start = (bf16[64,256]{1,0:T(8,128)(2,1)S(1)}, bf16[64,256]{1,0:T(8,128)(2,1)S(1)}, u32[]{:S(2)}, u32[]{:S(2)}) collective-permute-start(bf16[64,256]{1,0:T(8,128)(2,1)S(1)} %get-tuple-element.63.own_ref), channel_id=1, source_target_pairs={{0,8},{1,9},{2,10},{3,11},{4,12},{5,13},{6,14},{7,15},{8,0},{9,1},... | collective-permute-start | bytes 98312 | tf_op jit(solution)/shard_map/ppermute | solution.py:977
  18.7 7.4 %copy-start.4 = (bf16[256,1024]{1,0:T(8,128)(2,1)S(1)}, bf16[256,1024]{1,0:T(8,128)(2,1)}, u32[]{:S(2)}) copy-start(bf16[256,1024]{1,0:T(8,128)(2,1)} %expand_ref.3) | copy-start | bytes 1572868
  18.7 7.4 %copy-start.5 = (bf16[1024,256]{1,0:T(8,128)(2,1)S(1)}, bf16[1024,256]{1,0:T(8,128)(2,1)}, u32[]{:S(2)}) copy-start(bf16[1024,256]{1,0:T(8,128)(2,1)} %shrink_ref.3) | copy-start | bytes 1572868
  18.7 7.4 %copy-start.13 = (f32[256]{0:T(256)S(1)}, f32[256]{0:T(256)}, u32[]{:S(2)}) copy-start(f32[256]{0:T(256)} %param.25) | copy-start | bytes 3076
  26.0 6.2 %collective-permute-start.4 = (bf16[4,416,256]{2,1,0:T(8,128)(2,1)S(1)}, bf16[4,416,256]{2,1,0:T(8,128)(2,1)S(1)}, u32[]{:S(2)}, u32[]{:S(2)}) collective-permute-start(bf16[4,416,256]{2,1,0:T(8,128)(2,1)S(1)} %get-tuple-element.66), channel_id=1, source_target_pairs={{0,1},{1,0},{2,3},{3,2},{4,5},{5,4},{6,7},{7,6},{8,9},{9,8},{10,11... | collective-permute-start | bytes 2555912 | tf_op jit(solution)/shard_map/ppermute | solution.py:977
  30.0 7.9 %copy-start.6 = (bf16[256,768]{1,0:T(8,128)(2,1)S(1)}, bf16[256,768]{1,0:T(8,128)(2,1)}, u32[]{:S(2)}) copy-start(bf16[256,768]{1,0:T(8,128)(2,1)} %project_ref.3) | copy-start | bytes 1179652
  30.1 7.9 %copy-start.9 = (bf16[256,256]{1,0:T(8,128)(2,1)S(1)}, bf16[256,256]{1,0:T(8,128)(2,1)}, u32[]{:S(2)}) copy-start(bf16[256,256]{1,0:T(8,128)(2,1)} %output_ref.3) | copy-start | bytes 393220
  30.1 7.9 %copy-start.10 = (bf16[8,256]{1,0:T(8,128)(2,1)S(1)}, bf16[8,256]{1,0:T(8,128)(2,1)}, u32[]{:S(2)}) copy-start(bf16[8,256]{1,0:T(8,128)(2,1)} %table_ref.1) | copy-start | bytes 12292
  30.1 7.9 %copy-start.14 = (f32[256]{0:T(256)S(1)}, f32[256]{0:T(256)}, u32[]{:S(2)}) copy-start(f32[256]{0:T(256)} %param.22) | copy-start | bytes 3076
  30.1 2.2 %collective-permute-start.5 = (bf16[8,144,256]{2,1,0:T(8,128)(2,1)S(1)}, bf16[8,144,256]{2,1,0:T(8,128)(2,1)S(1)}, u32[]{:S(2)}, u32[]{:S(2)}) collective-permute-start(bf16[8,144,256]{2,1,0:T(8,128)(2,1)S(1)} %get-tuple-element.73), channel_id=1, source_target_pairs={{0,1},{1,0},{2,3},{3,2},{4,5},{5,4},{6,7},{7,6},{8,9},{9,8},{10,11... | collective-permute-start | bytes 1769480 | tf_op jit(solution)/shard_map/ppermute | solution.py:977
  32.7 10.6 %collective-permute-start.6 = (bf16[416,256]{1,0:T(8,128)(2,1)S(1)}, bf16[416,256]{1,0:T(8,128)(2,1)S(1)}, u32[]{:S(2)}, u32[]{:S(2)}) collective-permute-start(bf16[416,256]{1,0:T(8,128)(2,1)S(1)} %get-tuple-element.81), channel_id=1, source_target_pairs={{0,2},{1,3},{2,0},{3,1},{4,6},{5,7},{6,4},{7,5},{8,10},{9,11},{10,... | collective-permute-start | bytes 638984 | tf_op jit(solution)/shard_map/ppermute | solution.py:977
  34.8 8.9 %collective-permute-start.7 = (bf16[416,256]{1,0:T(8,128)(2,1)S(1)}, bf16[416,256]{1,0:T(8,128)(2,1)S(1)}, u32[]{:S(2)}, u32[]{:S(2)}) collective-permute-start(bf16[416,256]{1,0:T(8,128)(2,1)S(1)} %get-tuple-element.82), channel_id=1, source_target_pairs={{0,4},{1,5},{2,6},{3,7},{4,0},{5,1},{6,2},{7,3},{8,12},{9,13},{10,... | collective-permute-start | bytes 638984 | tf_op jit(solution)/shard_map/ppermute | solution.py:977
  36.1 10.4 %collective-permute-start.8 = (bf16[416,256]{1,0:T(8,128)(2,1)S(1)}, bf16[416,256]{1,0:T(8,128)(2,1)S(1)}, u32[]{:S(2)}, u32[]{:S(2)}) collective-permute-start(bf16[416,256]{1,0:T(8,128)(2,1)S(1)} %get-tuple-element.83), channel_id=1, source_target_pairs={{0,6},{1,7},{2,4},{3,5},{4,2},{5,3},{6,0},{7,1},{8,14},{9,15},{10,... | collective-permute-start | bytes 638984 | tf_op jit(solution)/shard_map/ppermute | solution.py:977
  36.4 10.1 %collective-permute-start.9 = (bf16[8,144,128]{2,1,0:T(8,128)(2,1)S(1)}, bf16[8,144,128]{2,1,0:T(8,128)(2,1)S(1)}, u32[]{:S(2)}, u32[]{:S(2)}) collective-permute-start(bf16[8,144,128]{2,1,0:T(8,128)(2,1)S(1)} %get-tuple-element.84), channel_id=1, source_target_pairs={{0,16},{1,17},{2,18},{3,19},{4,20},{5,21},{6,22},{7,23},{8,24},{9,... | collective-permute-start | bytes 884744 | tf_op jit(solution)/shard_map/ppermute | solution.py:977
  43.2 3.4 %collective-permute-start.10 = (bf16[4,64,256]{2,1,0:T(8,128)(2,1)S(1)}, bf16[4,64,256]{2,1,0:T(8,128)(2,1)S(1)}, u32[]{:S(2)}, u32[]{:S(2)}) collective-permute-start(bf16[4,64,256]{2,1,0:T(8,128)(2,1)S(1)} %get-tuple-element.88), channel_id=1, source_target_pairs={{0,1},{1,0},{2,3},{3,2},{4,5},{5,4},{6,7},{7,6},{8,9},{9,8},{10,11... | collective-permute-start | bytes 393224 | tf_op jit(solution)/shard_map/ppermute | solution.py:977
  43.3 3.3 %collective-permute-start.11 = (bf16[4,64,256]{2,1,0:T(8,128)(2,1)S(1)}, bf16[4,64,256]{2,1,0:T(8,128)(2,1)S(1)}, u32[]{:S(2)}, u32[]{:S(2)}) collective-permute-start(bf16[4,64,256]{2,1,0:T(8,128)(2,1)S(1)} %get-tuple-element.89), channel_id=1, source_target_pairs={{0,1},{1,0},{2,3},{3,2},{4,5},{5,4},{6,7},{7,6},{8,9},{9,8},{10,11... | collective-permute-start | bytes 393224 | tf_op jit(solution)/shard_map/ppermute | solution.py:977
  46.7 5.3 %collective-permute-start.12 = (bf16[272,256]{1,0:T(8,128)(2,1)S(1)}, bf16[272,256]{1,0:T(8,128)(2,1)S(1)}, u32[]{:S(2)}, u32[]{:S(2)}) collective-permute-start(bf16[272,256]{1,0:T(8,128)(2,1)S(1)} %get-tuple-element.91), channel_id=1, source_target_pairs={{0,2},{1,3},{2,0},{3,1},{4,6},{5,7},{6,4},{7,5},{8,10},{9,11},{10,... | collective-permute-start | bytes 417800 | tf_op jit(solution)/shard_map/ppermute | solution.py:977
  48.5 6.0 %collective-permute-start.13 = (bf16[272,256]{1,0:T(8,128)(2,1)S(1)}, bf16[272,256]{1,0:T(8,128)(2,1)S(1)}, u32[]{:S(2)}, u32[]{:S(2)}) collective-permute-start(bf16[272,256]{1,0:T(8,128)(2,1)S(1)} %get-tuple-element.92), channel_id=1, source_target_pairs={{0,4},{1,5},{2,6},{3,7},{4,0},{5,1},{6,2},{7,3},{8,12},{9,13},{10,... | collective-permute-start | bytes 417800 | tf_op jit(solution)/shard_map/ppermute | solution.py:977
  49.7 6.6 %collective-permute-start.14 = (bf16[272,256]{1,0:T(8,128)(2,1)S(1)}, bf16[272,256]{1,0:T(8,128)(2,1)S(1)}, u32[]{:S(2)}, u32[]{:S(2)}) collective-permute-start(bf16[272,256]{1,0:T(8,128)(2,1)S(1)} %get-tuple-element.93), channel_id=1, source_target_pairs={{0,6},{1,7},{2,4},{3,5},{4,2},{5,3},{6,0},{7,1},{8,14},{9,15},{10,... | collective-permute-start | bytes 417800 | tf_op jit(solution)/shard_map/ppermute | solution.py:977
  56.4 10.1 %collective-permute-start.15 = (bf16[560,256]{1,0:T(8,128)(2,1)S(1)}, bf16[560,256]{1,0:T(8,128)(2,1)S(1)}, u32[]{:S(2)}, u32[]{:S(2)}) collective-permute-start(bf16[560,256]{1,0:T(8,128)(2,1)S(1)} %get-tuple-element.94.near_ref), channel_id=1, source_target_pairs={{0,16},{1,17},{2,18},{3,19},{4,20},{5,21},{6,22},{7,23},{8,24},{9,... | collective-permute-start | bytes 860168 | tf_op jit(solution)/shard_map/ppermute | solution.py:977
  57.8 8.0 %collective-permute-start.17 = (bf16[144,256]{1,0:T(8,128)(2,1)S(1)}, bf16[144,256]{1,0:T(8,128)(2,1)S(1)}, u32[]{:S(2)}, u32[]{:S(2)}) collective-permute-start(bf16[144,256]{1,0:T(8,128)(2,1)S(1)} %get-tuple-element.95), channel_id=1, source_target_pairs={{0,24},{1,25},{2,26},{3,27},{4,28},{5,29},{6,30},{7,31},{8,16},{9,... | collective-permute-start | bytes 221192 | tf_op jit(solution)/shard_map/ppermute | solution.py:977
  60.4 6.1 %collective-permute-start.16 = (bf16[144,256]{1,0:T(8,128)(2,1)S(1)}, bf16[144,256]{1,0:T(8,128)(2,1)S(1)}, u32[]{:S(2)}, u32[]{:S(2)}) collective-permute-start(bf16[144,256]{1,0:T(8,128)(2,1)S(1)} %get-tuple-element.95), channel_id=1, source_target_pairs={{0,8},{1,9},{2,10},{3,11},{4,12},{5,13},{6,14},{7,15},{8,0},{9,1},... | collective-permute-start | bytes 221192 | tf_op jit(solution)/shard_map/ppermute | solution.py:977

commit v5 on v4

--- a/solution.py
+++ b/solution.py
@@ -133,10 +133,11 @@
 
 def gelu_parts(before):
     c = 0.7978845608028654
+    before = before.astype(bf16)
     square = before * before
-    half = 0.5 * jnp.tanh(before * (c + (c * 0.044715) * square)) + 0.5
+    half = bf16(0.5) * jnp.tanh(before * (bf16(c) + bf16(c * 0.044715) * square)) + bf16(0.5)
     value = before * half
-    slope = half + value * (1.0 - half) * (2.0 * c + (6.0 * c * 0.044715) * square)
+    slope = half + value * (bf16(1.0) - half) * (bf16(2.0 * c) + bf16(6.0 * c * 0.044715) * square)
     return (value, slope)
 
 
@@ -282,8 +283,8 @@
     for at in range(0, expand_ref.shape[1], 256):
         part = slice(at, at + 256)
         value, slope = gelu_parts(dot(normed, expand_ref[:, part]))
-        slope_ref[:, part] = slope.astype(bf16)
-        hidden_sum_ref[:, part] = dot(member, value.astype(bf16)).astype(bf16)
+        slope_ref[:, part] = slope
+        hidden_sum_ref[:, part] = dot(member, value).astype(bf16)
     high = middle.astype(bf16)
     low = (middle - high.astype(f32)).astype(bf16)
     fetches[9].wait()
@@ -323,7 +324,7 @@
 
 
 CHAR_FIRST_SLOT = 144
-CHAR_LAST_SLOT = 64
+CHAR_LAST_SLOT = 48
 
 
 def char_shard(slot, me):
@@ -334,18 +335,18 @@
     width = SLAB
     columns = gradient.shape[1] // width
     size = gradient.shape[0] // len(slots)
-    for number, (ref, place) in enumerate(slots):
+    for number, slot in enumerate(slots):
         first = pl.multiple_of(shard_of(number) * size, size)
         for column in range(columns):
             start = at + column * size
-            ref[place, start : start + size] = gradient[
+            slot[start : start + size] = gradient[
                 pl.ds(first, size), column * width : (column + 1) * width
             ].astype(bf16)
     return at + size * columns
 
 
 def slot_refs(*refs):
-    return [(ref, place) for ref in refs for place in range(ref.shape[0])]
+    return [ref.at[place] for ref in refs for place in range(ref.shape[0])]
 
 
 def char_mlp_back_kernel(
@@ -464,7 +465,6 @@
     grad_hbm,
     keep_ref,
     send_ref,
-    send_more_ref,
     chars_ref,
     languages_ref,
     dmixed,
@@ -503,8 +503,12 @@
     row_sum = jnp.sum(dx, axis=0, keepdims=True)
     normed_t = (normal * gain_attn_ref[...]).astype(bf16).T
     project_grad[...] = dot(normed_t, dqkv[...])
-    targets = slot_refs(keep_ref, send_ref, send_more_ref)
-    at = put_shards(project_grad, targets, lambda slot: char_shard(slot, me), 0)
+    targets = [
+        ref.at[pl.ds(place * CHAR_LAST_SLOT, CHAR_LAST_SLOT)]
+        for ref in (keep_ref, send_ref)
+        for place in range(shards // 2)
+    ]
+    put_shards(project_grad, targets, lambda slot: char_shard(slot, me), 0)
     extra = jnp.concatenate(
         [
             gain_attn_grad,
@@ -513,8 +517,9 @@
         ],
         axis=0,
     ).astype(bf16)
-    for ref, place in targets:
-        ref[place, at : at + 16] = extra
+    at = shards // 2 * CHAR_LAST_SLOT
+    for ref in (keep_ref, send_ref):
+        ref[at : at + 16] = extra
     leave.wait()
 
 
@@ -524,19 +529,17 @@
     gain_attn, project, output, _, _, _ = weights
     _, qkv, probs, _, _, _ = stored
     rows, width = dmiddle.shape
-    half = (shards // 2, CHAR_LAST_SLOT, width)
-    quarter = (shards // 4, CHAR_LAST_SLOT, width)
+    half = (shards // 2 * CHAR_LAST_SLOT + 16, width)
     vmem = pl.BlockSpec(memory_space=pltpu.VMEM)
     hbm = pl.BlockSpec(memory_space=pltpu.HBM)
     return pl.pallas_call(
         functools.partial(char_attn_back_kernel, slots, shards),
         in_specs=[pl.BlockSpec(memory_space=pl.ANY), hbm, hbm] + [vmem] * 8,
-        out_specs=[hbm, vmem, vmem, vmem],
+        out_specs=[hbm, vmem, vmem],
         out_shape=[
             jax.ShapeDtypeStruct((rows, width), f32),
             jax.ShapeDtypeStruct(half, bf16),
-            jax.ShapeDtypeStruct(quarter, bf16),
-            jax.ShapeDtypeStruct(quarter, bf16),
+            jax.ShapeDtypeStruct(half, bf16),
         ],
         scratch_shapes=[
             pltpu.VMEM((rows, width), bf16),
@@ -549,7 +552,7 @@
         ],
         compiler_params=pltpu.CompilerParams(vmem_limit_bytes=16 * MIB),
         cost_estimate=pl.CostEstimate(
-            flops=64 * rows * width * width, bytes_accessed=8 * MIB, transcendentals=0
+            flops=0, bytes_accessed=0, transcendentals=0
         ),
         name="char_attn_back",
     )(
@@ -653,9 +656,9 @@
     for at in range(0, expand_ref.shape[1], 256):
         part = slice(at, at + 256)
         value, bend = gelu_parts(dot(low, expand_ref[:, part]))
-        hidden[:, part] = value.astype(bf16)
+        hidden[:, part] = value
         dhidden = dot_nt(dz_all, shrink_ref[part, :]).astype(bf16)
-        dbefore[:, part] = dhidden * bend.astype(bf16)
+        dbefore[:, part] = dhidden * bend
     result[...] = middle[:length] + dot(hidden[:length], shrink_ref[...])
     leave = pltpu.make_async_copy(result, result_hbm, sem)
     leave.start()
@@ -718,8 +721,8 @@
         + [jnp.zeros((12, SLAB), f32)],
         axis=0,
     ).astype(bf16)
-    for ref, place in targets:
-        ref[place, at : at + 16] = extra
+    for target in targets:
+        target[at : at + 16] = extra
     leave.wait()
 
 
@@ -787,64 +790,90 @@
     return (jnp.where(section == 0, low, high), jnp.where(section == 0, high, low))
 
 
-def first_sum_kernel(word_keep, word_arrived, char_keep, char_arrived, *outs):
-    *word, stay_ref, go_ref = outs
+def word_sum_kernel(keep, arrived, *outs):
+    for place, ref in enumerate(outs):
+        ref[...] = added(keep[place], arrived[place])
+
+
+def word_sum(keep, arrived):
+    return pl.pallas_call(
+        word_sum_kernel,
+        out_shape=[jax.ShapeDtypeStruct((WORD_SLOT, SLAB), bf16)] * 4,
+        compiler_params=pltpu.CompilerParams(vmem_limit_bytes=12 * MIB),
+        name="word_sum",
+    )(keep, arrived)
+
+
+def first_sum_kernel(keep, arrived, stay_ref, go_ref):
     section, _ = position()
-    for place, ref in enumerate(word):
-        ref[...] = added(word_keep[place], word_arrived[place])
     half = SLAB // 2
-    for place in range(char_keep.shape[0]):
-        total = added(char_keep[place], char_arrived[place])
+    for place in range(keep.shape[0]):
+        total = added(keep[place], arrived[place])
         stay_ref[place], go_ref[place] = by_section(section, total[:, :half], total[:, half:])
 
 
-def first_sum(word, char):
-    half = jax.ShapeDtypeStruct(char[0].shape[:2] + (SLAB // 2,), bf16)
-    *pieces, stay, go = pl.pallas_call(
+def first_sum(keep, arrived):
+    half = jax.ShapeDtypeStruct(keep.shape[:2] + (SLAB // 2,), bf16)
+    return pl.pallas_call(
         first_sum_kernel,
-        out_shape=[jax.ShapeDtypeStruct((WORD_SLOT, SLAB), bf16)] * 4 + [half, half],
+        out_shape=[half, half],
         compiler_params=pltpu.CompilerParams(vmem_limit_bytes=12 * MIB),
         name="first_sum",
-    )(*word, *char)
-    return (pieces, stay, go)
-
-
-def second_sum_kernel(char, last_keep, arrived, arrived_more, *outs):
+    )(keep, arrived)
+
+
+def second_sum_kernel(first, keep, arrived, *outs):
+    _, me = position()
     half = SLAB // 2
+    extra = summed(keep[-16:], arrived[-16:])
     for place, out in enumerate(outs):
         at = CHAR_FIRST_SLOT
         for far in range(2):
             entry = 2 * place + far
-            out[:CHAR_FIRST_SLOT, far * half : (far + 1) * half] = char[entry]
-            many = arrived.shape[0]
-            other = arrived[entry] if entry < many else arrived_more[entry - many]
-            out[at : at + CHAR_LAST_SLOT] = added(last_keep[entry], other)
+            columns = slice(far * half, (far + 1) * half)
+            out[:CHAR_FIRST_SLOT, columns] = first[entry]
+            rows = slice(entry * CHAR_LAST_SLOT, (entry + 1) * CHAR_LAST_SLOT)
+            out[at : at + CHAR_LAST_SLOT] = added(keep[rows], arrived[rows])
             at += CHAR_LAST_SLOT
-
-
-def middle_sum_kernel(*refs):
-    *pieces, stay, arrived, word_ref, char_ref = refs
-    word_ref[...] = added(*[ref[...] for ref in pieces])
-    char_ref[...] = added(stay[...], arrived[...])
-
-
-def middle_sum(pieces, stay, arrived):
+            turn = lax.rem(SLAB - char_shard(entry, me) * 16, SLAB)
+            out[-16:, columns] = pltpu.roll(extra, turn, 1)[:, :half].astype(bf16)
+
+
+LONG = pl.CostEstimate(flops=20_000_000_000, bytes_accessed=8 * MIB, transcendentals=0)
+
+
+def total_kernel(*refs):
+    refs[-1][...] = added(*[ref[...] for ref in refs[:-1]])
+
+
+def total_of(*pieces):
     return pl.pallas_call(
-        middle_sum_kernel,
-        out_shape=[
-            jax.ShapeDtypeStruct(pieces[0].shape, bf16),
-            jax.ShapeDtypeStruct(stay.shape, bf16),
-        ],
+        total_kernel,
+        out_shape=jax.ShapeDtypeStruct(pieces[0].shape, bf16),
         compiler_params=pltpu.CompilerParams(vmem_limit_bytes=12 * MIB),
-        cost_estimate=pl.CostEstimate(
-            flops=20_000_000_000, bytes_accessed=8 * MIB, transcendentals=0
-        ),
-        name="middle_sum",
-    )(*pieces, stay, arrived)
+        cost_estimate=LONG,
+        name="total",
+    )(*pieces)
+
+
+def pair_kernel(one, other, _, out):
+    out[...] = added(one[...], other[...])
+
+
+def pair_of(one, other, after):
+    vmem = pl.BlockSpec(memory_space=pltpu.VMEM)
+    return pl.pallas_call(
+        pair_kernel,
+        in_specs=[vmem, vmem, pl.BlockSpec(memory_space=pl.ANY)],
+        out_shape=jax.ShapeDtypeStruct(one.shape, bf16),
+        compiler_params=pltpu.CompilerParams(vmem_limit_bytes=12 * MIB),
+        cost_estimate=LONG,
+        name="pair",
+    )(one, other, after)
 
 
 def second_sum(first, last):
-    rows = CHAR_FIRST_SLOT + 2 * CHAR_LAST_SLOT
+    rows = CHAR_FIRST_SLOT + 2 * CHAR_LAST_SLOT + 16
     return pl.pallas_call(
         second_sum_kernel,
         out_shape=[jax.ShapeDtypeStruct((rows, SLAB), bf16)] * 4,
@@ -865,6 +894,7 @@
         total = added(*[ref[:CHAR_FIRST_SLOT, columns] for ref in char])
         out[at : at + FOLD, :half] = total[:FOLD]
         out[at : at + FOLD, half:] = total[CHAR_FIRST_SLOT - FOLD :]
+        out[at : at + 16, half:] = added(*[ref[-16:, columns] for ref in char])
         first = CHAR_FIRST_SLOT + far * CHAR_LAST_SLOT
         at += FOLD
         out[at : at + CHAR_LAST_SLOT] = added(
@@ -892,15 +922,16 @@
     halves = by_section(section, own, section_ref[:word_rows].astype(f32))
     half = SLAB // 2
 
-    def unfold(near, far):
-        total = summed(near[word_rows : word_rows + FOLD], far[:FOLD])
+    mine_too = summed(near_ref[word_rows : word_rows + FOLD], high_ref[:FOLD])
+    theirs = summed(section_ref[word_rows : word_rows + FOLD], both_ref[:FOLD])
+
+    def unfold(total):
         return jnp.concatenate(
             [total[:, :half], total[2 * FOLD - CHAR_FIRST_SLOT :, half:]], axis=0
         )
 
-    first = jnp.concatenate(
-        by_section(section, unfold(near_ref, high_ref), unfold(section_ref, both_ref)), axis=1
-    )
+    first = jnp.concatenate(by_section(section, unfold(mine_too), unfold(theirs)), axis=1)
+    extra = mine_too[:16, half:] + theirs[:16, half:]
     last = summed(
         near_ref[word_rows + FOLD :],
         section_ref[word_rows + FOLD :],
@@ -936,11 +967,9 @@
                 ref[:, column * SLAB : (column + 1) * SLAB] = char[at : at + size]
                 at += size
     size = gain_attn_ref.shape[1]
-    extra = last[at : at + 16]
-    turned = mine(extra, size)
-    gain_attn_ref[...] = turned[0:1]
-    gain_mlp_ref[...] = turned[1:2]
-    table_ref[...] = turned[8:16]
+    gain_attn_ref[...] = extra[0:1, :size]
+    gain_mlp_ref[...] = extra[1:2, :size]
+    table_ref[...] = extra[8:16, :size]
     at = 0
     for ref in (w_input_ref, w_project_ref, w_output_ref, w_expand_ref, w_shrink_ref):
         size = ref.shape[0]
@@ -1004,14 +1033,13 @@
     result, dpooled, keep, send = word_group(
         (pooled,) + others, (cot, cot_far), word_input, word_weights, shards
     )
-    word = (keep, exchange(send, 0, CORE))
+    word = plane_exchange(word_sum(keep, exchange(send, 0, CORE)))
     dmiddle, gain_mlp_grad, keep, send = char_mlp_back(
         counts, char_weights, dpooled, stored, slots, shards
     )
-    pieces, stay, go = first_sum(word, (keep, exchange(send, 0, CORE)))
-    word = plane_exchange(pieces)
+    stay, go = first_sum(keep, exchange(send, 0, CORE))
     arrived = exchange(go, 1, 0)
-    chars_grad, keep, *sends = char_attn_back(
+    chars_grad, keep, send = char_attn_back(
         languages,
         chars,
         language_table,
@@ -1023,8 +1051,9 @@
         shards,
         stay,
     )
-    last = (keep,) + tuple(exchange(send, 0, CORE) for send in sends)
-    word, first = middle_sum(word, stay, arrived)
+    last = (keep, exchange(send, 0, CORE))
+    word = total_of(*word)
+    first = pair_of(stay, arrived, word)
     char = plane_exchange(second_sum(first, last))
     near, far = plane_sum(word, char)
     arrived = (exchange(near, 1, 0), exchange(far, 0, FAR), exchange(far, 1, FAR))

time: 67.7 us -> 65 us (0.960)
  starting transfers between devices: 23 us -> 21.2 us
  Pallas kernels: 25.5 us -> 24.4 us
    ppermute x18 -> x17, starting transfers between devices: 23 us -> 21.2 us  [exchange(): return lax.ppermute(value, ('section', 'dp'), pairs)]
    pallas_call x1, Pallas kernels: 7.36 us -> 6.46 us  [char_forward(): pl.pallas_call(functools.partial(char_forward_kernel, slots), in_specs=[h...]
    ppermute x18 -> x17, waiting for transfers between devices: 18 us -> 18.1 us  [exchange(): return lax.ppermute(value, ('section', 'dp'), pairs)]
  transfers between devices with their start and end apart: 18 -> 17, of which waited for: 9 -> 9; matrix products, arithmetic and copies ran while one was open for 0% -> 0% of each run, Pallas kernels for 25% -> 25%
where the time goes in v5:
time: 65 us; the launch traced here: 64.8 us
  Pallas kernels  24.4 us (38%)
  starting transfers between devices  21.2 us (33%)
  waiting for transfers between devices  18.1 us (28%)
  between operations  1.09 us (2%)
    ppermute x17, starting transfers between devices, exchange(): return lax.ppermute(value, ('section', 'dp'), pairs)  21.2 us
    ppermute x17, waiting for transfers between devices, exchange(): return lax.ppermute(value, ('section', 'dp'), pairs)  18.1 us
    pallas_call x1, Pallas kernels, word_group(): pl.pallas_call(functools.partial(word_kernel, length, shards), in_specs=[...  7.1 us
    pallas_call x1, Pallas kernels, char_forward(): pl.pallas_call(functools.partial(char_forward_kernel, slots), in_specs=[h...  6.46 us
    pallas_call x1, Pallas kernels, char_attn_back(): pl.pallas_call(functools.partial(char_attn_back_kernel, slots, shards), i...  5.2 us
    pallas_call x1, Pallas kernels, char_mlp_back(): pl.pallas_call(functools.partial(char_mlp_back_kernel, slots, shards), in...  3.87 us
  transfers between devices with their start and end apart: 17, of which 9 were waited for; matrix products, arithmetic and copies ran while one was open for 0% of the time, Pallas kernels for 25%

profile of v5, /device:TPU:0, one launch (start us, length us, event | category | flops | bytes accessed | tf_op | source)
XLA Modules:
  0.0 64.8 jit_solution(11862880139580623953)
XLA Ops:
  0.6 4.1 %collective-permute-start.3 = (bf16[2,64,512]{2,1,0:T(8,128)(2,1)}, bf16[2,64,512]{2,1,0:T(8,128)(2,1)S(1)}, u32[]{:S(2)}, u32[]{:S(2)}) collective-permute-start(bf16[2,64,512]{2,1,0:T(8,128)(2,1)} %bitcast.15), channel_id=1, source_target_pairs={{0,8},{1,9},{2,10},{3,11},{4,12},{5,13},{6,14},{7,15},{8,0},{9,1},... | collective-permute-start | bytes 393224 | tf_op jit(solution)/shard_map/ppermute | solution.py:1006
  4.8 0.0 copy-start.10
  4.8 0.0 copy-start.11
  4.8 0.0 copy-start.12
  4.8 0.0 copy-start.13
  4.8 6.5 %char_forward.1 = (bf16[64,256]{1,0:T(8,128)(2,1)S(1)}, bf16[64,1024]{1,0:T(8,128)(2,1)S(1)}, bf16[1024,768]{1,0:T(8,128)(2,1)S(1)}, f32[16,4096]{1,0:T(8,128)S(...) custom-call(bf16[2,1024,256]{2,1,0:T(8,128)(2,1)} %bitcast.21, ...), custom_call_target="tpu_custom_call" | custom-call | flops 4294967296 | bytes 8388608 | tf_op jit(solution)/shard_map/char_forward/pallas_call | solution.py:302
  11.3 0.1 collective-permute-start
  11.4 1.8 %collective-permute-start.1 = (bf16[64,256]{1,0:T(8,128)(2,1)S(1)}, bf16[64,256]{1,0:T(8,128)(2,1)S(1)}, u32[]{:S(2)}, u32[]{:S(2)}) collective-permute-start(bf16[64,256]{1,0:T(8,128)(2,1)S(1)} %get-tuple-element.60.own_ref), channel_id=1, source_target_pairs={{0,16},{1,17},{2,18},{3,19},{4,20},{5,21},{6,22},{7,23},{8,24},{9,... | collective-permute-start | bytes 98312 | tf_op jit(solution)/shard_map/ppermute | solution.py:1006
  13.2 2.6 %collective-permute-start.2 = (bf16[64,256]{1,0:T(8,128)(2,1)S(1)}, bf16[64,256]{1,0:T(8,128)(2,1)S(1)}, u32[]{:S(2)}, u32[]{:S(2)}) collective-permute-start(bf16[64,256]{1,0:T(8,128)(2,1)S(1)} %get-tuple-element.60.own_ref), channel_id=1, source_target_pairs={{0,24},{1,25},{2,26},{3,27},{4,28},{5,29},{6,30},{7,31},{8,16},{9,... | collective-permute-start | bytes 98312 | tf_op jit(solution)/shard_map/ppermute | solution.py:1006
  15.7 0.7 %collective-permute-done.far_ref = bf16[64,256]{1,0:T(8,128)(2,1)S(1)} collective-permute-done((bf16[64,256]{1,0:T(8,128)(2,1)S(1)}, bf16[64,256]{1,0:T(8,128)(2,1)S(1)}, u32[]{:S(2)}, u32[]{:S(2)}) %collective-permute-start) | collective-permute-done | bytes 32800 | tf_op jit(solution)/shard_map/ppermute | solution.py:1006
  16.5 0.0 collective-permute-done.1.section_ref
  16.5 2.4 %collective-permute-done.2.both_ref = bf16[64,256]{1,0:T(8,128)(2,1)S(1)} collective-permute-done((bf16[64,256]{1,0:T(8,128)(2,1)S(1)}, bf16[64,256]{1,0:T(8,128)(2,1)S(1)}, u32[]{:S(2)}, u32[]{:S(2)}) %collective-permute-start.2) | collective-permute-done | bytes 32800 | tf_op jit(solution)/shard_map/ppermute | solution.py:1006
  18.9 0.0 collective-permute-done.3.cot_far_ref
  18.9 0.0 copy-done.4
  18.9 0.0 copy-done.5
  18.9 0.0 copy-done.6
  18.9 0.0 copy-done.7
  18.9 0.0 copy-done.10
  18.9 0.0 copy-done.11
  18.9 0.0 copy-start.8
  19.0 0.0 copy-start.9
  19.0 0.0 copy-start.14
  19.0 7.1 %word_group.1 = (f32[64,512]{1,0:T(8,128)}, bf16[64,256]{1,0:T(8,128)(2,1)S(1)}, bf16[4,416,256]{2,1,0:T(8,128)(2,1)S(1)}, bf16[4,416,256]{2,1,0:T(8,128)(2,1)S(1)}) custom-call(bf16[64,256]{1,0:T(8,128)(2,1)S(1)} %get-tuple-element.60.own_ref, bf16[64,256]{1,0:T(8,128)(2,1)S(1)} %collective-permute-done.far_ref, ...), custom_call_target="tpu_custom_call" | custom-call | flops 6710886400 | bytes 8388608 | tf_op jit(solution)/shard_map/word_group/pallas_call | solution.py:738
  26.1 0.1 collective-permute-start.5
  26.2 3.9 %char_mlp_back.1 = (f32[1024,256]{1,0:T(8,128)S(1)}, f32[8,256]{1,0:T(8,128)S(1)}, bf16[8,144,256]{2,1,0:T(8,128)(2,1)S(1)}, bf16[8,144,256]{2,1,0:T(8,128)(2,1)S(1)}) custom-call(s32[2,1,64]{2,1,0:T(1,128)} %counts_hbm.3, f32[1,256]{1,0:T(1,128)S(1)} %bitcast.20, bf16[256,1024]{1,0:T(8,128)(2,1)S(1)} %copy-done.8, bf16[1024,256]{1,0:T(8,128)(2,1)S(1)} %copy-done.9, ...), custom_call_target="tpu_custom_call" | custom-call | flops 4294967296 | bytes 8388608 | tf_op jit(solution)/shard_map/char_mlp_back/pallas_call | solution.py:424
  30.1 0.0 copy-start
  30.1 0.0 copy-start.1
  30.1 0.0 copy-start.2
  30.1 0.0 copy-start.3
  30.1 0.5 collective-permute-start.4
  30.7 0.0 collective-permute-done.5.arrived
  30.7 0.2 word_sum.1
  30.9 1.6 %collective-permute-start.6 = (bf16[416,256]{1,0:T(8,128)(2,1)S(1)}, bf16[416,256]{1,0:T(8,128)(2,1)S(1)}, u32[]{:S(2)}, u32[]{:S(2)}) collective-permute-start(bf16[416,256]{1,0:T(8,128)(2,1)S(1)} %get-tuple-element.78), channel_id=1, source_target_pairs={{0,2},{1,3},{2,0},{3,1},{4,6},{5,7},{6,4},{7,5},{8,10},{9,11},{10,... | collective-permute-start | bytes 638984 | tf_op jit(solution)/shard_map/ppermute | solution.py:1006
  32.4 1.6 %collective-permute-start.7 = (bf16[416,256]{1,0:T(8,128)(2,1)S(1)}, bf16[416,256]{1,0:T(8,128)(2,1)S(1)}, u32[]{:S(2)}, u32[]{:S(2)}) collective-permute-start(bf16[416,256]{1,0:T(8,128)(2,1)S(1)} %get-tuple-element.79), channel_id=1, source_target_pairs={{0,4},{1,5},{2,6},{3,7},{4,0},{5,1},{6,2},{7,3},{8,12},{9,13},{10,... | collective-permute-start | bytes 638984 | tf_op jit(solution)/shard_map/ppermute | solution.py:1006
  34.0 0.4 collective-permute-start.8
  34.4 0.0 collective-permute-done.4.arrived
  34.4 0.2 first_sum.1
  34.6 0.4 collective-permute-start.9
  35.0 0.0 copy-done
  35.0 0.0 copy-done.2
  35.0 5.2 %char_attn_back.1 = (f32[1024,256]{1,0:T(8,128)}, bf16[400,256]{1,0:T(8,128)(2,1)S(1)}, bf16[400,256]{1,0:T(8,128)(2,1)S(1)}) custom-call(bf16[8,144,128]{2,1,0:T(8,128)(2,1)S(1)} %get-tuple-element.69._.one, bf16[2,1024,256]{2,1,0:T(8,128)(2,1)} %bitcast.22, s32[1,2]{1,0:T(1,128)} %bitcast.24, bf16[8,256]{1,0:T(8,128)(2,1)S(1)} %copy-done.2, ...), custom_call_target="tpu_custom_call" | custom-call | tf_op jit(solution)/shard_map/char_attn_back/pallas_call | solution.py:535
  40.2 0.1 collective-permute-start.10
  40.3 0.0 collective-permute-done.6.refs_1_
  40.3 0.3 collective-permute-done.7.refs_2_
  40.6 3.3 %collective-permute-done.8.refs_3_ = bf16[416,256]{1,0:T(8,128)(2,1)S(1)} collective-permute-done((bf16[416,256]{1,0:T(8,128)(2,1)S(1)}, bf16[416,256]{1,0:T(8,128)(2,1)S(1)}, u32[]{:S(2)}, u32[]{:S(2)}) %collective-permute-start.8) | collective-permute-done | bytes 213024 | tf_op jit(solution)/shard_map/ppermute | solution.py:1006
  43.9 0.1 total.1._.refs_0_
  44.0 0.0 collective-permute-done.9.other
  44.0 0.1 pair.1.first
  44.1 0.0 collective-permute-done.10.arrived
  44.1 0.1 second_sum.1
  44.2 1.6 %collective-permute-start.11 = (bf16[256,256]{1,0:T(8,128)(2,1)S(1)}, bf16[256,256]{1,0:T(8,128)(2,1)S(1)}, u32[]{:S(2)}, u32[]{:S(2)}) collective-permute-start(bf16[256,256]{1,0:T(8,128)(2,1)S(1)} %get-tuple-element.85), channel_id=1, source_target_pairs={{0,2},{1,3},{2,0},{3,1},{4,6},{5,7},{6,4},{7,5},{8,10},{9,11},{10,... | collective-permute-start | bytes 393224 | tf_op jit(solution)/shard_map/ppermute | solution.py:1006
  45.8 1.6 %collective-permute-start.12 = (bf16[256,256]{1,0:T(8,128)(2,1)S(1)}, bf16[256,256]{1,0:T(8,128)(2,1)S(1)}, u32[]{:S(2)}, u32[]{:S(2)}) collective-permute-start(bf16[256,256]{1,0:T(8,128)(2,1)S(1)} %get-tuple-element.86), channel_id=1, source_target_pairs={{0,4},{1,5},{2,6},{3,7},{4,0},{5,1},{6,2},{7,3},{8,12},{9,13},{10,... | collective-permute-start | bytes 393224 | tf_op jit(solution)/shard_map/ppermute | solution.py:1006
  47.4 0.4 collective-permute-start.13
  47.8 2.0 %collective-permute-done.11.refs_2_ = bf16[256,256]{1,0:T(8,128)(2,1)S(1)} collective-permute-done((bf16[256,256]{1,0:T(8,128)(2,1)S(1)}, bf16[256,256]{1,0:T(8,128)(2,1)S(1)}, u32[]{:S(2)}, u32[]{:S(2)}) %collective-permute-start.11) | collective-permute-done | bytes 131104 | tf_op jit(solution)/shard_map/ppermute | solution.py:1006
  49.7 1.5 %collective-permute-done.12.refs_3_ = bf16[256,256]{1,0:T(8,128)(2,1)S(1)} collective-permute-done((bf16[256,256]{1,0:T(8,128)(2,1)S(1)}, bf16[256,256]{1,0:T(8,128)(2,1)S(1)}, u32[]{:S(2)}, u32[]{:S(2)}) %collective-permute-start.12) | collective-permute-done | bytes 131104 | tf_op jit(solution)/shard_map/ppermute | solution.py:1006
  51.2 2.1 %collective-permute-done.13.refs_4_ = bf16[256,256]{1,0:T(8,128)(2,1)S(1)} collective-permute-done((bf16[256,256]{1,0:T(8,128)(2,1)S(1)}, bf16[256,256]{1,0:T(8,128)(2,1)S(1)}, u32[]{:S(2)}, u32[]{:S(2)}) %collective-permute-start.13) | collective-permute-done | bytes 131104 | tf_op jit(solution)/shard_map/ppermute | solution.py:1006
  53.4 0.1 plane_sum.1
  53.5 0.6 collective-permute-start.14
  54.1 2.8 %collective-permute-start.15 = (bf16[128,256]{1,0:T(8,128)(2,1)S(1)}, bf16[128,256]{1,0:T(8,128)(2,1)S(1)}, u32[]{:S(2)}, u32[]{:S(2)}) collective-permute-start(bf16[128,256]{1,0:T(8,128)(2,1)S(1)} %get-tuple-element.89), channel_id=1, source_target_pairs={{0,8},{1,9},{2,10},{3,11},{4,12},{5,13},{6,14},{7,15},{8,0},{9,1},... | collective-permute-start | bytes 196616 | tf_op jit(solution)/shard_map/ppermute | solution.py:1006
  56.9 1.0 %collective-permute-start.16 = (bf16[128,256]{1,0:T(8,128)(2,1)S(1)}, bf16[128,256]{1,0:T(8,128)(2,1)S(1)}, u32[]{:S(2)}, u32[]{:S(2)}) collective-permute-start(bf16[128,256]{1,0:T(8,128)(2,1)S(1)} %get-tuple-element.89), channel_id=1, source_target_pairs={{0,24},{1,25},{2,26},{3,27},{4,28},{5,29},{6,30},{7,31},{8,16},{9,... | collective-permute-start | bytes 196616 | tf_op jit(solution)/shard_map/ppermute | solution.py:1006
  57.9 3.1 %collective-permute-done.15.high_ref = bf16[128,256]{1,0:T(8,128)(2,1)S(1)} collective-permute-done((bf16[128,256]{1,0:T(8,128)(2,1)S(1)}, bf16[128,256]{1,0:T(8,128)(2,1)S(1)}, u32[]{:S(2)}, u32[]{:S(2)}) %collective-permute-start.15) | collective-permute-done | bytes 65568 | tf_op jit(solution)/shard_map/ppermute | solution.py:1006
  61.1 2.6 %collective-permute-done.16.both_ref = bf16[128,256]{1,0:T(8,128)(2,1)S(1)} collective-permute-done((bf16[128,256]{1,0:T(8,128)(2,1)S(1)}, bf16[128,256]{1,0:T(8,128)(2,1)S(1)}, u32[]{:S(2)}, u32[]{:S(2)}) %collective-permute-start.16) | collective-permute-done | bytes 65568 | tf_op jit(solution)/shard_map/ppermute | solution.py:1006
  63.6 0.0 collective-permute-done.14.section_ref
  63.6 1.0 %last_sum.1 = (f32[8,16]{1,0:T(8,128)}, f32[1,16]{1,0:T(1,128)}, f32[16,768]{1,0:T(8,128)}, f32[16,256]{1,0:T(8,128)}, f32[1,16]{1,0:T(1,128)}, /*index=5*/f32[1...) custom-call(bf16[544,256]{1,0:T(8,128)(2,1)S(1)} %get-tuple-element., ...), custom_call_target="tpu_custom_call" | custom-call | tf_op jit(solution)/shard_map/last_sum/pallas_call | solution.py:991
  (11 shorter events, 0.0 us)
Async XLA Ops:
  0.6 18.2 %collective-permute-start.3 = (bf16[2,64,512]{2,1,0:T(8,128)(2,1)}, bf16[2,64,512]{2,1,0:T(8,128)(2,1)S(1)}, u32[]{:S(2)}, u32[]{:S(2)}) collective-permute-start(bf16[2,64,512]{2,1,0:T(8,128)(2,1)} %bitcast.15), channel_id=1, source_target_pairs={{0,8},{1,9},{2,10},{3,11},{4,12},{5,13},{6,14},{7,15},{8,0},{9,1},... | collective-permute-start | bytes 393224 | tf_op jit(solution)/shard_map/ppermute | solution.py:1006
  4.8 14.1 %copy-start.4 = (bf16[512,2048]{1,0:T(8,128)(2,1)S(1)}, bf16[512,2048]{1,0:T(8,128)(2,1)}, u32[]{:S(2)}) copy-start(bf16[512,2048]{1,0:T(8,128)(2,1)} %expand_ref.2) | copy-start | bytes 6291460
  4.8 14.1 %copy-start.5 = (bf16[2048,512]{1,0:T(8,128)(2,1)S(1)}, bf16[2048,512]{1,0:T(8,128)(2,1)}, u32[]{:S(2)}) copy-start(bf16[2048,512]{1,0:T(8,128)(2,1)} %shrink_ref.2) | copy-start | bytes 6291460
  4.8 14.1 %copy-start.6 = (bf16[512,1536]{1,0:T(8,128)(2,1)S(1)}, bf16[512,1536]{1,0:T(8,128)(2,1)}, u32[]{:S(2)}) copy-start(bf16[512,1536]{1,0:T(8,128)(2,1)} %project_ref.2) | copy-start | bytes 4718596
  4.8 14.1 %copy-start.7 = (bf16[512,512]{1,0:T(8,128)(2,1)S(1)}, bf16[512,512]{1,0:T(8,128)(2,1)}, u32[]{:S(2)}) copy-start(bf16[512,512]{1,0:T(8,128)(2,1)} %output_ref.2) | copy-start | bytes 1572868
  4.8 14.2 %copy-start.10 = (bf16[256,512]{1,0:T(8,128)(2,1)S(1)}, bf16[256,512]{1,0:T(8,128)(2,1)}, u32[]{:S(2)}) copy-start(bf16[256,512]{1,0:T(8,128)(2,1)} %input_ref.1) | copy-start | bytes 786436
  4.8 14.2 %copy-start.11 = (bf16[2,1,64,512]{3,2,1,0:T(8,128)(2,1)S(1)}, bf16[2,1,64,512]{3,2,1,0:T(8,128)(2,1)}, u32[]{:S(2)}) copy-start(bf16[2,1,64,512]{3,2,1,0:T(8,128)(2,1)} %param.35) | copy-start | bytes 393220
  4.8 14.2 %copy-start.12 = (f32[512]{0:T(512)S(1)}, f32[512]{0:T(512)}, u32[]{:S(2)}) copy-start(f32[512]{0:T(512)} %param.29) | copy-start | bytes 6148
  4.8 14.2 %copy-start.13 = (f32[512]{0:T(512)S(1)}, f32[512]{0:T(512)}, u32[]{:S(2)}) copy-start(f32[512]{0:T(512)} %param.32) | copy-start | bytes 6148
  11.3 5.2 %collective-permute-start = (bf16[64,256]{1,0:T(8,128)(2,1)S(1)}, bf16[64,256]{1,0:T(8,128)(2,1)S(1)}, u32[]{:S(2)}, u32[]{:S(2)}) collective-permute-start(bf16[64,256]{1,0:T(8,128)(2,1)S(1)} %get-tuple-element.60.own_ref), channel_id=1, source_target_pairs={{0,8},{1,9},{2,10},{3,11},{4,12},{5,13},{6,14},{7,15},{8,0},{9,1},... | collective-permute-start | bytes 98312 | tf_op jit(solution)/shard_map/ppermute | solution.py:1006
  11.4 5.1 %collective-permute-start.1 = (bf16[64,256]{1,0:T(8,128)(2,1)S(1)}, bf16[64,256]{1,0:T(8,128)(2,1)S(1)}, u32[]{:S(2)}, u32[]{:S(2)}) collective-permute-start(bf16[64,256]{1,0:T(8,128)(2,1)S(1)} %get-tuple-element.60.own_ref), channel_id=1, source_target_pairs={{0,16},{1,17},{2,18},{3,19},{4,20},{5,21},{6,22},{7,23},{8,24},{9,... | collective-permute-start | bytes 98312 | tf_op jit(solution)/shard_map/ppermute | solution.py:1006
  13.2 5.7 %collective-permute-start.2 = (bf16[64,256]{1,0:T(8,128)(2,1)S(1)}, bf16[64,256]{1,0:T(8,128)(2,1)S(1)}, u32[]{:S(2)}, u32[]{:S(2)}) collective-permute-start(bf16[64,256]{1,0:T(8,128)(2,1)S(1)} %get-tuple-element.60.own_ref), channel_id=1, source_target_pairs={{0,24},{1,25},{2,26},{3,27},{4,28},{5,29},{6,30},{7,31},{8,16},{9,... | collective-permute-start | bytes 98312 | tf_op jit(solution)/shard_map/ppermute | solution.py:1006
  18.9 7.2 %copy-start.8 = (bf16[256,1024]{1,0:T(8,128)(2,1)S(1)}, bf16[256,1024]{1,0:T(8,128)(2,1)}, u32[]{:S(2)}) copy-start(bf16[256,1024]{1,0:T(8,128)(2,1)} %expand_ref.3) | copy-start | bytes 1572868
  19.0 7.2 %copy-start.9 = (bf16[1024,256]{1,0:T(8,128)(2,1)S(1)}, bf16[1024,256]{1,0:T(8,128)(2,1)}, u32[]{:S(2)}) copy-start(bf16[1024,256]{1,0:T(8,128)(2,1)} %shrink_ref.3) | copy-start | bytes 1572868
  19.0 7.2 %copy-start.14 = (f32[256]{0:T(256)S(1)}, f32[256]{0:T(256)}, u32[]{:S(2)}) copy-start(f32[256]{0:T(256)} %param.25) | copy-start | bytes 3076
  26.1 4.6 %collective-permute-start.5 = (bf16[4,416,256]{2,1,0:T(8,128)(2,1)S(1)}, bf16[4,416,256]{2,1,0:T(8,128)(2,1)S(1)}, u32[]{:S(2)}, u32[]{:S(2)}) collective-permute-start(bf16[4,416,256]{2,1,0:T(8,128)(2,1)S(1)} %get-tuple-element.76), channel_id=1, source_target_pairs={{0,1},{1,0},{2,3},{3,2},{4,5},{5,4},{6,7},{7,6},{8,9},{9,8},{10,11... | collective-permute-start | bytes 2555912 | tf_op jit(solution)/shard_map/ppermute | solution.py:1006
  30.1 4.9 %copy-start = (bf16[256,768]{1,0:T(8,128)(2,1)S(1)}, bf16[256,768]{1,0:T(8,128)(2,1)}, u32[]{:S(2)}) copy-start(bf16[256,768]{1,0:T(8,128)(2,1)} %project_ref.3) | copy-start | bytes 1179652
  30.1 4.9 %copy-start.1 = (bf16[256,256]{1,0:T(8,128)(2,1)S(1)}, bf16[256,256]{1,0:T(8,128)(2,1)}, u32[]{:S(2)}) copy-start(bf16[256,256]{1,0:T(8,128)(2,1)} %output_ref.3) | copy-start | bytes 393220
  30.1 4.9 %copy-start.2 = (bf16[8,256]{1,0:T(8,128)(2,1)S(1)}, bf16[8,256]{1,0:T(8,128)(2,1)}, u32[]{:S(2)}) copy-start(bf16[8,256]{1,0:T(8,128)(2,1)} %table_ref.1) | copy-start | bytes 12292
  30.1 4.9 %copy-start.3 = (f32[256]{0:T(256)S(1)}, f32[256]{0:T(256)}, u32[]{:S(2)}) copy-start(f32[256]{0:T(256)} %param.22) | copy-start | bytes 3076
  30.1 4.3 %collective-permute-start.4 = (bf16[8,144,256]{2,1,0:T(8,128)(2,1)S(1)}, bf16[8,144,256]{2,1,0:T(8,128)(2,1)S(1)}, u32[]{:S(2)}, u32[]{:S(2)}) collective-permute-start(bf16[8,144,256]{2,1,0:T(8,128)(2,1)S(1)} %get-tuple-element.68), channel_id=1, source_target_pairs={{0,1},{1,0},{2,3},{3,2},{4,5},{5,4},{6,7},{7,6},{8,9},{9,8},{10,11... | collective-permute-start | bytes 1769480 | tf_op jit(solution)/shard_map/ppermute | solution.py:1006
  30.9 9.4 %collective-permute-start.6 = (bf16[416,256]{1,0:T(8,128)(2,1)S(1)}, bf16[416,256]{1,0:T(8,128)(2,1)S(1)}, u32[]{:S(2)}, u32[]{:S(2)}) collective-permute-start(bf16[416,256]{1,0:T(8,128)(2,1)S(1)} %get-tuple-element.78), channel_id=1, source_target_pairs={{0,2},{1,3},{2,0},{3,1},{4,6},{5,7},{6,4},{7,5},{8,10},{9,11},{10,... | collective-permute-start | bytes 638984 | tf_op jit(solution)/shard_map/ppermute | solution.py:1006
  32.4 8.2 %collective-permute-start.7 = (bf16[416,256]{1,0:T(8,128)(2,1)S(1)}, bf16[416,256]{1,0:T(8,128)(2,1)S(1)}, u32[]{:S(2)}, u32[]{:S(2)}) collective-permute-start(bf16[416,256]{1,0:T(8,128)(2,1)S(1)} %get-tuple-element.79), channel_id=1, source_target_pairs={{0,4},{1,5},{2,6},{3,7},{4,0},{5,1},{6,2},{7,3},{8,12},{9,13},{10,... | collective-permute-start | bytes 638984 | tf_op jit(solution)/shard_map/ppermute | solution.py:1006
  34.0 9.8 %collective-permute-start.8 = (bf16[416,256]{1,0:T(8,128)(2,1)S(1)}, bf16[416,256]{1,0:T(8,128)(2,1)S(1)}, u32[]{:S(2)}, u32[]{:S(2)}) collective-permute-start(bf16[416,256]{1,0:T(8,128)(2,1)S(1)} %get-tuple-element.80), channel_id=1, source_target_pairs={{0,6},{1,7},{2,4},{3,5},{4,2},{5,3},{6,0},{7,1},{8,14},{9,15},{10,... | collective-permute-start | bytes 638984 | tf_op jit(solution)/shard_map/ppermute | solution.py:1006
  34.6 9.4 %collective-permute-start.9 = (bf16[8,144,128]{2,1,0:T(8,128)(2,1)S(1)}, bf16[8,144,128]{2,1,0:T(8,128)(2,1)S(1)}, u32[]{:S(2)}, u32[]{:S(2)}) collective-permute-start(bf16[8,144,128]{2,1,0:T(8,128)(2,1)S(1)} %get-tuple-element.81), channel_id=1, source_target_pairs={{0,16},{1,17},{2,18},{3,19},{4,20},{5,21},{6,22},{7,23},{8,24},{9,... | collective-permute-start | bytes 884744 | tf_op jit(solution)/shard_map/ppermute | solution.py:1006
  40.2 3.8 %collective-permute-start.10 = (bf16[400,256]{1,0:T(8,128)(2,1)S(1)}, bf16[400,256]{1,0:T(8,128)(2,1)S(1)}, u32[]{:S(2)}, u32[]{:S(2)}) collective-permute-start(bf16[400,256]{1,0:T(8,128)(2,1)S(1)} %get-tuple-element.83), channel_id=1, source_target_pairs={{0,1},{1,0},{2,3},{3,2},{4,5},{5,4},{6,7},{7,6},{8,9},{9,8},{10,11... | collective-permute-start | bytes 614408 | tf_op jit(solution)/shard_map/ppermute | solution.py:1006
  44.2 5.5 %collective-permute-start.11 = (bf16[256,256]{1,0:T(8,128)(2,1)S(1)}, bf16[256,256]{1,0:T(8,128)(2,1)S(1)}, u32[]{:S(2)}, u32[]{:S(2)}) collective-permute-start(bf16[256,256]{1,0:T(8,128)(2,1)S(1)} %get-tuple-element.85), channel_id=1, source_target_pairs={{0,2},{1,3},{2,0},{3,1},{4,6},{5,7},{6,4},{7,5},{8,10},{9,11},{10,... | collective-permute-start | bytes 393224 | tf_op jit(solution)/shard_map/ppermute | solution.py:1006
  45.8 5.4 %collective-permute-start.12 = (bf16[256,256]{1,0:T(8,128)(2,1)S(1)}, bf16[256,256]{1,0:T(8,128)(2,1)S(1)}, u32[]{:S(2)}, u32[]{:S(2)}) collective-permute-start(bf16[256,256]{1,0:T(8,128)(2,1)S(1)} %get-tuple-element.86), channel_id=1, source_target_pairs={{0,4},{1,5},{2,6},{3,7},{4,0},{5,1},{6,2},{7,3},{8,12},{9,13},{10,... | collective-permute-start | bytes 393224 | tf_op jit(solution)/shard_map/ppermute | solution.py:1006
  47.4 6.0 %collective-permute-start.13 = (bf16[256,256]{1,0:T(8,128)(2,1)S(1)}, bf16[256,256]{1,0:T(8,128)(2,1)S(1)}, u32[]{:S(2)}, u32[]{:S(2)}) collective-permute-start(bf16[256,256]{1,0:T(8,128)(2,1)S(1)} %get-tuple-element.87), channel_id=1, source_target_pairs={{0,6},{1,7},{2,4},{3,5},{4,2},{5,3},{6,0},{7,1},{8,14},{9,15},{10,... | collective-permute-start | bytes 393224 | tf_op jit(solution)/shard_map/ppermute | solution.py:1006
  53.5 10.2 %collective-permute-start.14 = (bf16[544,256]{1,0:T(8,128)(2,1)S(1)}, bf16[544,256]{1,0:T(8,128)(2,1)S(1)}, u32[]{:S(2)}, u32[]{:S(2)}) collective-permute-start(bf16[544,256]{1,0:T(8,128)(2,1)S(1)} %get-tuple-element.88.near_ref), channel_id=1, source_target_pairs={{0,16},{1,17},{2,18},{3,19},{4,20},{5,21},{6,22},{7,23},{8,24},{9,... | collective-permute-start | bytes 835592 | tf_op jit(solution)/shard_map/ppermute | solution.py:1006
  54.1 7.0 %collective-permute-start.15 = (bf16[128,256]{1,0:T(8,128)(2,1)S(1)}, bf16[128,256]{1,0:T(8,128)(2,1)S(1)}, u32[]{:S(2)}, u32[]{:S(2)}) collective-permute-start(bf16[128,256]{1,0:T(8,128)(2,1)S(1)} %get-tuple-element.89), channel_id=1, source_target_pairs={{0,8},{1,9},{2,10},{3,11},{4,12},{5,13},{6,14},{7,15},{8,0},{9,1},... | collective-permute-start | bytes 196616 | tf_op jit(solution)/shard_map/ppermute | solution.py:1006
  56.9 6.8 %collective-permute-start.16 = (bf16[128,256]{1,0:T(8,128)(2,1)S(1)}, bf16[128,256]{1,0:T(8,128)(2,1)S(1)}, u32[]{:S(2)}, u32[]{:S(2)}) collective-permute-start(bf16[128,256]{1,0:T(8,128)(2,1)S(1)} %get-tuple-element.89), channel_id=1, source_target_pairs={{0,24},{1,25},{2,26},{3,27},{4,28},{5,29},{6,30},{7,31},{8,16},{9,... | collective-permute-start | bytes 196616 | tf_op jit(solution)/shard_map/ppermute | solution.py:1006

commit v6 on v5

--- a/solution.py
+++ b/solution.py
@@ -280,9 +280,12 @@
     member = (lane // slots == rows_of(word_shape)) & ((lane % slots).astype(f32) < row_counts)
     member = jnp.where(member, 1.0, 0.0).astype(bf16)
     fetches[8].wait()
-    for at in range(0, expand_ref.shape[1], 256):
-        part = slice(at, at + 256)
-        value, slope = gelu_parts(dot(normed, expand_ref[:, part]))
+    parts = [slice(at, at + 256) for at in range(0, expand_ref.shape[1], 256)]
+    before = dot(normed, expand_ref[:, parts[0]])
+    for number, part in enumerate(parts):
+        value, slope = gelu_parts(before)
+        if number + 1 < len(parts):
+            before = dot(normed, expand_ref[:, parts[number + 1]])
         slope_ref[:, part] = slope
         hidden_sum_ref[:, part] = dot(member, value).astype(bf16)
     high = middle.astype(bf16)
@@ -391,25 +394,30 @@
     for at in range(0, expand_ref.shape[1], 256):
         part = slice(at, at + 256)
         dbefore[:, part] = dot(member, dhidden_words[:, part]).astype(bf16) * slope_ref[:, part]
-    dnormed = dot_nt(dbefore[...], expand_ref[...])
     normal, scale = unit(middle_ref[...])
     normed_t = (normal * gain_mlp_ref[...]).astype(bf16).T
-    gain_ref[...] = jnp.broadcast_to(
-        jnp.sum(dnormed * normal, axis=0, keepdims=True), gain_ref.shape
-    )
+    hidden_sum_t = hidden_sum_ref[...].T
+    targets = slot_refs(keep_ref, send_ref)
+
+    def put(gradient, at):
+        return put_shards(gradient, targets, lambda slot: char_shard(slot, me), at)
+
+    dnormed = dot_nt(dbefore[...], expand_ref[...])
+    expand_grad[...] = dot(normed_t, dbefore[...])
+    shrink_grad[...] = dot(hidden_sum_t, spread_high)
     dmiddle = (
         dot(member, spread_high)
         + dot(member, spread_low)
         + unit_back(dnormed, gain_mlp_ref[...], normal, scale)
     )
     dmiddle_ref[...] = dmiddle
-    expand_grad[...] = dot(normed_t, dbefore[...])
-    shrink_grad[...] = dot(hidden_sum_ref[...].T, spread_high)
     output_grad[...] = dot(mixed_ref[...], dmiddle.astype(bf16))
-    targets = slot_refs(keep_ref, send_ref)
-    at = 0
-    for gradient in (expand_grad, shrink_grad, output_grad):
-        at = put_shards(gradient, targets, lambda slot: char_shard(slot, me), at)
+    gain_ref[...] = jnp.broadcast_to(
+        jnp.sum(dnormed * normal, axis=0, keepdims=True), gain_ref.shape
+    )
+    at = put(expand_grad, 0)
+    at = put(shrink_grad, at)
+    put(output_grad, at)
 
 
 def char_mlp_back(counts, weights, dpooled, stored, slots, shards):
@@ -490,19 +498,19 @@
         dqkv[block * BLOCK : (block + 1) * BLOCK, which * SLAB : (which + 1) * SLAB] = value
 
     attend_back(load, load_dmixed, range(rows // BLOCK), probs_ref[...], store, slots)
-    dnormed = dot_nt(dqkv[...], project_ref[...])
     for fetch in fetches:
         fetch.wait()
     language = pick(languages_ref[...], section)
     normal, scale = unit(char_rows(chars_ref[...], table_ref, language))
+    normed_t = (normal * gain_attn_ref[...]).astype(bf16).T
+    dnormed = dot_nt(dqkv[...], project_ref[...])
+    project_grad[...] = dot(normed_t, dqkv[...])
     gain_attn_grad = jnp.sum(dnormed * normal, axis=0, keepdims=True)
     dx = dmiddle_ref[...] + unit_back(dnormed, gain_attn_ref[...], normal, scale)
     grad[...] = dx
     leave = pltpu.make_async_copy(grad, grad_hbm, sems.at[2])
     leave.start()
     row_sum = jnp.sum(dx, axis=0, keepdims=True)
-    normed_t = (normal * gain_attn_ref[...]).astype(bf16).T
-    project_grad[...] = dot(normed_t, dqkv[...])
     targets = [
         ref.at[pl.ds(place * CHAR_LAST_SLOT, CHAR_LAST_SLOT)]
         for ref in (keep_ref, send_ref)
@@ -577,9 +585,9 @@
     length,
     shards,
     own_ref,
+    both_ref,
+    section_ref,
     far_ref,
-    section_ref,
-    both_ref,
     cot_ref,
     cot_far_ref,
     input_ref,
@@ -659,17 +667,37 @@
         hidden[:, part] = value
         dhidden = dot_nt(dz_all, shrink_ref[part, :]).astype(bf16)
         dbefore[:, part] = dhidden * bend
-    result[...] = middle[:length] + dot(hidden[:length], shrink_ref[...])
-    leave = pltpu.make_async_copy(result, result_hbm, sem)
-    leave.start()
-
+
+    def shard_of(slot):
+        return (me & 7) ^ ((slot >> 2) | ((slot & 3) << 1))
+
+    def own_rows(flipped):
+        many = flipped.shape[0] // 2
+        return flipped[pl.ds(pl.multiple_of((me >> 3) * many, many), many), :]
+
+    def half_columns(ref, place):
+        many = ref.shape[1] // 2
+        return ref[:, pl.ds(pl.multiple_of(place * many, many), many)]
+
+    def own_columns(ref):
+        return half_columns(ref, section)
+
+    targets = slot_refs(keep_ref, send_ref)
+    hidden_t = half_columns(hidden, me >> 3).T
+    pooled_t[...] = pooled[...].T
+    normal, scale = unit(middle[...])
     dnormed = dot_nt(dbefore[...], expand_ref[...])
-    normal, scale = unit(middle[...])
-    gain_mlp_grad = jnp.sum(dnormed * normal, axis=0, keepdims=True)
+    expand_grad[...] = dot(own_rows(normed_mlp_t), own_columns(dbefore))
+    shrink_grad[...] = dot(hidden_t, own_columns(dz))
     dmiddle = dz_all.astype(f32) + unit_back(dnormed, gain_mlp_ref[...], normal, scale)
     dy_low = dmiddle.astype(bf16)
     dy[...] = dy_low
     dmixed[...] = dot_nt(dy_low, output_ref[...]).astype(bf16)
+    gain_mlp_grad = jnp.sum(dnormed * normal, axis=0, keepdims=True)
+    result[...] = middle[:length] + dot(hidden[:length], shrink_ref[...])
+    leave = pltpu.make_async_copy(result, result_hbm, sem)
+    leave.start()
+    output_grad[...] = dot(own_rows(mixed_t), own_columns(dy))
 
     def load_dmixed(tile):
         block, slab = tile
@@ -681,39 +709,16 @@
         dqkv[block * BLOCK : (block + 1) * BLOCK, at : at + SLAB] = value
 
     attend_back(load, load_dmixed, tiles, kept[...], store, length)
+    normal, scale = unit(start[...])
     dnormed = dot_nt(dqkv[...], project_ref[...])
-    normal, scale = unit(start[...])
-    gain_attn_grad = jnp.sum(dnormed * normal, axis=0, keepdims=True)
+    project_grad[...] = dot(own_rows(normed_t), own_columns(dqkv))
     dword = (dmiddle + unit_back(dnormed, gain_attn_ref[...], normal, scale)).astype(bf16)
     dpooled_ref[...] = dot_nt(dword[:length], input_ref[...]).astype(bf16)
     dstart[...] = dword
-
-    def shard_of(slot):
-        return (me & 7) ^ ((slot >> 2) | ((slot & 3) << 1))
-
-    def own_rows(flipped):
-        many = flipped.shape[0] // 2
-        return flipped[pl.ds(pl.multiple_of((me >> 3) * many, many), many), :]
-
-    def half_columns(ref, place):
-        many = ref.shape[1] // 2
-        return ref[:, pl.ds(pl.multiple_of(place * many, many), many)]
-
-    def own_columns(ref):
-        return half_columns(ref, section)
-
-    pooled_t[...] = pooled[...].T
-    hidden_t = half_columns(hidden, me >> 3).T
-    targets = slot_refs(keep_ref, send_ref)
+    gain_attn_grad = jnp.sum(dnormed * normal, axis=0, keepdims=True)
+    input_grad[...] = dot(own_rows(pooled_t), own_columns(dstart))
     at = 0
-    for lhs, rhs, ref in (
-        (own_rows(pooled_t), own_columns(dstart), input_grad),
-        (own_rows(normed_t), own_columns(dqkv), project_grad),
-        (own_rows(mixed_t), own_columns(dy), output_grad),
-        (own_rows(normed_mlp_t), own_columns(dbefore), expand_grad),
-        (hidden_t, own_columns(dz), shrink_grad),
-    ):
-        ref[...] = dot(lhs, rhs)
+    for ref in (input_grad, project_grad, output_grad, expand_grad, shrink_grad):
         at = put_shards(ref, targets, shard_of, at)
     extra = jnp.concatenate(
         [gain_attn_grad[:, :SLAB], gain_attn_grad[:, SLAB:]]
@@ -915,7 +920,7 @@
     )(word, *char)
 
 
-def last_sum_kernel(near_ref, section_ref, high_ref, both_ref, *outs):
+def last_sum_kernel(near_ref, both_ref, high_ref, section_ref, *outs):
     word_rows = WORD_SLOT
     section, me = position()
     own = near_ref[:word_rows].astype(f32)
@@ -1010,9 +1015,9 @@
 
 
 def plane_exchange(pieces):
-    return (pieces[0],) + tuple(
-        exchange(piece, 0, bits) for piece, bits in zip(pieces[1:], (SIDE, NEAR, SIDE | NEAR))
-    )
+    return tuple(
+        exchange(piece, 0, bits) for piece, bits in zip(pieces[:0:-1], (SIDE | NEAR, NEAR, SIDE))
+    ) + (pieces[0],)
 
 
 def local_grouped(
@@ -1029,7 +1034,7 @@
     counts = counts.reshape(micros, 1, words)
     languages = languages.reshape(1, micros)
     pooled, *stored = char_forward(languages, chars, counts, language_table, char_weights, slots)
-    others = (exchange(pooled, 0, FAR), exchange(pooled, 1, 0), exchange(pooled, 1, FAR))
+    others = (exchange(pooled, 1, FAR), exchange(pooled, 1, 0), exchange(pooled, 0, FAR))
     result, dpooled, keep, send = word_group(
         (pooled,) + others, (cot, cot_far), word_input, word_weights, shards
     )
@@ -1056,7 +1061,7 @@
     first = pair_of(stay, arrived, word)
     char = plane_exchange(second_sum(first, last))
     near, far = plane_sum(word, char)
-    arrived = (exchange(near, 1, 0), exchange(far, 0, FAR), exchange(far, 1, FAR))
+    arrived = (exchange(far, 1, FAR), exchange(far, 0, FAR), exchange(near, 1, 0))
     shapes = [(language_table.shape[0], language_table.shape[1] // shards)]
     for weight in char_weights + (word_input,) + word_weights:
         if weight.shape[0] == 1:

time: 65 us -> 62.8 us (0.966)
  waiting for transfers between devices: 18.1 us -> 15.6 us
  starting transfers between devices: 21.2 us -> 22.6 us
  Pallas kernels: 24.4 us -> 23.3 us
    ppermute x17, waiting for transfers between devices: 18.1 us -> 15.6 us  [exchange(): return lax.ppermute(value, ('section', 'dp'), pairs)]
    ppermute x17, starting transfers between devices: 21.2 us -> 22.6 us  [exchange(): return lax.ppermute(value, ('section', 'dp'), pairs)]
  transfers between devices with their start and end apart: 17 -> 17, of which waited for: 9 -> 7; matrix products, arithmetic and copies ran while one was open for 0% -> 0% of each run, Pallas kernels for 25% -> 25%
where the time goes in v6:
time: 62.8 us; the launch traced here: 62.6 us
  Pallas kernels  23.3 us (37%)
  starting transfers between devices  22.6 us (36%)
  waiting for transfers between devices  15.6 us (25%)
  between operations  1.09 us (2%)
    ppermute x17, starting transfers between devices, exchange(): return lax.ppermute(value, ('section', 'dp'), pairs)  22.6 us
    ppermute x17, waiting for transfers between devices, exchange(): return lax.ppermute(value, ('section', 'dp'), pairs)  15.6 us
    pallas_call x1, Pallas kernels, word_group(): pl.pallas_call(functools.partial(word_kernel, length, shards), in_specs=[...  6.64 us
    pallas_call x1, Pallas kernels, char_forward(): pl.pallas_call(functools.partial(char_forward_kernel, slots), in_specs=[h...  6.25 us
    pallas_call x1, Pallas kernels, char_attn_back(): pl.pallas_call(functools.partial(char_attn_back_kernel, slots, shards), i...  4.85 us
    pallas_call x1, Pallas kernels, char_mlp_back(): pl.pallas_call(functools.partial(char_mlp_back_kernel, slots, shards), in...  3.83 us
  transfers between devices with their start and end apart: 17, of which 7 were waited for; matrix products, arithmetic and copies ran while one was open for 0% of the time, Pallas kernels for 25%

profile of v6, /device:TPU:0, one launch (start us, length us, event | category | flops | bytes accessed | tf_op | source)
XLA Modules:
  0.0 62.6 jit_solution(10581115029599647631)
XLA Ops:
  0.6 4.1 %collective-permute-start.3 = (bf16[2,64,512]{2,1,0:T(8,128)(2,1)}, bf16[2,64,512]{2,1,0:T(8,128)(2,1)S(1)}, u32[]{:S(2)}, u32[]{:S(2)}) collective-permute-start(bf16[2,64,512]{2,1,0:T(8,128)(2,1)} %bitcast.15), channel_id=1, source_target_pairs={{0,8},{1,9},{2,10},{3,11},{4,12},{5,13},{6,14},{7,15},{8,0},{9,1},... | collective-permute-start | bytes 393224 | tf_op jit(solution)/shard_map/ppermute | solution.py:1011
  4.8 0.0 copy-start.10
  4.8 0.0 copy-start.11
  4.8 0.0 copy-start.12
  4.8 0.0 copy-start.13
  4.8 6.3 %char_forward.1 = (bf16[64,256]{1,0:T(8,128)(2,1)S(1)}, bf16[64,1024]{1,0:T(8,128)(2,1)S(1)}, bf16[1024,768]{1,0:T(8,128)(2,1)S(1)}, f32[16,4096]{1,0:T(8,128)S(...) custom-call(bf16[2,1024,256]{2,1,0:T(8,128)(2,1)} %bitcast.21, ...), custom_call_target="tpu_custom_call" | custom-call | flops 4294967296 | bytes 8388608 | tf_op jit(solution)/shard_map/char_forward/pallas_call | solution.py:305
  11.1 1.3 %collective-permute-start = (bf16[64,256]{1,0:T(8,128)(2,1)S(1)}, bf16[64,256]{1,0:T(8,128)(2,1)S(1)}, u32[]{:S(2)}, u32[]{:S(2)}) collective-permute-start(bf16[64,256]{1,0:T(8,128)(2,1)S(1)} %get-tuple-element.60.own_ref), channel_id=1, source_target_pairs={{0,24},{1,25},{2,26},{3,27},{4,28},{5,29},{6,30},{7,31},{8,16},{9,... | collective-permute-start | bytes 98312 | tf_op jit(solution)/shard_map/ppermute | solution.py:1011
  12.4 0.3 collective-permute-start.1
  12.7 2.8 %collective-permute-start.2 = (bf16[64,256]{1,0:T(8,128)(2,1)S(1)}, bf16[64,256]{1,0:T(8,128)(2,1)S(1)}, u32[]{:S(2)}, u32[]{:S(2)}) collective-permute-start(bf16[64,256]{1,0:T(8,128)(2,1)S(1)} %get-tuple-element.60.own_ref), channel_id=1, source_target_pairs={{0,8},{1,9},{2,10},{3,11},{4,12},{5,13},{6,14},{7,15},{8,0},{9,1},... | collective-permute-start | bytes 98312 | tf_op jit(solution)/shard_map/ppermute | solution.py:1011
  15.5 1.6 %collective-permute-done.both_ref = bf16[64,256]{1,0:T(8,128)(2,1)S(1)} collective-permute-done((bf16[64,256]{1,0:T(8,128)(2,1)S(1)}, bf16[64,256]{1,0:T(8,128)(2,1)S(1)}, u32[]{:S(2)}, u32[]{:S(2)}) %collective-permute-start) | collective-permute-done | bytes 32800 | tf_op jit(solution)/shard_map/ppermute | solution.py:1011
  17.1 0.0 collective-permute-done.1.section_ref
  17.1 0.4 collective-permute-done.2.far_ref
  17.5 0.0 collective-permute-done.3.cot_far_ref
  17.5 0.0 copy-done.4
  17.5 0.0 copy-done.5
  17.5 0.0 copy-done.6
  17.5 0.0 copy-done.7
  17.6 0.0 copy-done.10
  17.6 0.0 copy-done.11
  17.6 0.0 copy-done.12
  17.6 0.0 copy-done.13
  17.6 0.0 copy-start.8
  17.6 0.0 copy-start.9
  17.6 0.0 copy-start.14
  17.6 6.6 %word_group.1 = (f32[64,512]{1,0:T(8,128)}, bf16[64,256]{1,0:T(8,128)(2,1)S(1)}, bf16[4,416,256]{2,1,0:T(8,128)(2,1)S(1)}, bf16[4,416,256]{2,1,0:T(8,128)(2,1)S(1)}) custom-call(bf16[64,256]{1,0:T(8,128)(2,1)S(1)} %get-tuple-element.60.own_ref, bf16[64,256]{1,0:T(8,128)(2,1)S(1)} %collective-permute-done.both_ref, ...), custom_call_target="tpu_custom_call" | custom-call | flops 6710886400 | bytes 8388608 | tf_op jit(solution)/shard_map/word_group/pallas_call | solution.py:743
  24.3 0.1 collective-permute-start.5
  24.4 3.8 %char_mlp_back.1 = (f32[1024,256]{1,0:T(8,128)S(1)}, f32[8,256]{1,0:T(8,128)S(1)}, bf16[8,144,256]{2,1,0:T(8,128)(2,1)S(1)}, bf16[8,144,256]{2,1,0:T(8,128)(2,1)S(1)}) custom-call(s32[2,1,64]{2,1,0:T(1,128)} %counts_hbm.3, f32[1,256]{1,0:T(1,128)S(1)} %bitcast.20, bf16[256,1024]{1,0:T(8,128)(2,1)S(1)} %copy-done.8, bf16[1024,256]{1,0:T(8,128)(2,1)S(1)} %copy-done.9, ...), custom_call_target="tpu_custom_call" | custom-call | flops 4294967296 | bytes 8388608 | tf_op jit(solution)/shard_map/char_mlp_back/pallas_call | solution.py:432
  28.2 0.0 copy-start
  28.2 0.0 copy-start.1
  28.3 0.0 copy-start.2
  28.3 0.0 copy-start.3
  28.3 0.6 collective-permute-start.4
  28.8 0.0 collective-permute-done.5.arrived
  28.8 0.2 word_sum.1
  29.0 2.8 %collective-permute-start.6 = (bf16[416,256]{1,0:T(8,128)(2,1)S(1)}, bf16[416,256]{1,0:T(8,128)(2,1)S(1)}, u32[]{:S(2)}, u32[]{:S(2)}) collective-permute-start(bf16[416,256]{1,0:T(8,128)(2,1)S(1)} %get-tuple-element.77), channel_id=1, source_target_pairs={{0,6},{1,7},{2,4},{3,5},{4,2},{5,3},{6,0},{7,1},{8,14},{9,15},{10,... | collective-permute-start | bytes 638984 | tf_op jit(solution)/shard_map/ppermute | solution.py:1011
  31.9 0.8 %collective-permute-start.7 = (bf16[416,256]{1,0:T(8,128)(2,1)S(1)}, bf16[416,256]{1,0:T(8,128)(2,1)S(1)}, u32[]{:S(2)}, u32[]{:S(2)}) collective-permute-start(bf16[416,256]{1,0:T(8,128)(2,1)S(1)} %get-tuple-element.78), channel_id=1, source_target_pairs={{0,4},{1,5},{2,6},{3,7},{4,0},{5,1},{6,2},{7,3},{8,12},{9,13},{10,... | collective-permute-start | bytes 638984 | tf_op jit(solution)/shard_map/ppermute | solution.py:1011
  32.6 0.0 collective-permute-start.8
  32.6 0.0 collective-permute-done.4.arrived
  32.6 0.2 first_sum.1
  32.9 1.7 %collective-permute-start.9 = (bf16[8,144,128]{2,1,0:T(8,128)(2,1)S(1)}, bf16[8,144,128]{2,1,0:T(8,128)(2,1)S(1)}, u32[]{:S(2)}, u32[]{:S(2)}) collective-permute-start(bf16[8,144,128]{2,1,0:T(8,128)(2,1)S(1)} %get-tuple-element.81), channel_id=1, source_target_pairs={{0,16},{1,17},{2,18},{3,19},{4,20},{5,21},{6,22},{7,23},{8,24},{9,... | collective-permute-start | bytes 884744 | tf_op jit(solution)/shard_map/ppermute | solution.py:1011
  34.6 4.8 %char_attn_back.1 = (f32[1024,256]{1,0:T(8,128)}, bf16[400,256]{1,0:T(8,128)(2,1)S(1)}, bf16[400,256]{1,0:T(8,128)(2,1)S(1)}) custom-call(bf16[8,144,128]{2,1,0:T(8,128)(2,1)S(1)} %get-tuple-element.69._.one, bf16[2,1024,256]{2,1,0:T(8,128)(2,1)} %bitcast.22, s32[1,2]{1,0:T(1,128)} %bitcast.24, bf16[8,256]{1,0:T(8,128)(2,1)S(1)} %copy-done.2, ...), custom_call_target="tpu_custom_call" | custom-call | tf_op jit(solution)/shard_map/char_attn_back/pallas_call | solution.py:543
  39.5 0.1 collective-permute-start.10
  39.5 0.0 collective-permute-done.6.refs_0_
  39.5 2.9 %collective-permute-done.7.refs_1_ = bf16[416,256]{1,0:T(8,128)(2,1)S(1)} collective-permute-done((bf16[416,256]{1,0:T(8,128)(2,1)S(1)}, bf16[416,256]{1,0:T(8,128)(2,1)S(1)}, u32[]{:S(2)}, u32[]{:S(2)}) %collective-permute-start.7) | collective-permute-done | bytes 213024 | tf_op jit(solution)/shard_map/ppermute | solution.py:1011
  42.4 0.0 collective-permute-done.8.refs_2_
  42.4 0.1 total.1._.refs_0_
  42.5 0.0 collective-permute-done.9.other
  42.5 0.1 pair.1.first
  42.6 0.0 collective-permute-done.10.arrived
  42.6 0.1 second_sum.1
  42.7 2.2 %collective-permute-start.11 = (bf16[256,256]{1,0:T(8,128)(2,1)S(1)}, bf16[256,256]{1,0:T(8,128)(2,1)S(1)}, u32[]{:S(2)}, u32[]{:S(2)}) collective-permute-start(bf16[256,256]{1,0:T(8,128)(2,1)S(1)} %get-tuple-element.84), channel_id=1, source_target_pairs={{0,6},{1,7},{2,4},{3,5},{4,2},{5,3},{6,0},{7,1},{8,14},{9,15},{10,... | collective-permute-start | bytes 393224 | tf_op jit(solution)/shard_map/ppermute | solution.py:1011
  44.9 0.8 %collective-permute-start.12 = (bf16[256,256]{1,0:T(8,128)(2,1)S(1)}, bf16[256,256]{1,0:T(8,128)(2,1)S(1)}, u32[]{:S(2)}, u32[]{:S(2)}) collective-permute-start(bf16[256,256]{1,0:T(8,128)(2,1)S(1)} %get-tuple-element.85), channel_id=1, source_target_pairs={{0,4},{1,5},{2,6},{3,7},{4,0},{5,1},{6,2},{7,3},{8,12},{9,13},{10,... | collective-permute-start | bytes 393224 | tf_op jit(solution)/shard_map/ppermute | solution.py:1011
  45.7 0.6 collective-permute-start.13
  46.3 3.8 %collective-permute-done.11.refs_1_ = bf16[256,256]{1,0:T(8,128)(2,1)S(1)} collective-permute-done((bf16[256,256]{1,0:T(8,128)(2,1)S(1)}, bf16[256,256]{1,0:T(8,128)(2,1)S(1)}, u32[]{:S(2)}, u32[]{:S(2)}) %collective-permute-start.11) | collective-permute-done | bytes 131104 | tf_op jit(solution)/shard_map/ppermute | solution.py:1011
  50.1 1.8 %collective-permute-done.12.refs_2_ = bf16[256,256]{1,0:T(8,128)(2,1)S(1)} collective-permute-done((bf16[256,256]{1,0:T(8,128)(2,1)S(1)}, bf16[256,256]{1,0:T(8,128)(2,1)S(1)}, u32[]{:S(2)}, u32[]{:S(2)}) %collective-permute-start.12) | collective-permute-done | bytes 131104 | tf_op jit(solution)/shard_map/ppermute | solution.py:1011
  51.9 0.0 collective-permute-done.13.refs_3_
  51.9 0.1 plane_sum.1
  52.0 1.2 %collective-permute-start.16 = (bf16[544,256]{1,0:T(8,128)(2,1)S(1)}, bf16[544,256]{1,0:T(8,128)(2,1)S(1)}, u32[]{:S(2)}, u32[]{:S(2)}) collective-permute-start(bf16[544,256]{1,0:T(8,128)(2,1)S(1)} %get-tuple-element.88.near_ref), channel_id=1, source_target_pairs={{0,16},{1,17},{2,18},{3,19},{4,20},{5,21},{6,22},{7,23},{8,24},{9,... | collective-permute-start | bytes 835592 | tf_op jit(solution)/shard_map/ppermute | solution.py:1011
  53.2 2.6 %collective-permute-start.14 = (bf16[128,256]{1,0:T(8,128)(2,1)S(1)}, bf16[128,256]{1,0:T(8,128)(2,1)S(1)}, u32[]{:S(2)}, u32[]{:S(2)}) collective-permute-start(bf16[128,256]{1,0:T(8,128)(2,1)S(1)} %get-tuple-element.89), channel_id=1, source_target_pairs={{0,24},{1,25},{2,26},{3,27},{4,28},{5,29},{6,30},{7,31},{8,16},{9,... | collective-permute-start | bytes 196616 | tf_op jit(solution)/shard_map/ppermute | solution.py:1011
  55.8 0.6 collective-permute-start.15
  56.4 3.0 %collective-permute-done.14.both_ref = bf16[128,256]{1,0:T(8,128)(2,1)S(1)} collective-permute-done((bf16[128,256]{1,0:T(8,128)(2,1)S(1)}, bf16[128,256]{1,0:T(8,128)(2,1)S(1)}, u32[]{:S(2)}, u32[]{:S(2)}) %collective-permute-start.14) | collective-permute-done | bytes 65568 | tf_op jit(solution)/shard_map/ppermute | solution.py:1011
  59.4 2.1 %collective-permute-done.15.high_ref = bf16[128,256]{1,0:T(8,128)(2,1)S(1)} collective-permute-done((bf16[128,256]{1,0:T(8,128)(2,1)S(1)}, bf16[128,256]{1,0:T(8,128)(2,1)S(1)}, u32[]{:S(2)}, u32[]{:S(2)}) %collective-permute-start.15) | collective-permute-done | bytes 65568 | tf_op jit(solution)/shard_map/ppermute | solution.py:1011
  61.5 0.0 collective-permute-done.16.section_ref
  61.5 1.0 %last_sum.1 = (f32[8,16]{1,0:T(8,128)}, f32[1,16]{1,0:T(1,128)}, f32[16,768]{1,0:T(8,128)}, f32[16,256]{1,0:T(8,128)}, f32[1,16]{1,0:T(1,128)}, /*index=5*/f32[1...) custom-call(bf16[544,256]{1,0:T(8,128)(2,1)S(1)} %get-tuple-element., ...), custom_call_target="tpu_custom_call" | custom-call | tf_op jit(solution)/shard_map/last_sum/pallas_call | solution.py:996
  (11 shorter events, 0.0 us)
Async XLA Ops:
  0.6 16.9 %collective-permute-start.3 = (bf16[2,64,512]{2,1,0:T(8,128)(2,1)}, bf16[2,64,512]{2,1,0:T(8,128)(2,1)S(1)}, u32[]{:S(2)}, u32[]{:S(2)}) collective-permute-start(bf16[2,64,512]{2,1,0:T(8,128)(2,1)} %bitcast.15), channel_id=1, source_target_pairs={{0,8},{1,9},{2,10},{3,11},{4,12},{5,13},{6,14},{7,15},{8,0},{9,1},... | collective-permute-start | bytes 393224 | tf_op jit(solution)/shard_map/ppermute | solution.py:1011
  4.8 12.8 %copy-start.4 = (bf16[512,2048]{1,0:T(8,128)(2,1)S(1)}, bf16[512,2048]{1,0:T(8,128)(2,1)}, u32[]{:S(2)}) copy-start(bf16[512,2048]{1,0:T(8,128)(2,1)} %expand_ref.2) | copy-start | bytes 6291460
  4.8 12.8 %copy-start.5 = (bf16[2048,512]{1,0:T(8,128)(2,1)S(1)}, bf16[2048,512]{1,0:T(8,128)(2,1)}, u32[]{:S(2)}) copy-start(bf16[2048,512]{1,0:T(8,128)(2,1)} %shrink_ref.2) | copy-start | bytes 6291460
  4.8 12.8 %copy-start.6 = (bf16[512,1536]{1,0:T(8,128)(2,1)S(1)}, bf16[512,1536]{1,0:T(8,128)(2,1)}, u32[]{:S(2)}) copy-start(bf16[512,1536]{1,0:T(8,128)(2,1)} %project_ref.2) | copy-start | bytes 4718596
  4.8 12.8 %copy-start.7 = (bf16[512,512]{1,0:T(8,128)(2,1)S(1)}, bf16[512,512]{1,0:T(8,128)(2,1)}, u32[]{:S(2)}) copy-start(bf16[512,512]{1,0:T(8,128)(2,1)} %output_ref.2) | copy-start | bytes 1572868
  4.8 12.8 %copy-start.10 = (bf16[256,512]{1,0:T(8,128)(2,1)S(1)}, bf16[256,512]{1,0:T(8,128)(2,1)}, u32[]{:S(2)}) copy-start(bf16[256,512]{1,0:T(8,128)(2,1)} %input_ref.1) | copy-start | bytes 786436
  4.8 12.8 %copy-start.11 = (bf16[2,1,64,512]{3,2,1,0:T(8,128)(2,1)S(1)}, bf16[2,1,64,512]{3,2,1,0:T(8,128)(2,1)}, u32[]{:S(2)}) copy-start(bf16[2,1,64,512]{3,2,1,0:T(8,128)(2,1)} %param.35) | copy-start | bytes 393220
  4.8 12.8 %copy-start.12 = (f32[512]{0:T(512)S(1)}, f32[512]{0:T(512)}, u32[]{:S(2)}) copy-start(f32[512]{0:T(512)} %param.29) | copy-start | bytes 6148
  4.8 12.8 %copy-start.13 = (f32[512]{0:T(512)S(1)}, f32[512]{0:T(512)}, u32[]{:S(2)}) copy-start(f32[512]{0:T(512)} %param.32) | copy-start | bytes 6148
  11.1 6.1 %collective-permute-start = (bf16[64,256]{1,0:T(8,128)(2,1)S(1)}, bf16[64,256]{1,0:T(8,128)(2,1)S(1)}, u32[]{:S(2)}, u32[]{:S(2)}) collective-permute-start(bf16[64,256]{1,0:T(8,128)(2,1)S(1)} %get-tuple-element.60.own_ref), channel_id=1, source_target_pairs={{0,24},{1,25},{2,26},{3,27},{4,28},{5,29},{6,30},{7,31},{8,16},{9,... | collective-permute-start | bytes 98312 | tf_op jit(solution)/shard_map/ppermute | solution.py:1011
  12.4 4.8 %collective-permute-start.1 = (bf16[64,256]{1,0:T(8,128)(2,1)S(1)}, bf16[64,256]{1,0:T(8,128)(2,1)S(1)}, u32[]{:S(2)}, u32[]{:S(2)}) collective-permute-start(bf16[64,256]{1,0:T(8,128)(2,1)S(1)} %get-tuple-element.60.own_ref), channel_id=1, source_target_pairs={{0,16},{1,17},{2,18},{3,19},{4,20},{5,21},{6,22},{7,23},{8,24},{9,... | collective-permute-start | bytes 98312 | tf_op jit(solution)/shard_map/ppermute | solution.py:1011
  12.7 4.8 %collective-permute-start.2 = (bf16[64,256]{1,0:T(8,128)(2,1)S(1)}, bf16[64,256]{1,0:T(8,128)(2,1)S(1)}, u32[]{:S(2)}, u32[]{:S(2)}) collective-permute-start(bf16[64,256]{1,0:T(8,128)(2,1)S(1)} %get-tuple-element.60.own_ref), channel_id=1, source_target_pairs={{0,8},{1,9},{2,10},{3,11},{4,12},{5,13},{6,14},{7,15},{8,0},{9,1},... | collective-permute-start | bytes 98312 | tf_op jit(solution)/shard_map/ppermute | solution.py:1011
  17.6 6.8 %copy-start.8 = (bf16[256,1024]{1,0:T(8,128)(2,1)S(1)}, bf16[256,1024]{1,0:T(8,128)(2,1)}, u32[]{:S(2)}) copy-start(bf16[256,1024]{1,0:T(8,128)(2,1)} %expand_ref.3) | copy-start | bytes 1572868
  17.6 6.8 %copy-start.9 = (bf16[1024,256]{1,0:T(8,128)(2,1)S(1)}, bf16[1024,256]{1,0:T(8,128)(2,1)}, u32[]{:S(2)}) copy-start(bf16[1024,256]{1,0:T(8,128)(2,1)} %shrink_ref.3) | copy-start | bytes 1572868
  17.6 6.8 %copy-start.14 = (f32[256]{0:T(256)S(1)}, f32[256]{0:T(256)}, u32[]{:S(2)}) copy-start(f32[256]{0:T(256)} %param.25) | copy-start | bytes 3076
  24.3 4.5 %collective-permute-start.5 = (bf16[4,416,256]{2,1,0:T(8,128)(2,1)S(1)}, bf16[4,416,256]{2,1,0:T(8,128)(2,1)S(1)}, u32[]{:S(2)}, u32[]{:S(2)}) collective-permute-start(bf16[4,416,256]{2,1,0:T(8,128)(2,1)S(1)} %get-tuple-element.76), channel_id=1, source_target_pairs={{0,1},{1,0},{2,3},{3,2},{4,5},{5,4},{6,7},{7,6},{8,9},{9,8},{10,11... | collective-permute-start | bytes 2555912 | tf_op jit(solution)/shard_map/ppermute | solution.py:1011
  28.2 6.4 %copy-start = (bf16[256,768]{1,0:T(8,128)(2,1)S(1)}, bf16[256,768]{1,0:T(8,128)(2,1)}, u32[]{:S(2)}) copy-start(bf16[256,768]{1,0:T(8,128)(2,1)} %project_ref.3) | copy-start | bytes 1179652
  28.2 6.3 %copy-start.1 = (bf16[256,256]{1,0:T(8,128)(2,1)S(1)}, bf16[256,256]{1,0:T(8,128)(2,1)}, u32[]{:S(2)}) copy-start(bf16[256,256]{1,0:T(8,128)(2,1)} %output_ref.3) | copy-start | bytes 393220
  28.3 6.3 %copy-start.2 = (bf16[8,256]{1,0:T(8,128)(2,1)S(1)}, bf16[8,256]{1,0:T(8,128)(2,1)}, u32[]{:S(2)}) copy-start(bf16[8,256]{1,0:T(8,128)(2,1)} %table_ref.1) | copy-start | bytes 12292
  28.3 6.3 %copy-start.3 = (f32[256]{0:T(256)S(1)}, f32[256]{0:T(256)}, u32[]{:S(2)}) copy-start(f32[256]{0:T(256)} %param.22) | copy-start | bytes 3076
  28.3 4.4 %collective-permute-start.4 = (bf16[8,144,256]{2,1,0:T(8,128)(2,1)S(1)}, bf16[8,144,256]{2,1,0:T(8,128)(2,1)S(1)}, u32[]{:S(2)}, u32[]{:S(2)}) collective-permute-start(bf16[8,144,256]{2,1,0:T(8,128)(2,1)S(1)} %get-tuple-element.68), channel_id=1, source_target_pairs={{0,1},{1,0},{2,3},{3,2},{4,5},{5,4},{6,7},{7,6},{8,9},{9,8},{10,11... | collective-permute-start | bytes 1769480 | tf_op jit(solution)/shard_map/ppermute | solution.py:1011
  29.0 10.5 %collective-permute-start.6 = (bf16[416,256]{1,0:T(8,128)(2,1)S(1)}, bf16[416,256]{1,0:T(8,128)(2,1)S(1)}, u32[]{:S(2)}, u32[]{:S(2)}) collective-permute-start(bf16[416,256]{1,0:T(8,128)(2,1)S(1)} %get-tuple-element.77), channel_id=1, source_target_pairs={{0,6},{1,7},{2,4},{3,5},{4,2},{5,3},{6,0},{7,1},{8,14},{9,15},{10,... | collective-permute-start | bytes 638984 | tf_op jit(solution)/shard_map/ppermute | solution.py:1011
  31.9 10.6 %collective-permute-start.7 = (bf16[416,256]{1,0:T(8,128)(2,1)S(1)}, bf16[416,256]{1,0:T(8,128)(2,1)S(1)}, u32[]{:S(2)}, u32[]{:S(2)}) collective-permute-start(bf16[416,256]{1,0:T(8,128)(2,1)S(1)} %get-tuple-element.78), channel_id=1, source_target_pairs={{0,4},{1,5},{2,6},{3,7},{4,0},{5,1},{6,2},{7,3},{8,12},{9,13},{10,... | collective-permute-start | bytes 638984 | tf_op jit(solution)/shard_map/ppermute | solution.py:1011
  32.6 9.8 %collective-permute-start.8 = (bf16[416,256]{1,0:T(8,128)(2,1)S(1)}, bf16[416,256]{1,0:T(8,128)(2,1)S(1)}, u32[]{:S(2)}, u32[]{:S(2)}) collective-permute-start(bf16[416,256]{1,0:T(8,128)(2,1)S(1)} %get-tuple-element.79), channel_id=1, source_target_pairs={{0,2},{1,3},{2,0},{3,1},{4,6},{5,7},{6,4},{7,5},{8,10},{9,11},{10,... | collective-permute-start | bytes 638984 | tf_op jit(solution)/shard_map/ppermute | solution.py:1011
  32.9 9.7 %collective-permute-start.9 = (bf16[8,144,128]{2,1,0:T(8,128)(2,1)S(1)}, bf16[8,144,128]{2,1,0:T(8,128)(2,1)S(1)}, u32[]{:S(2)}, u32[]{:S(2)}) collective-permute-start(bf16[8,144,128]{2,1,0:T(8,128)(2,1)S(1)} %get-tuple-element.81), channel_id=1, source_target_pairs={{0,16},{1,17},{2,18},{3,19},{4,20},{5,21},{6,22},{7,23},{8,24},{9,... | collective-permute-start | bytes 884744 | tf_op jit(solution)/shard_map/ppermute | solution.py:1011
  39.5 3.2 %collective-permute-start.10 = (bf16[400,256]{1,0:T(8,128)(2,1)S(1)}, bf16[400,256]{1,0:T(8,128)(2,1)S(1)}, u32[]{:S(2)}, u32[]{:S(2)}) collective-permute-start(bf16[400,256]{1,0:T(8,128)(2,1)S(1)} %get-tuple-element.83), channel_id=1, source_target_pairs={{0,1},{1,0},{2,3},{3,2},{4,5},{5,4},{6,7},{7,6},{8,9},{9,8},{10,11... | collective-permute-start | bytes 614408 | tf_op jit(solution)/shard_map/ppermute | solution.py:1011
  42.7 7.3 %collective-permute-start.11 = (bf16[256,256]{1,0:T(8,128)(2,1)S(1)}, bf16[256,256]{1,0:T(8,128)(2,1)S(1)}, u32[]{:S(2)}, u32[]{:S(2)}) collective-permute-start(bf16[256,256]{1,0:T(8,128)(2,1)S(1)} %get-tuple-element.84), channel_id=1, source_target_pairs={{0,6},{1,7},{2,4},{3,5},{4,2},{5,3},{6,0},{7,1},{8,14},{9,15},{10,... | collective-permute-start | bytes 393224 | tf_op jit(solution)/shard_map/ppermute | solution.py:1011
  44.9 7.0 %collective-permute-start.12 = (bf16[256,256]{1,0:T(8,128)(2,1)S(1)}, bf16[256,256]{1,0:T(8,128)(2,1)S(1)}, u32[]{:S(2)}, u32[]{:S(2)}) collective-permute-start(bf16[256,256]{1,0:T(8,128)(2,1)S(1)} %get-tuple-element.85), channel_id=1, source_target_pairs={{0,4},{1,5},{2,6},{3,7},{4,0},{5,1},{6,2},{7,3},{8,12},{9,13},{10,... | collective-permute-start | bytes 393224 | tf_op jit(solution)/shard_map/ppermute | solution.py:1011
  45.7 6.2 %collective-permute-start.13 = (bf16[256,256]{1,0:T(8,128)(2,1)S(1)}, bf16[256,256]{1,0:T(8,128)(2,1)S(1)}, u32[]{:S(2)}, u32[]{:S(2)}) collective-permute-start(bf16[256,256]{1,0:T(8,128)(2,1)S(1)} %get-tuple-element.86), channel_id=1, source_target_pairs={{0,2},{1,3},{2,0},{3,1},{4,6},{5,7},{6,4},{7,5},{8,10},{9,11},{10,... | collective-permute-start | bytes 393224 | tf_op jit(solution)/shard_map/ppermute | solution.py:1011
  52.0 9.5 %collective-permute-start.16 = (bf16[544,256]{1,0:T(8,128)(2,1)S(1)}, bf16[544,256]{1,0:T(8,128)(2,1)S(1)}, u32[]{:S(2)}, u32[]{:S(2)}) collective-permute-start(bf16[544,256]{1,0:T(8,128)(2,1)S(1)} %get-tuple-element.88.near_ref), channel_id=1, source_target_pairs={{0,16},{1,17},{2,18},{3,19},{4,20},{5,21},{6,22},{7,23},{8,24},{9,... | collective-permute-start | bytes 835592 | tf_op jit(solution)/shard_map/ppermute | solution.py:1011
  53.2 6.2 %collective-permute-start.14 = (bf16[128,256]{1,0:T(8,128)(2,1)S(1)}, bf16[128,256]{1,0:T(8,128)(2,1)S(1)}, u32[]{:S(2)}, u32[]{:S(2)}) collective-permute-start(bf16[128,256]{1,0:T(8,128)(2,1)S(1)} %get-tuple-element.89), channel_id=1, source_target_pairs={{0,24},{1,25},{2,26},{3,27},{4,28},{5,29},{6,30},{7,31},{8,16},{9,... | collective-permute-start | bytes 196616 | tf_op jit(solution)/shard_map/ppermute | solution.py:1011
  55.8 5.7 %collective-permute-start.15 = (bf16[128,256]{1,0:T(8,128)(2,1)S(1)}, bf16[128,256]{1,0:T(8,128)(2,1)S(1)}, u32[]{:S(2)}, u32[]{:S(2)}) collective-permute-start(bf16[128,256]{1,0:T(8,128)(2,1)S(1)} %get-tuple-element.89), channel_id=1, source_target_pairs={{0,8},{1,9},{2,10},{3,11},{4,12},{5,13},{6,14},{7,15},{8,0},{9,1},... | collective-permute-start | bytes 196616 | tf_op jit(solution)/shard_map/ppermute | solution.py:1011

commit v7 on v6

--- a/solution.py
+++ b/solution.py
@@ -196,6 +196,7 @@
     shrink_hbm,
     pooled_ref,
     hidden_sum_ref,
+    counts_ref,
     qkv_ref,
     probs_ref,
     mixed_ref,
@@ -203,7 +204,6 @@
     slope_ref,
     chars_ref,
     languages_ref,
-    counts_ref,
     table_ref,
     gain_attn_ref,
     project_ref,
@@ -305,10 +305,11 @@
     return pl.pallas_call(
         functools.partial(char_forward_kernel, slots),
         in_specs=[hbm] * 10,
-        out_specs=[vmem] * 7,
+        out_specs=[vmem] * 8,
         out_shape=[
             jax.ShapeDtypeStruct((words, width), bf16),
             jax.ShapeDtypeStruct((words, hidden), bf16),
+            jax.ShapeDtypeStruct(counts.shape, counts.dtype),
             jax.ShapeDtypeStruct((rows, 3 * width), bf16),
             jax.ShapeDtypeStruct((slots, rows * HEADS), f32),
             jax.ShapeDtypeStruct((width, rows), bf16),
@@ -316,7 +317,7 @@
             jax.ShapeDtypeStruct((rows, hidden), bf16),
         ],
         scratch_shapes=[pltpu.VMEM(chars.shape[1:], bf16)]
-        + [pltpu.VMEM(array.shape, array.dtype) for array in fetched]
+        + [pltpu.VMEM(array.shape, array.dtype) for array in fetched if array is not counts]
         + [pltpu.SemaphoreType.DMA((10,))],
         compiler_params=pltpu.CompilerParams(vmem_limit_bytes=16 * MIB),
         cost_estimate=pl.CostEstimate(
@@ -327,6 +328,8 @@
 
 
 CHAR_FIRST_SLOT = 144
+CHAR_SECTION_SLOT = 80
+CHAR_CORE_SLOT = 112
 CHAR_LAST_SLOT = 48
 
 
@@ -355,12 +358,13 @@
 def char_mlp_back_kernel(
     slots,
     shards,
-    counts_hbm,
+    counts_ref,
     gain_mlp_ref,
     expand_ref,
     shrink_ref,
     dpooled_ref,
     hidden_sum_ref,
+    other_sum_ref,
     mixed_ref,
     middle_ref,
     slope_ref,
@@ -368,25 +372,24 @@
     gain_ref,
     keep_ref,
     send_ref,
-    counts_ref,
     dhidden_words,
+    dz,
     dbefore,
     expand_grad,
     shrink_grad,
     output_grad,
-    sem,
 ):
     section, me = position()
-    fetch = pltpu.make_async_copy(counts_hbm, counts_ref, sem)
-    fetch.start()
-    fetch.wait()
     counts = counts_ref[section]
     rows, width = middle_ref.shape
     words = counts.shape[-1]
-    spread = dpooled_ref[...].astype(f32) / counts_column(counts)
+    spread = dpooled_ref[:words].astype(f32) / counts_column(counts)
     spread_high = spread.astype(bf16)
     spread_low = (spread - spread_high.astype(f32)).astype(bf16)
     dhidden_words[...] = dot_nt(spread_high, shrink_ref[...]).astype(bf16)
+    dz[:words] = spread_high
+    other = dpooled_ref[words:].astype(f32) / counts_column(counts_ref[1 - section])
+    dz[words:] = other.astype(bf16)
     shape = (rows, words)
     row = rows_of(shape)
     member = (row // slots == lanes(shape)) & (row % slots < counts)
@@ -396,15 +399,14 @@
         dbefore[:, part] = dot(member, dhidden_words[:, part]).astype(bf16) * slope_ref[:, part]
     normal, scale = unit(middle_ref[...])
     normed_t = (normal * gain_mlp_ref[...]).astype(bf16).T
-    hidden_sum_t = hidden_sum_ref[...].T
-    targets = slot_refs(keep_ref, send_ref)
-
-    def put(gradient, at):
-        return put_shards(gradient, targets, lambda slot: char_shard(slot, me), at)
+    hidden_sums = jnp.concatenate([hidden_sum_ref[...], other_sum_ref[...]], axis=0)
+    hidden_sums_t = hidden_sums.T
 
     dnormed = dot_nt(dbefore[...], expand_ref[...])
     expand_grad[...] = dot(normed_t, dbefore[...])
-    shrink_grad[...] = dot(hidden_sum_t, spread_high)
+    half = width // 2
+    own_half = dz[:, pl.ds(pl.multiple_of(section * half, half), half)]
+    shrink_grad[...] = dot(hidden_sums_t, own_half)
     dmiddle = (
         dot(member, spread_high)
         + dot(member, spread_low)
@@ -415,23 +417,29 @@
     gain_ref[...] = jnp.broadcast_to(
         jnp.sum(dnormed * normal, axis=0, keepdims=True), gain_ref.shape
     )
-    at = put(expand_grad, 0)
-    at = put(shrink_grad, at)
-    put(output_grad, at)
-
-
-def char_mlp_back(counts, weights, dpooled, stored, slots, shards):
+    targets = slot_refs(keep_ref, send_ref)
+    at = 0
+    for gradient in (expand_grad, output_grad):
+        at = put_shards(gradient, targets, lambda slot: char_shard(slot, me), at)
+    size = shrink_grad.shape[0] // shards
+    for number, target in enumerate(targets):
+        first = pl.multiple_of(char_shard(number, me) * size, size)
+        piece = shrink_grad[pl.ds(first, size), :].astype(bf16)
+        target[at:, :half] = piece[: size // 2]
+        target[at:, half:] = piece[size // 2 :]
+
+
+def char_mlp_back(counts, weights, dpooled, stored, other_sum, slots, shards):
     _, _, output, gain_mlp, expand_w, shrink = weights
     hidden_sum, _, _, mixed, middle, slope = stored
     rows, width = middle.shape
     words = rows // slots
     hidden = expand_w.shape[1]
-    half = (shards // 2, CHAR_FIRST_SLOT, width)
+    half = (shards // 2, CHAR_CORE_SLOT, width)
     vmem = pl.BlockSpec(memory_space=pltpu.VMEM)
-    hbm = pl.BlockSpec(memory_space=pltpu.HBM)
     return pl.pallas_call(
         functools.partial(char_mlp_back_kernel, slots, shards),
-        in_specs=[hbm] + [vmem] * 8,
+        in_specs=[vmem] * 10,
         out_specs=[vmem] * 4,
         out_shape=[
             jax.ShapeDtypeStruct((rows, width), f32),
@@ -440,20 +448,30 @@
             jax.ShapeDtypeStruct(half, bf16),
         ],
         scratch_shapes=[
-            pltpu.VMEM(counts.shape, counts.dtype),
             pltpu.VMEM((words, hidden), bf16),
+            pltpu.VMEM((2 * words, width), bf16),
             pltpu.VMEM((rows, hidden), bf16),
             pltpu.VMEM(expand_w.shape, f32),
-            pltpu.VMEM(shrink.shape, f32),
+            pltpu.VMEM((hidden, width // 2), f32),
             pltpu.VMEM(output.shape, f32),
-            pltpu.SemaphoreType.DMA,
         ],
         compiler_params=pltpu.CompilerParams(vmem_limit_bytes=16 * MIB),
         cost_estimate=pl.CostEstimate(
             flops=64 * rows * width * width, bytes_accessed=8 * MIB, transcendentals=0
         ),
         name="char_mlp_back",
-    )(in_hbm(counts), gain_mlp, expand_w, shrink, dpooled, hidden_sum, mixed, middle, slope)
+    )(
+        counts,
+        gain_mlp,
+        expand_w,
+        shrink,
+        dpooled,
+        hidden_sum,
+        other_sum,
+        mixed,
+        middle,
+        slope,
+    )
 
 
 def char_attn_back_kernel(
@@ -525,9 +543,8 @@
         ],
         axis=0,
     ).astype(bf16)
-    at = shards // 2 * CHAR_LAST_SLOT
     for ref in (keep_ref, send_ref):
-        ref[at : at + 16] = extra
+        ref[ref.shape[0] - 16 :] = extra
     leave.wait()
 
 
@@ -578,7 +595,11 @@
     )
 
 
+LONG = pl.CostEstimate(flops=20_000_000_000, bytes_accessed=8 * MIB, transcendentals=0)
+
 WORD_SLOT = 416
+
+SHORT_FLOPS = 475_000_000
 
 
 def word_kernel(
@@ -629,10 +650,10 @@
     width = output_ref.shape[0]
     section, me = position()
     slabs = width // SLAB
-    for place, ref in enumerate((own_ref, far_ref, section_ref, both_ref)):
+    for place, ref in enumerate((own_ref, section_ref, far_ref, both_ref)):
         pooled[place * length : (place + 1) * length] = ref[...]
     for place, (ref, other) in enumerate(
-        ((cot_ref, section), (cot_far_ref, section), (cot_ref, 1 - section), (cot_far_ref, 1 - section))
+        ((cot_ref, section), (cot_ref, 1 - section), (cot_far_ref, section), (cot_far_ref, 1 - section))
     ):
         dz[place * length : (place + 1) * length] = ref[other]
 
@@ -713,7 +734,7 @@
     dnormed = dot_nt(dqkv[...], project_ref[...])
     project_grad[...] = dot(own_rows(normed_t), own_columns(dqkv))
     dword = (dmiddle + unit_back(dnormed, gain_attn_ref[...], normal, scale)).astype(bf16)
-    dpooled_ref[...] = dot_nt(dword[:length], input_ref[...]).astype(bf16)
+    dpooled_ref[...] = dot_nt(dword[: 2 * length], input_ref[...]).astype(bf16)
     dstart[...] = dword
     gain_attn_grad = jnp.sum(dnormed * normal, axis=0, keepdims=True)
     input_grad[...] = dot(own_rows(pooled_t), own_columns(dstart))
@@ -746,7 +767,7 @@
         out_specs=[hbm, vmem, vmem, vmem],
         out_shape=[
             jax.ShapeDtypeStruct((length, width), f32),
-            jax.ShapeDtypeStruct((length, channels), bf16),
+            jax.ShapeDtypeStruct((2 * length, channels), bf16),
             jax.ShapeDtypeStruct(half, bf16),
             jax.ShapeDtypeStruct(half, bf16),
         ],
@@ -809,42 +830,63 @@
     )(keep, arrived)
 
 
-def first_sum_kernel(keep, arrived, stay_ref, go_ref):
+def first_sum_kernel(keep, arrived, stay_ref, go_ref, shrink_ref):
     section, _ = position()
     half = SLAB // 2
     for place in range(keep.shape[0]):
         total = added(keep[place], arrived[place])
-        stay_ref[place], go_ref[place] = by_section(section, total[:, :half], total[:, half:])
+        rows = total[:CHAR_SECTION_SLOT]
+        stay_ref[place], go_ref[place] = by_section(section, rows[:, :half], rows[:, half:])
+        rows = total[CHAR_SECTION_SLOT:]
+        shrink_ref[place] = jnp.concatenate([rows[:, :half], rows[:, half:]], axis=0)
 
 
 def first_sum(keep, arrived):
-    half = jax.ShapeDtypeStruct(keep.shape[:2] + (SLAB // 2,), bf16)
+    half = jax.ShapeDtypeStruct((keep.shape[0], CHAR_SECTION_SLOT, SLAB // 2), bf16)
+    shrink = jax.ShapeDtypeStruct(
+        (keep.shape[0], CHAR_FIRST_SLOT - CHAR_SECTION_SLOT, SLAB // 2), bf16
+    )
     return pl.pallas_call(
         first_sum_kernel,
-        out_shape=[half, half],
+        out_shape=[half, half, shrink],
         compiler_params=pltpu.CompilerParams(vmem_limit_bytes=12 * MIB),
         name="first_sum",
     )(keep, arrived)
 
 
-def second_sum_kernel(first, keep, arrived, *outs):
+def section_sum_kernel(stay, arrived, out):
+    out[...] = added(stay[...], arrived[...])
+
+
+def section_sum(stay, arrived):
+    return pl.pallas_call(
+        section_sum_kernel,
+        out_shape=jax.ShapeDtypeStruct(stay.shape, bf16),
+        compiler_params=pltpu.CompilerParams(vmem_limit_bytes=12 * MIB),
+        cost_estimate=pl.CostEstimate(flops=SHORT_FLOPS, bytes_accessed=0, transcendentals=0),
+        name="section_sum",
+    )(stay, arrived)
+
+
+def second_sum_kernel(first, shrink, keep, core_arrived, *outs):
     _, me = position()
     half = SLAB // 2
-    extra = summed(keep[-16:], arrived[-16:])
+    extra = summed(keep[-16:], core_arrived[-16:])
     for place, out in enumerate(outs):
         at = CHAR_FIRST_SLOT
         for far in range(2):
             entry = 2 * place + far
             columns = slice(far * half, (far + 1) * half)
-            out[:CHAR_FIRST_SLOT, columns] = first[entry]
+            total = first[entry]
+            middle = CHAR_SECTION_SLOT - 16
+            out[:middle, columns] = total[:middle]
+            out[middle : CHAR_FIRST_SLOT - 16, columns] = shrink[entry]
+            out[CHAR_FIRST_SLOT - 16 : CHAR_FIRST_SLOT, columns] = total[middle:]
             rows = slice(entry * CHAR_LAST_SLOT, (entry + 1) * CHAR_LAST_SLOT)
-            out[at : at + CHAR_LAST_SLOT] = added(keep[rows], arrived[rows])
+            out[at : at + CHAR_LAST_SLOT] = added(keep[rows], core_arrived[rows])
             at += CHAR_LAST_SLOT
             turn = lax.rem(SLAB - char_shard(entry, me) * 16, SLAB)
             out[-16:, columns] = pltpu.roll(extra, turn, 1)[:, :half].astype(bf16)
-
-
-LONG = pl.CostEstimate(flops=20_000_000_000, bytes_accessed=8 * MIB, transcendentals=0)
 
 
 def total_kernel(*refs):
@@ -861,22 +903,6 @@
     )(*pieces)
 
 
-def pair_kernel(one, other, _, out):
-    out[...] = added(one[...], other[...])
-
-
-def pair_of(one, other, after):
-    vmem = pl.BlockSpec(memory_space=pltpu.VMEM)
-    return pl.pallas_call(
-        pair_kernel,
-        in_specs=[vmem, vmem, pl.BlockSpec(memory_space=pl.ANY)],
-        out_shape=jax.ShapeDtypeStruct(one.shape, bf16),
-        compiler_params=pltpu.CompilerParams(vmem_limit_bytes=12 * MIB),
-        cost_estimate=LONG,
-        name="pair",
-    )(one, other, after)
-
-
 def second_sum(first, last):
     rows = CHAR_FIRST_SLOT + 2 * CHAR_LAST_SLOT + 16
     return pl.pallas_call(
@@ -884,99 +910,81 @@
         out_shape=[jax.ShapeDtypeStruct((rows, SLAB), bf16)] * 4,
         compiler_params=pltpu.CompilerParams(vmem_limit_bytes=12 * MIB),
         name="second_sum",
-    )(first, *last)
+    )(*first, *last)
 
 
 FOLD = 80
 
 
 def plane_sum_kernel(*refs):
-    word, char, near_ref, far_ref = (refs[0], refs[1:5], refs[5], refs[6])
-    near_ref[:WORD_SLOT] = word[...]
     half = SLAB // 2
-    for far, out, at in ((0, near_ref, WORD_SLOT), (1, far_ref, 0)):
+    pieces = refs[:4]
+    for far, out in enumerate(refs[5:]):
         columns = slice(far * half, (far + 1) * half)
-        total = added(*[ref[:CHAR_FIRST_SLOT, columns] for ref in char])
-        out[at : at + FOLD, :half] = total[:FOLD]
-        out[at : at + FOLD, half:] = total[CHAR_FIRST_SLOT - FOLD :]
-        out[at : at + 16, half:] = added(*[ref[-16:, columns] for ref in char])
+        total = added(*[ref[:CHAR_FIRST_SLOT, columns] for ref in pieces])
+        out[:FOLD, :half] = total[:FOLD]
+        out[:FOLD, half:] = total[CHAR_FIRST_SLOT - FOLD :]
+        out[:16, half:] = added(*[ref[-16:, columns] for ref in pieces])
         first = CHAR_FIRST_SLOT + far * CHAR_LAST_SLOT
-        at += FOLD
-        out[at : at + CHAR_LAST_SLOT] = added(
-            *[ref[first : first + CHAR_LAST_SLOT] for ref in char]
-        )
-
-
-def plane_sum(word, char):
-    rows = FOLD + CHAR_LAST_SLOT
+        out[FOLD:] = added(*[ref[first : first + CHAR_LAST_SLOT] for ref in pieces])
+
+
+def plane_sum(pieces, after):
     return pl.pallas_call(
         plane_sum_kernel,
-        out_shape=[
-            jax.ShapeDtypeStruct((WORD_SLOT + rows, SLAB), bf16),
-            jax.ShapeDtypeStruct((rows, SLAB), bf16),
-        ],
+        in_specs=[pl.BlockSpec(memory_space=pltpu.VMEM)] * 4 + [pl.BlockSpec(memory_space=pl.ANY)],
+        out_shape=[jax.ShapeDtypeStruct((FOLD + CHAR_LAST_SLOT, SLAB), bf16)] * 2,
         compiler_params=pltpu.CompilerParams(vmem_limit_bytes=12 * MIB),
+        cost_estimate=LONG,
         name="plane_sum",
-    )(word, *char)
-
-
-def last_sum_kernel(near_ref, both_ref, high_ref, section_ref, *outs):
-    word_rows = WORD_SLOT
-    section, me = position()
-    own = near_ref[:word_rows].astype(f32)
-    halves = by_section(section, own, section_ref[:word_rows].astype(f32))
+    )(*pieces, after)
+
+
+def char_last_kernel(near_ref, both_ref, far_ref, section_ref, _, *outs):
+    section, _ = position()
     half = SLAB // 2
-
-    mine_too = summed(near_ref[word_rows : word_rows + FOLD], high_ref[:FOLD])
-    theirs = summed(section_ref[word_rows : word_rows + FOLD], both_ref[:FOLD])
+    mine = summed(near_ref[:FOLD], far_ref[:FOLD])
+    theirs = summed(section_ref[:FOLD], both_ref[:FOLD])
 
     def unfold(total):
         return jnp.concatenate(
             [total[:, :half], total[2 * FOLD - CHAR_FIRST_SLOT :, half:]], axis=0
         )
 
-    first = jnp.concatenate(by_section(section, unfold(mine_too), unfold(theirs)), axis=1)
-    extra = mine_too[:16, half:] + theirs[:16, half:]
-    last = summed(
-        near_ref[word_rows + FOLD :],
-        section_ref[word_rows + FOLD :],
-        high_ref[FOLD:],
-        both_ref[FOLD:],
-    )
-
-    def mine(vector, size):
-        turned = pltpu.roll(vector, lax.rem(SLAB - lax.rem(me * size, SLAB), SLAB), 1)
-        return turned[:, :size]
-
-    (
-        table_ref,
-        gain_attn_ref,
-        project_ref,
-        output_ref,
-        gain_mlp_ref,
-        expand_ref,
-        shrink_ref,
-        w_input_ref,
-        w_gain_attn_ref,
-        w_project_ref,
-        w_output_ref,
-        w_gain_mlp_ref,
-        w_expand_ref,
-        w_shrink_ref,
-    ) = outs
-    for char, refs in ((first, (expand_ref, shrink_ref, output_ref)), (last, (project_ref,))):
+    first = jnp.concatenate(by_section(section, unfold(mine), unfold(theirs)), axis=1)
+    extra = mine[:16, half:] + theirs[:16, half:]
+    last = summed(near_ref[FOLD:], section_ref[FOLD:], far_ref[FOLD:], both_ref[FOLD:])
+    table_ref, gain_attn_ref, project_ref, output_ref, gain_mlp_ref, expand_ref, shrink_ref = outs
+    for total, refs in ((first, (expand_ref, shrink_ref, output_ref)), (last, (project_ref,))):
         at = 0
         for ref in refs:
             size = ref.shape[0]
             for column in range(ref.shape[1] // SLAB):
-                ref[:, column * SLAB : (column + 1) * SLAB] = char[at : at + size]
+                ref[:, column * SLAB : (column + 1) * SLAB] = total[at : at + size]
                 at += size
     size = gain_attn_ref.shape[1]
     gain_attn_ref[...] = extra[0:1, :size]
     gain_mlp_ref[...] = extra[1:2, :size]
     table_ref[...] = extra[8:16, :size]
+
+
+def char_last(near, arrived, shapes, after):
+    return pl.pallas_call(
+        char_last_kernel,
+        in_specs=[pl.BlockSpec(memory_space=pltpu.VMEM)] * 4 + [pl.BlockSpec(memory_space=pltpu.HBM)],
+        out_shape=[jax.ShapeDtypeStruct(shape, f32) for shape in shapes],
+        compiler_params=pltpu.CompilerParams(vmem_limit_bytes=12 * MIB),
+        name="char_last",
+    )(near, *arrived, in_hbm(after))
+
+
+def word_last_kernel(own_ref, other_ref, *outs):
+    section, me = position()
+    own = own_ref[...].astype(f32)
+    halves = by_section(section, own, other_ref[...].astype(f32))
+    input_ref, gain_attn_ref, project_ref, output_ref, gain_mlp_ref, expand_ref, shrink_ref = outs
     at = 0
-    for ref in (w_input_ref, w_project_ref, w_output_ref, w_expand_ref, w_shrink_ref):
+    for ref in (input_ref, project_ref, output_ref, expand_ref, shrink_ref):
         size = ref.shape[0]
         columns = ref.shape[1] // (2 * SLAB)
         for column in range(columns):
@@ -984,21 +992,21 @@
                 first = (half * columns + column) * SLAB
                 ref[:, first : first + SLAB] = halves[half][at : at + size]
             at += size
-    size = w_gain_attn_ref.shape[1]
-    extra = own[at : at + 8]
-    turned = mine(extra, size)
+    size = gain_attn_ref.shape[1]
+    turn = lax.rem(SLAB - lax.rem(me * size, SLAB), SLAB)
+    turned = pltpu.roll(own[at : at + 8], turn, 1)[:, :size]
     upper = me * size >= SLAB
-    w_gain_attn_ref[...] = jnp.where(upper, turned[1:2], turned[0:1])
-    w_gain_mlp_ref[...] = jnp.where(upper, turned[3:4], turned[2:3])
-
-
-def last_sum(near, arrived, shapes):
+    gain_attn_ref[...] = jnp.where(upper, turned[1:2], turned[0:1])
+    gain_mlp_ref[...] = jnp.where(upper, turned[3:4], turned[2:3])
+
+
+def word_last(own, other, shapes):
     return pl.pallas_call(
-        last_sum_kernel,
+        word_last_kernel,
         out_shape=[jax.ShapeDtypeStruct(shape, f32) for shape in shapes],
         compiler_params=pltpu.CompilerParams(vmem_limit_bytes=12 * MIB),
-        name="last_sum",
-    )(near, *arrived)
+        name="word_last",
+    )(own, other)
 
 
 def exchange(value, section_bit, dp_bits):
@@ -1033,17 +1041,21 @@
     chars = chars.reshape(micros, rows, width)
     counts = counts.reshape(micros, 1, words)
     languages = languages.reshape(1, micros)
-    pooled, *stored = char_forward(languages, chars, counts, language_table, char_weights, slots)
+    pooled, hidden_sum, own_counts, *stored = char_forward(
+        languages, chars, counts, language_table, char_weights, slots
+    )
+    stored = (hidden_sum, *stored)
+    other_sum = exchange(hidden_sum, 1, 0)
     others = (exchange(pooled, 1, FAR), exchange(pooled, 1, 0), exchange(pooled, 0, FAR))
     result, dpooled, keep, send = word_group(
         (pooled,) + others, (cot, cot_far), word_input, word_weights, shards
     )
     word = plane_exchange(word_sum(keep, exchange(send, 0, CORE)))
     dmiddle, gain_mlp_grad, keep, send = char_mlp_back(
-        counts, char_weights, dpooled, stored, slots, shards
-    )
-    stay, go = first_sum(keep, exchange(send, 0, CORE))
-    arrived = exchange(go, 1, 0)
+        own_counts, char_weights, dpooled, stored, other_sum, slots, shards
+    )
+    stay, go, shrink = first_sum(keep, exchange(send, 0, CORE))
+    first = (section_sum(stay, exchange(go, 1, 0)), shrink)
     chars_grad, keep, send = char_attn_back(
         languages,
         chars,
@@ -1057,19 +1069,24 @@
         stay,
     )
     last = (keep, exchange(send, 0, CORE))
+    char = plane_exchange(second_sum(first, last))
     word = total_of(*word)
-    first = pair_of(stay, arrived, word)
-    char = plane_exchange(second_sum(first, last))
-    near, far = plane_sum(word, char)
+    near, far = plane_sum(char, word)
     arrived = (exchange(far, 1, FAR), exchange(far, 0, FAR), exchange(near, 1, 0))
-    shapes = [(language_table.shape[0], language_table.shape[1] // shards)]
-    for weight in char_weights + (word_input,) + word_weights:
-        if weight.shape[0] == 1:
-            shapes.append((1, weight.shape[1] // shards))
-        else:
-            shapes.append((weight.shape[0] // shards, weight.shape[1]))
-    totals = last_sum(near, arrived, shapes)
-    totals = [total[0] if total.shape[0] == 1 else total for total in totals]
+
+    def shard_shapes(weights):
+        for weight in weights:
+            if weight.shape[0] == 1:
+                yield (1, weight.shape[1] // shards)
+            else:
+                yield (weight.shape[0] // shards, weight.shape[1])
+
+    table_shape = (language_table.shape[0], language_table.shape[1] // shards)
+    word_shapes = list(shard_shapes((word_input,) + word_weights))
+    word_totals = word_last(word, exchange(word, 1, 0), word_shapes)
+    char_shapes = [table_shape, *shard_shapes(char_weights)]
+    char_totals = char_last(near, arrived, char_shapes, word_totals[0])
+    totals = [total[0] if total.shape[0] == 1 else total for total in char_totals + word_totals]
     return (result[None, None], chars_grad.reshape((1, 1, words, slots, width))) + tuple(totals)
 
 

time: 62.8 us -> 59.2 us (0.943)
  waiting for transfers between devices: 15.6 us -> 10.2 us
  starting transfers between devices: 22.6 us -> 24.6 us
    ppermute x17 -> x19, waiting for transfers between devices: 15.6 us -> 10.2 us  [exchange(): return lax.ppermute(value, ('section', 'dp'), pairs)]
    ppermute x17 -> x19, starting transfers between devices: 22.6 us -> 24.6 us  [exchange(): return lax.ppermute(value, ('section', 'dp'), pairs)]
    pallas_call x1, Pallas kernels: 3.83 us -> 3.12 us  [char_mlp_back(): pl.pallas_call(functools.partial(char_mlp_back_kernel, slots, shards), in...]
    pallas_call x4 -> x5, Pallas kernels: 1.34 us -> 1.85 us  [the longest x1 0.91 us: word_last(): pl.pallas_call(word_last_kernel, out_shape=[jax.ShapeDtypeStruct(shape, f...]
  transfers between devices with their start and end apart: 17 -> 19, of which waited for: 7 -> 8; matrix products, arithmetic and copies ran while one was open for 0% -> 0% of each run, Pallas kernels for 25% -> 38%
where the time goes in v7:
time: 59.2 us; the launch traced here: 59.1 us
  starting transfers between devices  24.6 us (42%)
  Pallas kernels  23.3 us (39%)
  waiting for transfers between devices  10.2 us (17%)
  between operations  0.93 us (2%)
    ppermute x19, starting transfers between devices, exchange(): return lax.ppermute(value, ('section', 'dp'), pairs)  24.6 us
    ppermute x19, waiting for transfers between devices, exchange(): return lax.ppermute(value, ('section', 'dp'), pairs)  10.2 us
    pallas_call x1, Pallas kernels, word_group(): pl.pallas_call(functools.partial(word_kernel, length, shards), in_specs=[...  6.76 us
    pallas_call x1, Pallas kernels, char_forward(): pl.pallas_call(functools.partial(char_forward_kernel, slots), in_specs=[h...  6.25 us
    pallas_call x1, Pallas kernels, char_attn_back(): pl.pallas_call(functools.partial(char_attn_back_kernel, slots, shards), i...  4.86 us
    pallas_call x1, Pallas kernels, char_mlp_back(): pl.pallas_call(functools.partial(char_mlp_back_kernel, slots, shards), in...  3.12 us
  transfers between devices with their start and end apart: 19, of which 8 were waited for; matrix products, arithmetic and copies ran while one was open for 0% of the time, Pallas kernels for 38%

profile of v7, /device:TPU:0, one launch (start us, length us, event | category | flops | bytes accessed | tf_op | source)
XLA Modules:
  0.0 59.1 jit_solution(3518545022733020094)
XLA Ops:
  0.6 4.1 %collective-permute-start.3 = (bf16[2,64,512]{2,1,0:T(8,128)(2,1)}, bf16[2,64,512]{2,1,0:T(8,128)(2,1)S(1)}, u32[]{:S(2)}, u32[]{:S(2)}) collective-permute-start(bf16[2,64,512]{2,1,0:T(8,128)(2,1)} %bitcast.15), channel_id=1, source_target_pairs={{0,8},{1,9},{2,10},{3,11},{4,12},{5,13},{6,14},{7,15},{8,0},{9,1},... | collective-permute-start | bytes 393224 | tf_op jit(solution)/shard_map/ppermute | solution.py:1019
  4.8 0.0 copy-start.10
  4.8 0.0 copy-start.11
  4.8 0.0 copy-start.12
  4.8 0.0 copy-start.13
  4.8 6.3 %char_forward.1 = (bf16[64,256]{1,0:T(8,128)(2,1)S(1)}, bf16[64,1024]{1,0:T(8,128)(2,1)S(1)}, s32[2,1,64]{2,1,0:T(1,128)S(1)}, bf16[1024,768]{1,0:T(8,128)(2,1)S...) custom-call(bf16[2,1024,256]{2,1,0:T(8,128)(2,1)} %bitcast.21, ...), custom_call_target="tpu_custom_call" | custom-call | flops 4294967296 | bytes 8388608 | tf_op jit(solution)/shard_map/char_forward/pallas_call | solution.py:305
  11.1 1.3 %collective-permute-start = (bf16[64,256]{1,0:T(8,128)(2,1)S(1)}, bf16[64,256]{1,0:T(8,128)(2,1)S(1)}, u32[]{:S(2)}, u32[]{:S(2)}) collective-permute-start(bf16[64,256]{1,0:T(8,128)(2,1)S(1)} %get-tuple-element.62.own_ref), channel_id=1, source_target_pairs={{0,24},{1,25},{2,26},{3,27},{4,28},{5,29},{6,30},{7,31},{8,16},{9,... | collective-permute-start | bytes 98312 | tf_op jit(solution)/shard_map/ppermute | solution.py:1019
  12.4 0.3 collective-permute-start.1
  12.7 2.8 %collective-permute-start.2 = (bf16[64,256]{1,0:T(8,128)(2,1)S(1)}, bf16[64,256]{1,0:T(8,128)(2,1)S(1)}, u32[]{:S(2)}, u32[]{:S(2)}) collective-permute-start(bf16[64,256]{1,0:T(8,128)(2,1)S(1)} %get-tuple-element.62.own_ref), channel_id=1, source_target_pairs={{0,8},{1,9},{2,10},{3,11},{4,12},{5,13},{6,14},{7,15},{8,0},{9,1},... | collective-permute-start | bytes 98312 | tf_op jit(solution)/shard_map/ppermute | solution.py:1019
  15.5 1.5 %collective-permute-start.4 = (bf16[64,1024]{1,0:T(8,128)(2,1)S(1)}, bf16[64,1024]{1,0:T(8,128)(2,1)S(1)}, u32[]{:S(2)}, u32[]{:S(2)}) collective-permute-start(bf16[64,1024]{1,0:T(8,128)(2,1)S(1)} %get-tuple-element.66.hidden_sum_ref), channel_id=1, source_target_pairs={{0,16},{1,17},{2,18},{3,19},{4,20},{5,21},{6,22},{7,23},{8,24},{9,... | collective-permute-start | bytes 393224 | tf_op jit(solution)/shard_map/ppermute | solution.py:1019
  17.0 0.2 collective-permute-done.both_ref
  17.2 0.0 collective-permute-done.1.section_ref
  17.2 0.3 collective-permute-done.2.far_ref
  17.5 0.0 collective-permute-done.3.cot_far_ref
  17.5 0.0 copy-done.4
  17.5 0.0 copy-done.5
  17.5 0.0 copy-done.6
  17.6 0.0 copy-start.8
  17.6 0.0 copy-start.9
  17.6 0.0 copy-start.14
  17.6 6.8 %word_group.1 = (f32[64,512]{1,0:T(8,128)}, bf16[128,256]{1,0:T(8,128)(2,1)S(1)}, bf16[4,416,256]{2,1,0:T(8,128)(2,1)S(1)}, bf16[4,416,256]{2,1,0:T(8,128)(2,1)S(1)}) custom-call(bf16[64,256]{1,0:T(8,128)(2,1)S(1)} %get-tuple-element.62.own_ref, bf16[64,256]{1,0:T(8,128)(2,1)S(1)} %collective-permute-done.both_ref, ...), custom_call_target="tpu_custom_call" | custom-call | flops 6710886400 | bytes 8388608 | tf_op jit(solution)/shard_map/word_group/pallas_call | solution.py:764
  24.4 0.1 collective-permute-start.11
  24.5 0.0 collective-permute-done.4.other_sum_ref
  24.5 3.1 %char_mlp_back.1 = (f32[1024,256]{1,0:T(8,128)S(1)}, f32[8,256]{1,0:T(8,128)S(1)}, bf16[8,112,256]{2,1,0:T(8,128)(2,1)S(1)}, bf16[8,112,256]{2,1,0:T(8,128)(2,1)S(1)}) custom-call(s32[2,1,64]{2,1,0:T(1,128)S(1)} %get-tuple-element.64.counts_ref, f32[1,256]{1,0:T(1,128)S(1)} %bitcast.20, bf16[256,1024]{1,0:T(8,128)(2,1)S(1)} %copy-done.8, ...), custom_call_target="tpu_custom_call" | custom-call | flops 4294967296 | bytes 8388608 | tf_op jit(solution)/shard_map/char_mlp_back/pallas_call | solution.py:440
  27.6 0.0 copy-start
  27.7 0.0 copy-start.1
  27.7 0.0 copy-start.2
  27.7 0.0 copy-start.3
  27.7 0.5 collective-permute-start.5
  28.2 0.0 collective-permute-done.11.arrived
  28.2 0.2 word_sum.1
  28.4 2.8 %collective-permute-start.12 = (bf16[416,256]{1,0:T(8,128)(2,1)S(1)}, bf16[416,256]{1,0:T(8,128)(2,1)S(1)}, u32[]{:S(2)}, u32[]{:S(2)}) collective-permute-start(bf16[416,256]{1,0:T(8,128)(2,1)S(1)} %get-tuple-element.88), channel_id=1, source_target_pairs={{0,6},{1,7},{2,4},{3,5},{4,2},{5,3},{6,0},{7,1},{8,14},{9,15},{10,... | collective-permute-start | bytes 638984 | tf_op jit(solution)/shard_map/ppermute | solution.py:1019
  31.3 0.8 %collective-permute-start.13 = (bf16[416,256]{1,0:T(8,128)(2,1)S(1)}, bf16[416,256]{1,0:T(8,128)(2,1)S(1)}, u32[]{:S(2)}, u32[]{:S(2)}) collective-permute-start(bf16[416,256]{1,0:T(8,128)(2,1)S(1)} %get-tuple-element.89), channel_id=1, source_target_pairs={{0,4},{1,5},{2,6},{3,7},{4,0},{5,1},{6,2},{7,3},{8,12},{9,13},{10,... | collective-permute-start | bytes 638984 | tf_op jit(solution)/shard_map/ppermute | solution.py:1019
  32.1 0.0 collective-permute-start.14
  32.1 0.0 collective-permute-done.5.arrived
  32.1 0.1 first_sum.1
  32.2 1.7 %collective-permute-start.6 = (bf16[8,80,128]{2,1,0:T(8,128)(2,1)S(1)}, bf16[8,80,128]{2,1,0:T(8,128)(2,1)S(1)}, u32[]{:S(2)}, u32[]{:S(2)}) collective-permute-start(bf16[8,80,128]{2,1,0:T(8,128)(2,1)S(1)} %get-tuple-element.78), channel_id=1, source_target_pairs={{0,16},{1,17},{2,18},{3,19},{4,20},{5,21},{6,22},{7,23},{8,24},{9,... | collective-permute-start | bytes 491528 | tf_op jit(solution)/shard_map/ppermute | solution.py:1019
  33.9 0.0 copy-done.2
  33.9 4.9 %char_attn_back.1 = (f32[1024,256]{1,0:T(8,128)}, bf16[400,256]{1,0:T(8,128)(2,1)S(1)}, bf16[400,256]{1,0:T(8,128)(2,1)S(1)}) custom-call(bf16[8,80,128]{2,1,0:T(8,128)(2,1)S(1)} %get-tuple-element.72._.stay, bf16[2,1024,256]{2,1,0:T(8,128)(2,1)} %bitcast.22, s32[1,2]{1,0:T(1,128)} %bitcast.24, bf16[8,256]{1,0:T(8,128)(2,1)S(1)} %copy-done.2, ...), custom_call_target="tpu_custom_call" | custom-call | tf_op jit(solution)/shard_map/char_attn_back/pallas_call | solution.py:560
  38.8 0.1 collective-permute-start.7
  38.9 0.0 collective-permute-done.6.arrived
  38.9 1.4 %collective-permute-done.7.core_arrived = bf16[400,256]{1,0:T(8,128)(2,1)S(1)} collective-permute-done((bf16[400,256]{1,0:T(8,128)(2,1)S(1)}, bf16[400,256]{1,0:T(8,128)(2,1)S(1)}, u32[]{:S(2)}, u32[]{:S(2)}) %collective-permute-start.7) | collective-permute-done | bytes 204832 | tf_op jit(solution)/shard_map/ppermute | solution.py:1019
  40.3 0.1 second_sum.1
  40.4 1.6 %collective-permute-start.10 = (bf16[256,256]{1,0:T(8,128)(2,1)S(1)}, bf16[256,256]{1,0:T(8,128)(2,1)S(1)}, u32[]{:S(2)}, u32[]{:S(2)}) collective-permute-start(bf16[256,256]{1,0:T(8,128)(2,1)S(1)} %get-tuple-element.84), channel_id=1, source_target_pairs={{0,2},{1,3},{2,0},{3,1},{4,6},{5,7},{6,4},{7,5},{8,10},{9,11},{10,... | collective-permute-start | bytes 393224 | tf_op jit(solution)/shard_map/ppermute | solution.py:1019
  42.0 1.5 %collective-permute-start.8 = (bf16[256,256]{1,0:T(8,128)(2,1)S(1)}, bf16[256,256]{1,0:T(8,128)(2,1)S(1)}, u32[]{:S(2)}, u32[]{:S(2)}) collective-permute-start(bf16[256,256]{1,0:T(8,128)(2,1)S(1)} %get-tuple-element.82), channel_id=1, source_target_pairs={{0,6},{1,7},{2,4},{3,5},{4,2},{5,3},{6,0},{7,1},{8,14},{9,15},{10,... | collective-permute-start | bytes 393224 | tf_op jit(solution)/shard_map/ppermute | solution.py:1019
  43.5 0.0 collective-permute-done.12.refs_0_
  43.6 0.4 collective-permute-start.9
  44.0 0.0 collective-permute-done.13.refs_1_
  44.0 0.0 collective-permute-done.14.refs_2_
  44.0 0.1 total.1.refs_4_.own_ref
  44.1 0.5 collective-permute-start.18
  44.6 3.8 %collective-permute-done.10.refs_2_ = bf16[256,256]{1,0:T(8,128)(2,1)S(1)} collective-permute-done((bf16[256,256]{1,0:T(8,128)(2,1)S(1)}, bf16[256,256]{1,0:T(8,128)(2,1)S(1)}, u32[]{:S(2)}, u32[]{:S(2)}) %collective-permute-start.10) | collective-permute-done | bytes 131104 | tf_op jit(solution)/shard_map/ppermute | solution.py:1019
  48.4 0.9 %collective-permute-done.8.refs_0_ = bf16[256,256]{1,0:T(8,128)(2,1)S(1)} collective-permute-done((bf16[256,256]{1,0:T(8,128)(2,1)S(1)}, bf16[256,256]{1,0:T(8,128)(2,1)S(1)}, u32[]{:S(2)}, u32[]{:S(2)}) %collective-permute-start.8) | collective-permute-done | bytes 131104 | tf_op jit(solution)/shard_map/ppermute | solution.py:1019
  49.3 0.8 %collective-permute-done.9.refs_1_ = bf16[256,256]{1,0:T(8,128)(2,1)S(1)} collective-permute-done((bf16[256,256]{1,0:T(8,128)(2,1)S(1)}, bf16[256,256]{1,0:T(8,128)(2,1)S(1)}, u32[]{:S(2)}, u32[]{:S(2)}) %collective-permute-start.9) | collective-permute-done | bytes 131104 | tf_op jit(solution)/shard_map/ppermute | solution.py:1019
  50.1 0.1 plane_sum.1
  50.2 2.8 %collective-permute-start.15 = (bf16[128,256]{1,0:T(8,128)(2,1)S(1)}, bf16[128,256]{1,0:T(8,128)(2,1)S(1)}, u32[]{:S(2)}, u32[]{:S(2)}) collective-permute-start(bf16[128,256]{1,0:T(8,128)(2,1)S(1)} %get-tuple-element.93), channel_id=1, source_target_pairs={{0,24},{1,25},{2,26},{3,27},{4,28},{5,29},{6,30},{7,31},{8,16},{9,... | collective-permute-start | bytes 196616 | tf_op jit(solution)/shard_map/ppermute | solution.py:1019
  52.9 0.4 collective-permute-start.16
  53.3 1.3 %collective-permute-start.17 = (bf16[128,256]{1,0:T(8,128)(2,1)S(1)}, bf16[128,256]{1,0:T(8,128)(2,1)S(1)}, u32[]{:S(2)}, u32[]{:S(2)}) collective-permute-start(bf16[128,256]{1,0:T(8,128)(2,1)S(1)} %get-tuple-element.92.near_ref), channel_id=1, source_target_pairs={{0,16},{1,17},{2,18},{3,19},{4,20},{5,21},{6,22},{7,23},{8,24},{9,... | collective-permute-start | bytes 196616 | tf_op jit(solution)/shard_map/ppermute | solution.py:1019
  54.6 0.0 collective-permute-done.18.other_ref
  54.6 0.9 %word_last.1 = (f32[16,512]{1,0:T(8,128)}, f32[1,32]{1,0:T(1,128)}, f32[32,1536]{1,0:T(8,128)}, f32[32,512]{1,0:T(8,128)}, f32[1,32]{1,0:T(1,128)}, /*index=5*/f32[32,2048]{1,0:T(8,128)}, f32[128,512]{1,0:T(8,128)}) custom-call(bf16[416,256]{1,0:T(8,128)(2,1)S(1)} %total.1.refs_4_.own_ref, bf16[416,256]{1,0:T(8,128)(2,1)S(1)} %collective-permute-done.18.other_ref), custom_call_target="tpu_custom_call" | custom-call | tf_op jit(solution)/shard_map/word_last/pallas_call | solution.py:1004
  55.5 0.9 %collective-permute-done.15.both_ref = bf16[128,256]{1,0:T(8,128)(2,1)S(1)} collective-permute-done((bf16[128,256]{1,0:T(8,128)(2,1)S(1)}, bf16[128,256]{1,0:T(8,128)(2,1)S(1)}, u32[]{:S(2)}, u32[]{:S(2)}) %collective-permute-start.15) | collective-permute-done | bytes 65568 | tf_op jit(solution)/shard_map/ppermute | solution.py:1019
  56.4 2.0 %collective-permute-done.16.far_ref = bf16[128,256]{1,0:T(8,128)(2,1)S(1)} collective-permute-done((bf16[128,256]{1,0:T(8,128)(2,1)S(1)}, bf16[128,256]{1,0:T(8,128)(2,1)S(1)}, u32[]{:S(2)}, u32[]{:S(2)}) %collective-permute-start.16) | collective-permute-done | bytes 65568 | tf_op jit(solution)/shard_map/ppermute | solution.py:1019
  58.4 0.0 collective-permute-done.17.section_ref
  58.4 0.7 %char_last.1 = (f32[8,16]{1,0:T(8,128)}, f32[1,16]{1,0:T(1,128)}, f32[16,768]{1,0:T(8,128)}, f32[16,256]{1,0:T(8,128)}, f32[1,16]{1,0:T(1,128)}, /*index=5*/f32[16,1024]{1,0:T(8,128)}, f32[64,256]{1,0:T(8,128)}) custom-call(bf16[128,256]{1,0:T(8,128)(2,1)S(1)} %get-tuple-element.92.near_ref, bf16[128,256]{1,0:T(8,128)(2,1)S(1)} %collective-permute-done.15.both_ref, ...), custom_call_target="tpu_custom_call" | custom-call | tf_op jit(solution)/shard_map/char_last/pallas_call | solution.py:972
  (16 shorter events, 0.1 us)
Async XLA Ops:
  0.6 16.9 %collective-permute-start.3 = (bf16[2,64,512]{2,1,0:T(8,128)(2,1)}, bf16[2,64,512]{2,1,0:T(8,128)(2,1)S(1)}, u32[]{:S(2)}, u32[]{:S(2)}) collective-permute-start(bf16[2,64,512]{2,1,0:T(8,128)(2,1)} %bitcast.15), channel_id=1, source_target_pairs={{0,8},{1,9},{2,10},{3,11},{4,12},{5,13},{6,14},{7,15},{8,0},{9,1},... | collective-permute-start | bytes 393224 | tf_op jit(solution)/shard_map/ppermute | solution.py:1019
  4.8 12.8 %copy-start.4 = (bf16[512,2048]{1,0:T(8,128)(2,1)S(1)}, bf16[512,2048]{1,0:T(8,128)(2,1)}, u32[]{:S(2)}) copy-start(bf16[512,2048]{1,0:T(8,128)(2,1)} %expand_ref.2) | copy-start | bytes 6291460
  4.8 12.8 %copy-start.5 = (bf16[2048,512]{1,0:T(8,128)(2,1)S(1)}, bf16[2048,512]{1,0:T(8,128)(2,1)}, u32[]{:S(2)}) copy-start(bf16[2048,512]{1,0:T(8,128)(2,1)} %shrink_ref.2) | copy-start | bytes 6291460
  4.8 12.8 %copy-start.6 = (bf16[512,1536]{1,0:T(8,128)(2,1)S(1)}, bf16[512,1536]{1,0:T(8,128)(2,1)}, u32[]{:S(2)}) copy-start(bf16[512,1536]{1,0:T(8,128)(2,1)} %project_ref.2) | copy-start | bytes 4718596
  4.8 12.8 %copy-start.7 = (bf16[512,512]{1,0:T(8,128)(2,1)S(1)}, bf16[512,512]{1,0:T(8,128)(2,1)}, u32[]{:S(2)}) copy-start(bf16[512,512]{1,0:T(8,128)(2,1)} %output_ref.2) | copy-start | bytes 1572868
  4.8 12.8 %copy-start.10 = (bf16[256,512]{1,0:T(8,128)(2,1)S(1)}, bf16[256,512]{1,0:T(8,128)(2,1)}, u32[]{:S(2)}) copy-start(bf16[256,512]{1,0:T(8,128)(2,1)} %input_ref.1) | copy-start | bytes 786436
  4.8 12.8 %copy-start.11 = (bf16[2,1,64,512]{3,2,1,0:T(8,128)(2,1)S(1)}, bf16[2,1,64,512]{3,2,1,0:T(8,128)(2,1)}, u32[]{:S(2)}) copy-start(bf16[2,1,64,512]{3,2,1,0:T(8,128)(2,1)} %param.35) | copy-start | bytes 393220
  4.8 12.8 %copy-start.12 = (f32[512]{0:T(512)S(1)}, f32[512]{0:T(512)}, u32[]{:S(2)}) copy-start(f32[512]{0:T(512)} %param.29) | copy-start | bytes 6148
  4.8 12.8 %copy-start.13 = (f32[512]{0:T(512)S(1)}, f32[512]{0:T(512)}, u32[]{:S(2)}) copy-start(f32[512]{0:T(512)} %param.32) | copy-start | bytes 6148
  11.1 6.2 %collective-permute-start = (bf16[64,256]{1,0:T(8,128)(2,1)S(1)}, bf16[64,256]{1,0:T(8,128)(2,1)S(1)}, u32[]{:S(2)}, u32[]{:S(2)}) collective-permute-start(bf16[64,256]{1,0:T(8,128)(2,1)S(1)} %get-tuple-element.62.own_ref), channel_id=1, source_target_pairs={{0,24},{1,25},{2,26},{3,27},{4,28},{5,29},{6,30},{7,31},{8,16},{9,... | collective-permute-start | bytes 98312 | tf_op jit(solution)/shard_map/ppermute | solution.py:1019
  12.4 4.9 %collective-permute-start.1 = (bf16[64,256]{1,0:T(8,128)(2,1)S(1)}, bf16[64,256]{1,0:T(8,128)(2,1)S(1)}, u32[]{:S(2)}, u32[]{:S(2)}) collective-permute-start(bf16[64,256]{1,0:T(8,128)(2,1)S(1)} %get-tuple-element.62.own_ref), channel_id=1, source_target_pairs={{0,16},{1,17},{2,18},{3,19},{4,20},{5,21},{6,22},{7,23},{8,24},{9,... | collective-permute-start | bytes 98312 | tf_op jit(solution)/shard_map/ppermute | solution.py:1019
  12.7 4.8 %collective-permute-start.2 = (bf16[64,256]{1,0:T(8,128)(2,1)S(1)}, bf16[64,256]{1,0:T(8,128)(2,1)S(1)}, u32[]{:S(2)}, u32[]{:S(2)}) collective-permute-start(bf16[64,256]{1,0:T(8,128)(2,1)S(1)} %get-tuple-element.62.own_ref), channel_id=1, source_target_pairs={{0,8},{1,9},{2,10},{3,11},{4,12},{5,13},{6,14},{7,15},{8,0},{9,1},... | collective-permute-start | bytes 98312 | tf_op jit(solution)/shard_map/ppermute | solution.py:1019
  15.5 9.0 %collective-permute-start.4 = (bf16[64,1024]{1,0:T(8,128)(2,1)S(1)}, bf16[64,1024]{1,0:T(8,128)(2,1)S(1)}, u32[]{:S(2)}, u32[]{:S(2)}) collective-permute-start(bf16[64,1024]{1,0:T(8,128)(2,1)S(1)} %get-tuple-element.66.hidden_sum_ref), channel_id=1, source_target_pairs={{0,16},{1,17},{2,18},{3,19},{4,20},{5,21},{6,22},{7,23},{8,24},{9,... | collective-permute-start | bytes 393224 | tf_op jit(solution)/shard_map/ppermute | solution.py:1019
  17.6 6.9 %copy-start.8 = (bf16[256,1024]{1,0:T(8,128)(2,1)S(1)}, bf16[256,1024]{1,0:T(8,128)(2,1)}, u32[]{:S(2)}) copy-start(bf16[256,1024]{1,0:T(8,128)(2,1)} %expand_ref.3) | copy-start | bytes 1572868
  17.6 6.9 %copy-start.9 = (bf16[1024,256]{1,0:T(8,128)(2,1)S(1)}, bf16[1024,256]{1,0:T(8,128)(2,1)}, u32[]{:S(2)}) copy-start(bf16[1024,256]{1,0:T(8,128)(2,1)} %shrink_ref.3) | copy-start | bytes 1572868
  17.6 6.9 %copy-start.14 = (f32[256]{0:T(256)S(1)}, f32[256]{0:T(256)}, u32[]{:S(2)}) copy-start(f32[256]{0:T(256)} %param.25) | copy-start | bytes 3076
  24.4 3.8 %collective-permute-start.11 = (bf16[4,416,256]{2,1,0:T(8,128)(2,1)S(1)}, bf16[4,416,256]{2,1,0:T(8,128)(2,1)S(1)}, u32[]{:S(2)}, u32[]{:S(2)}) collective-permute-start(bf16[4,416,256]{2,1,0:T(8,128)(2,1)S(1)} %get-tuple-element.87), channel_id=1, source_target_pairs={{0,1},{1,0},{2,3},{3,2},{4,5},{5,4},{6,7},{7,6},{8,9},{9,8},{10,11... | collective-permute-start | bytes 2555912 | tf_op jit(solution)/shard_map/ppermute | solution.py:1019
  27.6 6.3 %copy-start = (bf16[256,768]{1,0:T(8,128)(2,1)S(1)}, bf16[256,768]{1,0:T(8,128)(2,1)}, u32[]{:S(2)}) copy-start(bf16[256,768]{1,0:T(8,128)(2,1)} %project_ref.3) | copy-start | bytes 1179652
  27.7 6.3 %copy-start.1 = (bf16[256,256]{1,0:T(8,128)(2,1)S(1)}, bf16[256,256]{1,0:T(8,128)(2,1)}, u32[]{:S(2)}) copy-start(bf16[256,256]{1,0:T(8,128)(2,1)} %output_ref.3) | copy-start | bytes 393220
  27.7 6.2 %copy-start.2 = (bf16[8,256]{1,0:T(8,128)(2,1)S(1)}, bf16[8,256]{1,0:T(8,128)(2,1)}, u32[]{:S(2)}) copy-start(bf16[8,256]{1,0:T(8,128)(2,1)} %table_ref.1) | copy-start | bytes 12292
  27.7 6.2 %copy-start.3 = (f32[256]{0:T(256)S(1)}, f32[256]{0:T(256)}, u32[]{:S(2)}) copy-start(f32[256]{0:T(256)} %param.22) | copy-start | bytes 3076
  27.7 4.4 %collective-permute-start.5 = (bf16[8,112,256]{2,1,0:T(8,128)(2,1)S(1)}, bf16[8,112,256]{2,1,0:T(8,128)(2,1)S(1)}, u32[]{:S(2)}, u32[]{:S(2)}) collective-permute-start(bf16[8,112,256]{2,1,0:T(8,128)(2,1)S(1)} %get-tuple-element.71), channel_id=1, source_target_pairs={{0,1},{1,0},{2,3},{3,2},{4,5},{5,4},{6,7},{7,6},{8,9},{9,8},{10,11... | collective-permute-start | bytes 1376264 | tf_op jit(solution)/shard_map/ppermute | solution.py:1019
  28.4 15.1 %collective-permute-start.12 = (bf16[416,256]{1,0:T(8,128)(2,1)S(1)}, bf16[416,256]{1,0:T(8,128)(2,1)S(1)}, u32[]{:S(2)}, u32[]{:S(2)}) collective-permute-start(bf16[416,256]{1,0:T(8,128)(2,1)S(1)} %get-tuple-element.88), channel_id=1, source_target_pairs={{0,6},{1,7},{2,4},{3,5},{4,2},{5,3},{6,0},{7,1},{8,14},{9,15},{10,... | collective-permute-start | bytes 638984 | tf_op jit(solution)/shard_map/ppermute | solution.py:1019
  31.3 12.8 %collective-permute-start.13 = (bf16[416,256]{1,0:T(8,128)(2,1)S(1)}, bf16[416,256]{1,0:T(8,128)(2,1)S(1)}, u32[]{:S(2)}, u32[]{:S(2)}) collective-permute-start(bf16[416,256]{1,0:T(8,128)(2,1)S(1)} %get-tuple-element.89), channel_id=1, source_target_pairs={{0,4},{1,5},{2,6},{3,7},{4,0},{5,1},{6,2},{7,3},{8,12},{9,13},{10,... | collective-permute-start | bytes 638984 | tf_op jit(solution)/shard_map/ppermute | solution.py:1019
  32.1 12.0 %collective-permute-start.14 = (bf16[416,256]{1,0:T(8,128)(2,1)S(1)}, bf16[416,256]{1,0:T(8,128)(2,1)S(1)}, u32[]{:S(2)}, u32[]{:S(2)}) collective-permute-start(bf16[416,256]{1,0:T(8,128)(2,1)S(1)} %get-tuple-element.90), channel_id=1, source_target_pairs={{0,2},{1,3},{2,0},{3,1},{4,6},{5,7},{6,4},{7,5},{8,10},{9,11},{10,... | collective-permute-start | bytes 638984 | tf_op jit(solution)/shard_map/ppermute | solution.py:1019
  32.2 6.7 %collective-permute-start.6 = (bf16[8,80,128]{2,1,0:T(8,128)(2,1)S(1)}, bf16[8,80,128]{2,1,0:T(8,128)(2,1)S(1)}, u32[]{:S(2)}, u32[]{:S(2)}) collective-permute-start(bf16[8,80,128]{2,1,0:T(8,128)(2,1)S(1)} %get-tuple-element.78), channel_id=1, source_target_pairs={{0,16},{1,17},{2,18},{3,19},{4,20},{5,21},{6,22},{7,23},{8,24},{9,... | collective-permute-start | bytes 491528 | tf_op jit(solution)/shard_map/ppermute | solution.py:1019
  38.8 1.5 %collective-permute-start.7 = (bf16[400,256]{1,0:T(8,128)(2,1)S(1)}, bf16[400,256]{1,0:T(8,128)(2,1)S(1)}, u32[]{:S(2)}, u32[]{:S(2)}) collective-permute-start(bf16[400,256]{1,0:T(8,128)(2,1)S(1)} %get-tuple-element.81), channel_id=1, source_target_pairs={{0,1},{1,0},{2,3},{3,2},{4,5},{5,4},{6,7},{7,6},{8,9},{9,8},{10,11... | collective-permute-start | bytes 614408 | tf_op jit(solution)/shard_map/ppermute | solution.py:1019
  40.4 8.0 %collective-permute-start.10 = (bf16[256,256]{1,0:T(8,128)(2,1)S(1)}, bf16[256,256]{1,0:T(8,128)(2,1)S(1)}, u32[]{:S(2)}, u32[]{:S(2)}) collective-permute-start(bf16[256,256]{1,0:T(8,128)(2,1)S(1)} %get-tuple-element.84), channel_id=1, source_target_pairs={{0,2},{1,3},{2,0},{3,1},{4,6},{5,7},{6,4},{7,5},{8,10},{9,11},{10,... | collective-permute-start | bytes 393224 | tf_op jit(solution)/shard_map/ppermute | solution.py:1019
  42.0 7.3 %collective-permute-start.8 = (bf16[256,256]{1,0:T(8,128)(2,1)S(1)}, bf16[256,256]{1,0:T(8,128)(2,1)S(1)}, u32[]{:S(2)}, u32[]{:S(2)}) collective-permute-start(bf16[256,256]{1,0:T(8,128)(2,1)S(1)} %get-tuple-element.82), channel_id=1, source_target_pairs={{0,6},{1,7},{2,4},{3,5},{4,2},{5,3},{6,0},{7,1},{8,14},{9,15},{10,... | collective-permute-start | bytes 393224 | tf_op jit(solution)/shard_map/ppermute | solution.py:1019
  43.6 6.5 %collective-permute-start.9 = (bf16[256,256]{1,0:T(8,128)(2,1)S(1)}, bf16[256,256]{1,0:T(8,128)(2,1)S(1)}, u32[]{:S(2)}, u32[]{:S(2)}) collective-permute-start(bf16[256,256]{1,0:T(8,128)(2,1)S(1)} %get-tuple-element.83), channel_id=1, source_target_pairs={{0,4},{1,5},{2,6},{3,7},{4,0},{5,1},{6,2},{7,3},{8,12},{9,13},{10,... | collective-permute-start | bytes 393224 | tf_op jit(solution)/shard_map/ppermute | solution.py:1019
  44.1 10.5 %collective-permute-start.18 = (bf16[416,256]{1,0:T(8,128)(2,1)S(1)}, bf16[416,256]{1,0:T(8,128)(2,1)S(1)}, u32[]{:S(2)}, u32[]{:S(2)}) collective-permute-start(bf16[416,256]{1,0:T(8,128)(2,1)S(1)} %total.1.refs_4_.own_ref), channel_id=1, source_target_pairs={{0,16},{1,17},{2,18},{3,19},{4,20},{5,21},{6,22},{7,23},{8,24},{9,... | collective-permute-start | bytes 638984 | tf_op jit(solution)/shard_map/ppermute | solution.py:1019
  50.2 6.3 %collective-permute-start.15 = (bf16[128,256]{1,0:T(8,128)(2,1)S(1)}, bf16[128,256]{1,0:T(8,128)(2,1)S(1)}, u32[]{:S(2)}, u32[]{:S(2)}) collective-permute-start(bf16[128,256]{1,0:T(8,128)(2,1)S(1)} %get-tuple-element.93), channel_id=1, source_target_pairs={{0,24},{1,25},{2,26},{3,27},{4,28},{5,29},{6,30},{7,31},{8,16},{9,... | collective-permute-start | bytes 196616 | tf_op jit(solution)/shard_map/ppermute | solution.py:1019
  52.9 5.5 %collective-permute-start.16 = (bf16[128,256]{1,0:T(8,128)(2,1)S(1)}, bf16[128,256]{1,0:T(8,128)(2,1)S(1)}, u32[]{:S(2)}, u32[]{:S(2)}) collective-permute-start(bf16[128,256]{1,0:T(8,128)(2,1)S(1)} %get-tuple-element.93), channel_id=1, source_target_pairs={{0,8},{1,9},{2,10},{3,11},{4,12},{5,13},{6,14},{7,15},{8,0},{9,1},... | collective-permute-start | bytes 196616 | tf_op jit(solution)/shard_map/ppermute | solution.py:1019
  53.3 5.1 %collective-permute-start.17 = (bf16[128,256]{1,0:T(8,128)(2,1)S(1)}, bf16[128,256]{1,0:T(8,128)(2,1)S(1)}, u32[]{:S(2)}, u32[]{:S(2)}) collective-permute-start(bf16[128,256]{1,0:T(8,128)(2,1)S(1)} %get-tuple-element.92.near_ref), channel_id=1, source_target_pairs={{0,16},{1,17},{2,18},{3,19},{4,20},{5,21},{6,22},{7,23},{8,24},{9,... | collective-permute-start | bytes 196616 | tf_op jit(solution)/shard_map/ppermute | solution.py:1019

commit v8 on v7

--- a/solution.py
+++ b/solution.py
@@ -103,8 +103,10 @@
 def attend_back(load, load_dmixed, tiles, probs, store, length):
     dprobs = []
     for number, tile in enumerate(tiles):
-        stacked = stack_heads(load_dmixed(tile))
-        dprobs += compact_heads(dot_nt(load(tile, 2), stacked), length)
+        grads = load_dmixed(tile)
+        stacked = stack_heads(grads)
+        scores = dot_nt(stack_heads(load(tile, 2)), grads)
+        dprobs += [compact(scores[head * BLOCK : (head + 1) * BLOCK], length) for head in range(HEADS)]
         parts = jnp.concatenate(expand_heads(probs, number, length), axis=1)
         store(tile, 2, dot(parts, stacked).astype(bf16))
     dprobs = jnp.concatenate(dprobs, axis=1)
@@ -289,9 +291,8 @@
         slope_ref[:, part] = slope
         hidden_sum_ref[:, part] = dot(member, value).astype(bf16)
     high = middle.astype(bf16)
-    low = (middle - high.astype(f32)).astype(bf16)
     fetches[9].wait()
-    total = dot(member, high) + dot(member, low) + dot(hidden_sum_ref[...], shrink_ref[...])
+    total = dot(member, high) + dot(hidden_sum_ref[...], shrink_ref[...])
     pooled_ref[...] = (total / counts_column(counts)).astype(bf16)
 
 
@@ -372,6 +373,8 @@
     gain_ref,
     keep_ref,
     send_ref,
+    counts_wide,
+    spread,
     dhidden_words,
     dz,
     dbefore,
@@ -383,20 +386,26 @@
     counts = counts_ref[section]
     rows, width = middle_ref.shape
     words = counts.shape[-1]
-    spread = dpooled_ref[:words].astype(f32) / counts_column(counts)
-    spread_high = spread.astype(bf16)
-    spread_low = (spread - spread_high.astype(f32)).astype(bf16)
-    dhidden_words[...] = dot_nt(spread_high, shrink_ref[...]).astype(bf16)
+    column = counts_column(counts)
+    counts_wide[...] = jnp.broadcast_to(column, counts_wide.shape)
+    spread_value = dpooled_ref[:words].astype(f32) / column
+    spread[...] = spread_value
+    spread_high = spread_value.astype(bf16)
+    dhidden_words[...] = dot_nt(spread_high, shrink_ref[...]).astype(bf16).astype(f32)
     dz[:words] = spread_high
     other = dpooled_ref[words:].astype(f32) / counts_column(counts_ref[1 - section])
     dz[words:] = other.astype(bf16)
-    shape = (rows, words)
-    row = rows_of(shape)
-    member = (row // slots == lanes(shape)) & (row % slots < counts)
-    member = jnp.where(member, 1.0, 0.0).astype(bf16)
-    for at in range(0, expand_ref.shape[1], 256):
-        part = slice(at, at + 256)
-        dbefore[:, part] = dot(member, dhidden_words[:, part]).astype(bf16) * slope_ref[:, part]
+    slot = rows_of((slots, 128)).astype(f32)
+    for word in range(words):
+        at_word = slice(word * slots, (word + 1) * slots)
+        present = slot < counts_wide[word : word + 1, :]
+        for at in range(0, expand_ref.shape[1], 128):
+            part = slice(at, at + 128)
+            piece = jnp.where(present, dhidden_words[word : word + 1, part], 0.0).astype(bf16)
+            dbefore[at_word, part] = piece * slope_ref[at_word, part]
+        for at in range(0, width, 128):
+            part = slice(at, at + 128)
+            dmiddle_ref[at_word, part] = jnp.where(present, spread[word : word + 1, part], 0.0)
     normal, scale = unit(middle_ref[...])
     normed_t = (normal * gain_mlp_ref[...]).astype(bf16).T
     hidden_sums = jnp.concatenate([hidden_sum_ref[...], other_sum_ref[...]], axis=0)
@@ -407,11 +416,7 @@
     half = width // 2
     own_half = dz[:, pl.ds(pl.multiple_of(section * half, half), half)]
     shrink_grad[...] = dot(hidden_sums_t, own_half)
-    dmiddle = (
-        dot(member, spread_high)
-        + dot(member, spread_low)
-        + unit_back(dnormed, gain_mlp_ref[...], normal, scale)
-    )
+    dmiddle = dmiddle_ref[...] + unit_back(dnormed, gain_mlp_ref[...], normal, scale)
     dmiddle_ref[...] = dmiddle
     output_grad[...] = dot(mixed_ref[...], dmiddle.astype(bf16))
     gain_ref[...] = jnp.broadcast_to(
@@ -448,7 +453,9 @@
             jax.ShapeDtypeStruct(half, bf16),
         ],
         scratch_shapes=[
-            pltpu.VMEM((words, hidden), bf16),
+            pltpu.VMEM((words, 128), f32),
+            pltpu.VMEM((words, width), f32),
+            pltpu.VMEM((words, hidden), f32),
             pltpu.VMEM((2 * words, width), bf16),
             pltpu.VMEM((rows, hidden), bf16),
             pltpu.VMEM(expand_w.shape, f32),

time: 59.2 us -> 57.9 us (0.978)
  Pallas kernels: 23.3 us -> 22 us
    pallas_call x1, Pallas kernels: 3.12 us -> 2.46 us  [char_mlp_back(): pl.pallas_call(functools.partial(char_mlp_back_kernel, slots, shards), in...]
  transfers between devices with their start and end apart: 19 -> 19, of which waited for: 8 -> 8; matrix products, arithmetic and copies ran while one was open for 0% -> 0% of each run, Pallas kernels for 38% -> 37%
where the time goes in v8:
time: 57.9 us; the launch traced here: 57.8 us
  starting transfers between devices  24.6 us (42%)
  Pallas kernels  22 us (38%)
  waiting for transfers between devices  10.2 us (18%)
  between operations  0.93 us (2%)
    ppermute x19, starting transfers between devices, exchange(): return lax.ppermute(value, ('section', 'dp'), pairs)  24.6 us
    ppermute x19, waiting for transfers between devices, exchange(): return lax.ppermute(value, ('section', 'dp'), pairs)  10.2 us
    pallas_call x1, Pallas kernels, word_group(): pl.pallas_call(functools.partial(word_kernel, length, shards), in_specs=[...  6.42 us
    pallas_call x1, Pallas kernels, char_forward(): pl.pallas_call(functools.partial(char_forward_kernel, slots), in_specs=[h...  6 us
    pallas_call x1, Pallas kernels, char_attn_back(): pl.pallas_call(functools.partial(char_attn_back_kernel, slots, shards), i...  4.81 us
    pallas_call x1, Pallas kernels, char_mlp_back(): pl.pallas_call(functools.partial(char_mlp_back_kernel, slots, shards), in...  2.46 us
  transfers between devices with their start and end apart: 19, of which 8 were waited for; matrix products, arithmetic and copies ran while one was open for 0% of the time, Pallas kernels for 37%

profile of v8, /device:TPU:0, one launch (start us, length us, event | category | flops | bytes accessed | tf_op | source)
XLA Modules:
  0.0 57.8 jit_solution(1456092450844112850)
XLA Ops:
  0.6 4.1 %collective-permute-start.3 = (bf16[2,64,512]{2,1,0:T(8,128)(2,1)}, bf16[2,64,512]{2,1,0:T(8,128)(2,1)S(1)}, u32[]{:S(2)}, u32[]{:S(2)}) collective-permute-start(bf16[2,64,512]{2,1,0:T(8,128)(2,1)} %bitcast.15), channel_id=1, source_target_pairs={{0,8},{1,9},{2,10},{3,11},{4,12},{5,13},{6,14},{7,15},{8,0},{9,1},... | collective-permute-start | bytes 393224 | tf_op jit(solution)/shard_map/ppermute | solution.py:1026
  4.8 0.0 copy-start.10
  4.8 0.0 copy-start.11
  4.8 0.0 copy-start.12
  4.8 6.0 %char_forward.1 = (bf16[64,256]{1,0:T(8,128)(2,1)S(1)}, bf16[64,1024]{1,0:T(8,128)(2,1)S(1)}, s32[2,1,64]{2,1,0:T(1,128)S(1)}, bf16[1024,768]{1,0:T(8,128)(2,1)S...) custom-call(bf16[2,1024,256]{2,1,0:T(8,128)(2,1)} %bitcast.21, ...), custom_call_target="tpu_custom_call" | custom-call | flops 4294967296 | bytes 8388608 | tf_op jit(solution)/shard_map/char_forward/pallas_call | solution.py:306
  10.8 1.3 %collective-permute-start = (bf16[64,256]{1,0:T(8,128)(2,1)S(1)}, bf16[64,256]{1,0:T(8,128)(2,1)S(1)}, u32[]{:S(2)}, u32[]{:S(2)}) collective-permute-start(bf16[64,256]{1,0:T(8,128)(2,1)S(1)} %get-tuple-element.62.own_ref), channel_id=1, source_target_pairs={{0,24},{1,25},{2,26},{3,27},{4,28},{5,29},{6,30},{7,31},{8,16},{9,... | collective-permute-start | bytes 98312 | tf_op jit(solution)/shard_map/ppermute | solution.py:1026
  12.1 0.3 collective-permute-start.1
  12.4 2.8 %collective-permute-start.2 = (bf16[64,256]{1,0:T(8,128)(2,1)S(1)}, bf16[64,256]{1,0:T(8,128)(2,1)S(1)}, u32[]{:S(2)}, u32[]{:S(2)}) collective-permute-start(bf16[64,256]{1,0:T(8,128)(2,1)S(1)} %get-tuple-element.62.own_ref), channel_id=1, source_target_pairs={{0,8},{1,9},{2,10},{3,11},{4,12},{5,13},{6,14},{7,15},{8,0},{9,1},... | collective-permute-start | bytes 98312 | tf_op jit(solution)/shard_map/ppermute | solution.py:1026
  15.3 1.5 %collective-permute-start.4 = (bf16[64,1024]{1,0:T(8,128)(2,1)S(1)}, bf16[64,1024]{1,0:T(8,128)(2,1)S(1)}, u32[]{:S(2)}, u32[]{:S(2)}) collective-permute-start(bf16[64,1024]{1,0:T(8,128)(2,1)S(1)} %get-tuple-element.66.hidden_sum_ref), channel_id=1, source_target_pairs={{0,16},{1,17},{2,18},{3,19},{4,20},{5,21},{6,22},{7,23},{8,24},{9,... | collective-permute-start | bytes 393224 | tf_op jit(solution)/shard_map/ppermute | solution.py:1026
  16.7 0.2 collective-permute-done.both_ref
  17.0 0.0 collective-permute-done.1.section_ref
  17.0 0.3 collective-permute-done.2.far_ref
  17.3 0.0 collective-permute-done.3.cot_far_ref
  17.3 0.0 copy-start.8
  17.4 0.0 copy-start.9
  17.4 0.0 copy-start.14
  17.4 6.4 %word_group.1 = (f32[64,512]{1,0:T(8,128)}, bf16[128,256]{1,0:T(8,128)(2,1)S(1)}, bf16[4,416,256]{2,1,0:T(8,128)(2,1)S(1)}, bf16[4,416,256]{2,1,0:T(8,128)(2,1)S(1)}) custom-call(bf16[64,256]{1,0:T(8,128)(2,1)S(1)} %get-tuple-element.62.own_ref, bf16[64,256]{1,0:T(8,128)(2,1)S(1)} %collective-permute-done.both_ref, ...), custom_call_target="tpu_custom_call" | custom-call | flops 6710886400 | bytes 8388608 | tf_op jit(solution)/shard_map/word_group/pallas_call | solution.py:771
  23.8 0.1 collective-permute-start.11
  23.9 0.0 collective-permute-done.4.other_sum_ref
  23.9 0.0 copy-done.8
  23.9 0.0 copy-done.9
  23.9 0.0 copy-done.14
  23.9 2.5 %char_mlp_back.1 = (f32[1024,256]{1,0:T(8,128)S(1)}, f32[8,256]{1,0:T(8,128)S(1)}, bf16[8,112,256]{2,1,0:T(8,128)(2,1)S(1)}, bf16[8,112,256]{2,1,0:T(8,128)(2,1)S(1)}) custom-call(s32[2,1,64]{2,1,0:T(1,128)S(1)} %get-tuple-element.64.counts_ref, f32[1,256]{1,0:T(1,128)S(1)} %bitcast.20, bf16[256,1024]{1,0:T(8,128)(2,1)S(1)} %copy-done.8, ...), custom_call_target="tpu_custom_call" | custom-call | flops 4294967296 | bytes 8388608 | tf_op jit(solution)/shard_map/char_mlp_back/pallas_call | solution.py:445
  26.4 0.0 copy-start
  26.4 0.0 copy-start.1
  26.4 0.0 copy-start.2
  26.4 0.0 copy-start.3
  26.5 0.5 collective-permute-start.5
  27.0 0.0 collective-permute-done.11.arrived
  27.0 0.2 word_sum.1
  27.2 2.8 %collective-permute-start.12 = (bf16[416,256]{1,0:T(8,128)(2,1)S(1)}, bf16[416,256]{1,0:T(8,128)(2,1)S(1)}, u32[]{:S(2)}, u32[]{:S(2)}) collective-permute-start(bf16[416,256]{1,0:T(8,128)(2,1)S(1)} %get-tuple-element.88), channel_id=1, source_target_pairs={{0,6},{1,7},{2,4},{3,5},{4,2},{5,3},{6,0},{7,1},{8,14},{9,15},{10,... | collective-permute-start | bytes 638984 | tf_op jit(solution)/shard_map/ppermute | solution.py:1026
  30.0 0.8 %collective-permute-start.13 = (bf16[416,256]{1,0:T(8,128)(2,1)S(1)}, bf16[416,256]{1,0:T(8,128)(2,1)S(1)}, u32[]{:S(2)}, u32[]{:S(2)}) collective-permute-start(bf16[416,256]{1,0:T(8,128)(2,1)S(1)} %get-tuple-element.89), channel_id=1, source_target_pairs={{0,4},{1,5},{2,6},{3,7},{4,0},{5,1},{6,2},{7,3},{8,12},{9,13},{10,... | collective-permute-start | bytes 638984 | tf_op jit(solution)/shard_map/ppermute | solution.py:1026
  30.8 0.0 collective-permute-start.14
  30.8 0.0 collective-permute-done.5.arrived
  30.8 0.1 first_sum.1
  30.9 1.7 %collective-permute-start.6 = (bf16[8,80,128]{2,1,0:T(8,128)(2,1)S(1)}, bf16[8,80,128]{2,1,0:T(8,128)(2,1)S(1)}, u32[]{:S(2)}, u32[]{:S(2)}) collective-permute-start(bf16[8,80,128]{2,1,0:T(8,128)(2,1)S(1)} %get-tuple-element.78), channel_id=1, source_target_pairs={{0,16},{1,17},{2,18},{3,19},{4,20},{5,21},{6,22},{7,23},{8,24},{9,... | collective-permute-start | bytes 491528 | tf_op jit(solution)/shard_map/ppermute | solution.py:1026
  32.7 0.0 copy-done.1
  32.7 0.0 copy-done.3
  32.7 4.8 %char_attn_back.1 = (f32[1024,256]{1,0:T(8,128)}, bf16[400,256]{1,0:T(8,128)(2,1)S(1)}, bf16[400,256]{1,0:T(8,128)(2,1)S(1)}) custom-call(bf16[8,80,128]{2,1,0:T(8,128)(2,1)S(1)} %get-tuple-element.72._.stay, bf16[2,1024,256]{2,1,0:T(8,128)(2,1)} %bitcast.22, s32[1,2]{1,0:T(1,128)} %bitcast.24, bf16[8,256]{1,0:T(8,128)(2,1)S(1)} %copy-done.2, ...), custom_call_target="tpu_custom_call" | custom-call | tf_op jit(solution)/shard_map/char_attn_back/pallas_call | solution.py:567
  37.5 0.1 collective-permute-start.7
  37.6 0.0 collective-permute-done.6.arrived
  37.6 1.4 %collective-permute-done.7.core_arrived = bf16[400,256]{1,0:T(8,128)(2,1)S(1)} collective-permute-done((bf16[400,256]{1,0:T(8,128)(2,1)S(1)}, bf16[400,256]{1,0:T(8,128)(2,1)S(1)}, u32[]{:S(2)}, u32[]{:S(2)}) %collective-permute-start.7) | collective-permute-done | bytes 204832 | tf_op jit(solution)/shard_map/ppermute | solution.py:1026
  39.0 0.1 second_sum.1
  39.1 1.6 %collective-permute-start.10 = (bf16[256,256]{1,0:T(8,128)(2,1)S(1)}, bf16[256,256]{1,0:T(8,128)(2,1)S(1)}, u32[]{:S(2)}, u32[]{:S(2)}) collective-permute-start(bf16[256,256]{1,0:T(8,128)(2,1)S(1)} %get-tuple-element.84), channel_id=1, source_target_pairs={{0,2},{1,3},{2,0},{3,1},{4,6},{5,7},{6,4},{7,5},{8,10},{9,11},{10,... | collective-permute-start | bytes 393224 | tf_op jit(solution)/shard_map/ppermute | solution.py:1026
  40.7 1.5 %collective-permute-start.8 = (bf16[256,256]{1,0:T(8,128)(2,1)S(1)}, bf16[256,256]{1,0:T(8,128)(2,1)S(1)}, u32[]{:S(2)}, u32[]{:S(2)}) collective-permute-start(bf16[256,256]{1,0:T(8,128)(2,1)S(1)} %get-tuple-element.82), channel_id=1, source_target_pairs={{0,6},{1,7},{2,4},{3,5},{4,2},{5,3},{6,0},{7,1},{8,14},{9,15},{10,... | collective-permute-start | bytes 393224 | tf_op jit(solution)/shard_map/ppermute | solution.py:1026
  42.2 0.0 collective-permute-done.12.refs_0_
  42.2 0.4 collective-permute-start.9
  42.7 0.0 collective-permute-done.13.refs_1_
  42.7 0.0 collective-permute-done.14.refs_2_
  42.7 0.1 total.1.refs_4_.own_ref
  42.8 0.5 collective-permute-start.18
  43.3 3.7 %collective-permute-done.10.refs_2_ = bf16[256,256]{1,0:T(8,128)(2,1)S(1)} collective-permute-done((bf16[256,256]{1,0:T(8,128)(2,1)S(1)}, bf16[256,256]{1,0:T(8,128)(2,1)S(1)}, u32[]{:S(2)}, u32[]{:S(2)}) %collective-permute-start.10) | collective-permute-done | bytes 131104 | tf_op jit(solution)/shard_map/ppermute | solution.py:1026
  47.1 0.9 %collective-permute-done.8.refs_0_ = bf16[256,256]{1,0:T(8,128)(2,1)S(1)} collective-permute-done((bf16[256,256]{1,0:T(8,128)(2,1)S(1)}, bf16[256,256]{1,0:T(8,128)(2,1)S(1)}, u32[]{:S(2)}, u32[]{:S(2)}) %collective-permute-start.8) | collective-permute-done | bytes 131104 | tf_op jit(solution)/shard_map/ppermute | solution.py:1026
  48.0 0.8 %collective-permute-done.9.refs_1_ = bf16[256,256]{1,0:T(8,128)(2,1)S(1)} collective-permute-done((bf16[256,256]{1,0:T(8,128)(2,1)S(1)}, bf16[256,256]{1,0:T(8,128)(2,1)S(1)}, u32[]{:S(2)}, u32[]{:S(2)}) %collective-permute-start.9) | collective-permute-done | bytes 131104 | tf_op jit(solution)/shard_map/ppermute | solution.py:1026
  48.8 0.1 plane_sum.1
  48.8 2.8 %collective-permute-start.15 = (bf16[128,256]{1,0:T(8,128)(2,1)S(1)}, bf16[128,256]{1,0:T(8,128)(2,1)S(1)}, u32[]{:S(2)}, u32[]{:S(2)}) collective-permute-start(bf16[128,256]{1,0:T(8,128)(2,1)S(1)} %get-tuple-element.93), channel_id=1, source_target_pairs={{0,24},{1,25},{2,26},{3,27},{4,28},{5,29},{6,30},{7,31},{8,16},{9,... | collective-permute-start | bytes 196616 | tf_op jit(solution)/shard_map/ppermute | solution.py:1026
  51.6 0.4 collective-permute-start.16
  52.0 1.3 %collective-permute-start.17 = (bf16[128,256]{1,0:T(8,128)(2,1)S(1)}, bf16[128,256]{1,0:T(8,128)(2,1)S(1)}, u32[]{:S(2)}, u32[]{:S(2)}) collective-permute-start(bf16[128,256]{1,0:T(8,128)(2,1)S(1)} %get-tuple-element.92.near_ref), channel_id=1, source_target_pairs={{0,16},{1,17},{2,18},{3,19},{4,20},{5,21},{6,22},{7,23},{8,24},{9,... | collective-permute-start | bytes 196616 | tf_op jit(solution)/shard_map/ppermute | solution.py:1026
  53.3 0.0 collective-permute-done.18.other_ref
  53.3 0.9 %word_last.1 = (f32[16,512]{1,0:T(8,128)}, f32[1,32]{1,0:T(1,128)}, f32[32,1536]{1,0:T(8,128)}, f32[32,512]{1,0:T(8,128)}, f32[1,32]{1,0:T(1,128)}, /*index=5*/f32[32,2048]{1,0:T(8,128)}, f32[128,512]{1,0:T(8,128)}) custom-call(bf16[416,256]{1,0:T(8,128)(2,1)S(1)} %total.1.refs_4_.own_ref, bf16[416,256]{1,0:T(8,128)(2,1)S(1)} %collective-permute-done.18.other_ref), custom_call_target="tpu_custom_call" | custom-call | tf_op jit(solution)/shard_map/word_last/pallas_call | solution.py:1011
  54.2 0.9 %collective-permute-done.15.both_ref = bf16[128,256]{1,0:T(8,128)(2,1)S(1)} collective-permute-done((bf16[128,256]{1,0:T(8,128)(2,1)S(1)}, bf16[128,256]{1,0:T(8,128)(2,1)S(1)}, u32[]{:S(2)}, u32[]{:S(2)}) %collective-permute-start.15) | collective-permute-done | bytes 65568 | tf_op jit(solution)/shard_map/ppermute | solution.py:1026
  55.1 2.0 %collective-permute-done.16.far_ref = bf16[128,256]{1,0:T(8,128)(2,1)S(1)} collective-permute-done((bf16[128,256]{1,0:T(8,128)(2,1)S(1)}, bf16[128,256]{1,0:T(8,128)(2,1)S(1)}, u32[]{:S(2)}, u32[]{:S(2)}) %collective-permute-start.16) | collective-permute-done | bytes 65568 | tf_op jit(solution)/shard_map/ppermute | solution.py:1026
  57.1 0.0 collective-permute-done.17.section_ref
  57.1 0.7 %char_last.1 = (f32[8,16]{1,0:T(8,128)}, f32[1,16]{1,0:T(1,128)}, f32[16,768]{1,0:T(8,128)}, f32[16,256]{1,0:T(8,128)}, f32[1,16]{1,0:T(1,128)}, /*index=5*/f32[16,1024]{1,0:T(8,128)}, f32[64,256]{1,0:T(8,128)}) custom-call(bf16[128,256]{1,0:T(8,128)(2,1)S(1)} %get-tuple-element.92.near_ref, bf16[128,256]{1,0:T(8,128)(2,1)S(1)} %collective-permute-done.15.both_ref, ...), custom_call_target="tpu_custom_call" | custom-call | tf_op jit(solution)/shard_map/char_last/pallas_call | solution.py:979
  (16 shorter events, 0.1 us)
Async XLA Ops:
  0.6 16.6 %collective-permute-start.3 = (bf16[2,64,512]{2,1,0:T(8,128)(2,1)}, bf16[2,64,512]{2,1,0:T(8,128)(2,1)S(1)}, u32[]{:S(2)}, u32[]{:S(2)}) collective-permute-start(bf16[2,64,512]{2,1,0:T(8,128)(2,1)} %bitcast.15), channel_id=1, source_target_pairs={{0,8},{1,9},{2,10},{3,11},{4,12},{5,13},{6,14},{7,15},{8,0},{9,1},... | collective-permute-start | bytes 393224 | tf_op jit(solution)/shard_map/ppermute | solution.py:1026
  4.8 12.5 %copy-start.4 = (bf16[512,2048]{1,0:T(8,128)(2,1)S(1)}, bf16[512,2048]{1,0:T(8,128)(2,1)}, u32[]{:S(2)}) copy-start(bf16[512,2048]{1,0:T(8,128)(2,1)} %expand_ref.2) | copy-start | bytes 6291460
  4.8 12.5 %copy-start.5 = (bf16[2048,512]{1,0:T(8,128)(2,1)S(1)}, bf16[2048,512]{1,0:T(8,128)(2,1)}, u32[]{:S(2)}) copy-start(bf16[2048,512]{1,0:T(8,128)(2,1)} %shrink_ref.2) | copy-start | bytes 6291460
  4.8 12.5 %copy-start.6 = (bf16[512,1536]{1,0:T(8,128)(2,1)S(1)}, bf16[512,1536]{1,0:T(8,128)(2,1)}, u32[]{:S(2)}) copy-start(bf16[512,1536]{1,0:T(8,128)(2,1)} %project_ref.2) | copy-start | bytes 4718596
  4.8 12.5 %copy-start.7 = (bf16[512,512]{1,0:T(8,128)(2,1)S(1)}, bf16[512,512]{1,0:T(8,128)(2,1)}, u32[]{:S(2)}) copy-start(bf16[512,512]{1,0:T(8,128)(2,1)} %output_ref.2) | copy-start | bytes 1572868
  4.8 12.5 %copy-start.10 = (bf16[256,512]{1,0:T(8,128)(2,1)S(1)}, bf16[256,512]{1,0:T(8,128)(2,1)}, u32[]{:S(2)}) copy-start(bf16[256,512]{1,0:T(8,128)(2,1)} %input_ref.1) | copy-start | bytes 786436
  4.8 12.5 %copy-start.11 = (bf16[2,1,64,512]{3,2,1,0:T(8,128)(2,1)S(1)}, bf16[2,1,64,512]{3,2,1,0:T(8,128)(2,1)}, u32[]{:S(2)}) copy-start(bf16[2,1,64,512]{3,2,1,0:T(8,128)(2,1)} %param.35) | copy-start | bytes 393220
  4.8 12.5 %copy-start.12 = (f32[512]{0:T(512)S(1)}, f32[512]{0:T(512)}, u32[]{:S(2)}) copy-start(f32[512]{0:T(512)} %param.29) | copy-start | bytes 6148
  4.8 12.5 %copy-start.13 = (f32[512]{0:T(512)S(1)}, f32[512]{0:T(512)}, u32[]{:S(2)}) copy-start(f32[512]{0:T(512)} %param.32) | copy-start | bytes 6148
  10.8 6.2 %collective-permute-start = (bf16[64,256]{1,0:T(8,128)(2,1)S(1)}, bf16[64,256]{1,0:T(8,128)(2,1)S(1)}, u32[]{:S(2)}, u32[]{:S(2)}) collective-permute-start(bf16[64,256]{1,0:T(8,128)(2,1)S(1)} %get-tuple-element.62.own_ref), channel_id=1, source_target_pairs={{0,24},{1,25},{2,26},{3,27},{4,28},{5,29},{6,30},{7,31},{8,16},{9,... | collective-permute-start | bytes 98312 | tf_op jit(solution)/shard_map/ppermute | solution.py:1026
  12.1 4.9 %collective-permute-start.1 = (bf16[64,256]{1,0:T(8,128)(2,1)S(1)}, bf16[64,256]{1,0:T(8,128)(2,1)S(1)}, u32[]{:S(2)}, u32[]{:S(2)}) collective-permute-start(bf16[64,256]{1,0:T(8,128)(2,1)S(1)} %get-tuple-element.62.own_ref), channel_id=1, source_target_pairs={{0,16},{1,17},{2,18},{3,19},{4,20},{5,21},{6,22},{7,23},{8,24},{9,... | collective-permute-start | bytes 98312 | tf_op jit(solution)/shard_map/ppermute | solution.py:1026
  12.4 4.8 %collective-permute-start.2 = (bf16[64,256]{1,0:T(8,128)(2,1)S(1)}, bf16[64,256]{1,0:T(8,128)(2,1)S(1)}, u32[]{:S(2)}, u32[]{:S(2)}) collective-permute-start(bf16[64,256]{1,0:T(8,128)(2,1)S(1)} %get-tuple-element.62.own_ref), channel_id=1, source_target_pairs={{0,8},{1,9},{2,10},{3,11},{4,12},{5,13},{6,14},{7,15},{8,0},{9,1},... | collective-permute-start | bytes 98312 | tf_op jit(solution)/shard_map/ppermute | solution.py:1026
  15.3 8.6 %collective-permute-start.4 = (bf16[64,1024]{1,0:T(8,128)(2,1)S(1)}, bf16[64,1024]{1,0:T(8,128)(2,1)S(1)}, u32[]{:S(2)}, u32[]{:S(2)}) collective-permute-start(bf16[64,1024]{1,0:T(8,128)(2,1)S(1)} %get-tuple-element.66.hidden_sum_ref), channel_id=1, source_target_pairs={{0,16},{1,17},{2,18},{3,19},{4,20},{5,21},{6,22},{7,23},{8,24},{9,... | collective-permute-start | bytes 393224 | tf_op jit(solution)/shard_map/ppermute | solution.py:1026
  17.3 6.6 %copy-start.8 = (bf16[256,1024]{1,0:T(8,128)(2,1)S(1)}, bf16[256,1024]{1,0:T(8,128)(2,1)}, u32[]{:S(2)}) copy-start(bf16[256,1024]{1,0:T(8,128)(2,1)} %expand_ref.3) | copy-start | bytes 1572868
  17.4 6.6 %copy-start.9 = (bf16[1024,256]{1,0:T(8,128)(2,1)S(1)}, bf16[1024,256]{1,0:T(8,128)(2,1)}, u32[]{:S(2)}) copy-start(bf16[1024,256]{1,0:T(8,128)(2,1)} %shrink_ref.3) | copy-start | bytes 1572868
  17.4 6.6 %copy-start.14 = (f32[256]{0:T(256)S(1)}, f32[256]{0:T(256)}, u32[]{:S(2)}) copy-start(f32[256]{0:T(256)} %param.25) | copy-start | bytes 3076
  23.8 3.2 %collective-permute-start.11 = (bf16[4,416,256]{2,1,0:T(8,128)(2,1)S(1)}, bf16[4,416,256]{2,1,0:T(8,128)(2,1)S(1)}, u32[]{:S(2)}, u32[]{:S(2)}) collective-permute-start(bf16[4,416,256]{2,1,0:T(8,128)(2,1)S(1)} %get-tuple-element.87), channel_id=1, source_target_pairs={{0,1},{1,0},{2,3},{3,2},{4,5},{5,4},{6,7},{7,6},{8,9},{9,8},{10,11... | collective-permute-start | bytes 2555912 | tf_op jit(solution)/shard_map/ppermute | solution.py:1026
  26.4 6.3 %copy-start = (bf16[256,768]{1,0:T(8,128)(2,1)S(1)}, bf16[256,768]{1,0:T(8,128)(2,1)}, u32[]{:S(2)}) copy-start(bf16[256,768]{1,0:T(8,128)(2,1)} %project_ref.3) | copy-start | bytes 1179652
  26.4 6.2 %copy-start.1 = (bf16[256,256]{1,0:T(8,128)(2,1)S(1)}, bf16[256,256]{1,0:T(8,128)(2,1)}, u32[]{:S(2)}) copy-start(bf16[256,256]{1,0:T(8,128)(2,1)} %output_ref.3) | copy-start | bytes 393220
  26.4 6.2 %copy-start.2 = (bf16[8,256]{1,0:T(8,128)(2,1)S(1)}, bf16[8,256]{1,0:T(8,128)(2,1)}, u32[]{:S(2)}) copy-start(bf16[8,256]{1,0:T(8,128)(2,1)} %table_ref.1) | copy-start | bytes 12292
  26.4 6.2 %copy-start.3 = (f32[256]{0:T(256)S(1)}, f32[256]{0:T(256)}, u32[]{:S(2)}) copy-start(f32[256]{0:T(256)} %param.22) | copy-start | bytes 3076
  26.5 4.3 %collective-permute-start.5 = (bf16[8,112,256]{2,1,0:T(8,128)(2,1)S(1)}, bf16[8,112,256]{2,1,0:T(8,128)(2,1)S(1)}, u32[]{:S(2)}, u32[]{:S(2)}) collective-permute-start(bf16[8,112,256]{2,1,0:T(8,128)(2,1)S(1)} %get-tuple-element.71), channel_id=1, source_target_pairs={{0,1},{1,0},{2,3},{3,2},{4,5},{5,4},{6,7},{7,6},{8,9},{9,8},{10,11... | collective-permute-start | bytes 1376264 | tf_op jit(solution)/shard_map/ppermute | solution.py:1026
  27.2 15.0 %collective-permute-start.12 = (bf16[416,256]{1,0:T(8,128)(2,1)S(1)}, bf16[416,256]{1,0:T(8,128)(2,1)S(1)}, u32[]{:S(2)}, u32[]{:S(2)}) collective-permute-start(bf16[416,256]{1,0:T(8,128)(2,1)S(1)} %get-tuple-element.88), channel_id=1, source_target_pairs={{0,6},{1,7},{2,4},{3,5},{4,2},{5,3},{6,0},{7,1},{8,14},{9,15},{10,... | collective-permute-start | bytes 638984 | tf_op jit(solution)/shard_map/ppermute | solution.py:1026
  30.0 12.7 %collective-permute-start.13 = (bf16[416,256]{1,0:T(8,128)(2,1)S(1)}, bf16[416,256]{1,0:T(8,128)(2,1)S(1)}, u32[]{:S(2)}, u32[]{:S(2)}) collective-permute-start(bf16[416,256]{1,0:T(8,128)(2,1)S(1)} %get-tuple-element.89), channel_id=1, source_target_pairs={{0,4},{1,5},{2,6},{3,7},{4,0},{5,1},{6,2},{7,3},{8,12},{9,13},{10,... | collective-permute-start | bytes 638984 | tf_op jit(solution)/shard_map/ppermute | solution.py:1026
  30.8 11.9 %collective-permute-start.14 = (bf16[416,256]{1,0:T(8,128)(2,1)S(1)}, bf16[416,256]{1,0:T(8,128)(2,1)S(1)}, u32[]{:S(2)}, u32[]{:S(2)}) collective-permute-start(bf16[416,256]{1,0:T(8,128)(2,1)S(1)} %get-tuple-element.90), channel_id=1, source_target_pairs={{0,2},{1,3},{2,0},{3,1},{4,6},{5,7},{6,4},{7,5},{8,10},{9,11},{10,... | collective-permute-start | bytes 638984 | tf_op jit(solution)/shard_map/ppermute | solution.py:1026
  30.9 6.6 %collective-permute-start.6 = (bf16[8,80,128]{2,1,0:T(8,128)(2,1)S(1)}, bf16[8,80,128]{2,1,0:T(8,128)(2,1)S(1)}, u32[]{:S(2)}, u32[]{:S(2)}) collective-permute-start(bf16[8,80,128]{2,1,0:T(8,128)(2,1)S(1)} %get-tuple-element.78), channel_id=1, source_target_pairs={{0,16},{1,17},{2,18},{3,19},{4,20},{5,21},{6,22},{7,23},{8,24},{9,... | collective-permute-start | bytes 491528 | tf_op jit(solution)/shard_map/ppermute | solution.py:1026
  37.5 1.5 %collective-permute-start.7 = (bf16[400,256]{1,0:T(8,128)(2,1)S(1)}, bf16[400,256]{1,0:T(8,128)(2,1)S(1)}, u32[]{:S(2)}, u32[]{:S(2)}) collective-permute-start(bf16[400,256]{1,0:T(8,128)(2,1)S(1)} %get-tuple-element.81), channel_id=1, source_target_pairs={{0,1},{1,0},{2,3},{3,2},{4,5},{5,4},{6,7},{7,6},{8,9},{9,8},{10,11... | collective-permute-start | bytes 614408 | tf_op jit(solution)/shard_map/ppermute | solution.py:1026
  39.1 7.9 %collective-permute-start.10 = (bf16[256,256]{1,0:T(8,128)(2,1)S(1)}, bf16[256,256]{1,0:T(8,128)(2,1)S(1)}, u32[]{:S(2)}, u32[]{:S(2)}) collective-permute-start(bf16[256,256]{1,0:T(8,128)(2,1)S(1)} %get-tuple-element.84), channel_id=1, source_target_pairs={{0,2},{1,3},{2,0},{3,1},{4,6},{5,7},{6,4},{7,5},{8,10},{9,11},{10,... | collective-permute-start | bytes 393224 | tf_op jit(solution)/shard_map/ppermute | solution.py:1026
  40.7 7.3 %collective-permute-start.8 = (bf16[256,256]{1,0:T(8,128)(2,1)S(1)}, bf16[256,256]{1,0:T(8,128)(2,1)S(1)}, u32[]{:S(2)}, u32[]{:S(2)}) collective-permute-start(bf16[256,256]{1,0:T(8,128)(2,1)S(1)} %get-tuple-element.82), channel_id=1, source_target_pairs={{0,6},{1,7},{2,4},{3,5},{4,2},{5,3},{6,0},{7,1},{8,14},{9,15},{10,... | collective-permute-start | bytes 393224 | tf_op jit(solution)/shard_map/ppermute | solution.py:1026
  42.2 6.5 %collective-permute-start.9 = (bf16[256,256]{1,0:T(8,128)(2,1)S(1)}, bf16[256,256]{1,0:T(8,128)(2,1)S(1)}, u32[]{:S(2)}, u32[]{:S(2)}) collective-permute-start(bf16[256,256]{1,0:T(8,128)(2,1)S(1)} %get-tuple-element.83), channel_id=1, source_target_pairs={{0,4},{1,5},{2,6},{3,7},{4,0},{5,1},{6,2},{7,3},{8,12},{9,13},{10,... | collective-permute-start | bytes 393224 | tf_op jit(solution)/shard_map/ppermute | solution.py:1026
  42.8 10.5 %collective-permute-start.18 = (bf16[416,256]{1,0:T(8,128)(2,1)S(1)}, bf16[416,256]{1,0:T(8,128)(2,1)S(1)}, u32[]{:S(2)}, u32[]{:S(2)}) collective-permute-start(bf16[416,256]{1,0:T(8,128)(2,1)S(1)} %total.1.refs_4_.own_ref), channel_id=1, source_target_pairs={{0,16},{1,17},{2,18},{3,19},{4,20},{5,21},{6,22},{7,23},{8,24},{9,... | collective-permute-start | bytes 638984 | tf_op jit(solution)/shard_map/ppermute | solution.py:1026
  48.8 6.2 %collective-permute-start.15 = (bf16[128,256]{1,0:T(8,128)(2,1)S(1)}, bf16[128,256]{1,0:T(8,128)(2,1)S(1)}, u32[]{:S(2)}, u32[]{:S(2)}) collective-permute-start(bf16[128,256]{1,0:T(8,128)(2,1)S(1)} %get-tuple-element.93), channel_id=1, source_target_pairs={{0,24},{1,25},{2,26},{3,27},{4,28},{5,29},{6,30},{7,31},{8,16},{9,... | collective-permute-start | bytes 196616 | tf_op jit(solution)/shard_map/ppermute | solution.py:1026
  51.6 5.5 %collective-permute-start.16 = (bf16[128,256]{1,0:T(8,128)(2,1)S(1)}, bf16[128,256]{1,0:T(8,128)(2,1)S(1)}, u32[]{:S(2)}, u32[]{:S(2)}) collective-permute-start(bf16[128,256]{1,0:T(8,128)(2,1)S(1)} %get-tuple-element.93), channel_id=1, source_target_pairs={{0,8},{1,9},{2,10},{3,11},{4,12},{5,13},{6,14},{7,15},{8,0},{9,1},... | collective-permute-start | bytes 196616 | tf_op jit(solution)/shard_map/ppermute | solution.py:1026
  52.0 5.1 %collective-permute-start.17 = (bf16[128,256]{1,0:T(8,128)(2,1)S(1)}, bf16[128,256]{1,0:T(8,128)(2,1)S(1)}, u32[]{:S(2)}, u32[]{:S(2)}) collective-permute-start(bf16[128,256]{1,0:T(8,128)(2,1)S(1)} %get-tuple-element.92.near_ref), channel_id=1, source_target_pairs={{0,16},{1,17},{2,18},{3,19},{4,20},{5,21},{6,22},{7,23},{8,24},{9,... | collective-permute-start | bytes 196616 | tf_op jit(solution)/shard_map/ppermute | solution.py:1026

commit v9 on v8

--- a/solution.py
+++ b/solution.py
@@ -493,16 +493,17 @@
     output_ref,
     dmiddle_ref,
     gain_mlp_grad_ref,
+    word_gains_ref,
     qkv_ref,
     probs_ref,
-    grad_hbm,
+    grad_ref,
     keep_ref,
     send_ref,
+    extra_ref,
     chars_ref,
     languages_ref,
     dmixed,
     dqkv,
-    grad,
     project_grad,
     sems,
 ):
@@ -532,9 +533,7 @@
     project_grad[...] = dot(normed_t, dqkv[...])
     gain_attn_grad = jnp.sum(dnormed * normal, axis=0, keepdims=True)
     dx = dmiddle_ref[...] + unit_back(dnormed, gain_attn_ref[...], normal, scale)
-    grad[...] = dx
-    leave = pltpu.make_async_copy(grad, grad_hbm, sems.at[2])
-    leave.start()
+    grad_ref[...] = dx
     row_sum = jnp.sum(dx, axis=0, keepdims=True)
     targets = [
         ref.at[pl.ds(place * CHAR_LAST_SLOT, CHAR_LAST_SLOT)]
@@ -545,42 +544,51 @@
     extra = jnp.concatenate(
         [
             gain_attn_grad,
-            gain_mlp_grad_ref[:7],
+            gain_mlp_grad_ref[:1],
+            word_gains_ref[:6],
             jnp.where(rows_of((8, 1)) == language, row_sum, 0.0),
         ],
         axis=0,
     ).astype(bf16)
-    for ref in (keep_ref, send_ref):
-        ref[ref.shape[0] - 16 :] = extra
-    leave.wait()
+    extra_ref[...] = extra
 
 
 def char_attn_back(
-    languages, chars, table, weights, dmiddle, gain_mlp_grad, stored, slots, shards, after
+    languages,
+    chars,
+    table,
+    weights,
+    dmiddle,
+    gain_mlp_grad,
+    word_gains,
+    stored,
+    slots,
+    shards,
+    after,
 ):
     gain_attn, project, output, _, _, _ = weights
     _, qkv, probs, _, _, _ = stored
     rows, width = dmiddle.shape
-    half = (shards // 2 * CHAR_LAST_SLOT + 16, width)
+    half = (shards // 2 * CHAR_LAST_SLOT, width)
     vmem = pl.BlockSpec(memory_space=pltpu.VMEM)
     hbm = pl.BlockSpec(memory_space=pltpu.HBM)
     return pl.pallas_call(
         functools.partial(char_attn_back_kernel, slots, shards),
-        in_specs=[pl.BlockSpec(memory_space=pl.ANY), hbm, hbm] + [vmem] * 8,
-        out_specs=[hbm, vmem, vmem],
+        in_specs=[pl.BlockSpec(memory_space=pl.ANY), hbm, hbm] + [vmem] * 9,
+        out_specs=[vmem] * 4,
         out_shape=[
             jax.ShapeDtypeStruct((rows, width), f32),
             jax.ShapeDtypeStruct(half, bf16),
             jax.ShapeDtypeStruct(half, bf16),
+            jax.ShapeDtypeStruct((16, width), bf16),
         ],
         scratch_shapes=[
             pltpu.VMEM((rows, width), bf16),
             pltpu.VMEM(languages.shape, languages.dtype),
             pltpu.VMEM((rows, width), bf16),
             pltpu.VMEM((rows, 3 * width), bf16),
-            pltpu.VMEM((rows, width), f32),
             pltpu.VMEM(project.shape, f32),
-            pltpu.SemaphoreType.DMA((3,)),
+            pltpu.SemaphoreType.DMA((2,)),
         ],
         compiler_params=pltpu.CompilerParams(vmem_limit_bytes=16 * MIB),
         cost_estimate=pl.CostEstimate(
@@ -597,6 +605,7 @@
         output,
         dmiddle,
         gain_mlp_grad,
+        word_gains,
         qkv,
         probs,
     )
@@ -604,9 +613,9 @@
 
 LONG = pl.CostEstimate(flops=20_000_000_000, bytes_accessed=8 * MIB, transcendentals=0)
 
-WORD_SLOT = 416
-
-SHORT_FLOPS = 475_000_000
+WORD_SLOT = 400
+
+SHORT_FLOPS = 400_000_000
 
 
 def word_kernel(
@@ -627,6 +636,7 @@
     shrink_ref,
     result_hbm,
     dpooled_ref,
+    gains_ref,
     keep_ref,
     send_ref,
     pooled,
@@ -748,14 +758,12 @@
     at = 0
     for ref in (input_grad, project_grad, output_grad, expand_grad, shrink_grad):
         at = put_shards(ref, targets, shard_of, at)
-    extra = jnp.concatenate(
+    gains_ref[...] = 0.25 * jnp.concatenate(
         [gain_attn_grad[:, :SLAB], gain_attn_grad[:, SLAB:]]
         + [gain_mlp_grad[:, :SLAB], gain_mlp_grad[:, SLAB:]]
-        + [jnp.zeros((12, SLAB), f32)],
+        + [jnp.zeros((4, SLAB), f32)],
         axis=0,
-    ).astype(bf16)
-    for target in targets:
-        target[at : at + 16] = extra
+    )
     leave.wait()
 
 
@@ -771,10 +779,11 @@
     return pl.pallas_call(
         functools.partial(word_kernel, length, shards),
         in_specs=[vmem] * 13,
-        out_specs=[hbm, vmem, vmem, vmem],
+        out_specs=[hbm, vmem, vmem, vmem, vmem],
         out_shape=[
             jax.ShapeDtypeStruct((length, width), f32),
             jax.ShapeDtypeStruct((2 * length, channels), bf16),
+            jax.ShapeDtypeStruct((8, SLAB), f32),
             jax.ShapeDtypeStruct(half, bf16),
             jax.ShapeDtypeStruct(half, bf16),
         ],
@@ -875,10 +884,10 @@
     )(stay, arrived)
 
 
-def second_sum_kernel(first, shrink, keep, core_arrived, *outs):
+def second_sum_kernel(first, shrink, keep, core_arrived, own_extra, core_extra, *outs):
     _, me = position()
     half = SLAB // 2
-    extra = summed(keep[-16:], core_arrived[-16:])
+    extra = summed(own_extra[...], core_extra[...])
     for place, out in enumerate(outs):
         at = CHAR_FIRST_SLOT
         for far in range(2):
@@ -892,22 +901,45 @@
             rows = slice(entry * CHAR_LAST_SLOT, (entry + 1) * CHAR_LAST_SLOT)
             out[at : at + CHAR_LAST_SLOT] = added(keep[rows], core_arrived[rows])
             at += CHAR_LAST_SLOT
-            turn = lax.rem(SLAB - char_shard(entry, me) * 16, SLAB)
-            out[-16:, columns] = pltpu.roll(extra, turn, 1)[:, :half].astype(bf16)
+            shard = char_shard(entry, me)
+            turned = pltpu.roll(extra, lax.rem(SLAB - shard * 16, SLAB), 1)
+            word = pltpu.roll(extra, lax.rem(2 * SLAB - shard * 32, SLAB), 1)
+            upper = shard * 32 >= SLAB
+            block = jnp.concatenate(
+                [
+                    turned[:2],
+                    jnp.where(upper, word[3:4], word[2:3]),
+                    jnp.where(upper, word[5:6], word[4:5]),
+                    turned[4:],
+                ],
+                axis=0,
+            )
+            out[-16:, columns] = block[:, :half].astype(bf16)
 
 
 def total_kernel(*refs):
-    refs[-1][...] = added(*[ref[...] for ref in refs[:-1]])
-
-
-def total_of(*pieces):
+    *pieces, chars_ref, out, chars_hbm, sem = refs
+    leave = pltpu.make_async_copy(chars_ref, chars_hbm, sem)
+    leave.start()
+    out[...] = added(*[ref[...] for ref in pieces])
+    leave.wait()
+
+
+def total_of(*pieces, chars_grad):
+    vmem = pl.BlockSpec(memory_space=pltpu.VMEM)
     return pl.pallas_call(
         total_kernel,
-        out_shape=jax.ShapeDtypeStruct(pieces[0].shape, bf16),
+        in_specs=[vmem] * (len(pieces) + 1),
+        out_specs=[vmem, pl.BlockSpec(memory_space=pltpu.HBM)],
+        out_shape=[
+            jax.ShapeDtypeStruct(pieces[0].shape, bf16),
+            jax.ShapeDtypeStruct(chars_grad.shape, f32),
+        ],
+        scratch_shapes=[pltpu.SemaphoreType.DMA],
         compiler_params=pltpu.CompilerParams(vmem_limit_bytes=12 * MIB),
         cost_estimate=LONG,
         name="total",
-    )(*pieces)
+    )(*pieces, chars_grad)
 
 
 def second_sum(first, last):
@@ -961,7 +993,17 @@
     first = jnp.concatenate(by_section(section, unfold(mine), unfold(theirs)), axis=1)
     extra = mine[:16, half:] + theirs[:16, half:]
     last = summed(near_ref[FOLD:], section_ref[FOLD:], far_ref[FOLD:], both_ref[FOLD:])
-    table_ref, gain_attn_ref, project_ref, output_ref, gain_mlp_ref, expand_ref, shrink_ref = outs
+    (
+        table_ref,
+        gain_attn_ref,
+        project_ref,
+        output_ref,
+        gain_mlp_ref,
+        expand_ref,
+        shrink_ref,
+        word_gain_attn_ref,
+        word_gain_mlp_ref,
+    ) = outs
     for total, refs in ((first, (expand_ref, shrink_ref, output_ref)), (last, (project_ref,))):
         at = 0
         for ref in refs:
@@ -973,6 +1015,9 @@
     gain_attn_ref[...] = extra[0:1, :size]
     gain_mlp_ref[...] = extra[1:2, :size]
     table_ref[...] = extra[8:16, :size]
+    size = word_gain_attn_ref.shape[1]
+    word_gain_attn_ref[...] = extra[2:3, :size]
+    word_gain_mlp_ref[...] = extra[3:4, :size]
 
 
 def char_last(near, arrived, shapes, after):
@@ -986,12 +1031,11 @@
 
 
 def word_last_kernel(own_ref, other_ref, *outs):
-    section, me = position()
+    section, _ = position()
     own = own_ref[...].astype(f32)
     halves = by_section(section, own, other_ref[...].astype(f32))
-    input_ref, gain_attn_ref, project_ref, output_ref, gain_mlp_ref, expand_ref, shrink_ref = outs
     at = 0
-    for ref in (input_ref, project_ref, output_ref, expand_ref, shrink_ref):
+    for ref in outs:
         size = ref.shape[0]
         columns = ref.shape[1] // (2 * SLAB)
         for column in range(columns):
@@ -999,12 +1043,6 @@
                 first = (half * columns + column) * SLAB
                 ref[:, first : first + SLAB] = halves[half][at : at + size]
             at += size
-    size = gain_attn_ref.shape[1]
-    turn = lax.rem(SLAB - lax.rem(me * size, SLAB), SLAB)
-    turned = pltpu.roll(own[at : at + 8], turn, 1)[:, :size]
-    upper = me * size >= SLAB
-    gain_attn_ref[...] = jnp.where(upper, turned[1:2], turned[0:1])
-    gain_mlp_ref[...] = jnp.where(upper, turned[3:4], turned[2:3])
 
 
 def word_last(own, other, shapes):
@@ -1054,7 +1092,7 @@
     stored = (hidden_sum, *stored)
     other_sum = exchange(hidden_sum, 1, 0)
     others = (exchange(pooled, 1, FAR), exchange(pooled, 1, 0), exchange(pooled, 0, FAR))
-    result, dpooled, keep, send = word_group(
+    result, dpooled, word_gains, keep, send = word_group(
         (pooled,) + others, (cot, cot_far), word_input, word_weights, shards
     )
     word = plane_exchange(word_sum(keep, exchange(send, 0, CORE)))
@@ -1063,21 +1101,22 @@
     )
     stay, go, shrink = first_sum(keep, exchange(send, 0, CORE))
     first = (section_sum(stay, exchange(go, 1, 0)), shrink)
-    chars_grad, keep, send = char_attn_back(
+    chars_grad, keep, send, extra = char_attn_back(
         languages,
         chars,
         language_table,
         char_weights,
         dmiddle,
         gain_mlp_grad,
+        word_gains,
         stored,
         slots,
         shards,
         stay,
     )
-    last = (keep, exchange(send, 0, CORE))
+    last = (keep, exchange(send, 0, CORE), extra, exchange(extra, 0, CORE))
     char = plane_exchange(second_sum(first, last))
-    word = total_of(*word)
+    word, chars_grad = total_of(*word, chars_grad=chars_grad)
     near, far = plane_sum(char, word)
     arrived = (exchange(far, 1, FAR), exchange(far, 0, FAR), exchange(near, 1, 0))
 
@@ -1089,11 +1128,15 @@
                 yield (weight.shape[0] // shards, weight.shape[1])
 
     table_shape = (language_table.shape[0], language_table.shape[1] // shards)
-    word_shapes = list(shard_shapes((word_input,) + word_weights))
+    input_shape, attn_shape, project_shape, output_shape, mlp_shape, expand_shape, shrink_shape = (
+        shard_shapes((word_input,) + word_weights)
+    )
+    word_shapes = [input_shape, project_shape, output_shape, expand_shape, shrink_shape]
     word_totals = word_last(word, exchange(word, 1, 0), word_shapes)
-    char_shapes = [table_shape, *shard_shapes(char_weights)]
-    char_totals = char_last(near, arrived, char_shapes, word_totals[0])
-    totals = [total[0] if total.shape[0] == 1 else total for total in char_totals + word_totals]
+    char_shapes = [table_shape, *shard_shapes(char_weights), attn_shape, mlp_shape]
+    *char_totals, attn, mlp = char_last(near, arrived, char_shapes, word_totals[0])
+    totals = [*char_totals, word_totals[0], attn, *word_totals[1:3], mlp, *word_totals[3:]]
+    totals = [total[0] if total.shape[0] == 1 else total for total in totals]
     return (result[None, None], chars_grad.reshape((1, 1, words, slots, width))) + tuple(totals)
 
 

time: 57.9 us -> 57.4 us (level)
  waiting for transfers between devices: 10.2 us -> 8.65 us
  starting transfers between devices: 24.6 us -> 25.6 us
    ppermute x19 -> x20, waiting for transfers between devices: 10.2 us -> 8.65 us  [exchange(): return lax.ppermute(value, ('section', 'dp'), pairs)]
    ppermute x19 -> x20, starting transfers between devices: 24.6 us -> 25.6 us  [exchange(): return lax.ppermute(value, ('section', 'dp'), pairs)]
    pallas_call x1, Pallas kernels: 0.11 us -> 0.98 us  [total_of(): pl.pallas_call(total_kernel, in_specs=[vmem] * (len(pieces) + 1), out_spe...]
    pallas_call x1, Pallas kernels: 4.81 us -> 3.96 us  [char_attn_back(): pl.pallas_call(functools.partial(char_attn_back_kernel, slots, shards), i...]
  transfers between devices with their start and end apart: 19 -> 20, of which waited for: 8 -> 7; matrix products, arithmetic and copies ran while one was open for 0% -> 0% of each run, Pallas kernels for 37% -> 37%
where the time goes in v9:
time: 57.4 us; the launch traced here: 57.3 us
  starting transfers between devices  25.6 us (45%)
  Pallas kernels  22 us (38%)
  waiting for transfers between devices  8.65 us (15%)
  between operations  0.93 us (2%)
    ppermute x20, starting transfers between devices, exchange(): return lax.ppermute(value, ('section', 'dp'), pairs)  25.6 us
    ppermute x20, waiting for transfers between devices, exchange(): return lax.ppermute(value, ('section', 'dp'), pairs)  8.65 us
    pallas_call x1, Pallas kernels, word_group(): pl.pallas_call(functools.partial(word_kernel, length, shards), in_specs=[...  6.49 us
    pallas_call x1, Pallas kernels, char_forward(): pl.pallas_call(functools.partial(char_forward_kernel, slots), in_specs=[h...  5.97 us
    pallas_call x1, Pallas kernels, char_attn_back(): pl.pallas_call(functools.partial(char_attn_back_kernel, slots, shards), i...  3.96 us
    pallas_call x1, Pallas kernels, char_mlp_back(): pl.pallas_call(functools.partial(char_mlp_back_kernel, slots, shards), in...  2.39 us
  transfers between devices with their start and end apart: 20, of which 7 were waited for; matrix products, arithmetic and copies ran while one was open for 0% of the time, Pallas kernels for 37%

profile of v9, /device:TPU:0, one launch (start us, length us, event | category | flops | bytes accessed | tf_op | source)
XLA Modules:
  0.0 57.3 jit_solution(15636543171114956566)
XLA Ops:
  0.6 4.1 %collective-permute-start.3 = (bf16[2,64,512]{2,1,0:T(8,128)(2,1)}, bf16[2,64,512]{2,1,0:T(8,128)(2,1)S(1)}, u32[]{:S(2)}, u32[]{:S(2)}) collective-permute-start(bf16[2,64,512]{2,1,0:T(8,128)(2,1)} %bitcast.15), channel_id=1, source_target_pairs={{0,8},{1,9},{2,10},{3,11},{4,12},{5,13},{6,14},{7,15},{8,0},{9,1},... | collective-permute-start | bytes 393224 | tf_op jit(solution)/shard_map/ppermute | solution.py:1064
  4.8 0.0 copy-start.10
  4.8 0.0 copy-start.11
  4.8 0.0 copy-start.12
  4.8 0.0 copy-start.13
  4.8 6.0 %char_forward.1 = (bf16[64,256]{1,0:T(8,128)(2,1)S(1)}, bf16[64,1024]{1,0:T(8,128)(2,1)S(1)}, s32[2,1,64]{2,1,0:T(1,128)S(1)}, bf16[1024,768]{1,0:T(8,128)(2,1)S...) custom-call(bf16[2,1024,256]{2,1,0:T(8,128)(2,1)} %bitcast.21, ...), custom_call_target="tpu_custom_call" | custom-call | flops 4294967296 | bytes 8388608 | tf_op jit(solution)/shard_map/char_forward/pallas_call | solution.py:306
  10.8 1.3 %collective-permute-start = (bf16[64,256]{1,0:T(8,128)(2,1)S(1)}, bf16[64,256]{1,0:T(8,128)(2,1)S(1)}, u32[]{:S(2)}, u32[]{:S(2)}) collective-permute-start(bf16[64,256]{1,0:T(8,128)(2,1)S(1)} %get-tuple-element.66.own_ref), channel_id=1, source_target_pairs={{0,24},{1,25},{2,26},{3,27},{4,28},{5,29},{6,30},{7,31},{8,16},{9,... | collective-permute-start | bytes 98312 | tf_op jit(solution)/shard_map/ppermute | solution.py:1064
  12.1 0.3 collective-permute-start.1
  12.4 2.8 %collective-permute-start.2 = (bf16[64,256]{1,0:T(8,128)(2,1)S(1)}, bf16[64,256]{1,0:T(8,128)(2,1)S(1)}, u32[]{:S(2)}, u32[]{:S(2)}) collective-permute-start(bf16[64,256]{1,0:T(8,128)(2,1)S(1)} %get-tuple-element.66.own_ref), channel_id=1, source_target_pairs={{0,8},{1,9},{2,10},{3,11},{4,12},{5,13},{6,14},{7,15},{8,0},{9,1},... | collective-permute-start | bytes 98312 | tf_op jit(solution)/shard_map/ppermute | solution.py:1064
  15.2 1.5 %collective-permute-start.8 = (bf16[64,1024]{1,0:T(8,128)(2,1)S(1)}, bf16[64,1024]{1,0:T(8,128)(2,1)S(1)}, u32[]{:S(2)}, u32[]{:S(2)}) collective-permute-start(bf16[64,1024]{1,0:T(8,128)(2,1)S(1)} %get-tuple-element.76.hidden_sum_ref), channel_id=1, source_target_pairs={{0,16},{1,17},{2,18},{3,19},{4,20},{5,21},{6,22},{7,23},{8,24},{9,... | collective-permute-start | bytes 393224 | tf_op jit(solution)/shard_map/ppermute | solution.py:1064
  16.7 0.2 collective-permute-done.both_ref
  17.0 0.0 collective-permute-done.1.section_ref
  17.0 0.3 collective-permute-done.2.far_ref
  17.2 0.0 collective-permute-done.3.cot_far_ref
  17.2 0.0 copy-done.5
  17.3 0.0 copy-start.8
  17.3 0.0 copy-start.9
  17.3 0.0 copy-start.14
  17.3 6.5 %word_group.1 = (f32[64,512]{1,0:T(8,128)}, bf16[128,256]{1,0:T(8,128)(2,1)S(1)}, f32[8,256]{1,0:T(8,128)S(1)}, bf16[4,400,256]{2,1,0:T(8,128)(2,1)S(1)}, bf16[4,400,256]{2,1,0:T(8,128)(2,1)S(1)}) custom-call(bf16[64,256]{1,0:T(8,128)(2,1)S(1)} %get-tuple-element.66.own_ref, bf16[64,256]{1,0:T(8,128)(2,1)S(1)} %collective-permute-done.both_ref, ...), custom_call_target="tpu_custom_call" | custom-call | flops 6710886400 | bytes 8388608 | tf_op jit(solution)/shard_map/word_group/pallas_call | solution.py:779
  23.8 0.1 collective-permute-start.4
  23.9 0.0 collective-permute-done.8.other_sum_ref
  24.0 2.4 %char_mlp_back.1 = (f32[1024,256]{1,0:T(8,128)S(1)}, f32[8,256]{1,0:T(8,128)S(1)}, bf16[8,112,256]{2,1,0:T(8,128)(2,1)S(1)}, bf16[8,112,256]{2,1,0:T(8,128)(2,1)S(1)}) custom-call(s32[2,1,64]{2,1,0:T(1,128)S(1)} %get-tuple-element.74.counts_ref, f32[1,256]{1,0:T(1,128)S(1)} %bitcast.20, bf16[256,1024]{1,0:T(8,128)(2,1)S(1)} %copy-done.8, ...), custom_call_target="tpu_custom_call" | custom-call | flops 4294967296 | bytes 8388608 | tf_op jit(solution)/shard_map/char_mlp_back/pallas_call | solution.py:445
  26.4 0.0 copy-start
  26.4 0.0 copy-start.1
  26.4 0.0 copy-start.2
  26.4 0.0 copy-start.3
  26.4 0.5 collective-permute-start.9
  27.0 0.0 collective-permute-done.4.arrived
  27.0 0.2 word_sum.1
  27.1 2.8 %collective-permute-start.5 = (bf16[400,256]{1,0:T(8,128)(2,1)S(1)}, bf16[400,256]{1,0:T(8,128)(2,1)S(1)}, u32[]{:S(2)}, u32[]{:S(2)}) collective-permute-start(bf16[400,256]{1,0:T(8,128)(2,1)S(1)} %get-tuple-element.70), channel_id=1, source_target_pairs={{0,6},{1,7},{2,4},{3,5},{4,2},{5,3},{6,0},{7,1},{8,14},{9,15},{10,... | collective-permute-start | bytes 614408 | tf_op jit(solution)/shard_map/ppermute | solution.py:1064
  30.0 0.8 %collective-permute-start.6 = (bf16[400,256]{1,0:T(8,128)(2,1)S(1)}, bf16[400,256]{1,0:T(8,128)(2,1)S(1)}, u32[]{:S(2)}, u32[]{:S(2)}) collective-permute-start(bf16[400,256]{1,0:T(8,128)(2,1)S(1)} %get-tuple-element.71), channel_id=1, source_target_pairs={{0,4},{1,5},{2,6},{3,7},{4,0},{5,1},{6,2},{7,3},{8,12},{9,13},{10,... | collective-permute-start | bytes 614408 | tf_op jit(solution)/shard_map/ppermute | solution.py:1064
  30.8 0.0 collective-permute-start.7
  30.8 0.0 collective-permute-done.9.arrived
  30.8 0.1 first_sum.1
  30.9 1.7 %collective-permute-start.10 = (bf16[8,80,128]{2,1,0:T(8,128)(2,1)S(1)}, bf16[8,80,128]{2,1,0:T(8,128)(2,1)S(1)}, u32[]{:S(2)}, u32[]{:S(2)}) collective-permute-start(bf16[8,80,128]{2,1,0:T(8,128)(2,1)S(1)} %get-tuple-element.90), channel_id=1, source_target_pairs={{0,16},{1,17},{2,18},{3,19},{4,20},{5,21},{6,22},{7,23},{8,24},{9,... | collective-permute-start | bytes 491528 | tf_op jit(solution)/shard_map/ppermute | solution.py:1064
  32.6 0.0 copy-done.1
  32.6 4.0 %char_attn_back.1 = (f32[1024,256]{1,0:T(8,128)S(1)}, bf16[384,256]{1,0:T(8,128)(2,1)S(1)}, bf16[384,256]{1,0:T(8,128)(2,1)S(1)}, bf16[16,256]{1,0:T(8,128)(2,1)S(1)}) custom-call(bf16[8,80,128]{2,1,0:T(8,128)(2,1)S(1)} %get-tuple-element.82._.stay, bf16[2,1024,256]{2,1,0:T(8,128)(2,1)} %bitcast.22, s32[1,2]{1,0:T(1,128)} %bitcast.24, ...), custom_call_target="tpu_custom_call" | custom-call | tf_op jit(solution)/shard_map/char_attn_back/pallas_call | solution.py:575
  36.6 0.1 collective-permute-start.11
  36.7 0.0 collective-permute-done.10.arrived
  36.7 0.5 collective-permute-start.12
  37.2 0.9 %collective-permute-done.12.core_extra = bf16[16,256]{1,0:T(8,128)(2,1)S(1)} collective-permute-done((bf16[16,256]{1,0:T(8,128)(2,1)S(1)}, bf16[16,256]{1,0:T(8,128)(2,1)S(1)}, u32[]{:S(2)}, u32[]{:S(2)}) %collective-permute-start.12) | collective-permute-done | bytes 8224 | tf_op jit(solution)/shard_map/ppermute | solution.py:1064
  38.1 0.0 collective-permute-done.11.core_arrived
  38.1 0.2 second_sum.1
  38.3 2.6 %collective-permute-start.13 = (bf16[256,256]{1,0:T(8,128)(2,1)S(1)}, bf16[256,256]{1,0:T(8,128)(2,1)S(1)}, u32[]{:S(2)}, u32[]{:S(2)}) collective-permute-start(bf16[256,256]{1,0:T(8,128)(2,1)S(1)} %get-tuple-element.95), channel_id=1, source_target_pairs={{0,6},{1,7},{2,4},{3,5},{4,2},{5,3},{6,0},{7,1},{8,14},{9,15},{10,... | collective-permute-start | bytes 393224 | tf_op jit(solution)/shard_map/ppermute | solution.py:1064
  40.9 0.4 collective-permute-start.14
  41.3 0.0 collective-permute-done.5.refs_0_
  41.3 0.5 collective-permute-start.15
  41.8 0.0 collective-permute-done.6.refs_1_
  41.8 0.0 collective-permute-done.7.refs_2_
  41.8 1.0 %total.1 = (bf16[400,256]{1,0:T(8,128)(2,1)S(1)}, f32[1024,256]{1,0:T(8,128)}) custom-call(bf16[400,256]{1,0:T(8,128)(2,1)S(1)} %collective-permute-done.5.refs_0_, bf16[400,256]{1,0:T(8,128)(2,1)S(1)} %collective-permute-done.6.refs_1_, bf16[400,256]{1,0:T(8,128)(2,1)S(1)} %collective-permute-done.7.refs_2_, ...), custom_call_target="tpu_custom_call" | custom-call | flops 20000000000 | bytes 8388608 | tf_op jit(solution)/shard_map/total/pallas_call | solution.py:930
  42.8 1.1 %collective-permute-start.19 = (bf16[400,256]{1,0:T(8,128)(2,1)S(1)}, bf16[400,256]{1,0:T(8,128)(2,1)S(1)}, u32[]{:S(2)}, u32[]{:S(2)}) collective-permute-start(bf16[400,256]{1,0:T(8,128)(2,1)S(1)} %get-tuple-element.99.refs_4_.own_ref), channel_id=1, source_target_pairs={{0,16},{1,17},{2,18},{3,19},{4,20},{5,21},{6,22},{7,23},{8,24},{9,... | collective-permute-start | bytes 614408 | tf_op jit(solution)/shard_map/ppermute | solution.py:1064
  43.9 1.7 %collective-permute-done.13.refs_0_ = bf16[256,256]{1,0:T(8,128)(2,1)S(1)} collective-permute-done((bf16[256,256]{1,0:T(8,128)(2,1)S(1)}, bf16[256,256]{1,0:T(8,128)(2,1)S(1)}, u32[]{:S(2)}, u32[]{:S(2)}) %collective-permute-start.13) | collective-permute-done | bytes 131104 | tf_op jit(solution)/shard_map/ppermute | solution.py:1064
  45.6 2.2 %collective-permute-done.14.refs_1_ = bf16[256,256]{1,0:T(8,128)(2,1)S(1)} collective-permute-done((bf16[256,256]{1,0:T(8,128)(2,1)S(1)}, bf16[256,256]{1,0:T(8,128)(2,1)S(1)}, u32[]{:S(2)}, u32[]{:S(2)}) %collective-permute-start.14) | collective-permute-done | bytes 131104 | tf_op jit(solution)/shard_map/ppermute | solution.py:1064
  47.8 0.0 collective-permute-done.15.refs_2_
  47.8 0.1 plane_sum.1
  47.8 3.1 %collective-permute-start.16 = (bf16[128,256]{1,0:T(8,128)(2,1)S(1)}, bf16[128,256]{1,0:T(8,128)(2,1)S(1)}, u32[]{:S(2)}, u32[]{:S(2)}) collective-permute-start(bf16[128,256]{1,0:T(8,128)(2,1)S(1)} %get-tuple-element.101), channel_id=1, source_target_pairs={{0,24},{1,25},{2,26},{3,27},{4,28},{5,29},{6,30},{7,31},{8,16},{9,... | collective-permute-start | bytes 196616 | tf_op jit(solution)/shard_map/ppermute | solution.py:1064
  51.0 0.2 collective-permute-start.17
  51.2 1.1 %collective-permute-start.18 = (bf16[128,256]{1,0:T(8,128)(2,1)S(1)}, bf16[128,256]{1,0:T(8,128)(2,1)S(1)}, u32[]{:S(2)}, u32[]{:S(2)}) collective-permute-start(bf16[128,256]{1,0:T(8,128)(2,1)S(1)} %get-tuple-element.100.near_ref), channel_id=1, source_target_pairs={{0,16},{1,17},{2,18},{3,19},{4,20},{5,21},{6,22},{7,23},{8,24},{9,... | collective-permute-start | bytes 196616 | tf_op jit(solution)/shard_map/ppermute | solution.py:1064
  52.3 0.0 collective-permute-done.19.other_ref
  52.3 0.9 %word_last.1 = (f32[16,512]{1,0:T(8,128)}, f32[32,1536]{1,0:T(8,128)}, f32[32,512]{1,0:T(8,128)}, f32[32,2048]{1,0:T(8,128)}, f32[128,512]{1,0:T(8,128)}) custom-call(bf16[400,256]{1,0:T(8,128)(2,1)S(1)} %get-tuple-element.99.refs_4_.own_ref, bf16[400,256]{1,0:T(8,128)(2,1)S(1)} %collective-permute-done.19.other_ref), custom_call_target="tpu_custom_call" | custom-call | tf_op jit(solution)/shard_map/word_last/pallas_call | solution.py:1049
  53.2 1.2 %collective-permute-done.16.both_ref = bf16[128,256]{1,0:T(8,128)(2,1)S(1)} collective-permute-done((bf16[128,256]{1,0:T(8,128)(2,1)S(1)}, bf16[128,256]{1,0:T(8,128)(2,1)S(1)}, u32[]{:S(2)}, u32[]{:S(2)}) %collective-permute-start.16) | collective-permute-done | bytes 65568 | tf_op jit(solution)/shard_map/ppermute | solution.py:1064
  54.4 2.1 %collective-permute-done.17.far_ref = bf16[128,256]{1,0:T(8,128)(2,1)S(1)} collective-permute-done((bf16[128,256]{1,0:T(8,128)(2,1)S(1)}, bf16[128,256]{1,0:T(8,128)(2,1)S(1)}, u32[]{:S(2)}, u32[]{:S(2)}) %collective-permute-start.17) | collective-permute-done | bytes 65568 | tf_op jit(solution)/shard_map/ppermute | solution.py:1064
  56.5 0.0 collective-permute-done.18.section_ref
  56.6 0.7 %char_last.1 = (f32[8,16]{1,0:T(8,128)}, f32[1,16]{1,0:T(1,128)}, f32[16,768]{1,0:T(8,128)}, f32[16,256]{1,0:T(8,128)}, f32[1,16]{1,0:T(1,128)}, /*index=5*/f32[...) custom-call(bf16[128,256]{1,0:T(8,128)(2,1)S(1)} %get-tuple-element.100.near_ref, ...), custom_call_target="tpu_custom_call" | custom-call | tf_op jit(solution)/shard_map/char_last/pallas_call | solution.py:1024
  (18 shorter events, 0.1 us)
Async XLA Ops:
  0.6 16.6 %collective-permute-start.3 = (bf16[2,64,512]{2,1,0:T(8,128)(2,1)}, bf16[2,64,512]{2,1,0:T(8,128)(2,1)S(1)}, u32[]{:S(2)}, u32[]{:S(2)}) collective-permute-start(bf16[2,64,512]{2,1,0:T(8,128)(2,1)} %bitcast.15), channel_id=1, source_target_pairs={{0,8},{1,9},{2,10},{3,11},{4,12},{5,13},{6,14},{7,15},{8,0},{9,1},... | collective-permute-start | bytes 393224 | tf_op jit(solution)/shard_map/ppermute | solution.py:1064
  4.8 12.5 %copy-start.4 = (bf16[512,2048]{1,0:T(8,128)(2,1)S(1)}, bf16[512,2048]{1,0:T(8,128)(2,1)}, u32[]{:S(2)}) copy-start(bf16[512,2048]{1,0:T(8,128)(2,1)} %expand_ref.2) | copy-start | bytes 6291460
  4.8 12.5 %copy-start.5 = (bf16[2048,512]{1,0:T(8,128)(2,1)S(1)}, bf16[2048,512]{1,0:T(8,128)(2,1)}, u32[]{:S(2)}) copy-start(bf16[2048,512]{1,0:T(8,128)(2,1)} %shrink_ref.2) | copy-start | bytes 6291460
  4.8 12.5 %copy-start.6 = (bf16[512,1536]{1,0:T(8,128)(2,1)S(1)}, bf16[512,1536]{1,0:T(8,128)(2,1)}, u32[]{:S(2)}) copy-start(bf16[512,1536]{1,0:T(8,128)(2,1)} %project_ref.2) | copy-start | bytes 4718596
  4.8 12.5 %copy-start.7 = (bf16[512,512]{1,0:T(8,128)(2,1)S(1)}, bf16[512,512]{1,0:T(8,128)(2,1)}, u32[]{:S(2)}) copy-start(bf16[512,512]{1,0:T(8,128)(2,1)} %output_ref.2) | copy-start | bytes 1572868
  4.8 12.5 %copy-start.10 = (bf16[256,512]{1,0:T(8,128)(2,1)S(1)}, bf16[256,512]{1,0:T(8,128)(2,1)}, u32[]{:S(2)}) copy-start(bf16[256,512]{1,0:T(8,128)(2,1)} %input_ref.1) | copy-start | bytes 786436
  4.8 12.5 %copy-start.11 = (bf16[2,1,64,512]{3,2,1,0:T(8,128)(2,1)S(1)}, bf16[2,1,64,512]{3,2,1,0:T(8,128)(2,1)}, u32[]{:S(2)}) copy-start(bf16[2,1,64,512]{3,2,1,0:T(8,128)(2,1)} %param.35) | copy-start | bytes 393220
  4.8 12.5 %copy-start.12 = (f32[512]{0:T(512)S(1)}, f32[512]{0:T(512)}, u32[]{:S(2)}) copy-start(f32[512]{0:T(512)} %param.29) | copy-start | bytes 6148
  4.8 12.5 %copy-start.13 = (f32[512]{0:T(512)S(1)}, f32[512]{0:T(512)}, u32[]{:S(2)}) copy-start(f32[512]{0:T(512)} %param.32) | copy-start | bytes 6148
  10.8 6.2 %collective-permute-start = (bf16[64,256]{1,0:T(8,128)(2,1)S(1)}, bf16[64,256]{1,0:T(8,128)(2,1)S(1)}, u32[]{:S(2)}, u32[]{:S(2)}) collective-permute-start(bf16[64,256]{1,0:T(8,128)(2,1)S(1)} %get-tuple-element.66.own_ref), channel_id=1, source_target_pairs={{0,24},{1,25},{2,26},{3,27},{4,28},{5,29},{6,30},{7,31},{8,16},{9,... | collective-permute-start | bytes 98312 | tf_op jit(solution)/shard_map/ppermute | solution.py:1064
  12.1 4.9 %collective-permute-start.1 = (bf16[64,256]{1,0:T(8,128)(2,1)S(1)}, bf16[64,256]{1,0:T(8,128)(2,1)S(1)}, u32[]{:S(2)}, u32[]{:S(2)}) collective-permute-start(bf16[64,256]{1,0:T(8,128)(2,1)S(1)} %get-tuple-element.66.own_ref), channel_id=1, source_target_pairs={{0,16},{1,17},{2,18},{3,19},{4,20},{5,21},{6,22},{7,23},{8,24},{9,... | collective-permute-start | bytes 98312 | tf_op jit(solution)/shard_map/ppermute | solution.py:1064
  12.4 4.8 %collective-permute-start.2 = (bf16[64,256]{1,0:T(8,128)(2,1)S(1)}, bf16[64,256]{1,0:T(8,128)(2,1)S(1)}, u32[]{:S(2)}, u32[]{:S(2)}) collective-permute-start(bf16[64,256]{1,0:T(8,128)(2,1)S(1)} %get-tuple-element.66.own_ref), channel_id=1, source_target_pairs={{0,8},{1,9},{2,10},{3,11},{4,12},{5,13},{6,14},{7,15},{8,0},{9,1},... | collective-permute-start | bytes 98312 | tf_op jit(solution)/shard_map/ppermute | solution.py:1064
  15.2 8.7 %collective-permute-start.8 = (bf16[64,1024]{1,0:T(8,128)(2,1)S(1)}, bf16[64,1024]{1,0:T(8,128)(2,1)S(1)}, u32[]{:S(2)}, u32[]{:S(2)}) collective-permute-start(bf16[64,1024]{1,0:T(8,128)(2,1)S(1)} %get-tuple-element.76.hidden_sum_ref), channel_id=1, source_target_pairs={{0,16},{1,17},{2,18},{3,19},{4,20},{5,21},{6,22},{7,23},{8,24},{9,... | collective-permute-start | bytes 393224 | tf_op jit(solution)/shard_map/ppermute | solution.py:1064
  17.3 6.6 %copy-start.8 = (bf16[256,1024]{1,0:T(8,128)(2,1)S(1)}, bf16[256,1024]{1,0:T(8,128)(2,1)}, u32[]{:S(2)}) copy-start(bf16[256,1024]{1,0:T(8,128)(2,1)} %expand_ref.3) | copy-start | bytes 1572868
  17.3 6.6 %copy-start.9 = (bf16[1024,256]{1,0:T(8,128)(2,1)S(1)}, bf16[1024,256]{1,0:T(8,128)(2,1)}, u32[]{:S(2)}) copy-start(bf16[1024,256]{1,0:T(8,128)(2,1)} %shrink_ref.3) | copy-start | bytes 1572868
  17.3 6.6 %copy-start.14 = (f32[256]{0:T(256)S(1)}, f32[256]{0:T(256)}, u32[]{:S(2)}) copy-start(f32[256]{0:T(256)} %param.25) | copy-start | bytes 3076
  23.8 3.1 %collective-permute-start.4 = (bf16[4,400,256]{2,1,0:T(8,128)(2,1)S(1)}, bf16[4,400,256]{2,1,0:T(8,128)(2,1)S(1)}, u32[]{:S(2)}, u32[]{:S(2)}) collective-permute-start(bf16[4,400,256]{2,1,0:T(8,128)(2,1)S(1)} %get-tuple-element.69), channel_id=1, source_target_pairs={{0,1},{1,0},{2,3},{3,2},{4,5},{5,4},{6,7},{7,6},{8,9},{9,8},{10,11... | collective-permute-start | bytes 2457608 | tf_op jit(solution)/shard_map/ppermute | solution.py:1064
  26.4 6.3 %copy-start = (bf16[256,768]{1,0:T(8,128)(2,1)S(1)}, bf16[256,768]{1,0:T(8,128)(2,1)}, u32[]{:S(2)}) copy-start(bf16[256,768]{1,0:T(8,128)(2,1)} %project_ref.3) | copy-start | bytes 1179652
  26.4 6.3 %copy-start.1 = (bf16[256,256]{1,0:T(8,128)(2,1)S(1)}, bf16[256,256]{1,0:T(8,128)(2,1)}, u32[]{:S(2)}) copy-start(bf16[256,256]{1,0:T(8,128)(2,1)} %output_ref.3) | copy-start | bytes 393220
  26.4 6.2 %copy-start.2 = (bf16[8,256]{1,0:T(8,128)(2,1)S(1)}, bf16[8,256]{1,0:T(8,128)(2,1)}, u32[]{:S(2)}) copy-start(bf16[8,256]{1,0:T(8,128)(2,1)} %table_ref.1) | copy-start | bytes 12292
  26.4 6.2 %copy-start.3 = (f32[256]{0:T(256)S(1)}, f32[256]{0:T(256)}, u32[]{:S(2)}) copy-start(f32[256]{0:T(256)} %param.22) | copy-start | bytes 3076
  26.4 4.3 %collective-permute-start.9 = (bf16[8,112,256]{2,1,0:T(8,128)(2,1)S(1)}, bf16[8,112,256]{2,1,0:T(8,128)(2,1)S(1)}, u32[]{:S(2)}, u32[]{:S(2)}) collective-permute-start(bf16[8,112,256]{2,1,0:T(8,128)(2,1)S(1)} %get-tuple-element.81), channel_id=1, source_target_pairs={{0,1},{1,0},{2,3},{3,2},{4,5},{5,4},{6,7},{7,6},{8,9},{9,8},{10,11... | collective-permute-start | bytes 1376264 | tf_op jit(solution)/shard_map/ppermute | solution.py:1064
  27.1 14.2 %collective-permute-start.5 = (bf16[400,256]{1,0:T(8,128)(2,1)S(1)}, bf16[400,256]{1,0:T(8,128)(2,1)S(1)}, u32[]{:S(2)}, u32[]{:S(2)}) collective-permute-start(bf16[400,256]{1,0:T(8,128)(2,1)S(1)} %get-tuple-element.70), channel_id=1, source_target_pairs={{0,6},{1,7},{2,4},{3,5},{4,2},{5,3},{6,0},{7,1},{8,14},{9,15},{10,... | collective-permute-start | bytes 614408 | tf_op jit(solution)/shard_map/ppermute | solution.py:1064
  30.0 11.9 %collective-permute-start.6 = (bf16[400,256]{1,0:T(8,128)(2,1)S(1)}, bf16[400,256]{1,0:T(8,128)(2,1)S(1)}, u32[]{:S(2)}, u32[]{:S(2)}) collective-permute-start(bf16[400,256]{1,0:T(8,128)(2,1)S(1)} %get-tuple-element.71), channel_id=1, source_target_pairs={{0,4},{1,5},{2,6},{3,7},{4,0},{5,1},{6,2},{7,3},{8,12},{9,13},{10,... | collective-permute-start | bytes 614408 | tf_op jit(solution)/shard_map/ppermute | solution.py:1064
  30.8 11.1 %collective-permute-start.7 = (bf16[400,256]{1,0:T(8,128)(2,1)S(1)}, bf16[400,256]{1,0:T(8,128)(2,1)S(1)}, u32[]{:S(2)}, u32[]{:S(2)}) collective-permute-start(bf16[400,256]{1,0:T(8,128)(2,1)S(1)} %get-tuple-element.72), channel_id=1, source_target_pairs={{0,2},{1,3},{2,0},{3,1},{4,6},{5,7},{6,4},{7,5},{8,10},{9,11},{10,... | collective-permute-start | bytes 614408 | tf_op jit(solution)/shard_map/ppermute | solution.py:1064
  30.9 5.8 %collective-permute-start.10 = (bf16[8,80,128]{2,1,0:T(8,128)(2,1)S(1)}, bf16[8,80,128]{2,1,0:T(8,128)(2,1)S(1)}, u32[]{:S(2)}, u32[]{:S(2)}) collective-permute-start(bf16[8,80,128]{2,1,0:T(8,128)(2,1)S(1)} %get-tuple-element.90), channel_id=1, source_target_pairs={{0,16},{1,17},{2,18},{3,19},{4,20},{5,21},{6,22},{7,23},{8,24},{9,... | collective-permute-start | bytes 491528 | tf_op jit(solution)/shard_map/ppermute | solution.py:1064
  36.6 1.5 %collective-permute-start.11 = (bf16[384,256]{1,0:T(8,128)(2,1)S(1)}, bf16[384,256]{1,0:T(8,128)(2,1)S(1)}, u32[]{:S(2)}, u32[]{:S(2)}) collective-permute-start(bf16[384,256]{1,0:T(8,128)(2,1)S(1)} %get-tuple-element.93), channel_id=1, source_target_pairs={{0,1},{1,0},{2,3},{3,2},{4,5},{5,4},{6,7},{7,6},{8,9},{9,8},{10,11... | collective-permute-start | bytes 589832 | tf_op jit(solution)/shard_map/ppermute | solution.py:1064
  36.7 1.4 %collective-permute-start.12 = (bf16[16,256]{1,0:T(8,128)(2,1)S(1)}, bf16[16,256]{1,0:T(8,128)(2,1)S(1)}, u32[]{:S(2)}, u32[]{:S(2)}) collective-permute-start(bf16[16,256]{1,0:T(8,128)(2,1)S(1)} %get-tuple-element.94.own_extra), channel_id=1, source_target_pairs={{0,1},{1,0},{2,3},{3,2},{4,5},{5,4},{6,7},{7,6},{8,9},{9,8},{10,11... | collective-permute-start | bytes 24584 | tf_op jit(solution)/shard_map/ppermute | solution.py:1064
  38.3 7.3 %collective-permute-start.13 = (bf16[256,256]{1,0:T(8,128)(2,1)S(1)}, bf16[256,256]{1,0:T(8,128)(2,1)S(1)}, u32[]{:S(2)}, u32[]{:S(2)}) collective-permute-start(bf16[256,256]{1,0:T(8,128)(2,1)S(1)} %get-tuple-element.95), channel_id=1, source_target_pairs={{0,6},{1,7},{2,4},{3,5},{4,2},{5,3},{6,0},{7,1},{8,14},{9,15},{10,... | collective-permute-start | bytes 393224 | tf_op jit(solution)/shard_map/ppermute | solution.py:1064
  40.9 6.9 %collective-permute-start.14 = (bf16[256,256]{1,0:T(8,128)(2,1)S(1)}, bf16[256,256]{1,0:T(8,128)(2,1)S(1)}, u32[]{:S(2)}, u32[]{:S(2)}) collective-permute-start(bf16[256,256]{1,0:T(8,128)(2,1)S(1)} %get-tuple-element.96), channel_id=1, source_target_pairs={{0,4},{1,5},{2,6},{3,7},{4,0},{5,1},{6,2},{7,3},{8,12},{9,13},{10,... | collective-permute-start | bytes 393224 | tf_op jit(solution)/shard_map/ppermute | solution.py:1064
  41.3 6.4 %collective-permute-start.15 = (bf16[256,256]{1,0:T(8,128)(2,1)S(1)}, bf16[256,256]{1,0:T(8,128)(2,1)S(1)}, u32[]{:S(2)}, u32[]{:S(2)}) collective-permute-start(bf16[256,256]{1,0:T(8,128)(2,1)S(1)} %get-tuple-element.97), channel_id=1, source_target_pairs={{0,2},{1,3},{2,0},{3,1},{4,6},{5,7},{6,4},{7,5},{8,10},{9,11},{10,... | collective-permute-start | bytes 393224 | tf_op jit(solution)/shard_map/ppermute | solution.py:1064
  42.8 9.5 %collective-permute-start.19 = (bf16[400,256]{1,0:T(8,128)(2,1)S(1)}, bf16[400,256]{1,0:T(8,128)(2,1)S(1)}, u32[]{:S(2)}, u32[]{:S(2)}) collective-permute-start(bf16[400,256]{1,0:T(8,128)(2,1)S(1)} %get-tuple-element.99.refs_4_.own_ref), channel_id=1, source_target_pairs={{0,16},{1,17},{2,18},{3,19},{4,20},{5,21},{6,22},{7,23},{8,24},{9,... | collective-permute-start | bytes 614408 | tf_op jit(solution)/shard_map/ppermute | solution.py:1064
  47.8 6.6 %collective-permute-start.16 = (bf16[128,256]{1,0:T(8,128)(2,1)S(1)}, bf16[128,256]{1,0:T(8,128)(2,1)S(1)}, u32[]{:S(2)}, u32[]{:S(2)}) collective-permute-start(bf16[128,256]{1,0:T(8,128)(2,1)S(1)} %get-tuple-element.101), channel_id=1, source_target_pairs={{0,24},{1,25},{2,26},{3,27},{4,28},{5,29},{6,30},{7,31},{8,16},{9,... | collective-permute-start | bytes 196616 | tf_op jit(solution)/shard_map/ppermute | solution.py:1064
  51.0 5.6 %collective-permute-start.17 = (bf16[128,256]{1,0:T(8,128)(2,1)S(1)}, bf16[128,256]{1,0:T(8,128)(2,1)S(1)}, u32[]{:S(2)}, u32[]{:S(2)}) collective-permute-start(bf16[128,256]{1,0:T(8,128)(2,1)S(1)} %get-tuple-element.101), channel_id=1, source_target_pairs={{0,8},{1,9},{2,10},{3,11},{4,12},{5,13},{6,14},{7,15},{8,0},{9,1},... | collective-permute-start | bytes 196616 | tf_op jit(solution)/shard_map/ppermute | solution.py:1064
  51.2 5.4 %collective-permute-start.18 = (bf16[128,256]{1,0:T(8,128)(2,1)S(1)}, bf16[128,256]{1,0:T(8,128)(2,1)S(1)}, u32[]{:S(2)}, u32[]{:S(2)}) collective-permute-start(bf16[128,256]{1,0:T(8,128)(2,1)S(1)} %get-tuple-element.100.near_ref), channel_id=1, source_target_pairs={{0,16},{1,17},{2,18},{3,19},{4,20},{5,21},{6,22},{7,23},{8,24},{9,... | collective-permute-start | bytes 196616 | tf_op jit(solution)/shard_map/ppermute | solution.py:1064

commit v10 on v9

--- a/solution.py
+++ b/solution.py
@@ -13,6 +13,7 @@
 SLAB = 256
 HEADS = SLAB // HEAD
 BLOCK = 128
+PART = 128
 MIB = 1024 * 1024
 
 eps = 1e-05
@@ -213,6 +214,7 @@
     gain_mlp_ref,
     expand_ref,
     shrink_ref,
+    normed_ref,
     sems,
 ):
     section, _ = position()
@@ -251,11 +253,16 @@
     row_counts = counts_by_row(counts, rows, slots)
     for fetch in fetches[2:5]:
         fetch.wait()
-    x = char_rows(chars_ref[...], table_ref, pick(languages_ref[...], section))
-    normal, _ = unit(x)
-    normed = (normal * gain_attn_ref[...]).astype(bf16)
-    fetches[5].wait()
-    qkv_ref[...] = dot(normed, project_ref[...]).astype(bf16)
+    language = pick(languages_ref[...], section)
+    parts = [slice(at, at + PART) for at in range(0, rows, PART)]
+    for number, part in enumerate(parts):
+        x = char_rows(chars_ref[part], table_ref, language)
+        middle_ref[part] = x
+        normal, _ = unit(x)
+        normed = (normal * gain_attn_ref[...]).astype(bf16)
+        if number == 0:
+            fetches[5].wait()
+        qkv_ref[part] = dot(normed, project_ref[...]).astype(bf16)
     blocks = range(rows // BLOCK)
 
     def load(block, which):
@@ -270,19 +277,20 @@
     probs_ref[...] = probs
     for block in blocks:
         mixed_ref[:, block * BLOCK : (block + 1) * BLOCK] = mixed[block]
-    mixed = mixed_ref[...].T
     fetches[6].wait()
-    middle = x + dot(mixed, output_ref[...])
-    middle_ref[...] = middle
-    normal, _ = unit(middle)
     fetches[7].wait()
-    normed = (normal * gain_mlp_ref[...]).astype(bf16)
+    for part in parts:
+        middle = middle_ref[part] + dot(mixed_ref[:, part].T, output_ref[...])
+        middle_ref[part] = middle
+        normal, _ = unit(middle)
+        normed_ref[part] = (normal * gain_mlp_ref[...]).astype(bf16)
     word_shape = (words, rows)
     lane = lanes(word_shape)
     member = (lane // slots == rows_of(word_shape)) & ((lane % slots).astype(f32) < row_counts)
     member = jnp.where(member, 1.0, 0.0).astype(bf16)
     fetches[8].wait()
     parts = [slice(at, at + 256) for at in range(0, expand_ref.shape[1], 256)]
+    normed = normed_ref[...]
     before = dot(normed, expand_ref[:, parts[0]])
     for number, part in enumerate(parts):
         value, slope = gelu_parts(before)
@@ -290,7 +298,7 @@
             before = dot(normed, expand_ref[:, parts[number + 1]])
         slope_ref[:, part] = slope
         hidden_sum_ref[:, part] = dot(member, value).astype(bf16)
-    high = middle.astype(bf16)
+    high = middle_ref[...].astype(bf16)
     fetches[9].wait()
     total = dot(member, high) + dot(hidden_sum_ref[...], shrink_ref[...])
     pooled_ref[...] = (total / counts_column(counts)).astype(bf16)
@@ -319,7 +327,7 @@
         ],
         scratch_shapes=[pltpu.VMEM(chars.shape[1:], bf16)]
         + [pltpu.VMEM(array.shape, array.dtype) for array in fetched if array is not counts]
-        + [pltpu.SemaphoreType.DMA((10,))],
+        + [pltpu.VMEM(chars.shape[1:], bf16), pltpu.SemaphoreType.DMA((10,))],
         compiler_params=pltpu.CompilerParams(vmem_limit_bytes=16 * MIB),
         cost_estimate=pl.CostEstimate(
             flops=64 * rows * width * width, bytes_accessed=8 * MIB, transcendentals=0

time: 57.4 us -> 56.9 us (level)
  Pallas kernels: 22 us -> 21.4 us
where the time goes in v10:
time: 56.9 us; the launch traced here: 56.7 us
  starting transfers between devices  25.6 us (45%)
  Pallas kernels  21.4 us (38%)
  waiting for transfers between devices  8.64 us (15%)
  between operations  0.93 us (2%)
    ppermute x20, starting transfers between devices, exchange(): return lax.ppermute(value, ('section', 'dp'), pairs)  25.6 us
    ppermute x20, waiting for transfers between devices, exchange(): return lax.ppermute(value, ('section', 'dp'), pairs)  8.64 us
    pallas_call x1, Pallas kernels, word_group(): pl.pallas_call(functools.partial(word_kernel, length, shards), in_specs=[...  6.5 us
    pallas_call x1, Pallas kernels, char_forward(): pl.pallas_call(functools.partial(char_forward_kernel, slots), in_specs=[h...  5.41 us
    pallas_call x1, Pallas kernels, char_attn_back(): pl.pallas_call(functools.partial(char_attn_back_kernel, slots, shards), i...  3.96 us
    pallas_call x1, Pallas kernels, char_mlp_back(): pl.pallas_call(functools.partial(char_mlp_back_kernel, slots, shards), in...  2.21 us
  transfers between devices with their start and end apart: 20, of which 7 were waited for; matrix products, arithmetic and copies ran while one was open for 0% of the time, Pallas kernels for 37%

profile of v10, /device:TPU:0, one launch (start us, length us, event | category | flops | bytes accessed | tf_op | source)
XLA Modules:
  0.0 56.7 jit_solution(8871195035826093512)
XLA Ops:
  0.6 4.1 %collective-permute-start.3 = (bf16[2,64,512]{2,1,0:T(8,128)(2,1)}, bf16[2,64,512]{2,1,0:T(8,128)(2,1)S(1)}, u32[]{:S(2)}, u32[]{:S(2)}) collective-permute-start(bf16[2,64,512]{2,1,0:T(8,128)(2,1)} %bitcast.15), channel_id=1, source_target_pairs={{0,8},{1,9},{2,10},{3,11},{4,12},{5,13},{6,14},{7,15},{8,0},{9,1},... | collective-permute-start | bytes 393224 | tf_op jit(solution)/shard_map/ppermute | solution.py:1072
  4.8 0.0 copy-start.10
  4.8 0.0 copy-start.11
  4.8 5.4 %char_forward.1 = (bf16[64,256]{1,0:T(8,128)(2,1)S(1)}, bf16[64,1024]{1,0:T(8,128)(2,1)S(1)}, s32[2,1,64]{2,1,0:T(1,128)S(1)}, bf16[1024,768]{1,0:T(8,128)(2,1)S...) custom-call(bf16[2,1024,256]{2,1,0:T(8,128)(2,1)} %bitcast.21, ...), custom_call_target="tpu_custom_call" | custom-call | flops 4294967296 | bytes 8388608 | tf_op jit(solution)/shard_map/char_forward/pallas_call | solution.py:314
  10.2 1.3 %collective-permute-start = (bf16[64,256]{1,0:T(8,128)(2,1)S(1)}, bf16[64,256]{1,0:T(8,128)(2,1)S(1)}, u32[]{:S(2)}, u32[]{:S(2)}) collective-permute-start(bf16[64,256]{1,0:T(8,128)(2,1)S(1)} %get-tuple-element.66.own_ref), channel_id=1, source_target_pairs={{0,24},{1,25},{2,26},{3,27},{4,28},{5,29},{6,30},{7,31},{8,16},{9,... | collective-permute-start | bytes 98312 | tf_op jit(solution)/shard_map/ppermute | solution.py:1072
  11.5 0.3 collective-permute-start.1
  11.9 2.8 %collective-permute-start.2 = (bf16[64,256]{1,0:T(8,128)(2,1)S(1)}, bf16[64,256]{1,0:T(8,128)(2,1)S(1)}, u32[]{:S(2)}, u32[]{:S(2)}) collective-permute-start(bf16[64,256]{1,0:T(8,128)(2,1)S(1)} %get-tuple-element.66.own_ref), channel_id=1, source_target_pairs={{0,8},{1,9},{2,10},{3,11},{4,12},{5,13},{6,14},{7,15},{8,0},{9,1},... | collective-permute-start | bytes 98312 | tf_op jit(solution)/shard_map/ppermute | solution.py:1072
  14.7 1.5 %collective-permute-start.8 = (bf16[64,1024]{1,0:T(8,128)(2,1)S(1)}, bf16[64,1024]{1,0:T(8,128)(2,1)S(1)}, u32[]{:S(2)}, u32[]{:S(2)}) collective-permute-start(bf16[64,1024]{1,0:T(8,128)(2,1)S(1)} %get-tuple-element.76.hidden_sum_ref), channel_id=1, source_target_pairs={{0,16},{1,17},{2,18},{3,19},{4,20},{5,21},{6,22},{7,23},{8,24},{9,... | collective-permute-start | bytes 393224 | tf_op jit(solution)/shard_map/ppermute | solution.py:1072
  16.2 0.2 collective-permute-done.both_ref
  16.4 0.0 collective-permute-done.1.section_ref
  16.4 0.3 collective-permute-done.2.far_ref
  16.7 0.0 collective-permute-done.3.cot_far_ref
  16.8 0.0 copy-start.8
  16.8 0.0 copy-start.9
  16.8 0.0 copy-start.14
  16.8 6.5 %word_group.1 = (f32[64,512]{1,0:T(8,128)}, bf16[128,256]{1,0:T(8,128)(2,1)S(1)}, f32[8,256]{1,0:T(8,128)S(1)}, bf16[4,400,256]{2,1,0:T(8,128)(2,1)S(1)}, bf16[4,400,256]{2,1,0:T(8,128)(2,1)S(1)}) custom-call(bf16[64,256]{1,0:T(8,128)(2,1)S(1)} %get-tuple-element.66.own_ref, bf16[64,256]{1,0:T(8,128)(2,1)S(1)} %collective-permute-done.both_ref, ...), custom_call_target="tpu_custom_call" | custom-call | flops 6710886400 | bytes 8388608 | tf_op jit(solution)/shard_map/word_group/pallas_call | solution.py:787
  23.3 0.1 collective-permute-start.4
  23.4 0.0 collective-permute-done.8.other_sum_ref
  23.4 0.0 copy-done.8
  23.4 0.0 copy-done.9
  23.4 0.0 copy-done.14
  23.4 2.2 %char_mlp_back.1 = (f32[1024,256]{1,0:T(8,128)S(1)}, f32[8,256]{1,0:T(8,128)S(1)}, bf16[8,112,256]{2,1,0:T(8,128)(2,1)S(1)}, bf16[8,112,256]{2,1,0:T(8,128)(2,1)S(1)}) custom-call(s32[2,1,64]{2,1,0:T(1,128)S(1)} %get-tuple-element.74.counts_ref, f32[1,256]{1,0:T(1,128)S(1)} %bitcast.20, bf16[256,1024]{1,0:T(8,128)(2,1)S(1)} %copy-done.8, ...), custom_call_target="tpu_custom_call" | custom-call | flops 4294967296 | bytes 8388608 | tf_op jit(solution)/shard_map/char_mlp_back/pallas_call | solution.py:453
  25.6 0.0 copy-start
  25.6 0.0 copy-start.1
  25.7 0.0 copy-start.2
  25.7 0.0 copy-start.3
  25.7 0.5 collective-permute-start.9
  26.2 0.0 collective-permute-done.4.arrived
  26.2 0.4 word_sum.1
  26.6 2.8 %collective-permute-start.5 = (bf16[400,256]{1,0:T(8,128)(2,1)S(1)}, bf16[400,256]{1,0:T(8,128)(2,1)S(1)}, u32[]{:S(2)}, u32[]{:S(2)}) collective-permute-start(bf16[400,256]{1,0:T(8,128)(2,1)S(1)} %get-tuple-element.70), channel_id=1, source_target_pairs={{0,6},{1,7},{2,4},{3,5},{4,2},{5,3},{6,0},{7,1},{8,14},{9,15},{10,... | collective-permute-start | bytes 614408 | tf_op jit(solution)/shard_map/ppermute | solution.py:1072
  29.4 0.8 %collective-permute-start.6 = (bf16[400,256]{1,0:T(8,128)(2,1)S(1)}, bf16[400,256]{1,0:T(8,128)(2,1)S(1)}, u32[]{:S(2)}, u32[]{:S(2)}) collective-permute-start(bf16[400,256]{1,0:T(8,128)(2,1)S(1)} %get-tuple-element.71), channel_id=1, source_target_pairs={{0,4},{1,5},{2,6},{3,7},{4,0},{5,1},{6,2},{7,3},{8,12},{9,13},{10,... | collective-permute-start | bytes 614408 | tf_op jit(solution)/shard_map/ppermute | solution.py:1072
  30.2 0.0 collective-permute-start.7
  30.2 0.0 collective-permute-done.9.arrived
  30.2 0.1 first_sum.1
  30.4 1.7 %collective-permute-start.10 = (bf16[8,80,128]{2,1,0:T(8,128)(2,1)S(1)}, bf16[8,80,128]{2,1,0:T(8,128)(2,1)S(1)}, u32[]{:S(2)}, u32[]{:S(2)}) collective-permute-start(bf16[8,80,128]{2,1,0:T(8,128)(2,1)S(1)} %get-tuple-element.90), channel_id=1, source_target_pairs={{0,16},{1,17},{2,18},{3,19},{4,20},{5,21},{6,22},{7,23},{8,24},{9,... | collective-permute-start | bytes 491528 | tf_op jit(solution)/shard_map/ppermute | solution.py:1072
  32.1 0.0 copy-done.2
  32.1 4.0 %char_attn_back.1 = (f32[1024,256]{1,0:T(8,128)S(1)}, bf16[384,256]{1,0:T(8,128)(2,1)S(1)}, bf16[384,256]{1,0:T(8,128)(2,1)S(1)}, bf16[16,256]{1,0:T(8,128)(2,1)S(1)}) custom-call(bf16[8,80,128]{2,1,0:T(8,128)(2,1)S(1)} %get-tuple-element.82._.stay, bf16[2,1024,256]{2,1,0:T(8,128)(2,1)} %bitcast.22, s32[1,2]{1,0:T(1,128)} %bitcast.24, ...), custom_call_target="tpu_custom_call" | custom-call | tf_op jit(solution)/shard_map/char_attn_back/pallas_call | solution.py:583
  36.1 0.1 collective-permute-start.11
  36.1 0.0 collective-permute-done.10.arrived
  36.1 0.5 collective-permute-start.12
  36.7 0.9 %collective-permute-done.12.core_extra = bf16[16,256]{1,0:T(8,128)(2,1)S(1)} collective-permute-done((bf16[16,256]{1,0:T(8,128)(2,1)S(1)}, bf16[16,256]{1,0:T(8,128)(2,1)S(1)}, u32[]{:S(2)}, u32[]{:S(2)}) %collective-permute-start.12) | collective-permute-done | bytes 8224 | tf_op jit(solution)/shard_map/ppermute | solution.py:1072
  37.6 0.0 collective-permute-done.11.core_arrived
  37.6 0.2 second_sum.1
  37.7 2.6 %collective-permute-start.13 = (bf16[256,256]{1,0:T(8,128)(2,1)S(1)}, bf16[256,256]{1,0:T(8,128)(2,1)S(1)}, u32[]{:S(2)}, u32[]{:S(2)}) collective-permute-start(bf16[256,256]{1,0:T(8,128)(2,1)S(1)} %get-tuple-element.95), channel_id=1, source_target_pairs={{0,6},{1,7},{2,4},{3,5},{4,2},{5,3},{6,0},{7,1},{8,14},{9,15},{10,... | collective-permute-start | bytes 393224 | tf_op jit(solution)/shard_map/ppermute | solution.py:1072
  40.3 0.4 collective-permute-start.14
  40.8 0.0 collective-permute-done.5.refs_0_
  40.8 0.5 collective-permute-start.15
  41.3 0.0 collective-permute-done.6.refs_1_
  41.3 0.0 collective-permute-done.7.refs_2_
  41.3 1.0 %total.1 = (bf16[400,256]{1,0:T(8,128)(2,1)S(1)}, f32[1024,256]{1,0:T(8,128)}) custom-call(bf16[400,256]{1,0:T(8,128)(2,1)S(1)} %collective-permute-done.5.refs_0_, bf16[400,256]{1,0:T(8,128)(2,1)S(1)} %collective-permute-done.6.refs_1_, bf16[400,256]{1,0:T(8,128)(2,1)S(1)} %collective-permute-done.7.refs_2_, ...), custom_call_target="tpu_custom_call" | custom-call | flops 20000000000 | bytes 8388608 | tf_op jit(solution)/shard_map/total/pallas_call | solution.py:938
  42.3 1.1 %collective-permute-start.19 = (bf16[400,256]{1,0:T(8,128)(2,1)S(1)}, bf16[400,256]{1,0:T(8,128)(2,1)S(1)}, u32[]{:S(2)}, u32[]{:S(2)}) collective-permute-start(bf16[400,256]{1,0:T(8,128)(2,1)S(1)} %get-tuple-element.99.refs_4_.own_ref), channel_id=1, source_target_pairs={{0,16},{1,17},{2,18},{3,19},{4,20},{5,21},{6,22},{7,23},{8,24},{9,... | collective-permute-start | bytes 614408 | tf_op jit(solution)/shard_map/ppermute | solution.py:1072
  43.3 1.7 %collective-permute-done.13.refs_0_ = bf16[256,256]{1,0:T(8,128)(2,1)S(1)} collective-permute-done((bf16[256,256]{1,0:T(8,128)(2,1)S(1)}, bf16[256,256]{1,0:T(8,128)(2,1)S(1)}, u32[]{:S(2)}, u32[]{:S(2)}) %collective-permute-start.13) | collective-permute-done | bytes 131104 | tf_op jit(solution)/shard_map/ppermute | solution.py:1072
  45.0 2.2 %collective-permute-done.14.refs_1_ = bf16[256,256]{1,0:T(8,128)(2,1)S(1)} collective-permute-done((bf16[256,256]{1,0:T(8,128)(2,1)S(1)}, bf16[256,256]{1,0:T(8,128)(2,1)S(1)}, u32[]{:S(2)}, u32[]{:S(2)}) %collective-permute-start.14) | collective-permute-done | bytes 131104 | tf_op jit(solution)/shard_map/ppermute | solution.py:1072
  47.2 0.0 collective-permute-done.15.refs_2_
  47.2 0.1 plane_sum.1
  47.3 3.1 %collective-permute-start.16 = (bf16[128,256]{1,0:T(8,128)(2,1)S(1)}, bf16[128,256]{1,0:T(8,128)(2,1)S(1)}, u32[]{:S(2)}, u32[]{:S(2)}) collective-permute-start(bf16[128,256]{1,0:T(8,128)(2,1)S(1)} %get-tuple-element.101), channel_id=1, source_target_pairs={{0,24},{1,25},{2,26},{3,27},{4,28},{5,29},{6,30},{7,31},{8,16},{9,... | collective-permute-start | bytes 196616 | tf_op jit(solution)/shard_map/ppermute | solution.py:1072
  50.4 0.2 collective-permute-start.17
  50.6 1.1 %collective-permute-start.18 = (bf16[128,256]{1,0:T(8,128)(2,1)S(1)}, bf16[128,256]{1,0:T(8,128)(2,1)S(1)}, u32[]{:S(2)}, u32[]{:S(2)}) collective-permute-start(bf16[128,256]{1,0:T(8,128)(2,1)S(1)} %get-tuple-element.100.near_ref), channel_id=1, source_target_pairs={{0,16},{1,17},{2,18},{3,19},{4,20},{5,21},{6,22},{7,23},{8,24},{9,... | collective-permute-start | bytes 196616 | tf_op jit(solution)/shard_map/ppermute | solution.py:1072
  51.7 0.0 collective-permute-done.19.other_ref
  51.7 0.9 %word_last.1 = (f32[16,512]{1,0:T(8,128)}, f32[32,1536]{1,0:T(8,128)}, f32[32,512]{1,0:T(8,128)}, f32[32,2048]{1,0:T(8,128)}, f32[128,512]{1,0:T(8,128)}) custom-call(bf16[400,256]{1,0:T(8,128)(2,1)S(1)} %get-tuple-element.99.refs_4_.own_ref, bf16[400,256]{1,0:T(8,128)(2,1)S(1)} %collective-permute-done.19.other_ref), custom_call_target="tpu_custom_call" | custom-call | tf_op jit(solution)/shard_map/word_last/pallas_call | solution.py:1057
  52.7 1.2 %collective-permute-done.16.both_ref = bf16[128,256]{1,0:T(8,128)(2,1)S(1)} collective-permute-done((bf16[128,256]{1,0:T(8,128)(2,1)S(1)}, bf16[128,256]{1,0:T(8,128)(2,1)S(1)}, u32[]{:S(2)}, u32[]{:S(2)}) %collective-permute-start.16) | collective-permute-done | bytes 65568 | tf_op jit(solution)/shard_map/ppermute | solution.py:1072
  53.8 2.2 %collective-permute-done.17.far_ref = bf16[128,256]{1,0:T(8,128)(2,1)S(1)} collective-permute-done((bf16[128,256]{1,0:T(8,128)(2,1)S(1)}, bf16[128,256]{1,0:T(8,128)(2,1)S(1)}, u32[]{:S(2)}, u32[]{:S(2)}) %collective-permute-start.17) | collective-permute-done | bytes 65568 | tf_op jit(solution)/shard_map/ppermute | solution.py:1072
  56.0 0.0 collective-permute-done.18.section_ref
  56.0 0.7 %char_last.1 = (f32[8,16]{1,0:T(8,128)}, f32[1,16]{1,0:T(1,128)}, f32[16,768]{1,0:T(8,128)}, f32[16,256]{1,0:T(8,128)}, f32[1,16]{1,0:T(1,128)}, /*index=5*/f32[...) custom-call(bf16[128,256]{1,0:T(8,128)(2,1)S(1)} %get-tuple-element.100.near_ref, ...), custom_call_target="tpu_custom_call" | custom-call | tf_op jit(solution)/shard_map/char_last/pallas_call | solution.py:1032
  (18 shorter events, 0.1 us)
Async XLA Ops:
  0.6 16.0 %collective-permute-start.3 = (bf16[2,64,512]{2,1,0:T(8,128)(2,1)}, bf16[2,64,512]{2,1,0:T(8,128)(2,1)S(1)}, u32[]{:S(2)}, u32[]{:S(2)}) collective-permute-start(bf16[2,64,512]{2,1,0:T(8,128)(2,1)} %bitcast.15), channel_id=1, source_target_pairs={{0,8},{1,9},{2,10},{3,11},{4,12},{5,13},{6,14},{7,15},{8,0},{9,1},... | collective-permute-start | bytes 393224 | tf_op jit(solution)/shard_map/ppermute | solution.py:1072
  4.8 11.9 %copy-start.4 = (bf16[512,2048]{1,0:T(8,128)(2,1)S(1)}, bf16[512,2048]{1,0:T(8,128)(2,1)}, u32[]{:S(2)}) copy-start(bf16[512,2048]{1,0:T(8,128)(2,1)} %expand_ref.2) | copy-start | bytes 6291460
  4.8 11.9 %copy-start.5 = (bf16[2048,512]{1,0:T(8,128)(2,1)S(1)}, bf16[2048,512]{1,0:T(8,128)(2,1)}, u32[]{:S(2)}) copy-start(bf16[2048,512]{1,0:T(8,128)(2,1)} %shrink_ref.2) | copy-start | bytes 6291460
  4.8 11.9 %copy-start.6 = (bf16[512,1536]{1,0:T(8,128)(2,1)S(1)}, bf16[512,1536]{1,0:T(8,128)(2,1)}, u32[]{:S(2)}) copy-start(bf16[512,1536]{1,0:T(8,128)(2,1)} %project_ref.2) | copy-start | bytes 4718596
  4.8 11.9 %copy-start.7 = (bf16[512,512]{1,0:T(8,128)(2,1)S(1)}, bf16[512,512]{1,0:T(8,128)(2,1)}, u32[]{:S(2)}) copy-start(bf16[512,512]{1,0:T(8,128)(2,1)} %output_ref.2) | copy-start | bytes 1572868
  4.8 12.0 %copy-start.10 = (bf16[256,512]{1,0:T(8,128)(2,1)S(1)}, bf16[256,512]{1,0:T(8,128)(2,1)}, u32[]{:S(2)}) copy-start(bf16[256,512]{1,0:T(8,128)(2,1)} %input_ref.1) | copy-start | bytes 786436
  4.8 12.0 %copy-start.11 = (bf16[2,1,64,512]{3,2,1,0:T(8,128)(2,1)S(1)}, bf16[2,1,64,512]{3,2,1,0:T(8,128)(2,1)}, u32[]{:S(2)}) copy-start(bf16[2,1,64,512]{3,2,1,0:T(8,128)(2,1)} %param.35) | copy-start | bytes 393220
  4.8 12.0 %copy-start.12 = (f32[512]{0:T(512)S(1)}, f32[512]{0:T(512)}, u32[]{:S(2)}) copy-start(f32[512]{0:T(512)} %param.29) | copy-start | bytes 6148
  4.8 12.0 %copy-start.13 = (f32[512]{0:T(512)S(1)}, f32[512]{0:T(512)}, u32[]{:S(2)}) copy-start(f32[512]{0:T(512)} %param.32) | copy-start | bytes 6148
  10.2 6.2 %collective-permute-start = (bf16[64,256]{1,0:T(8,128)(2,1)S(1)}, bf16[64,256]{1,0:T(8,128)(2,1)S(1)}, u32[]{:S(2)}, u32[]{:S(2)}) collective-permute-start(bf16[64,256]{1,0:T(8,128)(2,1)S(1)} %get-tuple-element.66.own_ref), channel_id=1, source_target_pairs={{0,24},{1,25},{2,26},{3,27},{4,28},{5,29},{6,30},{7,31},{8,16},{9,... | collective-permute-start | bytes 98312 | tf_op jit(solution)/shard_map/ppermute | solution.py:1072
  11.5 4.9 %collective-permute-start.1 = (bf16[64,256]{1,0:T(8,128)(2,1)S(1)}, bf16[64,256]{1,0:T(8,128)(2,1)S(1)}, u32[]{:S(2)}, u32[]{:S(2)}) collective-permute-start(bf16[64,256]{1,0:T(8,128)(2,1)S(1)} %get-tuple-element.66.own_ref), channel_id=1, source_target_pairs={{0,16},{1,17},{2,18},{3,19},{4,20},{5,21},{6,22},{7,23},{8,24},{9,... | collective-permute-start | bytes 98312 | tf_op jit(solution)/shard_map/ppermute | solution.py:1072
  11.9 4.8 %collective-permute-start.2 = (bf16[64,256]{1,0:T(8,128)(2,1)S(1)}, bf16[64,256]{1,0:T(8,128)(2,1)S(1)}, u32[]{:S(2)}, u32[]{:S(2)}) collective-permute-start(bf16[64,256]{1,0:T(8,128)(2,1)S(1)} %get-tuple-element.66.own_ref), channel_id=1, source_target_pairs={{0,8},{1,9},{2,10},{3,11},{4,12},{5,13},{6,14},{7,15},{8,0},{9,1},... | collective-permute-start | bytes 98312 | tf_op jit(solution)/shard_map/ppermute | solution.py:1072
  14.7 8.7 %collective-permute-start.8 = (bf16[64,1024]{1,0:T(8,128)(2,1)S(1)}, bf16[64,1024]{1,0:T(8,128)(2,1)S(1)}, u32[]{:S(2)}, u32[]{:S(2)}) collective-permute-start(bf16[64,1024]{1,0:T(8,128)(2,1)S(1)} %get-tuple-element.76.hidden_sum_ref), channel_id=1, source_target_pairs={{0,16},{1,17},{2,18},{3,19},{4,20},{5,21},{6,22},{7,23},{8,24},{9,... | collective-permute-start | bytes 393224 | tf_op jit(solution)/shard_map/ppermute | solution.py:1072
  16.8 6.6 %copy-start.8 = (bf16[256,1024]{1,0:T(8,128)(2,1)S(1)}, bf16[256,1024]{1,0:T(8,128)(2,1)}, u32[]{:S(2)}) copy-start(bf16[256,1024]{1,0:T(8,128)(2,1)} %expand_ref.3) | copy-start | bytes 1572868
  16.8 6.6 %copy-start.9 = (bf16[1024,256]{1,0:T(8,128)(2,1)S(1)}, bf16[1024,256]{1,0:T(8,128)(2,1)}, u32[]{:S(2)}) copy-start(bf16[1024,256]{1,0:T(8,128)(2,1)} %shrink_ref.3) | copy-start | bytes 1572868
  16.8 6.6 %copy-start.14 = (f32[256]{0:T(256)S(1)}, f32[256]{0:T(256)}, u32[]{:S(2)}) copy-start(f32[256]{0:T(256)} %param.25) | copy-start | bytes 3076
  23.3 2.9 %collective-permute-start.4 = (bf16[4,400,256]{2,1,0:T(8,128)(2,1)S(1)}, bf16[4,400,256]{2,1,0:T(8,128)(2,1)S(1)}, u32[]{:S(2)}, u32[]{:S(2)}) collective-permute-start(bf16[4,400,256]{2,1,0:T(8,128)(2,1)S(1)} %get-tuple-element.69), channel_id=1, source_target_pairs={{0,1},{1,0},{2,3},{3,2},{4,5},{5,4},{6,7},{7,6},{8,9},{9,8},{10,11... | collective-permute-start | bytes 2457608 | tf_op jit(solution)/shard_map/ppermute | solution.py:1072
  25.6 6.5 %copy-start = (bf16[256,768]{1,0:T(8,128)(2,1)S(1)}, bf16[256,768]{1,0:T(8,128)(2,1)}, u32[]{:S(2)}) copy-start(bf16[256,768]{1,0:T(8,128)(2,1)} %project_ref.3) | copy-start | bytes 1179652
  25.6 6.4 %copy-start.1 = (bf16[256,256]{1,0:T(8,128)(2,1)S(1)}, bf16[256,256]{1,0:T(8,128)(2,1)}, u32[]{:S(2)}) copy-start(bf16[256,256]{1,0:T(8,128)(2,1)} %output_ref.3) | copy-start | bytes 393220
  25.7 6.4 %copy-start.2 = (bf16[8,256]{1,0:T(8,128)(2,1)S(1)}, bf16[8,256]{1,0:T(8,128)(2,1)}, u32[]{:S(2)}) copy-start(bf16[8,256]{1,0:T(8,128)(2,1)} %table_ref.1) | copy-start | bytes 12292
  25.7 6.4 %copy-start.3 = (f32[256]{0:T(256)S(1)}, f32[256]{0:T(256)}, u32[]{:S(2)}) copy-start(f32[256]{0:T(256)} %param.22) | copy-start | bytes 3076
  25.7 4.5 %collective-permute-start.9 = (bf16[8,112,256]{2,1,0:T(8,128)(2,1)S(1)}, bf16[8,112,256]{2,1,0:T(8,128)(2,1)S(1)}, u32[]{:S(2)}, u32[]{:S(2)}) collective-permute-start(bf16[8,112,256]{2,1,0:T(8,128)(2,1)S(1)} %get-tuple-element.81), channel_id=1, source_target_pairs={{0,1},{1,0},{2,3},{3,2},{4,5},{5,4},{6,7},{7,6},{8,9},{9,8},{10,11... | collective-permute-start | bytes 1376264 | tf_op jit(solution)/shard_map/ppermute | solution.py:1072
  26.6 14.2 %collective-permute-start.5 = (bf16[400,256]{1,0:T(8,128)(2,1)S(1)}, bf16[400,256]{1,0:T(8,128)(2,1)S(1)}, u32[]{:S(2)}, u32[]{:S(2)}) collective-permute-start(bf16[400,256]{1,0:T(8,128)(2,1)S(1)} %get-tuple-element.70), channel_id=1, source_target_pairs={{0,6},{1,7},{2,4},{3,5},{4,2},{5,3},{6,0},{7,1},{8,14},{9,15},{10,... | collective-permute-start | bytes 614408 | tf_op jit(solution)/shard_map/ppermute | solution.py:1072
  29.4 11.9 %collective-permute-start.6 = (bf16[400,256]{1,0:T(8,128)(2,1)S(1)}, bf16[400,256]{1,0:T(8,128)(2,1)S(1)}, u32[]{:S(2)}, u32[]{:S(2)}) collective-permute-start(bf16[400,256]{1,0:T(8,128)(2,1)S(1)} %get-tuple-element.71), channel_id=1, source_target_pairs={{0,4},{1,5},{2,6},{3,7},{4,0},{5,1},{6,2},{7,3},{8,12},{9,13},{10,... | collective-permute-start | bytes 614408 | tf_op jit(solution)/shard_map/ppermute | solution.py:1072
  30.2 11.1 %collective-permute-start.7 = (bf16[400,256]{1,0:T(8,128)(2,1)S(1)}, bf16[400,256]{1,0:T(8,128)(2,1)S(1)}, u32[]{:S(2)}, u32[]{:S(2)}) collective-permute-start(bf16[400,256]{1,0:T(8,128)(2,1)S(1)} %get-tuple-element.72), channel_id=1, source_target_pairs={{0,2},{1,3},{2,0},{3,1},{4,6},{5,7},{6,4},{7,5},{8,10},{9,11},{10,... | collective-permute-start | bytes 614408 | tf_op jit(solution)/shard_map/ppermute | solution.py:1072
  30.4 5.8 %collective-permute-start.10 = (bf16[8,80,128]{2,1,0:T(8,128)(2,1)S(1)}, bf16[8,80,128]{2,1,0:T(8,128)(2,1)S(1)}, u32[]{:S(2)}, u32[]{:S(2)}) collective-permute-start(bf16[8,80,128]{2,1,0:T(8,128)(2,1)S(1)} %get-tuple-element.90), channel_id=1, source_target_pairs={{0,16},{1,17},{2,18},{3,19},{4,20},{5,21},{6,22},{7,23},{8,24},{9,... | collective-permute-start | bytes 491528 | tf_op jit(solution)/shard_map/ppermute | solution.py:1072
  36.1 1.5 %collective-permute-start.11 = (bf16[384,256]{1,0:T(8,128)(2,1)S(1)}, bf16[384,256]{1,0:T(8,128)(2,1)S(1)}, u32[]{:S(2)}, u32[]{:S(2)}) collective-permute-start(bf16[384,256]{1,0:T(8,128)(2,1)S(1)} %get-tuple-element.93), channel_id=1, source_target_pairs={{0,1},{1,0},{2,3},{3,2},{4,5},{5,4},{6,7},{7,6},{8,9},{9,8},{10,11... | collective-permute-start | bytes 589832 | tf_op jit(solution)/shard_map/ppermute | solution.py:1072
  36.1 1.4 %collective-permute-start.12 = (bf16[16,256]{1,0:T(8,128)(2,1)S(1)}, bf16[16,256]{1,0:T(8,128)(2,1)S(1)}, u32[]{:S(2)}, u32[]{:S(2)}) collective-permute-start(bf16[16,256]{1,0:T(8,128)(2,1)S(1)} %get-tuple-element.94.own_extra), channel_id=1, source_target_pairs={{0,1},{1,0},{2,3},{3,2},{4,5},{5,4},{6,7},{7,6},{8,9},{9,8},{10,11... | collective-permute-start | bytes 24584 | tf_op jit(solution)/shard_map/ppermute | solution.py:1072
  37.7 7.3 %collective-permute-start.13 = (bf16[256,256]{1,0:T(8,128)(2,1)S(1)}, bf16[256,256]{1,0:T(8,128)(2,1)S(1)}, u32[]{:S(2)}, u32[]{:S(2)}) collective-permute-start(bf16[256,256]{1,0:T(8,128)(2,1)S(1)} %get-tuple-element.95), channel_id=1, source_target_pairs={{0,6},{1,7},{2,4},{3,5},{4,2},{5,3},{6,0},{7,1},{8,14},{9,15},{10,... | collective-permute-start | bytes 393224 | tf_op jit(solution)/shard_map/ppermute | solution.py:1072
  40.3 6.9 %collective-permute-start.14 = (bf16[256,256]{1,0:T(8,128)(2,1)S(1)}, bf16[256,256]{1,0:T(8,128)(2,1)S(1)}, u32[]{:S(2)}, u32[]{:S(2)}) collective-permute-start(bf16[256,256]{1,0:T(8,128)(2,1)S(1)} %get-tuple-element.96), channel_id=1, source_target_pairs={{0,4},{1,5},{2,6},{3,7},{4,0},{5,1},{6,2},{7,3},{8,12},{9,13},{10,... | collective-permute-start | bytes 393224 | tf_op jit(solution)/shard_map/ppermute | solution.py:1072
  40.8 6.4 %collective-permute-start.15 = (bf16[256,256]{1,0:T(8,128)(2,1)S(1)}, bf16[256,256]{1,0:T(8,128)(2,1)S(1)}, u32[]{:S(2)}, u32[]{:S(2)}) collective-permute-start(bf16[256,256]{1,0:T(8,128)(2,1)S(1)} %get-tuple-element.97), channel_id=1, source_target_pairs={{0,2},{1,3},{2,0},{3,1},{4,6},{5,7},{6,4},{7,5},{8,10},{9,11},{10,... | collective-permute-start | bytes 393224 | tf_op jit(solution)/shard_map/ppermute | solution.py:1072
  42.3 9.4 %collective-permute-start.19 = (bf16[400,256]{1,0:T(8,128)(2,1)S(1)}, bf16[400,256]{1,0:T(8,128)(2,1)S(1)}, u32[]{:S(2)}, u32[]{:S(2)}) collective-permute-start(bf16[400,256]{1,0:T(8,128)(2,1)S(1)} %get-tuple-element.99.refs_4_.own_ref), channel_id=1, source_target_pairs={{0,16},{1,17},{2,18},{3,19},{4,20},{5,21},{6,22},{7,23},{8,24},{9,... | collective-permute-start | bytes 614408 | tf_op jit(solution)/shard_map/ppermute | solution.py:1072
  47.3 6.6 %collective-permute-start.16 = (bf16[128,256]{1,0:T(8,128)(2,1)S(1)}, bf16[128,256]{1,0:T(8,128)(2,1)S(1)}, u32[]{:S(2)}, u32[]{:S(2)}) collective-permute-start(bf16[128,256]{1,0:T(8,128)(2,1)S(1)} %get-tuple-element.101), channel_id=1, source_target_pairs={{0,24},{1,25},{2,26},{3,27},{4,28},{5,29},{6,30},{7,31},{8,16},{9,... | collective-permute-start | bytes 196616 | tf_op jit(solution)/shard_map/ppermute | solution.py:1072
  50.4 5.6 %collective-permute-start.17 = (bf16[128,256]{1,0:T(8,128)(2,1)S(1)}, bf16[128,256]{1,0:T(8,128)(2,1)S(1)}, u32[]{:S(2)}, u32[]{:S(2)}) collective-permute-start(bf16[128,256]{1,0:T(8,128)(2,1)S(1)} %get-tuple-element.101), channel_id=1, source_target_pairs={{0,8},{1,9},{2,10},{3,11},{4,12},{5,13},{6,14},{7,15},{8,0},{9,1},... | collective-permute-start | bytes 196616 | tf_op jit(solution)/shard_map/ppermute | solution.py:1072
  50.6 5.4 %collective-permute-start.18 = (bf16[128,256]{1,0:T(8,128)(2,1)S(1)}, bf16[128,256]{1,0:T(8,128)(2,1)S(1)}, u32[]{:S(2)}, u32[]{:S(2)}) collective-permute-start(bf16[128,256]{1,0:T(8,128)(2,1)S(1)} %get-tuple-element.100.near_ref), channel_id=1, source_target_pairs={{0,16},{1,17},{2,18},{3,19},{4,20},{5,21},{6,22},{7,23},{8,24},{9,... | collective-permute-start | bytes 196616 | tf_op jit(solution)/shard_map/ppermute | solution.py:1072

commit v11 on v10

--- a/solution.py
+++ b/solution.py
@@ -101,7 +101,7 @@
     return (probs, mixed)
 
 
-def attend_back(load, load_dmixed, tiles, probs, store, length):
+def attend_back(load, load_dmixed, tiles, probs, store, length, between=None):
     dprobs = []
     for number, tile in enumerate(tiles):
         grads = load_dmixed(tile)
@@ -112,6 +112,8 @@
         store(tile, 2, dot(parts, stacked).astype(bf16))
     dprobs = jnp.concatenate(dprobs, axis=1)
     dscores = probs * (dprobs - jnp.sum(probs * dprobs, axis=0, keepdims=True))
+    if between is not None:
+        between()
     scaling = HEAD**-0.5
     for number, tile in enumerate(tiles):
         parts = expand_heads(dscores, number, length)
@@ -531,12 +533,18 @@
     def store(block, which, value):
         dqkv[block * BLOCK : (block + 1) * BLOCK, which * SLAB : (which + 1) * SLAB] = value
 
-    attend_back(load, load_dmixed, range(rows // BLOCK), probs_ref[...], store, slots)
-    for fetch in fetches:
-        fetch.wait()
-    language = pick(languages_ref[...], section)
-    normal, scale = unit(char_rows(chars_ref[...], table_ref, language))
-    normed_t = (normal * gain_attn_ref[...]).astype(bf16).T
+    kept = []
+
+    def norms():
+        for fetch in fetches:
+            fetch.wait()
+        language = pick(languages_ref[...], section)
+        normal, scale = unit(char_rows(chars_ref[...], table_ref, language))
+        kept.extend((language, normal, scale, (normal * gain_attn_ref[...]).astype(bf16).T))
+
+    blocks = range(rows // BLOCK)
+    attend_back(load, load_dmixed, blocks, probs_ref[...], store, slots, norms)
+    language, normal, scale, normed_t = kept
     dnormed = dot_nt(dqkv[...], project_ref[...])
     project_grad[...] = dot(normed_t, dqkv[...])
     gain_attn_grad = jnp.sum(dnormed * normal, axis=0, keepdims=True)

time: 56.9 us -> 56.9 us (level)
  waiting for transfers between devices: 8.64 us -> 9.43 us
  Pallas kernels: 21.4 us -> 20.7 us
    ppermute x20, waiting for transfers between devices: 8.64 us -> 9.43 us  [exchange(): return lax.ppermute(value, ('section', 'dp'), pairs)]
    pallas_call x1, Pallas kernels: 3.96 us -> 3.25 us  [char_attn_back(): pl.pallas_call(functools.partial(char_attn_back_kernel, slots, shards), i...]
  transfers between devices with their start and end apart: 20 -> 20, of which waited for: 7 -> 8; matrix products, arithmetic and copies ran while one was open for 0% -> 0% of each run, Pallas kernels for 37% -> 35%
where the time goes in v11:
time: 56.9 us; the launch traced here: 56.7 us
  starting transfers between devices  25.5 us (45%)
  Pallas kernels  20.7 us (36%)
  waiting for transfers between devices  9.43 us (17%)
  between operations  0.93 us (2%)
    ppermute x20, starting transfers between devices, exchange(): return lax.ppermute(value, ('section', 'dp'), pairs)  25.5 us
    ppermute x20, waiting for transfers between devices, exchange(): return lax.ppermute(value, ('section', 'dp'), pairs)  9.43 us
    pallas_call x1, Pallas kernels, word_group(): pl.pallas_call(functools.partial(word_kernel, length, shards), in_specs=[...  6.5 us
    pallas_call x1, Pallas kernels, char_forward(): pl.pallas_call(functools.partial(char_forward_kernel, slots), in_specs=[h...  5.41 us
    pallas_call x1, Pallas kernels, char_attn_back(): pl.pallas_call(functools.partial(char_attn_back_kernel, slots, shards), i...  3.25 us
    pallas_call x1, Pallas kernels, char_mlp_back(): pl.pallas_call(functools.partial(char_mlp_back_kernel, slots, shards), in...  2.21 us
  transfers between devices with their start and end apart: 20, of which 8 were waited for; matrix products, arithmetic and copies ran while one was open for 0% of the time, Pallas kernels for 35%

profile of v11, /device:TPU:0, one launch (start us, length us, event | category | flops | bytes accessed | tf_op | source)
XLA Modules:
  0.0 56.7 jit_solution(15716843035675898386)
XLA Ops:
  0.6 4.1 %collective-permute-start.3 = (bf16[2,64,512]{2,1,0:T(8,128)(2,1)}, bf16[2,64,512]{2,1,0:T(8,128)(2,1)S(1)}, u32[]{:S(2)}, u32[]{:S(2)}) collective-permute-start(bf16[2,64,512]{2,1,0:T(8,128)(2,1)} %bitcast.15), channel_id=1, source_target_pairs={{0,8},{1,9},{2,10},{3,11},{4,12},{5,13},{6,14},{7,15},{8,0},{9,1},... | collective-permute-start | bytes 393224 | tf_op jit(solution)/shard_map/ppermute | solution.py:1080
  4.8 0.0 copy-start.10
  4.8 0.0 copy-start.11
  4.8 0.0 copy-start.12
  4.8 5.4 %char_forward.1 = (bf16[64,256]{1,0:T(8,128)(2,1)S(1)}, bf16[64,1024]{1,0:T(8,128)(2,1)S(1)}, s32[2,1,64]{2,1,0:T(1,128)S(1)}, bf16[1024,768]{1,0:T(8,128)(2,1)S...) custom-call(bf16[2,1024,256]{2,1,0:T(8,128)(2,1)} %bitcast.21, ...), custom_call_target="tpu_custom_call" | custom-call | flops 4294967296 | bytes 8388608 | tf_op jit(solution)/shard_map/char_forward/pallas_call | solution.py:316
  10.2 1.3 %collective-permute-start = (bf16[64,256]{1,0:T(8,128)(2,1)S(1)}, bf16[64,256]{1,0:T(8,128)(2,1)S(1)}, u32[]{:S(2)}, u32[]{:S(2)}) collective-permute-start(bf16[64,256]{1,0:T(8,128)(2,1)S(1)} %get-tuple-element.66.own_ref), channel_id=1, source_target_pairs={{0,24},{1,25},{2,26},{3,27},{4,28},{5,29},{6,30},{7,31},{8,16},{9,... | collective-permute-start | bytes 98312 | tf_op jit(solution)/shard_map/ppermute | solution.py:1080
  11.5 0.3 collective-permute-start.1
  11.9 2.8 %collective-permute-start.2 = (bf16[64,256]{1,0:T(8,128)(2,1)S(1)}, bf16[64,256]{1,0:T(8,128)(2,1)S(1)}, u32[]{:S(2)}, u32[]{:S(2)}) collective-permute-start(bf16[64,256]{1,0:T(8,128)(2,1)S(1)} %get-tuple-element.66.own_ref), channel_id=1, source_target_pairs={{0,8},{1,9},{2,10},{3,11},{4,12},{5,13},{6,14},{7,15},{8,0},{9,1},... | collective-permute-start | bytes 98312 | tf_op jit(solution)/shard_map/ppermute | solution.py:1080
  14.7 1.5 %collective-permute-start.8 = (bf16[64,1024]{1,0:T(8,128)(2,1)S(1)}, bf16[64,1024]{1,0:T(8,128)(2,1)S(1)}, u32[]{:S(2)}, u32[]{:S(2)}) collective-permute-start(bf16[64,1024]{1,0:T(8,128)(2,1)S(1)} %get-tuple-element.76.hidden_sum_ref), channel_id=1, source_target_pairs={{0,16},{1,17},{2,18},{3,19},{4,20},{5,21},{6,22},{7,23},{8,24},{9,... | collective-permute-start | bytes 393224 | tf_op jit(solution)/shard_map/ppermute | solution.py:1080
  16.2 0.2 collective-permute-done.both_ref
  16.4 0.0 collective-permute-done.1.section_ref
  16.4 0.3 collective-permute-done.2.far_ref
  16.7 0.0 collective-permute-done.3.cot_far_ref
  16.7 0.0 copy-done.4
  16.8 0.0 copy-start.8
  16.8 0.0 copy-start.9
  16.8 0.0 copy-start.14
  16.8 6.5 %word_group.1 = (f32[64,512]{1,0:T(8,128)}, bf16[128,256]{1,0:T(8,128)(2,1)S(1)}, f32[8,256]{1,0:T(8,128)S(1)}, bf16[4,400,256]{2,1,0:T(8,128)(2,1)S(1)}, bf16[4,400,256]{2,1,0:T(8,128)(2,1)S(1)}) custom-call(bf16[64,256]{1,0:T(8,128)(2,1)S(1)} %get-tuple-element.66.own_ref, bf16[64,256]{1,0:T(8,128)(2,1)S(1)} %collective-permute-done.both_ref, ...), custom_call_target="tpu_custom_call" | custom-call | flops 6710886400 | bytes 8388608 | tf_op jit(solution)/shard_map/word_group/pallas_call | solution.py:795
  23.3 0.1 collective-permute-start.4
  23.4 0.0 collective-permute-done.8.other_sum_ref
  23.4 2.2 %char_mlp_back.1 = (f32[1024,256]{1,0:T(8,128)S(1)}, f32[8,256]{1,0:T(8,128)S(1)}, bf16[8,112,256]{2,1,0:T(8,128)(2,1)S(1)}, bf16[8,112,256]{2,1,0:T(8,128)(2,1)S(1)}) custom-call(s32[2,1,64]{2,1,0:T(1,128)S(1)} %get-tuple-element.74.counts_ref, f32[1,256]{1,0:T(1,128)S(1)} %bitcast.20, bf16[256,1024]{1,0:T(8,128)(2,1)S(1)} %copy-done.8, ...), custom_call_target="tpu_custom_call" | custom-call | flops 4294967296 | bytes 8388608 | tf_op jit(solution)/shard_map/char_mlp_back/pallas_call | solution.py:455
  25.6 0.0 copy-start
  25.6 0.0 copy-start.1
  25.7 0.0 copy-start.2
  25.7 0.0 copy-start.3
  25.7 0.5 collective-permute-start.9
  26.2 0.0 collective-permute-done.4.arrived
  26.2 0.4 word_sum.1
  26.6 2.8 %collective-permute-start.5 = (bf16[400,256]{1,0:T(8,128)(2,1)S(1)}, bf16[400,256]{1,0:T(8,128)(2,1)S(1)}, u32[]{:S(2)}, u32[]{:S(2)}) collective-permute-start(bf16[400,256]{1,0:T(8,128)(2,1)S(1)} %get-tuple-element.70), channel_id=1, source_target_pairs={{0,6},{1,7},{2,4},{3,5},{4,2},{5,3},{6,0},{7,1},{8,14},{9,15},{10,... | collective-permute-start | bytes 614408 | tf_op jit(solution)/shard_map/ppermute | solution.py:1080
  29.4 0.8 %collective-permute-start.6 = (bf16[400,256]{1,0:T(8,128)(2,1)S(1)}, bf16[400,256]{1,0:T(8,128)(2,1)S(1)}, u32[]{:S(2)}, u32[]{:S(2)}) collective-permute-start(bf16[400,256]{1,0:T(8,128)(2,1)S(1)} %get-tuple-element.71), channel_id=1, source_target_pairs={{0,4},{1,5},{2,6},{3,7},{4,0},{5,1},{6,2},{7,3},{8,12},{9,13},{10,... | collective-permute-start | bytes 614408 | tf_op jit(solution)/shard_map/ppermute | solution.py:1080
  30.2 0.0 collective-permute-start.7
  30.2 0.0 collective-permute-done.9.arrived
  30.2 0.1 first_sum.1
  30.4 1.7 %collective-permute-start.10 = (bf16[8,80,128]{2,1,0:T(8,128)(2,1)S(1)}, bf16[8,80,128]{2,1,0:T(8,128)(2,1)S(1)}, u32[]{:S(2)}, u32[]{:S(2)}) collective-permute-start(bf16[8,80,128]{2,1,0:T(8,128)(2,1)S(1)} %get-tuple-element.90), channel_id=1, source_target_pairs={{0,16},{1,17},{2,18},{3,19},{4,20},{5,21},{6,22},{7,23},{8,24},{9,... | collective-permute-start | bytes 491528 | tf_op jit(solution)/shard_map/ppermute | solution.py:1080
  32.1 0.0 copy-done.1
  32.1 0.0 copy-done.3
  32.1 3.3 %char_attn_back.1 = (f32[1024,256]{1,0:T(8,128)S(1)}, bf16[384,256]{1,0:T(8,128)(2,1)S(1)}, bf16[384,256]{1,0:T(8,128)(2,1)S(1)}, bf16[16,256]{1,0:T(8,128)(2,1)S(1)}) custom-call(bf16[8,80,128]{2,1,0:T(8,128)(2,1)S(1)} %get-tuple-element.82._.stay, bf16[2,1024,256]{2,1,0:T(8,128)(2,1)} %bitcast.22, s32[1,2]{1,0:T(1,128)} %bitcast.24, ...), custom_call_target="tpu_custom_call" | custom-call | tf_op jit(solution)/shard_map/char_attn_back/pallas_call | solution.py:591
  35.4 0.1 collective-permute-start.11
  35.4 0.6 collective-permute-done.10.arrived
  36.0 0.0 collective-permute-start.12
  36.0 1.1 %collective-permute-done.12.core_extra = bf16[16,256]{1,0:T(8,128)(2,1)S(1)} collective-permute-done((bf16[16,256]{1,0:T(8,128)(2,1)S(1)}, bf16[16,256]{1,0:T(8,128)(2,1)S(1)}, u32[]{:S(2)}, u32[]{:S(2)}) %collective-permute-start.12) | collective-permute-done | bytes 8224 | tf_op jit(solution)/shard_map/ppermute | solution.py:1080
  37.2 0.0 collective-permute-done.11.core_arrived
  37.2 0.2 second_sum.1
  37.3 2.5 %collective-permute-start.13 = (bf16[256,256]{1,0:T(8,128)(2,1)S(1)}, bf16[256,256]{1,0:T(8,128)(2,1)S(1)}, u32[]{:S(2)}, u32[]{:S(2)}) collective-permute-start(bf16[256,256]{1,0:T(8,128)(2,1)S(1)} %get-tuple-element.95), channel_id=1, source_target_pairs={{0,6},{1,7},{2,4},{3,5},{4,2},{5,3},{6,0},{7,1},{8,14},{9,15},{10,... | collective-permute-start | bytes 393224 | tf_op jit(solution)/shard_map/ppermute | solution.py:1080
  39.8 0.8 %collective-permute-start.14 = (bf16[256,256]{1,0:T(8,128)(2,1)S(1)}, bf16[256,256]{1,0:T(8,128)(2,1)S(1)}, u32[]{:S(2)}, u32[]{:S(2)}) collective-permute-start(bf16[256,256]{1,0:T(8,128)(2,1)S(1)} %get-tuple-element.96), channel_id=1, source_target_pairs={{0,4},{1,5},{2,6},{3,7},{4,0},{5,1},{6,2},{7,3},{8,12},{9,13},{10,... | collective-permute-start | bytes 393224 | tf_op jit(solution)/shard_map/ppermute | solution.py:1080
  40.6 0.0 collective-permute-done.5.refs_0_
  40.6 0.3 collective-permute-start.15
  40.9 0.0 collective-permute-done.6.refs_1_
  40.9 0.0 collective-permute-done.7.refs_2_
  40.9 1.0 %total.1 = (bf16[400,256]{1,0:T(8,128)(2,1)S(1)}, f32[1024,256]{1,0:T(8,128)}) custom-call(bf16[400,256]{1,0:T(8,128)(2,1)S(1)} %collective-permute-done.5.refs_0_, bf16[400,256]{1,0:T(8,128)(2,1)S(1)} %collective-permute-done.6.refs_1_, bf16[400,256]{1,0:T(8,128)(2,1)S(1)} %collective-permute-done.7.refs_2_, ...), custom_call_target="tpu_custom_call" | custom-call | flops 20000000000 | bytes 8388608 | tf_op jit(solution)/shard_map/total/pallas_call | solution.py:946
  41.9 1.5 %collective-permute-start.19 = (bf16[400,256]{1,0:T(8,128)(2,1)S(1)}, bf16[400,256]{1,0:T(8,128)(2,1)S(1)}, u32[]{:S(2)}, u32[]{:S(2)}) collective-permute-start(bf16[400,256]{1,0:T(8,128)(2,1)S(1)} %get-tuple-element.99.refs_4_.own_ref), channel_id=1, source_target_pairs={{0,16},{1,17},{2,18},{3,19},{4,20},{5,21},{6,22},{7,23},{8,24},{9,... | collective-permute-start | bytes 614408 | tf_op jit(solution)/shard_map/ppermute | solution.py:1080
  43.3 1.3 %collective-permute-done.13.refs_0_ = bf16[256,256]{1,0:T(8,128)(2,1)S(1)} collective-permute-done((bf16[256,256]{1,0:T(8,128)(2,1)S(1)}, bf16[256,256]{1,0:T(8,128)(2,1)S(1)}, u32[]{:S(2)}, u32[]{:S(2)}) %collective-permute-start.13) | collective-permute-done | bytes 131104 | tf_op jit(solution)/shard_map/ppermute | solution.py:1080
  44.6 2.4 %collective-permute-done.14.refs_1_ = bf16[256,256]{1,0:T(8,128)(2,1)S(1)} collective-permute-done((bf16[256,256]{1,0:T(8,128)(2,1)S(1)}, bf16[256,256]{1,0:T(8,128)(2,1)S(1)}, u32[]{:S(2)}, u32[]{:S(2)}) %collective-permute-start.14) | collective-permute-done | bytes 131104 | tf_op jit(solution)/shard_map/ppermute | solution.py:1080
  47.0 0.0 collective-permute-done.15.refs_2_
  47.0 0.1 plane_sum.1
  47.1 3.3 %collective-permute-start.16 = (bf16[128,256]{1,0:T(8,128)(2,1)S(1)}, bf16[128,256]{1,0:T(8,128)(2,1)S(1)}, u32[]{:S(2)}, u32[]{:S(2)}) collective-permute-start(bf16[128,256]{1,0:T(8,128)(2,1)S(1)} %get-tuple-element.101), channel_id=1, source_target_pairs={{0,24},{1,25},{2,26},{3,27},{4,28},{5,29},{6,30},{7,31},{8,16},{9,... | collective-permute-start | bytes 196616 | tf_op jit(solution)/shard_map/ppermute | solution.py:1080
  50.4 0.2 collective-permute-start.17
  50.6 0.9 %collective-permute-start.18 = (bf16[128,256]{1,0:T(8,128)(2,1)S(1)}, bf16[128,256]{1,0:T(8,128)(2,1)S(1)}, u32[]{:S(2)}, u32[]{:S(2)}) collective-permute-start(bf16[128,256]{1,0:T(8,128)(2,1)S(1)} %get-tuple-element.100.near_ref), channel_id=1, source_target_pairs={{0,16},{1,17},{2,18},{3,19},{4,20},{5,21},{6,22},{7,23},{8,24},{9,... | collective-permute-start | bytes 196616 | tf_op jit(solution)/shard_map/ppermute | solution.py:1080
  51.5 0.0 collective-permute-done.19.other_ref
  51.5 0.9 %word_last.1 = (f32[16,512]{1,0:T(8,128)}, f32[32,1536]{1,0:T(8,128)}, f32[32,512]{1,0:T(8,128)}, f32[32,2048]{1,0:T(8,128)}, f32[128,512]{1,0:T(8,128)}) custom-call(bf16[400,256]{1,0:T(8,128)(2,1)S(1)} %get-tuple-element.99.refs_4_.own_ref, bf16[400,256]{1,0:T(8,128)(2,1)S(1)} %collective-permute-done.19.other_ref), custom_call_target="tpu_custom_call" | custom-call | tf_op jit(solution)/shard_map/word_last/pallas_call | solution.py:1065
  52.4 1.9 %collective-permute-done.16.both_ref = bf16[128,256]{1,0:T(8,128)(2,1)S(1)} collective-permute-done((bf16[128,256]{1,0:T(8,128)(2,1)S(1)}, bf16[128,256]{1,0:T(8,128)(2,1)S(1)}, u32[]{:S(2)}, u32[]{:S(2)}) %collective-permute-start.16) | collective-permute-done | bytes 65568 | tf_op jit(solution)/shard_map/ppermute | solution.py:1080
  54.4 1.6 %collective-permute-done.17.far_ref = bf16[128,256]{1,0:T(8,128)(2,1)S(1)} collective-permute-done((bf16[128,256]{1,0:T(8,128)(2,1)S(1)}, bf16[128,256]{1,0:T(8,128)(2,1)S(1)}, u32[]{:S(2)}, u32[]{:S(2)}) %collective-permute-start.17) | collective-permute-done | bytes 65568 | tf_op jit(solution)/shard_map/ppermute | solution.py:1080
  56.0 0.0 collective-permute-done.18.section_ref
  56.0 0.7 %char_last.1 = (f32[8,16]{1,0:T(8,128)}, f32[1,16]{1,0:T(1,128)}, f32[16,768]{1,0:T(8,128)}, f32[16,256]{1,0:T(8,128)}, f32[1,16]{1,0:T(1,128)}, /*index=5*/f32[...) custom-call(bf16[128,256]{1,0:T(8,128)(2,1)S(1)} %get-tuple-element.100.near_ref, ...), custom_call_target="tpu_custom_call" | custom-call | tf_op jit(solution)/shard_map/char_last/pallas_call | solution.py:1040
  (18 shorter events, 0.1 us)
Async XLA Ops:
  0.6 16.0 %collective-permute-start.3 = (bf16[2,64,512]{2,1,0:T(8,128)(2,1)}, bf16[2,64,512]{2,1,0:T(8,128)(2,1)S(1)}, u32[]{:S(2)}, u32[]{:S(2)}) collective-permute-start(bf16[2,64,512]{2,1,0:T(8,128)(2,1)} %bitcast.15), channel_id=1, source_target_pairs={{0,8},{1,9},{2,10},{3,11},{4,12},{5,13},{6,14},{7,15},{8,0},{9,1},... | collective-permute-start | bytes 393224 | tf_op jit(solution)/shard_map/ppermute | solution.py:1080
  4.8 11.9 %copy-start.4 = (bf16[512,2048]{1,0:T(8,128)(2,1)S(1)}, bf16[512,2048]{1,0:T(8,128)(2,1)}, u32[]{:S(2)}) copy-start(bf16[512,2048]{1,0:T(8,128)(2,1)} %expand_ref.2) | copy-start | bytes 6291460
  4.8 11.9 %copy-start.5 = (bf16[2048,512]{1,0:T(8,128)(2,1)S(1)}, bf16[2048,512]{1,0:T(8,128)(2,1)}, u32[]{:S(2)}) copy-start(bf16[2048,512]{1,0:T(8,128)(2,1)} %shrink_ref.2) | copy-start | bytes 6291460
  4.8 11.9 %copy-start.6 = (bf16[512,1536]{1,0:T(8,128)(2,1)S(1)}, bf16[512,1536]{1,0:T(8,128)(2,1)}, u32[]{:S(2)}) copy-start(bf16[512,1536]{1,0:T(8,128)(2,1)} %project_ref.2) | copy-start | bytes 4718596
  4.8 11.9 %copy-start.7 = (bf16[512,512]{1,0:T(8,128)(2,1)S(1)}, bf16[512,512]{1,0:T(8,128)(2,1)}, u32[]{:S(2)}) copy-start(bf16[512,512]{1,0:T(8,128)(2,1)} %output_ref.2) | copy-start | bytes 1572868
  4.8 12.0 %copy-start.10 = (bf16[256,512]{1,0:T(8,128)(2,1)S(1)}, bf16[256,512]{1,0:T(8,128)(2,1)}, u32[]{:S(2)}) copy-start(bf16[256,512]{1,0:T(8,128)(2,1)} %input_ref.1) | copy-start | bytes 786436
  4.8 12.0 %copy-start.11 = (bf16[2,1,64,512]{3,2,1,0:T(8,128)(2,1)S(1)}, bf16[2,1,64,512]{3,2,1,0:T(8,128)(2,1)}, u32[]{:S(2)}) copy-start(bf16[2,1,64,512]{3,2,1,0:T(8,128)(2,1)} %param.35) | copy-start | bytes 393220
  4.8 12.0 %copy-start.12 = (f32[512]{0:T(512)S(1)}, f32[512]{0:T(512)}, u32[]{:S(2)}) copy-start(f32[512]{0:T(512)} %param.29) | copy-start | bytes 6148
  4.8 12.0 %copy-start.13 = (f32[512]{0:T(512)S(1)}, f32[512]{0:T(512)}, u32[]{:S(2)}) copy-start(f32[512]{0:T(512)} %param.32) | copy-start | bytes 6148
  10.2 6.2 %collective-permute-start = (bf16[64,256]{1,0:T(8,128)(2,1)S(1)}, bf16[64,256]{1,0:T(8,128)(2,1)S(1)}, u32[]{:S(2)}, u32[]{:S(2)}) collective-permute-start(bf16[64,256]{1,0:T(8,128)(2,1)S(1)} %get-tuple-element.66.own_ref), channel_id=1, source_target_pairs={{0,24},{1,25},{2,26},{3,27},{4,28},{5,29},{6,30},{7,31},{8,16},{9,... | collective-permute-start | bytes 98312 | tf_op jit(solution)/shard_map/ppermute | solution.py:1080
  11.5 4.9 %collective-permute-start.1 = (bf16[64,256]{1,0:T(8,128)(2,1)S(1)}, bf16[64,256]{1,0:T(8,128)(2,1)S(1)}, u32[]{:S(2)}, u32[]{:S(2)}) collective-permute-start(bf16[64,256]{1,0:T(8,128)(2,1)S(1)} %get-tuple-element.66.own_ref), channel_id=1, source_target_pairs={{0,16},{1,17},{2,18},{3,19},{4,20},{5,21},{6,22},{7,23},{8,24},{9,... | collective-permute-start | bytes 98312 | tf_op jit(solution)/shard_map/ppermute | solution.py:1080
  11.9 4.8 %collective-permute-start.2 = (bf16[64,256]{1,0:T(8,128)(2,1)S(1)}, bf16[64,256]{1,0:T(8,128)(2,1)S(1)}, u32[]{:S(2)}, u32[]{:S(2)}) collective-permute-start(bf16[64,256]{1,0:T(8,128)(2,1)S(1)} %get-tuple-element.66.own_ref), channel_id=1, source_target_pairs={{0,8},{1,9},{2,10},{3,11},{4,12},{5,13},{6,14},{7,15},{8,0},{9,1},... | collective-permute-start | bytes 98312 | tf_op jit(solution)/shard_map/ppermute | solution.py:1080
  14.7 8.7 %collective-permute-start.8 = (bf16[64,1024]{1,0:T(8,128)(2,1)S(1)}, bf16[64,1024]{1,0:T(8,128)(2,1)S(1)}, u32[]{:S(2)}, u32[]{:S(2)}) collective-permute-start(bf16[64,1024]{1,0:T(8,128)(2,1)S(1)} %get-tuple-element.76.hidden_sum_ref), channel_id=1, source_target_pairs={{0,16},{1,17},{2,18},{3,19},{4,20},{5,21},{6,22},{7,23},{8,24},{9,... | collective-permute-start | bytes 393224 | tf_op jit(solution)/shard_map/ppermute | solution.py:1080
  16.8 6.6 %copy-start.8 = (bf16[256,1024]{1,0:T(8,128)(2,1)S(1)}, bf16[256,1024]{1,0:T(8,128)(2,1)}, u32[]{:S(2)}) copy-start(bf16[256,1024]{1,0:T(8,128)(2,1)} %expand_ref.3) | copy-start | bytes 1572868
  16.8 6.6 %copy-start.9 = (bf16[1024,256]{1,0:T(8,128)(2,1)S(1)}, bf16[1024,256]{1,0:T(8,128)(2,1)}, u32[]{:S(2)}) copy-start(bf16[1024,256]{1,0:T(8,128)(2,1)} %shrink_ref.3) | copy-start | bytes 1572868
  16.8 6.6 %copy-start.14 = (f32[256]{0:T(256)S(1)}, f32[256]{0:T(256)}, u32[]{:S(2)}) copy-start(f32[256]{0:T(256)} %param.25) | copy-start | bytes 3076
  23.3 2.9 %collective-permute-start.4 = (bf16[4,400,256]{2,1,0:T(8,128)(2,1)S(1)}, bf16[4,400,256]{2,1,0:T(8,128)(2,1)S(1)}, u32[]{:S(2)}, u32[]{:S(2)}) collective-permute-start(bf16[4,400,256]{2,1,0:T(8,128)(2,1)S(1)} %get-tuple-element.69), channel_id=1, source_target_pairs={{0,1},{1,0},{2,3},{3,2},{4,5},{5,4},{6,7},{7,6},{8,9},{9,8},{10,11... | collective-permute-start | bytes 2457608 | tf_op jit(solution)/shard_map/ppermute | solution.py:1080
  25.6 6.5 %copy-start = (bf16[256,768]{1,0:T(8,128)(2,1)S(1)}, bf16[256,768]{1,0:T(8,128)(2,1)}, u32[]{:S(2)}) copy-start(bf16[256,768]{1,0:T(8,128)(2,1)} %project_ref.3) | copy-start | bytes 1179652
  25.6 6.4 %copy-start.1 = (bf16[256,256]{1,0:T(8,128)(2,1)S(1)}, bf16[256,256]{1,0:T(8,128)(2,1)}, u32[]{:S(2)}) copy-start(bf16[256,256]{1,0:T(8,128)(2,1)} %output_ref.3) | copy-start | bytes 393220
  25.7 6.4 %copy-start.2 = (bf16[8,256]{1,0:T(8,128)(2,1)S(1)}, bf16[8,256]{1,0:T(8,128)(2,1)}, u32[]{:S(2)}) copy-start(bf16[8,256]{1,0:T(8,128)(2,1)} %table_ref.1) | copy-start | bytes 12292
  25.7 6.4 %copy-start.3 = (f32[256]{0:T(256)S(1)}, f32[256]{0:T(256)}, u32[]{:S(2)}) copy-start(f32[256]{0:T(256)} %param.22) | copy-start | bytes 3076
  25.7 4.5 %collective-permute-start.9 = (bf16[8,112,256]{2,1,0:T(8,128)(2,1)S(1)}, bf16[8,112,256]{2,1,0:T(8,128)(2,1)S(1)}, u32[]{:S(2)}, u32[]{:S(2)}) collective-permute-start(bf16[8,112,256]{2,1,0:T(8,128)(2,1)S(1)} %get-tuple-element.81), channel_id=1, source_target_pairs={{0,1},{1,0},{2,3},{3,2},{4,5},{5,4},{6,7},{7,6},{8,9},{9,8},{10,11... | collective-permute-start | bytes 1376264 | tf_op jit(solution)/shard_map/ppermute | solution.py:1080
  26.6 14.0 %collective-permute-start.5 = (bf16[400,256]{1,0:T(8,128)(2,1)S(1)}, bf16[400,256]{1,0:T(8,128)(2,1)S(1)}, u32[]{:S(2)}, u32[]{:S(2)}) collective-permute-start(bf16[400,256]{1,0:T(8,128)(2,1)S(1)} %get-tuple-element.70), channel_id=1, source_target_pairs={{0,6},{1,7},{2,4},{3,5},{4,2},{5,3},{6,0},{7,1},{8,14},{9,15},{10,... | collective-permute-start | bytes 614408 | tf_op jit(solution)/shard_map/ppermute | solution.py:1080
  29.4 11.5 %collective-permute-start.6 = (bf16[400,256]{1,0:T(8,128)(2,1)S(1)}, bf16[400,256]{1,0:T(8,128)(2,1)S(1)}, u32[]{:S(2)}, u32[]{:S(2)}) collective-permute-start(bf16[400,256]{1,0:T(8,128)(2,1)S(1)} %get-tuple-element.71), channel_id=1, source_target_pairs={{0,4},{1,5},{2,6},{3,7},{4,0},{5,1},{6,2},{7,3},{8,12},{9,13},{10,... | collective-permute-start | bytes 614408 | tf_op jit(solution)/shard_map/ppermute | solution.py:1080
  30.2 10.7 %collective-permute-start.7 = (bf16[400,256]{1,0:T(8,128)(2,1)S(1)}, bf16[400,256]{1,0:T(8,128)(2,1)S(1)}, u32[]{:S(2)}, u32[]{:S(2)}) collective-permute-start(bf16[400,256]{1,0:T(8,128)(2,1)S(1)} %get-tuple-element.72), channel_id=1, source_target_pairs={{0,2},{1,3},{2,0},{3,1},{4,6},{5,7},{6,4},{7,5},{8,10},{9,11},{10,... | collective-permute-start | bytes 614408 | tf_op jit(solution)/shard_map/ppermute | solution.py:1080
  30.4 5.6 %collective-permute-start.10 = (bf16[8,80,128]{2,1,0:T(8,128)(2,1)S(1)}, bf16[8,80,128]{2,1,0:T(8,128)(2,1)S(1)}, u32[]{:S(2)}, u32[]{:S(2)}) collective-permute-start(bf16[8,80,128]{2,1,0:T(8,128)(2,1)S(1)} %get-tuple-element.90), channel_id=1, source_target_pairs={{0,16},{1,17},{2,18},{3,19},{4,20},{5,21},{6,22},{7,23},{8,24},{9,... | collective-permute-start | bytes 491528 | tf_op jit(solution)/shard_map/ppermute | solution.py:1080
  35.4 1.8 %collective-permute-start.11 = (bf16[384,256]{1,0:T(8,128)(2,1)S(1)}, bf16[384,256]{1,0:T(8,128)(2,1)S(1)}, u32[]{:S(2)}, u32[]{:S(2)}) collective-permute-start(bf16[384,256]{1,0:T(8,128)(2,1)S(1)} %get-tuple-element.93), channel_id=1, source_target_pairs={{0,1},{1,0},{2,3},{3,2},{4,5},{5,4},{6,7},{7,6},{8,9},{9,8},{10,11... | collective-permute-start | bytes 589832 | tf_op jit(solution)/shard_map/ppermute | solution.py:1080
  36.0 1.2 %collective-permute-start.12 = (bf16[16,256]{1,0:T(8,128)(2,1)S(1)}, bf16[16,256]{1,0:T(8,128)(2,1)S(1)}, u32[]{:S(2)}, u32[]{:S(2)}) collective-permute-start(bf16[16,256]{1,0:T(8,128)(2,1)S(1)} %get-tuple-element.94.own_extra), channel_id=1, source_target_pairs={{0,1},{1,0},{2,3},{3,2},{4,5},{5,4},{6,7},{7,6},{8,9},{9,8},{10,11... | collective-permute-start | bytes 24584 | tf_op jit(solution)/shard_map/ppermute | solution.py:1080
  37.3 7.3 %collective-permute-start.13 = (bf16[256,256]{1,0:T(8,128)(2,1)S(1)}, bf16[256,256]{1,0:T(8,128)(2,1)S(1)}, u32[]{:S(2)}, u32[]{:S(2)}) collective-permute-start(bf16[256,256]{1,0:T(8,128)(2,1)S(1)} %get-tuple-element.95), channel_id=1, source_target_pairs={{0,6},{1,7},{2,4},{3,5},{4,2},{5,3},{6,0},{7,1},{8,14},{9,15},{10,... | collective-permute-start | bytes 393224 | tf_op jit(solution)/shard_map/ppermute | solution.py:1080
  39.8 7.2 %collective-permute-start.14 = (bf16[256,256]{1,0:T(8,128)(2,1)S(1)}, bf16[256,256]{1,0:T(8,128)(2,1)S(1)}, u32[]{:S(2)}, u32[]{:S(2)}) collective-permute-start(bf16[256,256]{1,0:T(8,128)(2,1)S(1)} %get-tuple-element.96), channel_id=1, source_target_pairs={{0,4},{1,5},{2,6},{3,7},{4,0},{5,1},{6,2},{7,3},{8,12},{9,13},{10,... | collective-permute-start | bytes 393224 | tf_op jit(solution)/shard_map/ppermute | solution.py:1080
  40.6 6.4 %collective-permute-start.15 = (bf16[256,256]{1,0:T(8,128)(2,1)S(1)}, bf16[256,256]{1,0:T(8,128)(2,1)S(1)}, u32[]{:S(2)}, u32[]{:S(2)}) collective-permute-start(bf16[256,256]{1,0:T(8,128)(2,1)S(1)} %get-tuple-element.97), channel_id=1, source_target_pairs={{0,2},{1,3},{2,0},{3,1},{4,6},{5,7},{6,4},{7,5},{8,10},{9,11},{10,... | collective-permute-start | bytes 393224 | tf_op jit(solution)/shard_map/ppermute | solution.py:1080
  41.9 9.7 %collective-permute-start.19 = (bf16[400,256]{1,0:T(8,128)(2,1)S(1)}, bf16[400,256]{1,0:T(8,128)(2,1)S(1)}, u32[]{:S(2)}, u32[]{:S(2)}) collective-permute-start(bf16[400,256]{1,0:T(8,128)(2,1)S(1)} %get-tuple-element.99.refs_4_.own_ref), channel_id=1, source_target_pairs={{0,16},{1,17},{2,18},{3,19},{4,20},{5,21},{6,22},{7,23},{8,24},{9,... | collective-permute-start | bytes 614408 | tf_op jit(solution)/shard_map/ppermute | solution.py:1080
  47.1 7.3 %collective-permute-start.16 = (bf16[128,256]{1,0:T(8,128)(2,1)S(1)}, bf16[128,256]{1,0:T(8,128)(2,1)S(1)}, u32[]{:S(2)}, u32[]{:S(2)}) collective-permute-start(bf16[128,256]{1,0:T(8,128)(2,1)S(1)} %get-tuple-element.101), channel_id=1, source_target_pairs={{0,24},{1,25},{2,26},{3,27},{4,28},{5,29},{6,30},{7,31},{8,16},{9,... | collective-permute-start | bytes 196616 | tf_op jit(solution)/shard_map/ppermute | solution.py:1080
  50.4 5.6 %collective-permute-start.17 = (bf16[128,256]{1,0:T(8,128)(2,1)S(1)}, bf16[128,256]{1,0:T(8,128)(2,1)S(1)}, u32[]{:S(2)}, u32[]{:S(2)}) collective-permute-start(bf16[128,256]{1,0:T(8,128)(2,1)S(1)} %get-tuple-element.101), channel_id=1, source_target_pairs={{0,8},{1,9},{2,10},{3,11},{4,12},{5,13},{6,14},{7,15},{8,0},{9,1},... | collective-permute-start | bytes 196616 | tf_op jit(solution)/shard_map/ppermute | solution.py:1080
  50.6 5.4 %collective-permute-start.18 = (bf16[128,256]{1,0:T(8,128)(2,1)S(1)}, bf16[128,256]{1,0:T(8,128)(2,1)S(1)}, u32[]{:S(2)}, u32[]{:S(2)}) collective-permute-start(bf16[128,256]{1,0:T(8,128)(2,1)S(1)} %get-tuple-element.100.near_ref), channel_id=1, source_target_pairs={{0,16},{1,17},{2,18},{3,19},{4,20},{5,21},{6,22},{7,23},{8,24},{9,... | collective-permute-start | bytes 196616 | tf_op jit(solution)/shard_map/ppermute | solution.py:1080
